TPU v7x, 32 devices: a whole 2x2x4 slice. The times are simulated.
32 devices in a mesh: ctx: 8 (over z, y), head: 4 (over x, core).
Axes of the slice: x: 2, y: 2, z: 4, core: 2. Of those that a mesh axis runs over, the one named last changes fastest.
Arguments:
- tokens: bfloat16 [2, 2048, 2048], P(None, 'ctx'), may hold values from -6 to 6, as said below
- cotangent: bfloat16 [2, 2048, 2048], P(None, 'ctx'), may hold values from -6 to 6, as said below
- lengths: int32 [2, 2], replicated, may hold values from 1 to 31, as said below
- norm_in: bfloat16 [2048], P('ctx'), may hold values from 0.5 to 1.5
- w_query: bfloat16 [2048, 1024], P('ctx', 'head'), may hold values from -0.125 to 0.125
- w_key: bfloat16 [2048, 1024], P('ctx', 'head'), may hold values from -0.125 to 0.125
- w_value: bfloat16 [2048, 2048], P('ctx', 'head'), may hold values from -0.125 to 0.125
- w_outgate: bfloat16 [2048, 2048], P('ctx', 'head'), may hold values from -0.125 to 0.125
- w_rank: bfloat16 [2048, 16], P('ctx'), may hold values from -0.125 to 0.125
- w_decay: bfloat16 [4, 16, 256], P('head', None, 'ctx'), may hold values from -1.5 to 1.5
- decay_bias: bfloat16 [4, 256], P('head', 'ctx'), may hold values from -3 to 6
- head_gain: bfloat16 [512], P('ctx'), may hold values from 0.5 to 1.5
- w_out: bfloat16 [2048, 2048], P('head', 'ctx'), may hold values from -0.25 to 0.25
- norm_mid: bfloat16 [2048], P('ctx'), may hold values from 0.5 to 1.5
- w_gate: bfloat16 [2048, 5632], P('ctx', 'head'), may hold values from -0.125 to 0.125
- w_up: bfloat16 [2048, 5632], P('ctx', 'head'), may hold values from -0.125 to 0.125
- w_down: bfloat16 [5632, 2048], P('head', 'ctx'), may hold values from -0.15625 to 0.15625
Outputs:
- block_out: bfloat16 [2, 2048, 2048], P(None, 'ctx')
- input_grad: float32 [2, 2048, 2048], P(None, 'ctx')
- grad_norm_in: float32 [2048], P('ctx')
- grad_query: float32 [2048, 1024], P('ctx', 'head')
- grad_key: float32 [2048, 1024], P('ctx', 'head')
- grad_value: float32 [2048, 2048], P('ctx', 'head')
- grad_outgate: float32 [2048, 2048], P('ctx', 'head')
- grad_rank: float32 [2048, 16], P('ctx')
- grad_decay: float32 [4, 16, 256], P('head', None, 'ctx')
- grad_bias: float32 [4, 256], P('head', 'ctx')
- grad_head_gain: float32 [512], P('ctx')
- grad_out: float32 [2048, 2048], P('head', 'ctx')
- grad_norm_mid: float32 [2048], P('ctx')
- grad_gate: float32 [2048, 5632], P('ctx', 'head')
- grad_up: float32 [2048, 5632], P('ctx', 'head')
- grad_down: float32 [5632, 2048], P('head', 'ctx')
Inputs may be any that keep to these rules, and one draw needn't show every extreme that they name: Each micro-batch packs its sequences in order from slot 0, each lengths * 64 slots long, all together at most 2048 slots; the slots after the last sequence are padding. In every micro-batch one sequence has slots on the first and on the last index of ctx. `tokens`: independent entries of mean 0 and deviation 1. `cotangent`: independent entries of mean 0 and deviation 1.
All inputs are finite; a program needn't handle non-finite values.
Results may differ from a plain program's by a relative error of at most 0.025.
Values may be sent and summed in bfloat16 or wider, within the bound.
No kernel may reach another device: no remote copies, remote signals or barrier semaphores. Data moves between devices by JAX's collectives and lax.ppermute only.
A program may use at most 192 MiB of HBM per device.

v0:
```python
import jax
import jax.numpy as jnp
from jax import lax
from jax.sharding import PartitionSpec as P

GROUP = 64


EPS = 1e-06
HIGH = lax.Precision.HIGHEST


def carried_in(value, axis, join, neutral):
    count, mine = (lax.axis_size(axis), lax.axis_index(axis))
    pieces = jax.tree.map(lambda part: lax.all_gather(part, axis), value)
    subtotal = jax.tree.map(
        lambda part, zero: jnp.full_like(part, 0) + jnp.asarray(zero, part.dtype), value, neutral
    )

    def carried_lap(position, subtotal):
        longer = join(subtotal, jax.tree.map(lambda part: part[position], pieces))
        return jax.tree.map(lambda new, old: jnp.where(position < mine, new, old), longer, subtotal)

    return lax.fori_loop(0, count - 1, carried_lap, subtotal)


def entering(array, axis, combine, identity):
    count, place = (lax.axis_size(axis), lax.axis_index(axis))
    everything = jax.tree.map(
        lambda part, kind: lax.all_gather(part.astype(kind), axis),
        array,
        jax.tree.map(lambda a: jnp.bfloat16 if a.dtype == jnp.float32 else a.dtype, array),
    )
    start = jax.tree.map(
        lambda part, zero: jnp.broadcast_to(jnp.asarray(zero, part.dtype), part.shape),
        array,
        identity,
    )

    def entering_lap(k, before):
        at = count - 1 - k
        reached = at > place
        new = combine(
            before, jax.tree.map(lambda part, own: part[at].astype(own.dtype), everything, array)
        )
        return jax.tree.map(lambda a, b: jnp.where(reached, a, b), new, before)

    return lax.fori_loop(0, count, entering_lap, start)


def rms_norm(value, gain):
    return value * lax.rsqrt(jnp.mean(value * value, axis=-1, keepdims=True) + EPS) * gain


def times_trans(left, right):
    return lax.dot_general(
        left, right, (((1,), (1,)), ((), ())), preferred_element_type=jnp.float32
    )


def inner_rows(left, right):
    return lax.dot_general(
        left, right, (((0,), (0,)), ((), ())), preferred_element_type=jnp.float32
    )


def project(left, right):
    return jnp.dot(left, right, preferred_element_type=jnp.float32)


def combine(earlier, later):
    return (earlier[0] * later[0], later[0][..., :, None] * earlier[1] + later[1])


def gated_head(mixed_out, outgate, gain_head):
    return rms_norm(mixed_out, gain_head) * jax.nn.silu(outgate)


def swiglu(gate_proj, up_proj):
    return jax.nn.silu(gate_proj) * up_proj


def decay_of(logits):
    return jax.nn.log_sigmoid(logits) / 16.0


def fetch_weights(shards):
    return (
        lax.all_gather(shards[0], "ctx", axis=0, tiled=True),
        lax.all_gather(shards[1], "ctx", axis=0, tiled=True),
        lax.all_gather(shards[2], "ctx", axis=0, tiled=True),
        lax.all_gather(shards[3], "ctx", axis=0, tiled=True),
        lax.all_gather(shards[4], "ctx", axis=0, tiled=True),
        lax.all_gather(shards[5], "ctx", axis=0, tiled=True),
        lax.all_gather(shards[6], "ctx", axis=2, tiled=True),
        lax.all_gather(shards[7], "ctx", axis=1, tiled=True),
        lax.all_gather(shards[8], "ctx", axis=0, tiled=True),
        lax.all_gather(shards[9], "ctx", axis=1, tiled=True),
        lax.all_gather(shards[10], "ctx", axis=0, tiled=True),
        lax.all_gather(shards[11], "ctx", axis=0, tiled=True),
        lax.all_gather(shards[12], "ctx", axis=0, tiled=True),
        lax.all_gather(shards[13], "ctx", axis=1, tiled=True),
    )


def chain_parts(key_rows, values, decays, resets):
    cumulative = jnp.cumsum(decays, axis=1)
    last_cum = cumulative[:, -1, :]
    carried = key_rows * jnp.exp(last_cum[:, None, :] - cumulative)
    update = jnp.einsum("nsd,nse->nde", carried, values, precision=HIGH)
    return (jnp.exp(last_cum) * (1.0 - resets)[:, None], update)


def group_apply(queries, key_rows, values, decays, prior_state):
    score_scale = queries.shape[-1] ** (-0.5)
    width = queries.shape[1]
    cumulative = jnp.cumsum(decays, axis=1)
    last_cum = cumulative[:, -1, :]
    causal = (jnp.arange(width)[:, None] >= jnp.arange(width)[None, :]).astype(jnp.float32)
    inter_part = jnp.einsum(
        "ncd,nde->nce", queries * jnp.exp(cumulative) * score_scale, prior_state, precision=HIGH
    )
    pair_decay = jnp.exp(cumulative[:, :, None, :] - cumulative[:, None, :, :])
    scores = jnp.einsum("ntd,nsd,ntsd->nts", queries, key_rows, pair_decay, precision=HIGH) * (
        score_scale * causal
    )
    intra_part = jnp.einsum("nts,nse->nte", scores, values, precision=HIGH)
    carried = key_rows * jnp.exp(last_cum[:, None, :] - cumulative)
    new_state = jnp.exp(last_cum)[:, :, None] * prior_state + jnp.einsum(
        "nsd,nse->nde", carried, values, precision=HIGH
    )
    return (inter_part + intra_part, new_state)


def layout(lengths_row, group_ids, slot_ids):
    ends = jnp.cumsum(lengths_row)
    starts = jnp.concatenate([jnp.zeros((1,), jnp.int32), ends])
    resets = jnp.any(group_ids[:, None] == starts[None, :], axis=1).astype(jnp.float32)
    slot_mask = (slot_ids < ends[-1] * GROUP).astype(jnp.float32)
    return (resets, slot_mask)


def per_device(
    tokens,
    cotangent,
    lengths,
    norm_in,
    w_query,
    w_key,
    w_value,
    w_outgate,
    w_rank,
    w_decay,
    decay_bias,
    head_gain,
    w_out,
    norm_mid,
    w_gate,
    w_up,
    w_down,
):
    shards = (
        norm_in,
        w_query,
        w_key,
        w_value,
        w_outgate,
        w_rank,
        w_decay,
        decay_bias,
        head_gain,
        w_out,
        norm_mid,
        w_gate,
        w_up,
        w_down,
    )
    micro_count = tokens.shape[0]
    slot_rows = tokens.shape[1]
    group_count = slot_rows // GROUP
    place = lax.axis_index("ctx")
    slot_ids = place * slot_rows + jnp.arange(slot_rows, dtype=jnp.int32)
    group_ids = place * group_count + jnp.arange(group_count, dtype=jnp.int32)
    f32 = jnp.float32
    bf16 = jnp.bfloat16
    outputs = []
    input_grads = []
    totals = None
    for batch_index in range(micro_count):
        gathered = fetch_weights(shards)
        (
            gain_in,
            full_query,
            full_key,
            full_value,
            full_outgate,
            full_rank,
            full_decay,
            full_bias,
            gain_head,
            full_out,
            gain_mid,
            full_gate,
            full_up,
            full_down,
        ) = gathered
        gain_in = gain_in.astype(f32)
        gain_head = gain_head.astype(f32)
        gain_mid = gain_mid.astype(f32)
        inputs = tokens[batch_index].astype(f32)
        resets, slot_mask = layout(lengths[batch_index], group_ids, slot_ids)
        normed_in = rms_norm(inputs, gain_in).astype(bf16)
        queries = project(normed_in, full_query).astype(bf16)
        key_rows = project(normed_in, full_key).astype(bf16)
        values = project(normed_in, full_value).astype(bf16)
        outgate = project(normed_in, full_outgate).astype(bf16)
        low_rank = project(normed_in, full_rank).astype(bf16)
        logits = project(low_rank, full_decay[0]) + full_bias[0].astype(f32)
        decays = decay_of(logits)
        query_blocks = queries.astype(f32).reshape(group_count, GROUP, -1)
        key_blocks = key_rows.astype(f32).reshape(group_count, GROUP, -1)
        value_blocks = values.astype(f32).reshape(group_count, GROUP, -1)
        decay_blocks = decays.reshape(group_count, GROUP, -1)
        keep, update = chain_parts(key_blocks, value_blocks, decay_blocks, resets)
        prefix_keep, prefix_update = lax.associative_scan(combine, (keep, update))
        ones_keep = jnp.ones_like(keep[0])
        zero_state = jnp.zeros_like(update[0])
        enter_keep, enter_state = carried_in(
            (prefix_keep[-1], prefix_update[-1]), "ctx", combine, (ones_keep, zero_state)
        )
        before_keep = jnp.concatenate([jnp.ones_like(keep[:1]), prefix_keep[:-1]])
        before_update = jnp.concatenate([jnp.zeros_like(update[:1]), prefix_update[:-1]])
        prior_state = (before_keep[:, :, None] * enter_state[None] + before_update) * (
            1.0 - resets
        )[:, None, None]
        mixed_out = group_apply(query_blocks, key_blocks, value_blocks, decay_blocks, prior_state)[
            0
        ]
        mixed_out = mixed_out.reshape(slot_rows, -1)
        outgate_f = outgate.astype(f32)
        gated_out = gated_head(mixed_out, outgate_f, gain_head).astype(bf16)
        attention = lax.psum(project(gated_out, full_out).astype(jnp.bfloat16), "head").astype(
            jnp.float32
        )
        residual = inputs + attention
        normed_mid = rms_norm(residual, gain_mid).astype(bf16)
        gate_proj = project(normed_mid, full_gate)
        up_proj = project(normed_mid, full_up)
        hidden = swiglu(gate_proj, up_proj).astype(bf16)
        feed = lax.psum(project(hidden, full_down).astype(jnp.bfloat16), "head").astype(jnp.float32)
        outputs.append((residual + feed).astype(bf16))
        regathered = (
            lax.all_gather(shards[0], "ctx", axis=0, tiled=True),
            lax.all_gather(shards[1], "ctx", axis=0, tiled=True),
            lax.all_gather(shards[2], "ctx", axis=0, tiled=True),
            lax.all_gather(shards[3], "ctx", axis=0, tiled=True),
            lax.all_gather(shards[4], "ctx", axis=0, tiled=True),
            lax.all_gather(shards[5], "ctx", axis=0, tiled=True),
            lax.all_gather(shards[6], "ctx", axis=2, tiled=True),
            lax.all_gather(shards[7], "ctx", axis=1, tiled=True),
            lax.all_gather(shards[8], "ctx", axis=0, tiled=True),
            lax.all_gather(shards[9], "ctx", axis=1, tiled=True),
            lax.all_gather(shards[10], "ctx", axis=0, tiled=True),
            lax.all_gather(shards[11], "ctx", axis=0, tiled=True),
            lax.all_gather(shards[12], "ctx", axis=0, tiled=True),
            lax.all_gather(shards[13], "ctx", axis=1, tiled=True),
        )
        (
            back_gain_in,
            back_query,
            back_key,
            back_value,
            back_outgate,
            back_rank,
            back_decay,
            back_bias,
            back_gain_head,
            back_out,
            back_gain_mid,
            back_gate,
            back_up,
            back_down,
        ) = regathered
        out_grad = cotangent[batch_index].astype(f32) * slot_mask[:, None]
        out_low = out_grad.astype(bf16)
        hidden_grad = times_trans(out_low, back_down)
        grad_down = inner_rows(hidden, out_low)
        _, swiglu_back = jax.vjp(swiglu, gate_proj, up_proj)
        gate_grad, up_grad = swiglu_back(hidden_grad)
        gate_low = gate_grad.astype(bf16)
        up_low = up_grad.astype(bf16)
        grad_gate = inner_rows(normed_mid, gate_low)
        grad_up = inner_rows(normed_mid, up_low)
        mid_part = times_trans(gate_low, back_gate) + times_trans(up_low, back_up)
        mid_grad = lax.psum(mid_part.astype(jnp.bfloat16), "head").astype(jnp.float32)
        _, mid_back = jax.vjp(rms_norm, residual, back_gain_mid.astype(f32))
        resid_norm_grad, grad_gain_mid = mid_back(mid_grad)
        resid_grad = out_grad + resid_norm_grad
        resid_low = resid_grad.astype(bf16)
        grad_out = inner_rows(gated_out, resid_low)
        gated_grad = times_trans(resid_low, back_out)
        _, head_back = jax.vjp(gated_head, mixed_out, outgate_f, back_gain_head.astype(f32))
        mixed_grad, outgate_grad, head_gain_part = head_back(gated_grad)
        mixed_blocks_grad = mixed_grad.reshape(group_count, GROUP, -1)
        score_scale = query_blocks.shape[-1] ** (-0.5)
        scaled_queries = query_blocks * jnp.exp(jnp.cumsum(decay_blocks, axis=1)) * score_scale
        carry_in = jnp.einsum("ncd,nce->nde", scaled_queries, mixed_blocks_grad, precision=HIGH)
        carry_in = carry_in * (1.0 - resets)[:, None, None]
        suffix_keep, suffix_grad = lax.associative_scan(combine, (keep, carry_in), reverse=True)
        exit_keep, exit_grad = entering(
            (suffix_keep[0], suffix_grad[0]), "ctx", combine, (ones_keep, zero_state)
        )
        after_keep = jnp.concatenate([suffix_keep[1:], jnp.ones_like(keep[:1])])
        after_grad = jnp.concatenate([suffix_grad[1:], jnp.zeros_like(carry_in[:1])])
        state_grad = after_keep[:, :, None] * exit_grad[None] + after_grad
        _, group_back = jax.vjp(
            group_apply, query_blocks, key_blocks, value_blocks, decay_blocks, prior_state
        )
        query_grad, key_grad, value_grad, decay_grad, _ = group_back(
            (mixed_blocks_grad, state_grad)
        )
        _, logit_back = jax.vjp(decay_of, logits)
        logit_low = logit_back(decay_grad.reshape(slot_rows, -1))[0].astype(bf16)
        grad_bias = jnp.sum(logit_low.astype(f32), axis=0)[None]
        grad_decay = inner_rows(low_rank, logit_low)[None]
        rank_part = times_trans(logit_low, back_decay[0])
        query_low = query_grad.reshape(slot_rows, -1).astype(bf16)
        key_low = key_grad.reshape(slot_rows, -1).astype(bf16)
        value_low = value_grad.reshape(slot_rows, -1).astype(bf16)
        outgate_low = outgate_grad.astype(bf16)
        in_part = (
            times_trans(query_low, back_query)
            + times_trans(key_low, back_key)
            + times_trans(value_low, back_value)
            + times_trans(outgate_low, back_outgate)
        )
        in_sum, rank_sum, head_gain_grad = (
            lax.psum(in_part.astype(jnp.bfloat16), "head").astype(jnp.float32),
            lax.psum(rank_part.astype(jnp.bfloat16), "head").astype(jnp.float32),
            lax.psum(head_gain_part.astype(jnp.bfloat16), "head").astype(jnp.float32),
        )
        rank_low = rank_sum.astype(bf16)
        grad_rank = inner_rows(normed_in, rank_low)
        in_grad = in_sum + times_trans(rank_low, back_rank)
        _, in_back = jax.vjp(rms_norm, inputs, back_gain_in.astype(f32))
        input_norm_grad, grad_gain_in = in_back(in_grad)
        input_grads.append(resid_grad + input_norm_grad)
        step_grads = (
            grad_gain_in,
            inner_rows(normed_in, query_low),
            inner_rows(normed_in, key_low),
            inner_rows(normed_in, value_low),
            inner_rows(normed_in, outgate_low),
            grad_rank,
            grad_decay,
            grad_bias,
            head_gain_grad,
            grad_out,
            grad_gain_mid,
            grad_gate,
            grad_up,
            grad_down,
        )
        if totals is None:
            totals = step_grads
        else:
            totals = tuple((total + grad_term for total, grad_term in zip(totals, step_grads)))
    reduced = (
        lax.psum_scatter(
            totals[0].astype(jnp.bfloat16), "ctx", scatter_dimension=0, tiled=True
        ).astype(jnp.float32),
        lax.psum_scatter(
            totals[1].astype(jnp.bfloat16), "ctx", scatter_dimension=0, tiled=True
        ).astype(jnp.float32),
        lax.psum_scatter(
            totals[2].astype(jnp.bfloat16), "ctx", scatter_dimension=0, tiled=True
        ).astype(jnp.float32),
        lax.psum_scatter(
            totals[3].astype(jnp.bfloat16), "ctx", scatter_dimension=0, tiled=True
        ).astype(jnp.float32),
        lax.psum_scatter(
            totals[4].astype(jnp.bfloat16), "ctx", scatter_dimension=0, tiled=True
        ).astype(jnp.float32),
        lax.psum_scatter(
            totals[5].astype(jnp.bfloat16), "ctx", scatter_dimension=0, tiled=True
        ).astype(jnp.float32),
        lax.psum_scatter(
            totals[6].astype(jnp.bfloat16), "ctx", scatter_dimension=2, tiled=True
        ).astype(jnp.float32),
        lax.psum_scatter(
            totals[7].astype(jnp.bfloat16), "ctx", scatter_dimension=1, tiled=True
        ).astype(jnp.float32),
        lax.psum_scatter(
            totals[8].astype(jnp.bfloat16), "ctx", scatter_dimension=0, tiled=True
        ).astype(jnp.float32),
        lax.psum_scatter(
            totals[9].astype(jnp.bfloat16), "ctx", scatter_dimension=1, tiled=True
        ).astype(jnp.float32),
        lax.psum_scatter(
            totals[10].astype(jnp.bfloat16), "ctx", scatter_dimension=0, tiled=True
        ).astype(jnp.float32),
        lax.psum_scatter(
            totals[11].astype(jnp.bfloat16), "ctx", scatter_dimension=0, tiled=True
        ).astype(jnp.float32),
        lax.psum_scatter(
            totals[12].astype(jnp.bfloat16), "ctx", scatter_dimension=0, tiled=True
        ).astype(jnp.float32),
        lax.psum_scatter(
            totals[13].astype(jnp.bfloat16), "ctx", scatter_dimension=1, tiled=True
        ).astype(jnp.float32),
    )
    return (
        jnp.stack(outputs),
        jnp.stack(input_grads),
        reduced[0],
        reduced[1],
        reduced[2],
        reduced[3],
        reduced[4],
        reduced[5],
        reduced[6],
        reduced[7],
        reduced[8],
        reduced[9],
        reduced[10],
        reduced[11],
        reduced[12],
        reduced[13],
    )


def solution(mesh):
    in_specs = (
        P(None, "ctx", None),
        P(None, "ctx", None),
        P(),
        P("ctx"),
        P("ctx", "head"),
        P("ctx", "head"),
        P("ctx", "head"),
        P("ctx", "head"),
        P("ctx", None),
        P("head", None, "ctx"),
        P("head", "ctx"),
        P("ctx"),
        P("head", "ctx"),
        P("ctx"),
        P("ctx", "head"),
        P("ctx", "head"),
        P("head", "ctx"),
    )
    out_specs = (
        P(None, "ctx", None),
        P(None, "ctx", None),
        P("ctx"),
        P("ctx", "head"),
        P("ctx", "head"),
        P("ctx", "head"),
        P("ctx", "head"),
        P("ctx", None),
        P("head", None, "ctx"),
        P("head", "ctx"),
        P("ctx"),
        P("head", "ctx"),
        P("ctx"),
        P("ctx", "head"),
        P("ctx", "head"),
        P("head", "ctx"),
    )
    return jax.shard_map(
        per_device, mesh=mesh, in_specs=in_specs, out_specs=out_specs, check_vma=False
    )
```

profile of v0, /device:TPU:0, one launch (start us, length us, event | category | flops | bytes accessed | tf_op | source)
XLA Modules:
  0.0 1994.4 jit_solution(11948037655227560373)
XLA Ops:
  10.8 22.3 %all-gather = bf16[8,1,256]{2,1,0:T(2,128)(2,1)S(1)} all-gather(bf16[1,1,256]{2,1,0:T(2,128)(2,1)S(1)} %reshape.547), channel_id=1, replica_groups=mesh['ctx'=8,'head'=4] {'ctx'}, dimensions={0}, use_global_device_ids=true | all-gather | bytes 4608 | tf_op jit(solution)/shard_map/all_gather | solution.py:89
  38.1 17.9 all-reduce.48
  55.9 30.7 %all_gather.46 = bf16[2048,16]{0,1:T(8,128)(2,1)S(1)} all-gather(bf16[256,16]{0,1:T(8,128)(2,1)S(1)} %copy-done.182), channel_id=1, replica_groups=mesh['ctx'=8,'head'=4] {'ctx'}, dimensions={0}, use_global_device_ids=true | all-gather | bytes 73728 | tf_op jit(solution)/shard_map/all_gather | solution.py:94
  86.8 30.8 %all_gather.47 = bf16[1,16,256]{1,0,2:T(2,128)(2,1)S(1)} all-gather(bf16[1,16,32]{1,0,2:T(2,128)(2,1)S(1)} %copy.42), channel_id=1, replica_groups=mesh['ctx'=8,'head'=4] {'ctx'}, dimensions={2}, use_global_device_ids=true | all-gather | bytes 9216 | tf_op jit(solution)/shard_map/all_gather | solution.py:95
  179.2 18.5 all-gather.1
  202.7 17.3 all-gather.3
  233.2 4.2 fusion.10
  237.5 4.2 fusion.8
  248.4 3.5 slice_add_fusion.14
  259.0 11.7 all-gather.25.cloned.1.call-done
  270.7 13.3 while.60
  284.0 4.1 multiply_reduce_fusion.7
  290.1 54.9 %all-gather.37.cloned.1.call-done = f32[8,256,512]{2,1,0:T(8,128)} async-done(((f32[1,256,512]{2,1,0:T(8,128)}), f32[8,256,512]{2,1,0:T(8,128)}) %all-gather.37.cloned.1.call-update) | async-done | bytes 4194320 | tf_op jit(solution)/shard_map/all_gather | solution.py:15
  345.0 13.3 while.61
  358.3 4.2 multiply_reduce_fusion.6
  364.3 3.8 multiply_convert_fusion.7
  368.2 28.2 %all-gather.29.cloned.1.call-done = bf16[512,2048]{1,0:T(8,128)(2,1)} async-done(((bf16[512,256]{1,0:T(8,128)(2,1)}), bf16[512,2048]{1,0:T(8,128)(2,1)}) %all-gather.29.cloned.1.call-update) | async-done | bytes 2097168 | tf_op jit(solution)/shard_map/all_gather | solution.py:98
  396.4 3.5 convolution_convert_fusion
  405.5 18.1 all-gather.2
  426.0 25.5 %all-reduce.61.cloned.1.call-done = (bf16[256,2048]{1,0:T(8,128)(2,1)}, bf16[256,2048]{1,0:T(8,128)(2,1)}) async-done(((bf16[256,2048]{1,0:T(8,128)(2,1)}, bf16[256,2048]{1,0:T(8,128)(2,1)}), (bf16[256,2048]{1,0:T(8,128)(2,1)}, bf16[256,2048]{1,0:T(8,128)(2,1)})) %all-reduce.61.cloned.1.call-update) | async-done | bytes 2097168 | tf_op jit(solution)/shard_map/psum | solution.py:242
  457.6 89.1 %all-gather.31.cloned.1.call-done = bf16[2048,1408]{1,0:T(8,128)(2,1)} async-done(((bf16[256,1408]{1,0:T(8,128)(2,1)}), bf16[2048,1408]{1,0:T(8,128)(2,1)}) %all-gather.31.cloned.1.call-update) | async-done | bytes 5767184 | tf_op jit(solution)/shard_map/all_gather | solution.py:100
  546.7 5.9 fusion.284
  552.6 87.3 %all-gather.33.cloned.1.call-done = bf16[2048,1408]{1,0:T(8,128)(2,1)} async-done(((bf16[256,1408]{1,0:T(8,128)(2,1)}), bf16[2048,1408]{1,0:T(8,128)(2,1)}) %all-gather.33.cloned.1.call-update) | async-done | bytes 5767184 | tf_op jit(solution)/shard_map/all_gather | solution.py:101
  639.8 6.0 fusion.285
  651.7 82.2 %all-gather.35.cloned.1.call-done = bf16[1408,2048]{1,0:T(8,128)(2,1)} async-done(((bf16[1408,256]{1,0:T(8,128)(2,1)}), bf16[1408,2048]{1,0:T(8,128)(2,1)}) %all-gather.35.cloned.1.call-update) | async-done | bytes 5767184 | tf_op jit(solution)/shard_map/all_gather | solution.py:102
  733.9 7.1 multiply_convert_fusion.2
  741.9 4.6 fusion.288
  761.7 18.0 all-gather.5
  787.3 17.0 all-gather.4
  812.0 4.7 fusion.49
  854.8 3.7 pad.320
  878.0 5.3 fusion.4
  883.3 5.8 fusion.5
  889.1 4.4 fusion.6
  893.4 5.6 fusion.7
  899.1 6.4 fusion.14
  905.5 6.4 fusion.17
  912.0 3.8 fusion.260
  915.8 21.7 %while.63 = (s32[]{:T(128)}, f32[256,512]{1,0:T(8,128)}, s32[]{:T(128)}, bf16[8,256]{1,0:T(8,128)(2,1)}, bf16[8,256,512]{2,1,0:T(8,128)(2,1)}, /*index=5*/s32[]{:T(128)}, s32[]{:T(128)}, s32[]{:T(128)}, s32[]{:T(128)}) while((s32[]{:T(128)}, f32[256,512]{1,0:T(8,128)}, s32[]{:T(128)}, bf16[8,256]{1,0:T(8,128)(2,1)}, ...), condition=%wide.region_37.39_spmd.clone, body=%wide.region_36.38_spmd.clone.sunk | while | flops 655624 | bytes 1313455 | solution.py:48
  943.7 20.2 %all-gather.39.cloned.1.call-done = bf16[8,256,512]{2,1,0:T(8,128)(2,1)} async-done(((bf16[1,256,512]{2,1,0:T(8,128)(2,1)}), bf16[8,256,512]{2,1,0:T(8,128)(2,1)}) %all-gather.39.cloned.1.call-update) | async-done | bytes 2097168 | tf_op jit(solution)/shard_map/all_gather | solution.py:30
  963.9 21.9 %while.62 = (s32[]{:T(128)}, f32[256,512]{1,0:T(8,128)}, s32[]{:T(128)}, bf16[8,256]{1,0:T(8,128)(2,1)}, bf16[8,256,512]{2,1,0:T(8,128)(2,1)}, /*index=5*/s32[]{:T(128)}, s32[]{:T(128)}, s32[]{:T(128)}, s32[]{:T(128)}) while((s32[]{:T(128)}, f32[256,512]{1,0:T(8,128)}, s32[]{:T(128)}, bf16[8,256]{1,0:T(8,128)(2,1)}, ...), condition=%wide.region_24.25_spmd.clone, body=%wide.region_23.24_spmd.clone.sunk | while | flops 655624 | bytes 1313455 | solution.py:48
  994.7 4.0 reduce_window_sum.52
  1005.1 5.0 fusion.167
  1010.1 3.9 reduce_window_sum.53
  1017.1 11.4 all-reduce.49
  1034.3 4.4 add_convert_fusion.4
  1047.5 5.7 convolution_convert_fusion.2
  1053.3 5.6 convolution_convert_fusion.3
  1088.1 4.3 add_convert_fusion.2
  1095.8 4.4 add_convert_fusion.1
  1104.5 4.3 add_convert_fusion
  1111.5 42.8 %reduce-scatter.34.cloned.1.call-done = bf16[32,16]{1,0:T(8,128)(2,1)} async-done(((bf16[256,16]{1,0:T(8,128)(2,1)}), bf16[32,16]{1,0:T(8,128)(2,1)}) %reduce-scatter.34.cloned.1.call-update) | async-done | bytes 1040
  1155.7 54.9 %reduce-scatter.24.cloned.1.call-done = bf16[256,16]{0,1:T(8,128)(2,1)} async-done(((bf16[2048,16]{0,1:T(8,128)(2,1)}), bf16[256,16]{0,1:T(8,128)(2,1)}) %reduce-scatter.24.cloned.1.call-update) | async-done | bytes 8208 | tf_op jit(solution)/shard_map/reduce_scatter | solution.py:384
  1211.9 68.8 %reduce-scatter.22.cloned.1.call-done = bf16[256,512]{1,0:T(8,128)(2,1)} async-done(((bf16[2048,512]{1,0:T(8,128)(2,1)}), bf16[256,512]{1,0:T(8,128)(2,1)}) %reduce-scatter.22.cloned.1.call-update) | async-done | bytes 262160 | tf_op jit(solution)/shard_map/reduce_scatter | solution.py:381
  1282.5 69.7 %reduce-scatter.26.cloned.1.call-done = bf16[512,256]{1,0:T(8,128)(2,1)} async-done(((bf16[512,2048]{1,0:T(8,128)(2,1)}), bf16[512,256]{1,0:T(8,128)(2,1)}) %reduce-scatter.26.cloned.1.call-update) | async-done | bytes 262160 | tf_op jit(solution)/shard_map/reduce_scatter | solution.py:396
  1354.0 64.0 %reduce-scatter.16.cloned.1.call-done = bf16[256,256]{1,0:T(8,128)(2,1)} async-done(((bf16[2048,256]{1,0:T(8,128)(2,1)}), bf16[256,256]{1,0:T(8,128)(2,1)}) %reduce-scatter.16.cloned.1.call-update) | async-done | bytes 131088 | tf_op jit(solution)/shard_map/reduce_scatter | solution.py:372
  1419.6 64.7 %reduce-scatter.18.cloned.1.call-done = bf16[256,256]{1,0:T(8,128)(2,1)} async-done(((bf16[2048,256]{1,0:T(8,128)(2,1)}), bf16[256,256]{1,0:T(8,128)(2,1)}) %reduce-scatter.18.cloned.1.call-update) | async-done | bytes 131088 | tf_op jit(solution)/shard_map/reduce_scatter | solution.py:375
  1485.9 86.6 %all-reduce.57.cloned.1.call-done = (bf16[256,2048]{1,0:T(8,128)(2,1)}, bf16[256,2048]{1,0:T(8,128)(2,1)}, bf16[256,2048]{1,0:T(8,128)(2,1)}, bf16[256,2048]{1,0:T(8,128)(2,1)}) async-done(((bf16[256,2048]{1,0:T(8,128)(2,1)}, bf16[256,2048]{1,0:T(8,128)(2,1)}, bf16[256,2048]{1,0:T(8,128)(2,1)}, bf16[256,2048]{1,0:T(8,128)(2,1)}), (bf16[256,2048]{1,0:T(8,128)(2,1)}, bf16[256,2048]{1,0:T(8,128)(2,1)}, ...) | async-done | bytes 4194320 | tf_op jit(solution)/shard_map/psum | solution.py:250
  1577.0 22.6 %all-reduce.47 = (bf16[2048]{0:T(1024)(128)(2,1)S(1)}, bf16[512]{0:T(512)(128)(2,1)S(1)}, bf16[2048]{0:T(1024)(128)(2,1)S(1)}) all-reduce(bf16[2048]{0:T(1024)(128)(2,1)S(1)} %add_convert_fusion.11, bf16[512]{0:T(512)(128)(2,1)S(1)} %add_convert_fusion.12, ...), channel_id=2, replica_groups=mesh['ctx'=8,'head'=4] {'ctx'}, use_global_device_ids=true, to_apply=%region_48.50.clone | all-reduce | flops 4608 | bytes 18432
  1600.9 5.4 fusion.61
  1610.3 34.2 %reduce-scatter.20.cloned.1.call-done = bf16[256,512]{1,0:T(8,128)(2,1)} async-done(((bf16[2048,512]{1,0:T(8,128)(2,1)}), bf16[256,512]{1,0:T(8,128)(2,1)}) %reduce-scatter.20.cloned.1.call-update) | async-done | bytes 262160 | tf_op jit(solution)/shard_map/reduce_scatter | solution.py:378
  1646.3 111.1 %reduce-scatter.28.cloned.1.call-done = bf16[256,1408]{1,0:T(8,128)(2,1)} async-done(((bf16[2048,1408]{1,0:T(8,128)(2,1)}), bf16[256,1408]{1,0:T(8,128)(2,1)}) %reduce-scatter.28.cloned.1.call-update) | async-done | bytes 720912 | tf_op jit(solution)/shard_map/reduce_scatter | solution.py:402
  1759.7 111.5 %reduce-scatter.30.cloned.1.call-done = bf16[256,1408]{1,0:T(8,128)(2,1)} async-done(((bf16[2048,1408]{1,0:T(8,128)(2,1)}), bf16[256,1408]{1,0:T(8,128)(2,1)}) %reduce-scatter.30.cloned.1.call-update) | async-done | bytes 720912 | tf_op jit(solution)/shard_map/reduce_scatter | solution.py:405
  1873.6 111.8 %reduce-scatter.32.cloned.1.call-done = bf16[1408,256]{1,0:T(8,128)(2,1)} async-done(((bf16[1408,2048]{1,0:T(8,128)(2,1)}), bf16[1408,256]{1,0:T(8,128)(2,1)}) %reduce-scatter.32.cloned.1.call-update) | async-done | bytes 720912 | tf_op jit(solution)/shard_map/reduce_scatter | solution.py:408
  (825 shorter events, 385.4 us)
Async XLA Ops:
  7.2 28.5 %copy-start.196 = (u32[32]{0:T(128)S(1)}, u32[32]{0:T(128)}, u32[]{:S(2)}) copy-start(u32[32]{0:T(128)} %constant.313) | copy-start | bytes 388
  7.2 110.5 %copy-start = (bf16[2,256,2048]{2,1,0:T(8,128)(2,1)S(1)}, bf16[2,256,2048]{2,1,0:T(8,128)(2,1)}, u32[]{:S(2)}) copy-start(bf16[2,256,2048]{2,1,0:T(8,128)(2,1)} %param.26) | copy-start | bytes 6291460
  7.2 30.4 %copy-start.206 = (bf16[1,32]{1,0:T(2,128)(2,1)S(1)}, bf16[1,32]{1,0:T(2,128)(2,1)}, u32[]{:S(2)}) copy-start(bf16[1,32]{1,0:T(2,128)(2,1)} %param.36) | copy-start | bytes 196
  7.2 30.6 %copy-start.207 = (bf16[64]{0:T(256)(128)(2,1)S(1)}, bf16[64]{0:T(256)(128)(2,1)}, u32[]{:S(2)}) copy-start(bf16[64]{0:T(256)(128)(2,1)} %param.37) | copy-start | bytes 388
  7.2 48.7 %copy-start.182 = (bf16[256,16]{0,1:T(8,128)(2,1)S(1)}, bf16[256,16]{0,1:T(8,128)(2,1)}, u32[]{:S(2)}) copy-start(bf16[256,16]{0,1:T(8,128)(2,1)} %param.34) | copy-start | bytes 24580
  7.2 79.4 %copy-start.195 = (bf16[1,16,32]{2,1,0:T(8,128)(2,1)S(1)}, bf16[1,16,32]{2,1,0:T(8,128)(2,1)}, u32[]{:S(2)}) copy-start(bf16[1,16,32]{2,1,0:T(8,128)(2,1)} %param.35) | copy-start | bytes 3076
  7.2 116.2 %all-gather.21.cloned.1.call-start = ((), (), s32[]{:S(2)}) async-start(), calls=%async_computation.12 | async-start | bytes 1179648 | tf_op jit(solution)/shard_map/all_gather | solution.py:91
  8.0 117.9 %all-gather.23.cloned.1.call-start = ((), (), s32[]{:S(2)}) async-start(), calls=%async_computation.13 | async-start | bytes 2359296 | tf_op jit(solution)/shard_map/all_gather | solution.py:92
  8.7 219.4 %all-gather.19.cloned.1.call-start = ((), (), s32[]{:S(2)}) async-start(), calls=%async_computation.11 | async-start | bytes 1179648 | tf_op jit(solution)/shard_map/all_gather | solution.py:90
  9.5 246.3 %all-gather.27.cloned.1.call-start = ((), (), s32[]{:S(2)}) async-start(), calls=%async_computation.15 | async-start | bytes 2359296 | tf_op jit(solution)/shard_map/all_gather | solution.py:93
  10.0 260.7 %all-gather.25.cloned.1.call-start = ((), (), s32[]{:S(2)}) async-start(), calls=%async_computation.14 | async-start | bytes 4718592 | tf_op jit(solution)/shard_map/all_gather | solution.py:15
  35.6 84.7 %copy-start.156 = (f32[256]{0:T(256)}, f32[256]{0:T(256)S(1)}, u32[]{:S(2)}) copy-start(f32[256]{0:T(256)S(1)} %get-tuple-element.559) | copy-start | bytes 3076
  35.6 83.8 %copy-start.199 = (s32[2,2]{1,0:T(2,128)S(1)}, s32[2,2]{1,0:T(2,128)}, u32[]{:S(2)}) copy-start(s32[2,2]{1,0:T(2,128)} %param.28) | copy-start | bytes 52
  35.6 90.3 %copy-start.127 = (f32[256]{0:T(256)}, f32[256]{0:T(256)S(1)}, u32[]{:S(2)}) copy-start(f32[256]{0:T(256)S(1)} %fusion.226) | copy-start | bytes 3076
  55.9 63.3 %copy-start.209 = (f32[256]{0:T(256)}, f32[256]{0:T(256)S(1)}, u32[]{:S(2)}) copy-start(f32[256]{0:T(256)S(1)} %add.725) | copy-start | bytes 3076
  86.7 31.0 %copy-start.102 = (bf16[2048,16]{0,1:T(8,128)(2,1)}, bf16[2048,16]{0,1:T(8,128)(2,1)S(1)}, u32[]{:S(2)}) copy-start(bf16[2048,16]{0,1:T(8,128)(2,1)S(1)} %all_gather.46) | copy-start | bytes 196612
  117.7 26.0 %copy-start.119 = (bf16[1,16,256]{2,1,0:T(8,128)(2,1)}, bf16[1,16,256]{2,1,0:T(8,128)(2,1)S(1)}, u32[]{:S(2)}) copy-start(bf16[1,16,256]{2,1,0:T(8,128)(2,1)S(1)} %copy.43) | copy-start | bytes 24580
  118.2 7.8 copy-start.183
  119.5 8.8 copy-start.114
  141.7 203.3 %all-gather.37.cloned.1.call-start = ((), (), s32[]{:S(2)}) async-start(), calls=%async_computation.20 | async-start | bytes 4718592 | tf_op jit(solution)/shard_map/all_gather | solution.py:15
  161.2 66.9 %copy-start.128 = (f32[256]{0:T(256)S(1)}, f32[256]{0:T(256)}, u32[]{:S(2)}) copy-start(f32[256]{0:T(256)} %copy-done.127) | copy-start | bytes 3076
  163.3 233.1 %all-gather.29.cloned.1.call-start = ((), (), s32[]{:S(2)}) async-start(), calls=%async_computation.16 | async-start | bytes 2359296 | tf_op jit(solution)/shard_map/all_gather | solution.py:98
  164.1 287.5 %all-reduce.61.cloned.1.call-start = ((), (), s32[]{:S(2)}) async-start(), calls=%async_computation.36 | async-start | bytes 4194304 | tf_op jit(solution)/shard_map/psum | solution.py:242
  165.4 59.6 %copy-start.142 = (f32[2,256]{1,0:T(2,128)}, f32[2,256]{1,0:T(2,128)S(1)}, u32[]{:S(2)}) copy-start(f32[2,256]{1,0:T(2,128)S(1)} %pad_add_fusion.19) | copy-start | bytes 6148
  225.7 132.6 %copy-start.125 = (f32[4,256]{1,0:T(4,128)}, f32[4,256]{1,0:T(4,128)S(1)}, u32[]{:S(2)}) copy-start(f32[4,256]{1,0:T(4,128)S(1)} %concatenate.61) | copy-start | bytes 12292
  289.5 55.5 %copy-start.171 = (f32[256]{0:T(256)}, f32[256]{0:T(256)S(1)}, u32[]{:S(2)}) copy-start(f32[256]{0:T(256)S(1)} %add.648) | copy-start | bytes 3076
  401.6 145.1 %all-gather.31.cloned.1.call-start = ((), (), s32[]{:S(2)}) async-start(), calls=%async_computation.17 | async-start | bytes 6488064 | tf_op jit(solution)/shard_map/all_gather | solution.py:100
  402.4 237.5 %all-gather.33.cloned.1.call-start = ((), (), s32[]{:S(2)}) async-start(), calls=%async_computation.18 | async-start | bytes 6488064 | tf_op jit(solution)/shard_map/all_gather | solution.py:101
  403.0 330.9 %all-gather.35.cloned.1.call-start = ((), (), s32[]{:S(2)}) async-start(), calls=%async_computation.19 | async-start | bytes 6488064 | tf_op jit(solution)/shard_map/all_gather | solution.py:102
  403.7 408.2 %all-reduce.59.cloned.1.call-start = ((), (), s32[]{:S(2)}) async-start(), calls=%async_computation.35 | async-start | bytes 4194304 | tf_op jit(solution)/shard_map/psum | solution.py:295
  639.8 8.9 slice-start.2
  733.9 12.6 copy-start.217
  733.9 12.6 copy-start.218
  741.0 11.1 copy-start.82
  741.8 8.4 slice-start
  741.8 10.3 slice-start.4
  757.9 157.9 %all-gather.41.cloned.1.call-start = ((), (), s32[]{:S(2)}) async-start(), calls=%async_computation.22 | async-start | bytes 2359296 | tf_op jit(solution)/shard_map/all_gather | solution.py:30
  866.5 97.4 %all-gather.39.cloned.1.call-start = ((), (), s32[]{:S(2)}) async-start(), calls=%async_computation.21 | async-start | bytes 2359296 | tf_op jit(solution)/shard_map/all_gather | solution.py:30
  911.9 198.3 %reduce-scatter.36.cloned.1.call-start = ((), (), s32[]{:S(2)}) async-start(), calls=%async_computation.33 | async-start | bytes 73728
  915.8 21.7 %copy-start.122 = (f32[4,256]{1,0:T(4,128)S(1)}, f32[4,256]{1,0:T(4,128)}, u32[]{:S(2)}) copy-start(f32[4,256]{1,0:T(4,128)} %concatenate.69) | copy-start | bytes 12292
  963.9 22.0 %copy-start.115 = (f32[4,1,256]{2,0,1:T(4,128)S(1)}, f32[4,1,256]{2,0,1:T(4,128)}, u32[]{:S(2)}) copy-start(f32[4,1,256]{2,0,1:T(4,128)} %copy-done.114) | copy-start | bytes 12292
  991.5 13.6 copy-start.118
  994.7 10.4 copy-start.23
  1010.1 20.2 %copy-start.194 = (f32[256]{0:T(256)S(1)}, f32[256]{0:T(256)}, u32[]{:S(2)}) copy-start(f32[256]{0:T(256)} %get-tuple-element.630) | copy-start | bytes 3076
  1010.1 21.2 %copy-start.124 = (f32[16,256]{1,0:T(8,128)S(1)}, f32[16,256]{1,0:T(8,128)}, u32[]{:S(2)}) copy-start(f32[16,256]{1,0:T(8,128)} %fusion.290) | copy-start | bytes 49156
  1010.1 21.2 %copy-start.185 = (bf16[256,16]{0,1:T(8,128)(2,1)S(1)}, bf16[256,16]{0,1:T(8,128)(2,1)}, u32[]{:S(2)}) copy-start(bf16[256,16]{0,1:T(8,128)(2,1)} %copy-done.184) | copy-start | bytes 24580
  1014.0 18.2 copy-start.136
  1031.0 123.3 %reduce-scatter.34.cloned.1.call-start = ((), (), s32[]{:S(2)}) async-start(), calls=%async_computation.32 | async-start | bytes 73728
  1032.2 178.4 %reduce-scatter.24.cloned.1.call-start = ((), (), s32[]{:S(2)}) async-start(), calls=%async_computation.27 | async-start | bytes 73728 | tf_op jit(solution)/shard_map/reduce_scatter | solution.py:384
  1034.3 246.4 %reduce-scatter.22.cloned.1.call-start = ((), (), s32[]{:S(2)}) async-start(), calls=%async_computation.26 | async-start | bytes 2359296 | tf_op jit(solution)/shard_map/reduce_scatter | solution.py:381
  1038.8 313.4 %reduce-scatter.26.cloned.1.call-start = ((), (), s32[]{:S(2)}) async-start(), calls=%async_computation.28 | async-start | bytes 2359296 | tf_op jit(solution)/shard_map/reduce_scatter | solution.py:396
  1044.3 373.6 %reduce-scatter.16.cloned.1.call-start = ((), (), s32[]{:S(2)}) async-start(), calls=%async_computation.23 | async-start | bytes 1179648 | tf_op jit(solution)/shard_map/reduce_scatter | solution.py:372
  1047.5 436.8 %reduce-scatter.18.cloned.1.call-start = ((), (), s32[]{:S(2)}) async-start(), calls=%async_computation.24 | async-start | bytes 1179648 | tf_op jit(solution)/shard_map/reduce_scatter | solution.py:375
  1066.0 506.5 %all-reduce.57.cloned.1.call-start = ((), (), s32[]{:S(2)}) async-start(), calls=%async_computation.34 | async-start | bytes 8388608 | tf_op jit(solution)/shard_map/psum | solution.py:250
  1080.0 564.5 %reduce-scatter.20.cloned.1.call-start = ((), (), s32[]{:S(2)}) async-start(), calls=%async_computation.25 | async-start | bytes 2359296 | tf_op jit(solution)/shard_map/reduce_scatter | solution.py:378
  1083.8 673.6 %reduce-scatter.28.cloned.1.call-start = ((), (), s32[]{:S(2)}) async-start(), calls=%async_computation.29 | async-start | bytes 6488064 | tf_op jit(solution)/shard_map/reduce_scatter | solution.py:402
  1092.5 778.8 %reduce-scatter.30.cloned.1.call-start = ((), (), s32[]{:S(2)}) async-start(), calls=%async_computation.30 | async-start | bytes 6488064 | tf_op jit(solution)/shard_map/reduce_scatter | solution.py:405
  1100.2 885.2 %reduce-scatter.32.cloned.1.call-start = ((), (), s32[]{:S(2)}) async-start(), calls=%async_computation.31 | async-start | bytes 6488064 | tf_op jit(solution)/shard_map/reduce_scatter | solution.py:408
  1108.8 463.7 %copy-start.103 = (bf16[2048,16]{0,1:T(8,128)(2,1)S(1)}, bf16[2048,16]{0,1:T(8,128)(2,1)}, u32[]{:S(2)}) copy-start(bf16[2048,16]{0,1:T(8,128)(2,1)} %copy-done.102) | copy-start | bytes 196612
  1108.8 463.7 %copy-start.180 = (bf16[256,16]{0,1:T(8,128)(2,1)S(1)}, bf16[256,16]{0,1:T(8,128)(2,1)}, u32[]{:S(2)}) copy-start(bf16[256,16]{0,1:T(8,128)(2,1)} %copy-done.179) | copy-start | bytes 24580
  1354.0 220.3 %copy-start.205 = (bf16[256,16]{0,1:T(8,128)(2,1)S(1)}, bf16[256,16]{0,1:T(8,128)(2,1)}, u32[]{:S(2)}) copy-start(bf16[256,16]{0,1:T(8,128)(2,1)} %copy-done.204) | copy-start | bytes 24580
  1574.3 26.6 %copy-start.157 = (f32[256]{0:T(256)S(1)}, f32[256]{0:T(256)}, u32[]{:S(2)}) copy-start(f32[256]{0:T(256)} %copy-done.156) | copy-start | bytes 3076
  1574.3 26.5 %copy-start.158 = (f32[256]{0:T(256)S(1)}, f32[256]{0:T(256)}, u32[]{:S(2)}) copy-start(f32[256]{0:T(256)} %get-tuple-element.560) | copy-start | bytes 3076
  1574.3 26.6 %copy-start.9 = (bf16[256,2048]{1,0:T(8,128)(2,1)S(1)}, bf16[256,2048]{1,0:T(8,128)(2,1)}, u32[]{:S(2)}) copy-start(bf16[256,2048]{1,0:T(8,128)(2,1)} %get-tuple-element.626) | copy-start | bytes 3145732
  (187 other events, 565.5 us)
Sparse Core Ops, SparseCore 0:
  10.2 43.0 all-gather.20
  55.4 49.0 all-gather.22
  106.7 39.3 all-gather.18
  148.1 48.1 all-gather.26
  198.8 71.9 all-gather.24
  273.3 71.6 all-gather.36
  347.0 49.3 all-gather.28
  401.7 49.7 all-reduce.60
  454.0 92.6 all-gather.30
  549.0 90.8 all-gather.32
  642.1 91.7 all-gather.34
  758.0 49.7 all-reduce.58
  866.7 47.4 all-gather.40
  916.1 47.7 all-gather.38
  1031.1 59.6 reduce-scatter.35
  1094.0 60.2 reduce-scatter.33
  1157.9 52.6 reduce-scatter.23
  1214.0 66.6 reduce-scatter.21
  1284.8 67.3 reduce-scatter.25
  1355.5 62.4 reduce-scatter.15
  1421.7 62.4 reduce-scatter.17
  1487.4 85.0 all-reduce.56
  1576.4 68.0 reduce-scatter.19
  1648.5 108.9 reduce-scatter.27
  1761.5 109.7 reduce-scatter.29
  1875.2 110.1 reduce-scatter.31
where the time goes:
time: 2010 us; the launch traced here: 1990 us
  waiting for transfers between devices  1220 us (61%)
  blocking collectives  224 us (11%)
  other arithmetic  222 us (11%)
  matrix products  187 us (9%)
  local copies, waits for them, and re-layouts  113 us (6%)
  between operations  20.7 us (1%)
    reduce_scatter x1, waiting for transfers between devices, per_device(): lax.psum_scatter(totals[13].astype(jnp.bfloat16), 'ctx', scatter_dimensio...  112 us
    reduce_scatter x1, waiting for transfers between devices, per_device(): lax.psum_scatter(totals[12].astype(jnp.bfloat16), 'ctx', scatter_dimensio...  112 us
    reduce_scatter x1, waiting for transfers between devices, per_device(): lax.psum_scatter(totals[11].astype(jnp.bfloat16), 'ctx', scatter_dimensio...  111 us
    all_gather x1, waiting for transfers between devices, fetch_weights(): lax.all_gather(shards[11], 'ctx', axis=0, tiled=True)  89.1 us
    all_gather x1, waiting for transfers between devices, fetch_weights(): lax.all_gather(shards[12], 'ctx', axis=0, tiled=True)  87.3 us
    psum x1, waiting for transfers between devices, per_device(): lax.psum(project(hidden, full_down).astype(jnp.bfloat16), 'head')  86.6 us
    all_gather x1, waiting for transfers between devices, fetch_weights(): lax.all_gather(shards[13], 'ctx', axis=1, tiled=True)  82.2 us
    reduce_scatter x1, waiting for transfers between devices, per_device(): lax.psum_scatter(totals[9].astype(jnp.bfloat16), 'ctx', scatter_dimension...  69.7 us
  transfers between devices with their start and end apart: 26, of which 19 were waited for; matrix products, arithmetic and copies ran while one was open for 18% of the time, Pallas kernels for 0%

commit v1 on v0

v1 whole, which is shorter than its diff:
```python
import functools

import numpy as np

import jax
import jax.numpy as jnp
from jax import lax
from jax.experimental import pallas as pl
from jax.experimental.pallas import tpu as pltpu
from jax.sharding import Mesh
from jax.sharding import PartitionSpec as P

GROUP = 64
EPS = 1e-06
LEVELS = (32, 16, 8, 4, 2, 1)
f32 = jnp.float32
bf16 = jnp.bfloat16
NZ = 4


def dot(a, b, dims):
    return lax.dot_general(a, b, (dims, ((), ())), preferred_element_type=f32)


def nn(a, b):
    return dot(a, b, ((1,), (0,)))


def nt(a, b):
    return dot(a, b, ((1,), (1,)))


def tn(a, b):
    return dot(a, b, ((0,), (0,)))


def swap(x, axis):
    return lax.ppermute(x, axis, [(0, 1), (1, 0)])


def add_low(a, b):
    return (a.astype(f32) + b.astype(f32)).astype(bf16)


def both_in_order(piece, axis, dim):
    other = swap(piece, axis)
    first = lax.axis_index(axis) == 0
    return jnp.where(
        first, jnp.stack([piece, other], dim), jnp.stack([other, piece], dim)
    )


def silu(v):
    return v * jax.nn.sigmoid(v)


def silu_grad(v):
    sig = jax.nn.sigmoid(v)
    return sig * (1.0 + v * (1.0 - sig))


def inv_rms(v):
    return lax.rsqrt(jnp.mean(v * v, axis=-1, keepdims=True) + EPS)


def norm_back(h, r, gain, grad):
    scaled = gain * grad
    inner = jnp.mean(h * scaled, axis=-1, keepdims=True)
    return r * scaled - h * (r * r * r) * inner


def level_map(rows):
    t = np.arange(rows)[:, None]
    u = np.arange(rows)[None, :]
    out = np.zeros((rows, rows), np.int32)
    for at, half in enumerate(LEVELS):
        hit = (t // (2 * half) == u // (2 * half)) & ((t // half) % 2 == 1) & ((u // half) % 2 == 0)
        out[hit] = at + 1
    out[t == u] = len(LEVELS) + 1
    return out


def lower_map(rows):
    t = np.arange(rows)[:, None]
    u = np.arange(rows)[None, :]
    return ((t // GROUP == u // GROUP) & (t >= u)).astype(np.float32)


def ones_times(ones, value):
    hi = value.astype(bf16)
    rest = value - hi.astype(f32)
    mid = rest.astype(bf16)
    low = (rest - mid.astype(f32)).astype(bf16)
    return nn(ones, hi) + (nn(ones, mid) + nn(ones, low))


def level_decay(cum, half):
    rows, width = cum.shape
    span = max(2 * half, 8)
    parts = cum.reshape(rows // span, span, width)
    if half >= 4:
        mid = parts[:, half - 1 : half, :]
    else:
        at = lax.broadcasted_iota(jnp.int32, parts.shape, 1)
        mid = parts[:, half - 1 : half, :]
        for start in range(2 * half, span, 2 * half):
            mid = jnp.where(at >= start, parts[:, start + half - 1 : start + half, :], mid)
    return jnp.exp(-jnp.abs(parts - mid)).reshape(rows, width)


def block_of(array, at):
    return array[at * GROUP : (at + 1) * GROUP, :]


def scan_forward(qkv_ref, decay_ref, lower_ref, level_ref, open_ref, out_ref, query_ref, state_ref, keep_ref):
    step = pl.program_id(0)
    rows, width = decay_ref.shape
    count = rows // GROUP
    scale = width**-0.5
    queries = qkv_ref[:, :width].astype(f32) * scale
    keys = qkv_ref[:, width : 2 * width].astype(f32)
    values = qkv_ref[:, 2 * width :]
    levels = level_ref[...]
    cum = ones_times(lower_ref[...], decay_ref[...])
    scores = jnp.where(
        levels == len(LEVELS) + 1, nt(queries.astype(bf16), keys.astype(bf16)), 0.0
    )
    for at, half in enumerate(LEVELS):
        decay = level_decay(cum, half)
        part = nt((queries * decay).astype(bf16), (keys * decay).astype(bf16))
        scores = jnp.where(levels == at + 1, part, scores)
    local = nn(scores.astype(bf16), values)
    faded = queries * jnp.exp(cum)
    state = jnp.zeros((values.shape[1], width), f32)
    keep = jnp.ones((1, width), f32)
    for c in range(count):
        is_open = open_ref[step, c]
        state = state * is_open
        keep = keep * is_open
        faded_c = block_of(faded, c)
        cum_c = block_of(cum, c)
        last = cum_c[GROUP - 1 :, :]
        here = block_of(local, c)
        if c:
            here = here + nt(faded_c.astype(bf16), state.astype(bf16))
        out_ref[c * GROUP : (c + 1) * GROUP, :] = here
        query_ref[c * GROUP : (c + 1) * GROUP, :] = (faded_c * keep).astype(bf16)
        carried = (block_of(keys, c) * jnp.exp(last - cum_c)).astype(bf16)
        update = tn(block_of(values, c), carried)
        shrink = jnp.exp(last)
        state = state * shrink + update
        keep = keep * shrink
    state_ref[0] = state.astype(bf16)
    keep_ref[0] = jnp.broadcast_to(keep, keep_ref.shape[1:])


def scan_backward(qkv_ref, decay_ref, logit_ref, grad_ref, enter_ref, leave_ref, lower_ref, upper_ref, level_ref, open_ref, out_ref, logit_out_ref, local_ref, past_ref):
    step = pl.program_id(0)
    rows, width = decay_ref.shape
    count = rows // GROUP
    scale = width**-0.5
    queries = qkv_ref[:, :width].astype(f32) * scale
    keys = qkv_ref[:, width : 2 * width].astype(f32)
    values = qkv_ref[:, 2 * width :]
    grads = grad_ref[...]
    levels = level_ref[...]
    cum = ones_times(lower_ref[...], decay_ref[...])
    pair_grad = nt(grads, values)
    on_diagonal = levels == len(LEVELS) + 1
    own = jnp.sum(jnp.where(on_diagonal, pair_grad, 0.0), axis=1, keepdims=True)
    scores = jnp.where(on_diagonal, nt(queries.astype(bf16), keys.astype(bf16)), 0.0)
    query_grad = jnp.zeros((rows, width), f32)
    key_grad = jnp.zeros((rows, width), f32)
    for at, half in enumerate(LEVELS):
        decay = level_decay(cum, half)
        query_l = (queries * decay).astype(bf16)
        key_l = (keys * decay).astype(bf16)
        hit = levels == at + 1
        scores = jnp.where(hit, nt(query_l, key_l), scores)
        grad_l = jnp.where(hit, pair_grad, 0.0).astype(bf16)
        query_grad = query_grad + nn(grad_l, key_l) * decay
        key_grad = key_grad + tn(grad_l, query_l) * decay
    value_grad = tn(scores.astype(bf16), grads)
    rising = jnp.exp(cum)
    faded = queries * rising
    state = enter_ref[0].astype(f32)
    for c in range(count):
        state = state * open_ref[step, c]
        past_ref[c] = state
        cum_c = block_of(cum, c)
        last = cum_c[GROUP - 1 :, :]
        if c < count - 1:
            carried = (block_of(keys, c) * jnp.exp(last - cum_c)).astype(bf16)
            state = state * jnp.exp(last) + tn(block_of(values, c), carried)
    after = leave_ref[0].astype(f32)
    for c in range(count - 1, -1, -1):
        span = slice(c * GROUP, (c + 1) * GROUP)
        past = past_ref[c]
        cum_c = block_of(cum, c)
        last = cum_c[GROUP - 1 :, :]
        shrink = jnp.exp(last)
        fading = jnp.exp(last - cum_c)
        keys_c = block_of(keys, c)
        queries_c = block_of(queries, c)
        grads_c = block_of(grads, c)
        after_low = after.astype(bf16)
        query_c = block_of(query_grad, c) + nn(grads_c, past.astype(bf16)) * block_of(rising, c)
        key_far = nn(block_of(values, c), after_low) * fading
        key_c = block_of(key_grad, c) + key_far
        value_c = block_of(value_grad, c) + nt((keys_c * fading).astype(bf16), after_low)
        own_c = block_of(own, c)
        out_ref[span, :width] = ((query_c + own_c * keys_c) * scale).astype(bf16)
        out_ref[span, width : 2 * width] = (key_c + own_c * queries_c).astype(bf16)
        out_ref[span, 2 * width :] = value_c.astype(bf16)
        local_ref[span, :] = queries_c * query_c - keys_c * key_c
        at_last = jnp.sum(keys_c * key_far, axis=0, keepdims=True) + shrink * jnp.sum(
            past * after, axis=0, keepdims=True
        )
        logit_out_ref[span, :] = jnp.broadcast_to(at_last, (GROUP, width))
        if c:
            after = (after * shrink + tn(grads_c, block_of(faded, c).astype(bf16))) * open_ref[step, c]
    decay_grad = ones_times(upper_ref[...], local_ref[...]) + logit_out_ref[...]
    logit_out_ref[...] = decay_grad * jax.nn.sigmoid(-logit_ref[...]) * (1.0 / 16.0)


def call_forward(qkv, decays, is_open, micro_count):
    rows = qkv.shape[0] // micro_count
    width = decays.shape[1]
    wide = qkv.shape[1] - 2 * width
    lower = jnp.asarray(lower_map(rows), bf16)
    level = jnp.asarray(level_map(rows))
    whole = lambda m: (0, 0)
    mine = lambda m: (m, 0)
    mine3 = lambda m: (m, 0, 0)
    return pl.pallas_call(
        scan_forward,
        grid=(micro_count,),
        in_specs=[
            pl.BlockSpec((rows, qkv.shape[1]), mine),
            pl.BlockSpec((rows, width), mine),
            pl.BlockSpec((rows, rows), whole),
            pl.BlockSpec((rows, rows), whole),
            pl.BlockSpec(memory_space=pltpu.SMEM),
        ],
        out_specs=[
            pl.BlockSpec((rows, wide), mine),
            pl.BlockSpec((rows, width), mine),
            pl.BlockSpec((1, wide, width), mine3),
            pl.BlockSpec((1, 8, width), mine3),
        ],
        out_shape=[
            jax.ShapeDtypeStruct((micro_count * rows, wide), f32),
            jax.ShapeDtypeStruct((micro_count * rows, width), bf16),
            jax.ShapeDtypeStruct((micro_count, wide, width), bf16),
            jax.ShapeDtypeStruct((micro_count, 8, width), f32),
        ],
        compiler_params=pltpu.CompilerParams(vmem_limit_bytes=40 * 2**20),
        cost_estimate=pl.CostEstimate(flops=2_000_000_000, bytes_accessed=8_000_000, transcendentals=1_500_000),
        name="scan_forward",
    )(qkv, decays, lower, level, is_open)


def call_backward(qkv, decays, logits, grads, enter, leave, is_open, micro_count):
    rows = qkv.shape[0] // micro_count
    width = decays.shape[1]
    wide = qkv.shape[1] - 2 * width
    lower = jnp.asarray(lower_map(rows), bf16)
    upper = jnp.asarray(lower_map(rows).T, bf16)
    level = jnp.asarray(level_map(rows))
    whole = lambda m: (0, 0)
    mine = lambda m: (m, 0)
    mine3 = lambda m: (m, 0, 0)
    return pl.pallas_call(
        scan_backward,
        grid=(micro_count,),
        in_specs=[
            pl.BlockSpec((rows, qkv.shape[1]), mine),
            pl.BlockSpec((rows, width), mine),
            pl.BlockSpec((rows, width), mine),
            pl.BlockSpec((rows, wide), mine),
            pl.BlockSpec((1, wide, width), mine3),
            pl.BlockSpec((1, wide, width), mine3),
            pl.BlockSpec((rows, rows), whole),
            pl.BlockSpec((rows, rows), whole),
            pl.BlockSpec((rows, rows), whole),
            pl.BlockSpec(memory_space=pltpu.SMEM),
        ],
        out_specs=[
            pl.BlockSpec((rows, qkv.shape[1]), mine),
            pl.BlockSpec((rows, width), mine),
        ],
        out_shape=[
            jax.ShapeDtypeStruct((micro_count * rows, qkv.shape[1]), bf16),
            jax.ShapeDtypeStruct((micro_count * rows, width), f32),
        ],
        scratch_shapes=[
            pltpu.VMEM((rows, width), f32),
            pltpu.VMEM((rows // GROUP, wide, width), f32),
        ],
        compiler_params=pltpu.CompilerParams(vmem_limit_bytes=40 * 2**20),
        cost_estimate=pl.CostEstimate(flops=5_000_000_000, bytes_accessed=12_000_000, transcendentals=1_500_000),
        name="scan_backward",
    )(qkv, decays, logits, grads, enter, leave, lower, upper, level, is_open)


def pass_states(state, keep, reverse):
    ctx = ("z", "y")
    count = lax.axis_size(ctx)
    micro, wide, width = state.shape
    strip = wide // count
    parts = state.reshape(micro, count, strip, width).transpose(1, 0, 2, 3)
    parts = parts.reshape(count, micro * strip, width)
    keep_hi = keep.astype(bf16)
    keep_lo = (keep - keep_hi.astype(f32)).astype(bf16)
    extra = jnp.concatenate([keep_hi, keep_lo, jnp.zeros((16 - 2 * micro, width), bf16)])
    sent = jnp.concatenate(
        [parts, jnp.broadcast_to(extra[None], (count, 16, width))], axis=1
    )
    got = lax.all_to_all(sent, ctx, 0, 0)
    tail = got[:, micro * strip :, :].astype(f32)
    keeps = tail[:, :micro] + tail[:, micro : 2 * micro]
    states = got[:, : micro * strip, :].reshape(count, micro, strip, width)
    running = jnp.zeros((micro, strip, width), f32)
    entering = [None] * count
    order = range(count - 1, -1, -1) if reverse else range(count)
    for at in order:
        entering[at] = running.astype(bf16)
        running = running * keeps[at][:, None, :] + states[at].astype(f32)
    back = lax.all_to_all(jnp.stack(entering), ctx, 0, 0)
    return back.transpose(1, 0, 2, 3).reshape(micro, wide, width)


def gather_plane(piece):
    count = lax.axis_size("y")
    if count == 2:
        a, b = piece[0], piece[1]
        a_y, b_x = swap(a, "y"), swap(b, "x")
        a = jnp.stack([a, a_y])
        b = jnp.stack([b, b_x])
        a_x, b_y = swap(a, "x"), swap(b, "y")
        a = jnp.stack([a, a_x])
        b = jnp.stack([b, b_y], axis=1)
        here = jnp.stack([a, b])
    else:
        rows = [piece]
        for k in range(1, count):
            rows.append(lax.ppermute(piece, "y", [((i + k) % count, i) for i in range(count)]))
        here = jnp.stack(rows, axis=1)
        here = jnp.stack([here, swap(here, "x")], axis=1)
    return jnp.stack([here, swap(here, "c")])


def scatter_plane(parts):
    count = lax.axis_size("y")
    here = add_low(parts[0], swap(parts[1], "c"))
    if count == 2:
        a, b = here[0], here[1]
        a_got, b_got = swap(a[1], "x"), swap(b[:, 1], "y")
        a = add_low(a[0], a_got)
        b = add_low(b[:, 0], b_got)
        a_got, b_got = swap(a[1], "y"), swap(b[1], "x")
        a = a[0].astype(f32) + a_got.astype(f32)
        b = b[0].astype(f32) + b_got.astype(f32)
        return jnp.stack([a, b])
    here = add_low(here[:, 0], swap(here[:, 1], "x"))
    total = here[:, 0].astype(f32)
    for k in range(1, count):
        got = lax.ppermute(here[:, k], "y", [(i, (i + k) % count) for i in range(count)])
        total = total + got.astype(f32)
    return total


def scatter_head(part):
    micro, slots, width = part.shape
    c, x = lax.axis_index("c"), lax.axis_index("x")
    view = part.reshape(micro, 2, slots // 2, width)
    mine = lax.dynamic_index_in_dim(view, c, 1, keepdims=False)
    other = lax.dynamic_index_in_dim(view, 1 - c, 1, keepdims=False)
    mine = add_low(mine, swap(other, "c"))
    view = mine.reshape(micro, 2, slots // 4, width)
    mine = lax.dynamic_index_in_dim(view, x, 1, keepdims=False)
    other = lax.dynamic_index_in_dim(view, 1 - x, 1, keepdims=False)
    return mine.astype(f32) + swap(other, "x").astype(f32)


def gather_head(piece):
    micro, quarter, width = piece.shape
    both = both_in_order(piece, "x", 1)
    both = both_in_order(both, "c", 1)
    return both.reshape(micro, 4 * quarter, width)


def own_quarter(array):
    micro, slots, width = array.shape
    c, x = lax.axis_index("c"), lax.axis_index("x")
    view = array.reshape(micro, 4, slots // 4, width)
    return lax.dynamic_index_in_dim(view, 2 * c + x, 1, keepdims=False)


def others_y(piece):
    count = lax.axis_size("y")
    out = [piece]
    for k in range(1, count):
        out.append(lax.ppermute(piece, "y", [((i + k) % count, i) for i in range(count)]))
    return out


def relative_columns(array, k):
    count, y = lax.axis_size("y"), lax.axis_index("y")
    t, depth = array.shape
    view = array.reshape(t, NZ, count, depth // (NZ * count))
    at = lax.rem(y + k, count)
    return lax.dynamic_index_in_dim(view, at, 2, keepdims=False).reshape(t, -1)


def absolute_columns(parts):
    count, y = lax.axis_size("y"), lax.axis_index("y")
    t = parts[0].shape[0]
    views = [p.reshape(t, NZ, -1) for p in parts]
    if count == 2:
        stacked = jnp.where(y == 0, jnp.stack(views, 2), jnp.stack(views[::-1], 2))
    else:
        stacked = jnp.roll(jnp.stack(views, 2), y, axis=2)
    return stacked.reshape(t, -1)


def sum_rows(parts):
    count = lax.axis_size("y")
    total = parts[0].astype(f32)
    for k in range(1, count):
        got = lax.ppermute(parts[k], "y", [(i, (i + k) % count) for i in range(count)])
        total = total + got.astype(f32)
    return lax.psum_scatter(total.astype(bf16), "z", scatter_dimension=0, tiled=True).astype(f32)


def per_device(
    tokens, cotangent, lengths, norm_in, w_query, w_key, w_value, w_outgate, w_rank,
    w_decay, decay_bias, head_gain, w_out, norm_mid, w_gate, w_up, w_down,
):
    ctx = ("z", "y")
    ny = lax.axis_size("y")
    nctx = NZ * ny
    y = lax.axis_index("y")
    place = lax.axis_index(ctx)
    micro, slots, depth = tokens.shape
    groups = slots // GROUP
    rl = w_query.shape[0]
    width = w_query.shape[1]
    wide = w_value.shape[1]
    rank = w_rank.shape[1]
    ff = w_gate.shape[1]
    fl = ff // ny
    total = micro * slots

    w_qkv = jnp.concatenate([w_query, w_key, w_value], axis=1)
    w_go = jnp.concatenate([w_outgate, w_out.T], axis=1)
    qkv_parts = others_y(lax.all_gather(w_qkv, "z", axis=0, tiled=True))
    go_parts = others_y(lax.all_gather(w_go, "z", axis=0, tiled=True))

    small = jnp.concatenate(
        [norm_in, norm_mid, w_rank.T.reshape(-1), w_decay[0].reshape(-1), decay_bias[0], head_gain]
    )
    n_small = small.shape[0]
    pad = -n_small % 1024
    small = jnp.pad(small, (0, pad)).reshape(1, -1, 128)
    small = jnp.broadcast_to(small, (nctx,) + small.shape[1:])
    small = lax.all_to_all(small, ctx, 0, 0).reshape(nctx, -1)
    at = 0

    def take(size):
        nonlocal at
        at += size
        return small[:, at - size : at]

    gain_in = take(rl).reshape(1, depth).astype(f32)
    gain_mid = take(rl).reshape(1, depth).astype(f32)
    rank_t = take(rank * rl).reshape(nctx, rank, rl).transpose(1, 0, 2).reshape(rank, depth)
    dl = width // nctx
    decay_w = take(rank * dl).reshape(nctx, rank, dl).transpose(1, 0, 2).reshape(rank, width)
    bias = take(dl).reshape(1, width).astype(f32)
    gain_head = take(wide // nctx).reshape(1, wide).astype(f32)

    def unit_pieces(weight):
        return weight.reshape(rl, ny, fl).transpose(1, 0, 2)

    ff_local = jnp.concatenate(
        [unit_pieces(w_gate), unit_pieces(w_up), unit_pieces(w_down.T)], axis=2
    )
    ff_unit = jnp.zeros((ny, rl, 3 * fl), bf16)
    own = lax.dynamic_index_in_dim(ff_local, y, 0)
    ff_unit = lax.dynamic_update_slice_in_dim(ff_unit, own, y, 0)
    for k in range(1, ny):
        sent = lax.dynamic_index_in_dim(ff_local, lax.rem(y + k, ny), 0)
        got = lax.ppermute(sent, "y", [(i, (i + k) % ny) for i in range(ny)])
        ff_unit = lax.dynamic_update_slice_in_dim(ff_unit, got, lax.rem(y - k + ny, ny), 0)
    ff_full = lax.all_gather(ff_unit.reshape(ny * rl, 3 * fl), "z", axis=0, tiled=True)

    slot_ids = place * slots + jnp.arange(slots, dtype=jnp.int32)
    group_ids = place * groups + jnp.arange(groups, dtype=jnp.int32)
    end = jnp.zeros((micro, 1), jnp.int32)
    reset = group_ids[None, :] == end
    for i in range(lengths.shape[1]):
        end = end + lengths[:, i : i + 1]
        reset = reset | (group_ids[None, :] == end)
    is_open = 1.0 - reset.astype(f32)
    slot_mask = (slot_ids[None, :] < end * GROUP).astype(bf16)

    out_low = cotangent * slot_mask[:, :, None]
    c_at, x_at = lax.axis_index("c"), lax.axis_index("x")
    quarter = slots // 4
    view = out_low.reshape(micro, 2, 2, quarter, depth)
    near = lax.dynamic_index_in_dim(view, c_at, 1, keepdims=False)
    far = lax.dynamic_index_in_dim(view, 1 - c_at, 1, keepdims=False)

    def x_order(half):
        first = lax.dynamic_index_in_dim(half, x_at, 1, keepdims=False)
        second = lax.dynamic_index_in_dim(half, 1 - x_at, 1, keepdims=False)
        return jnp.stack([first, second], 1)

    near, far = x_order(near), x_order(far)
    near_y = others_y(near)[1:]
    near_y = jnp.stack(near_y, 2)
    far_y = swap(near_y, "c")
    plane_low = jnp.stack(
        [
            jnp.concatenate([near[:, :, None], near_y], 2),
            jnp.concatenate([far[:, :, None], far_y], 2),
        ]
    ).reshape(-1, depth)

    inputs = tokens.astype(f32).reshape(total, depth)
    r_in = inv_rms(inputs)
    normed_in = (inputs * r_in * gain_in).astype(bf16)
    normed_parts = [relative_columns(normed_in, k) for k in range(ny)]
    low_rank = nt(normed_in, rank_t).astype(bf16)
    logits = nn(low_rank, decay_w) + bias
    decays = jax.nn.log_sigmoid(logits) / 16.0
    qkv = sum(nn(n, w) for n, w in zip(normed_parts, qkv_parts)).astype(bf16)

    local_out, far_query, state, keep = call_forward(qkv, decays, is_open, micro)
    keep = keep[:, 0, :]
    enter = pass_states(state, keep, False)

    outgate = sum(nn(n, w[:, :wide]) for n, w in zip(normed_parts, go_parts))
    outgate = outgate.astype(bf16).astype(f32)
    mixed = local_out + jnp.concatenate(
        [nt(far_query[m * slots : (m + 1) * slots], enter[m]) for m in range(micro)]
    )
    r_head = inv_rms(mixed)
    gated = (mixed * r_head * gain_head * silu(outgate)).astype(bf16)
    attention = jnp.concatenate([nt(gated, w[:, wide:]) for w in go_parts], axis=1)
    attention = scatter_head(attention.astype(bf16).reshape(micro, slots, depth))
    attention = attention.reshape(micro * quarter, depth)
    step = depth // ny
    attention = absolute_columns([attention[:, k * step : (k + 1) * step] for k in range(ny)])
    inputs_own = own_quarter(tokens).reshape(-1, depth).astype(f32)
    residual = inputs_own + attention

    r_mid = inv_rms(residual)
    normed_mid = (residual * r_mid * gain_mid).astype(bf16)
    plane_mid = gather_plane(normed_mid.reshape(micro, quarter, depth))
    plane_shape = plane_mid.shape
    plane_mid = plane_mid.reshape(-1, depth)
    ff_gate, ff_up, ff_down_t = (ff_full[:, i * fl : (i + 1) * fl] for i in range(3))
    gate_proj = nn(plane_mid, ff_gate)
    up_proj = nn(plane_mid, ff_up)
    hidden = (silu(gate_proj) * up_proj).astype(bf16)
    hidden_grad = nn(plane_low, ff_down_t)
    gate_low = (hidden_grad * up_proj * silu_grad(gate_proj)).astype(bf16)
    up_low = (hidden_grad * silu(gate_proj)).astype(bf16)
    mid_part = (nt(gate_low, ff_gate) + nt(up_low, ff_up)).astype(bf16)
    mid_grad = scatter_plane(mid_part.reshape(plane_shape)).reshape(-1, depth)
    ff_grad = jnp.concatenate(
        [tn(plane_mid, gate_low), tn(plane_mid, up_low), tn(plane_low, hidden)], axis=1
    ).astype(bf16)
    ff_grad = lax.psum_scatter(ff_grad, "z", scatter_dimension=0, tiled=True)
    feed_part = nt(hidden, ff_down_t).astype(bf16)

    out_grad = own_quarter(out_low).reshape(-1, depth).astype(f32)
    resid_grad = out_grad + norm_back(residual, r_mid, gain_mid, mid_grad)
    grad_norm_mid = jnp.sum(mid_grad * residual * r_mid, axis=0)
    resid_low = gather_head(resid_grad.astype(bf16).reshape(micro, quarter, depth))
    resid_low = resid_low.reshape(total, depth)
    resid_parts = [relative_columns(resid_low, k) for k in range(ny)]
    gated_grad = sum(nn(n, w[:, wide:]) for n, w in zip(resid_parts, go_parts))

    unit = mixed * r_head
    gate_act = silu(outgate)
    unit_grad = gated_grad * gate_act
    outgate_low = (gated_grad * unit * gain_head * silu_grad(outgate)).astype(bf16)
    mixed_grad = norm_back(mixed, r_head, gain_head, unit_grad).astype(bf16)
    grad_gain = jnp.sum(unit_grad * unit, axis=0)
    state_grad = jnp.stack(
        [
            tn(mixed_grad[m * slots : (m + 1) * slots], far_query[m * slots : (m + 1) * slots])
            for m in range(micro)
        ]
    ).astype(bf16)
    leave = pass_states(state_grad, keep, True)
    qkv_low, logit_grad = call_backward(
        qkv, decays, logits, mixed_grad, enter, leave, is_open, micro
    )
    logit_low = logit_grad.astype(bf16)

    go_grads = [
        jnp.concatenate([tn(n, outgate_low), tn(r, gated)], axis=1).astype(bf16)
        for n, r in zip(normed_parts, resid_parts)
    ]
    go_grad = sum_rows(go_grads)

    rank_part = nt(logit_low, decay_w).astype(bf16)
    rank_pad = jnp.pad(rank_part, ((0, 0), (0, 128 - rank)))
    in_part = [
        (nt(qkv_low, wq) + nt(outgate_low, wg[:, :wide])).astype(bf16)
        for wq, wg in zip(qkv_parts, go_parts)
    ]
    in_sum = jnp.concatenate(in_part + [rank_pad], axis=1)
    in_sum = scatter_head(in_sum.reshape(micro, slots, depth + 128)).reshape(-1, depth + 128)
    qkv_grads = [tn(n, qkv_low).astype(bf16) for n in normed_parts]
    qkv_grad = sum_rows(qkv_grads)
    rank_low = in_sum[:, depth : depth + rank].astype(bf16)
    in_grad = absolute_columns([in_sum[:, k * step : (k + 1) * step] for k in range(ny)])
    in_grad = in_grad + nn(rank_low, rank_t)
    r_own = inv_rms(inputs_own)
    input_own = resid_grad + norm_back(inputs_own, r_own, gain_in, in_grad)
    grad_norm_in = jnp.sum(in_grad * inputs_own * r_own, axis=0)
    normed_own = own_quarter(normed_in.reshape(micro, slots, depth)).reshape(-1, depth)
    grad_rank_t = tn(rank_low, normed_own)
    input_grad = gather_head(input_own.astype(bf16).reshape(micro, quarter, depth)).astype(f32)

    feed = scatter_plane(feed_part.reshape(plane_shape)).reshape(-1, depth)
    block_own = (residual + feed).astype(bf16).reshape(micro, quarter, depth)
    block_out = gather_head(block_own)

    grad_decay = tn(low_rank, logit_low)
    grad_bias = jnp.sum(logit_low.astype(f32), axis=0)
    by_ctx = lambda v: v.reshape(nctx, -1)
    across = lambda v, n: v.reshape(v.shape[0], nctx, n).transpose(1, 0, 2).reshape(nctx, -1)
    summed = jnp.concatenate(
        [by_ctx(grad_norm_in), by_ctx(grad_norm_mid), across(grad_rank_t, rl), by_ctx(grad_gain)], axis=1
    )
    headed = jnp.concatenate([across(grad_decay, dl), by_ctx(grad_bias)], axis=1)
    n_summed, n_headed = summed.shape[1], headed.shape[1]
    pad_s, pad_h = -n_summed % 1024, -n_headed % 1024
    tail = jnp.concatenate(
        [jnp.pad(summed, ((0, 0), (0, pad_s))), jnp.pad(headed, ((0, 0), (0, pad_h)))], axis=1
    ).reshape(nctx, -1, 128)
    tail = jnp.sum(lax.all_to_all(tail, ctx, 0, 0), axis=0)
    cut = (n_summed + pad_s) // 128
    summed, headed = tail[:cut], tail[cut:].reshape(-1)
    summed = summed + swap(summed, "c")
    summed = (summed + swap(summed, "x")).reshape(-1)
    g_norm_in = summed[:rl]
    g_norm_mid = summed[rl : 2 * rl]
    g_rank = summed[2 * rl : (2 + rank) * rl].reshape(rank, rl).T
    g_gain = summed[(2 + rank) * rl : n_summed]
    g_decay = headed[: rank * dl].reshape(1, rank, dl)
    g_bias = headed[rank * dl : n_headed].reshape(1, dl)

    ff_grad = ff_grad.reshape(ny, rl, 3 * fl)
    pieces = jnp.zeros((ny, rl, 3 * fl), bf16)
    pieces = lax.dynamic_update_slice_in_dim(
        pieces, lax.dynamic_index_in_dim(ff_grad, y, 0), y, 0
    )
    for k in range(1, ny):
        sent = lax.dynamic_index_in_dim(ff_grad, lax.rem(y + k, ny), 0)
        got = lax.ppermute(sent, "y", [(i, (i + k) % ny) for i in range(ny)])
        pieces = lax.dynamic_update_slice_in_dim(pieces, got, lax.rem(y - k + ny, ny), 0)

    def joined(i):
        part = pieces[:, :, i * fl : (i + 1) * fl]
        return part.transpose(1, 0, 2).reshape(rl, ff)

    return (
        block_out,
        input_grad,
        g_norm_in,
        qkv_grad[:, :width],
        qkv_grad[:, width : 2 * width],
        qkv_grad[:, 2 * width :],
        go_grad[:, :wide],
        g_rank,
        g_decay,
        g_bias,
        g_gain,
        go_grad[:, wide:].T,
        g_norm_mid,
        joined(0).astype(f32),
        joined(1).astype(f32),
        joined(2).T.astype(f32),
    )


def solution(mesh):
    ctx = mesh.shape["ctx"]
    shape = (NZ, ctx // NZ, 2, mesh.shape["head"] // 2)
    fine = Mesh(mesh.devices.reshape(shape), ("z", "y", "x", "c"))
    c, h = ("z", "y"), ("x", "c")
    in_specs = (
        P(None, c, None), P(None, c, None), P(), P(c), P(c, h), P(c, h), P(c, h), P(c, h), P(c, None),
        P(h, None, c), P(h, c), P(c), P(h, c), P(c), P(c, h), P(c, h), P(h, c),
    )
    out_specs = (
        P(None, c, None), P(None, c, None), P(c), P(c, h), P(c, h), P(c, h), P(c, h), P(c, None),
        P(h, None, c), P(h, c), P(c), P(h, c), P(c), P(c, h), P(c, h), P(h, c),
    )
    return jax.shard_map(
        per_device, mesh=fine, in_specs=in_specs, out_specs=out_specs, check_vma=False
    )
```

time: 2010 us -> 791 us (0.39)
  waiting for transfers between devices: 1220 us -> 337 us
  blocking collectives: 224 us -> 32.9 us
  other arithmetic: 222 us -> 91.8 us
  matrix products: 187 us -> 102 us
  starting transfers between devices: 1.84 us -> 56.9 us
  local copies, waits for them, and re-layouts: 113 us -> 136 us
    reduce_scatter x9 -> x3, waiting for transfers between devices: 691 us -> 35.8 us  [the longest x2 34.5 us: sum_rows(): lax.psum_scatter(total.astype(bf16), 'z', scatter_dimension=0, tiled=True)]
    all_gather x12 -> x3, waiting for transfers between devices: 374 us -> 25.4 us  [the longest x1 21.2 us: per_device(): qkv_parts = others_y(lax.all_gather(w_qkv, 'z', axis=0, tiled=True))]
    ppermute x0 -> x35, waiting for transfers between devices: none -> 216 us  [the longest x28 84 us: swap(): return lax.ppermute(x, axis, [(0, 1), (1, 0)])]
    all_gather x8 -> x0, blocking collectives: 173 us -> none  [the longest x2 35.7 us: carried_in(): pieces = jax.tree.map(lambda part: lax.all_gather(part, axis), value)]
    psum x3 -> x0, waiting for transfers between devices: 112 us -> none  [the longest x1 86.6 us: per_device(): lax.psum(project(hidden, full_down).astype(jnp.bfloat16), 'head')]
    dot_general x78 -> x37, matrix products: 187 us -> 102 us  [dot(): return lax.dot_general(a, b, (dims, ((), ())), preferred_element_type=f32)]
    all_to_all x0 -> x5, waiting for transfers between devices: none -> 59.9 us  [the longest x2 42.5 us: pass_states(): back = lax.all_to_all(jnp.stack(entering), ctx, 0, 0)]
    unnamed x28 -> x6, waiting for transfers between devices: 48.3 us -> 0.1 us
  transfers between devices with their start and end apart: 26 -> 46, of which waited for: 19 -> 28; matrix products, arithmetic and copies ran while one was open for 18% -> 30% of each run, Pallas kernels for 0% -> 2%
where the time goes in v1:
time: 791 us; the launch traced here: 785 us
  waiting for transfers between devices  337 us (43%)
  local copies, waits for them, and re-layouts  136 us (17%)
  matrix products  102 us (13%)
  other arithmetic  91.8 us (12%)
  starting transfers between devices  56.9 us (7%)
  blocking collectives  32.9 us (4%)
  between operations  16.2 us (2%)
  Pallas kernels  12.7 us (2%)
    dot_general x37, matrix products, dot(): return lax.dot_general(a, b, (dims, ((), ())), preferred_element_type=f32)  102 us
    ppermute x28, waiting for transfers between devices, swap(): return lax.ppermute(x, axis, [(0, 1), (1, 0)])  84 us
    ppermute x2, waiting for transfers between devices, sum_rows(): lax.ppermute(parts[k], 'y', [(i, (i + k) % count) for i in range(count)])  67.4 us
    ppermute x3, waiting for transfers between devices, others_y(): lax.ppermute(piece, 'y', [((i + k) % count, i) for i in range(count)])  64.5 us
    all_to_all x2, waiting for transfers between devices, pass_states(): back = lax.all_to_all(jnp.stack(entering), ctx, 0, 0)  42.5 us
    dynamic_slice x6, local copies, waits for them, and re-layouts, relative_columns(): return lax.dynamic_index_in_dim(view, at, 2, keepdims=False).reshape(t, -1)  38.2 us
    reduce_scatter x2, waiting for transfers between devices, sum_rows(): lax.psum_scatter(total.astype(bf16), 'z', scatter_dimension=0, tiled=True)  34.5 us
    all_to_all x1, blocking collectives, pass_states(): got = lax.all_to_all(sent, ctx, 0, 0)  32.9 us
  transfers between devices with their start and end apart: 46, of which 28 were waited for; matrix products, arithmetic and copies ran while one was open for 30% of the time, Pallas kernels for 2%

profile of v1, /device:TPU:0, one launch (start us, length us, event | category | flops | bytes accessed | tf_op | source)
XLA Modules:
  0.0 785.5 jit_solution(1501857864301227007)
XLA Ops:
  14.2 7.3 all-to-all-start
  28.5 5.3 reshape.1349
  34.3 5.4 multiply_convert_fusion.1
  39.7 21.2 %all-gather.4.cloned.1.call-done = bf16[1024,1024]{1,0:T(8,128)(2,1)} async-done(((bf16[256,1024]{1,0:T(8,128)(2,1)}), bf16[1024,1024]{1,0:T(8,128)(2,1)}) %all-gather.4.cloned.1.call-update) | async-done | bytes 2097168 | tf_op jit(solution)/shard_map/all_gather | solution.py:457
  62.4 8.6 %constant_dynamic-slice_fusion.6 = (bf16[512,4,1,256]{3,2,1,0:T(2,128)(2,1)}, bf16[512,4,1,256]{3,2,1,0:T(2,128)(2,1)}) fusion(bf16[512,4,2,256]{3,2,1,0:T(2,128)(2,1)} %multiply_convert_fusion.1, s32[]{:T(128)S(6)} %select_n.181, s32[]{:T(128)S(6)} %select_n.180), kind=kLoop, calls=%fused_computation.293 | loop fusion | bytes 4194312 | tf_op jit(solution)/shard_map/jit(dynamic_index_in_dim)/dynamic_slice | solution.py:413
  72.8 4.6 copy.240
  77.4 4.9 copy.241
  85.5 3.1 fusion.124
  88.6 20.2 %collective-permute-done = bf16[1024,1024]{1,0:T(8,128)(2,1)} collective-permute-done((bf16[1024,1024]{1,0:T(8,128)(2,1)}, bf16[1024,1024]{1,0:T(8,128)(2,1)}, u32[]{:S(2)}, u32[]{:S(2)}) %collective-permute-start) | collective-permute-done | bytes 2097184 | tf_op jit(solution)/shard_map/ppermute | solution.py:404
  111.8 4.5 scan_forward.1
  118.0 4.2 all-to-all-start.1
  125.2 4.1 copy.249
  129.3 8.5 %all-to-all-done.1 = bf16[8,144,256]{2,1,0:T(8,128)(2,1)} async-done(((bf16[8,144,256]{2,1,0:T(8,128)(2,1)}), bf16[8,144,256]{2,1,0:T(8,128)(2,1)}, u32[]{:S(2)}, u32[]{:S(2)}) %all-to-all-start.1) | async-done | bytes 589856 | tf_op jit(solution)/shard_map/all_to_all | solution.py:319
  144.5 3.6 all-to-all-start.2
  153.5 21.6 %all-to-all-done.2 = bf16[8,2,64,256]{3,2,1,0:T(8,128)(2,1)S(1)} async-done(((bf16[8,2,64,256]{3,2,1,0:T(8,128)(2,1)}), bf16[8,2,64,256]{3,2,1,0:T(8,128)(2,1)S(1)}, u32[]{:S(2)}, u32[]{:S(2)}) %all-to-all-start.2) | async-done | bytes 524320 | tf_op jit(solution)/shard_map/all_to_all | solution.py:329
  176.1 25.1 %collective-permute-done.1 = bf16[1024,1024]{0,1:T(8,128)(2,1)} collective-permute-done((bf16[1024,1024]{0,1:T(8,128)(2,1)}, bf16[1024,1024]{0,1:T(8,128)(2,1)}, u32[]{:S(2)}, u32[]{:S(2)}) %collective-permute-start.1) | collective-permute-done | bytes 2097184 | tf_op jit(solution)/shard_map/ppermute | solution.py:404
  201.2 3.0 multiply_convert_fusion.6
  214.7 12.5 %collective-permute-done.3 = bf16[2,64,2048]{2,1,0:T(8,128)(2,1)S(1)} collective-permute-done((bf16[2,64,2048]{2,1,0:T(8,128)(2,1)S(1)}, bf16[2,64,2048]{2,1,0:T(8,128)(2,1)S(1)}, u32[]{:S(2)}, u32[]{:S(2)}) %collective-permute-start.3) | collective-permute-done | bytes 524320 | tf_op jit(solution)/shard_map/ppermute | solution.py:38
  231.1 3.2 select_n.188
  234.3 3.1 select_n.189
  245.0 4.3 collective-permute-done.4
  255.4 7.4 collective-permute-done.5
  262.9 4.9 collective-permute-done.7
  268.3 19.2 %collective-permute-done.17 = bf16[2,2,64,2048]{3,2,1,0:T(8,128)(2,1)S(1)} collective-permute-done((bf16[2,2,64,2048]{3,2,1,0:T(8,128)(2,1)S(1)}, bf16[2,2,64,2048]{3,2,1,0:T(8,128)(2,1)S(1)}, u32[]{:S(2)}, u32[]{:S(2)}) %collective-permute-start.17) | collective-permute-done | bytes 1048608 | tf_op jit(solution)/shard_map/ppermute | solution.py:404
  295.8 4.2 all-gather.8.cloned.1.call-done
  300.0 9.0 %fusion.8 = f32[1024,704]{0,1:T(8,128)} fusion(bf16[1024,2048]{1,0:T(8,128)(2,1)} %bitcast.516, bf16[2048,2112]{1,0:T(8,128)(2,1)} %all-gather.8.cloned.1.call-done), kind=kOutput, calls=%fused_computation.28 | convolution fusion | flops 2952790016 | bytes 10223616 | tf_op jit(solution)/shard_map/dot_general | solution.py:22
  309.0 3.3 fusion.12
  312.4 7.1 multiply_convert_fusion.2
  319.5 5.7 convolution_convert_fusion
  328.6 5.9 fusion.10
  334.6 7.4 add_convert_fusion
  345.0 3.0 select_n.191
  359.5 10.5 %collective-permute-done.11 = bf16[2,64,2048]{2,1,0:T(8,128)(2,1)S(1)} collective-permute-done((bf16[2,64,2048]{2,1,0:T(8,128)(2,1)S(1)}, bf16[2,64,2048]{2,1,0:T(8,128)(2,1)S(1)}, u32[]{:S(2)}, u32[]{:S(2)}) %collective-permute-start.11) | collective-permute-done | bytes 524320 | tf_op jit(solution)/shard_map/ppermute | solution.py:38
  373.4 7.8 collective-permute-done.20
  384.7 3.8 collective-permute-done.12
  388.6 4.3 collective-permute-done.21
  398.0 3.1 add_convert_fusion.6
  401.0 9.4 %collective-permute-done.24 = bf16[2,64,2048]{2,1,0:T(8,128)(2,1)} collective-permute-done((bf16[2,64,2048]{2,1,0:T(8,128)(2,1)}, bf16[2,64,2048]{2,1,0:T(8,128)(2,1)}, u32[]{:S(2)}, u32[]{:S(2)}) %collective-permute-start.24) | collective-permute-done | bytes 524320 | tf_op jit(solution)/shard_map/ppermute | solution.py:38
  415.9 3.3 maximum_select_fusion.1
  419.1 4.9 select_n.204
  424.0 8.5 %constant_dynamic-slice_fusion.3 = (bf16[512,4,1,256]{3,2,1,0:T(2,128)(2,1)}, bf16[512,4,1,256]{3,2,1,0:T(2,128)(2,1)}) fusion(bf16[512,4,2,256]{3,2,1,0:T(2,128)(2,1)} %select_n.204, s32[]{:T(128)S(6)} %select_n.181, s32[]{:T(128)S(6)} %select_n.180), kind=kLoop, calls=%fused_computation.289 | loop fusion | bytes 4194312 | tf_op jit(solution)/shard_map/jit(dynamic_index_in_dim)/dynamic_slice | solution.py:413
  432.5 5.9 copy.268
  441.4 5.8 copy.267
  449.7 3.7 multiply_reduce_fusion.1
  458.1 44.6 %collective-permute-done.33 = bf16[1024,1024]{0,1:T(8,128)(2,1)S(1)} collective-permute-done((bf16[1024,1024]{0,1:T(8,128)(2,1)S(1)}, bf16[1024,1024]{0,1:T(8,128)(2,1)S(1)}, u32[]{:S(2)}, u32[]{:S(2)}) %collective-permute-start.33) | collective-permute-done | bytes 2097184 | tf_op jit(solution)/shard_map/ppermute | solution.py:431
  505.3 5.9 convolution_convert_fusion.2
  511.3 3.4 convolution_convert_fusion.3
  514.7 3.4 convolution_convert_fusion.1
  518.1 4.1 pad_maximum_fusion
  525.2 32.9 %all_to_all.30 = bf16[8,144,256]{2,1,0:T(8,128)(2,1)S(1)} all-to-all(bf16[8,144,256]{2,1,0:T(8,128)(2,1)S(1)} %pad_maximum_fusion.14), channel_id=1, replica_groups=mesh['z'=4,'y'=2,'x'=2,'c'=2] {'z','y'}, dimensions={0} | all-to-all | bytes 1179648 | tf_op jit(solution)/shard_map/all_to_all | solution.py:319
  563.4 4.2 all-to-all-start.4
  571.2 3.3 fusion.54
  574.5 20.9 %all-to-all-done.4 = bf16[8,2,64,256]{3,2,1,0:T(8,128)(2,1)} async-done(((bf16[8,2,64,256]{3,2,1,0:T(8,128)(2,1)}), bf16[8,2,64,256]{3,2,1,0:T(8,128)(2,1)}, u32[]{:S(2)}, u32[]{:S(2)}) %all-to-all-start.4) | async-done | bytes 524320 | tf_op jit(solution)/shard_map/all_to_all | solution.py:329
  597.7 8.2 %scan_backward.1 = (bf16[512,1024]{1,0:T(8,128)(2,1)S(1)}, f32[512,256]{1,0:T(8,128)S(1)}) custom-call(bf16[512,1024]{1,0:T(8,128)(2,1)S(1)} %copy-done.10, f32[512,256]{1,0:T(8,128)S(1)} %copy-done.8, f32[512,256]{1,0:T(8,128)S(1)} %get-tuple-element.220.logit_ref, bf16[512,512]{1,0:T(8,128)(2,1)S(1)} %subtract_convert_fusion.grad_ref, ...), custom_call_target="tpu_custom_call" | custom-call | flops 5000000000 | bytes 12000000 | tf_op jit(solution)/shard_map/scan_backward/pallas_call | solution.py:273
  607.2 3.3 fusion.125
  634.7 9.3 %collective-permute-done.27 = bf16[2,64,2176]{2,1,0:T(8,128)(2,1)} collective-permute-done((bf16[2,64,2176]{2,1,0:T(8,128)(2,1)}, bf16[2,64,2176]{2,1,0:T(8,128)(2,1)}, u32[]{:S(2)}, u32[]{:S(2)}) %collective-permute-start.27) | collective-permute-done | bytes 557088 | tf_op jit(solution)/shard_map/ppermute | solution.py:38
  651.7 3.2 select_n.206
  657.7 22.7 %collective-permute-done.32 = bf16[1024,1024]{1,0:T(8,128)(2,1)} collective-permute-done((bf16[1024,1024]{1,0:T(8,128)(2,1)}, bf16[1024,1024]{1,0:T(8,128)(2,1)}, u32[]{:S(2)}, u32[]{:S(2)}) %collective-permute-start.32) | collective-permute-done | bytes 2097184 | tf_op jit(solution)/shard_map/ppermute | solution.py:431
  680.5 4.3 add_convert_fusion.2
  685.6 5.2 all-to-all-start.5
  697.4 8.9 %all-to-all-done.5 = f32[8,48,128]{2,1,0:T(8,128)S(1)} async-done(((f32[8,48,128]{2,1,0:T(8,128)}), f32[8,48,128]{2,1,0:T(8,128)S(1)}, u32[]{:S(2)}, u32[]{:S(2)}) %all-to-all-start.5) | async-done | bytes 196640 | tf_op jit(solution)/shard_map/all_to_all | solution.py:648
  719.5 4.6 reshape.1395
  724.1 5.4 constant_dynamic-slice_fusion
  733.9 34.5 %reduce-scatter.4.cloned.1.call-done = bf16[256,1024]{1,0:T(8,128)(2,1)} async-done(((bf16[1024,1024]{1,0:T(8,128)(2,1)}), bf16[256,1024]{1,0:T(8,128)(2,1)}) %reduce-scatter.4.cloned.1.call-update) | async-done | bytes 524304 | tf_op jit(solution)/shard_map/reduce_scatter | solution.py:433
  (482 shorter events, 210.7 us)
Async XLA Ops:
  7.2 14.4 %copy-start.59 = (bf16[256,1408]{1,0:T(8,128)(2,1)S(1)}, bf16[256,1408]{1,0:T(8,128)(2,1)}, u32[]{:S(2)}) copy-start(bf16[256,1408]{1,0:T(8,128)(2,1)} %param.36) | copy-start | bytes 2162692
  7.2 14.7 %copy-start.60 = (bf16[256,1408]{1,0:T(8,128)(2,1)S(1)}, bf16[256,1408]{1,0:T(8,128)(2,1)}, u32[]{:S(2)}) copy-start(bf16[256,1408]{1,0:T(8,128)(2,1)} %param.37) | copy-start | bytes 2162692
  7.2 53.7 %all-gather.4.cloned.1.call-start = ((), (), s32[]{:S(2)}) async-start(), calls=%async_computation.9 | async-start | bytes 2621440 | tf_op jit(solution)/shard_map/all_gather | solution.py:457
  14.2 20.0 %all-to-all-start = ((bf16[8,48,128]{2,1,0:T(8,128)(2,1)}), bf16[8,48,128]{2,1,0:T(8,128)(2,1)S(1)}, u32[]{:S(2)}, u32[]{:S(2)}) async-start(bf16[8,48,128]{2,1,0:T(8,128)(2,1)} %broadcast_in_dim.11), calls=%async_computation | async-start | bytes 196608 | tf_op jit(solution)/shard_map/all_to_all | solution.py:467
  21.5 126.9 %all-gather.6.cloned.1.call-start = ((), (), s32[]{:S(2)}) async-start(), calls=%async_computation.10 | async-start | bytes 2621440 | tf_op jit(solution)/shard_map/all_gather | solution.py:458
  25.0 97.9 %collective-permute-start.9 = (bf16[1,256,2112]{1,2,0:T(8,128)(2,1)}, bf16[1,256,2112]{1,2,0:T(8,128)(2,1)}, u32[]{:S(2)}, u32[]{:S(2)}) collective-permute-start(bf16[1,256,2112]{1,2,0:T(8,128)(2,1)} %get-tuple-element.141), channel_id=1, source_target_pairs={{0,4},{4,0},{1,5},{5,1},{2,6},{6,2},{3,7},{7,3},{8,12},{12,8},{9,1... | collective-permute-start | bytes 3244040 | tf_op jit(solution)/shard_map/ppermute | solution.py:494
  33.8 37.1 %copy-start.77 = (f32[2,256]{1,0:T(2,128)}, f32[2,256]{1,0:T(2,128)S(1)}, u32[]{:S(2)}) copy-start(f32[2,256]{1,0:T(2,128)S(1)} %get-tuple-element.215) | copy-start | bytes 6148
  34.2 77.5 %copy-start = (f32[2,4]{1,0:T(2,128)}, f32[2,4]{1,0:T(2,128)S(1)}, u32[]{:S(2)}) copy-start(f32[2,4]{1,0:T(2,128)S(1)} %fusion.106.open_ref) | copy-start | bytes 100
  34.3 36.6 %copy-start.71 = (f32[1,2,8,128]{3,1,2,0:T(2,128)}, f32[1,2,8,128]{3,1,2,0:T(2,128)S(1)}, u32[]{:S(2)}) copy-start(f32[1,2,8,128]{3,1,2,0:T(2,128)S(1)} %copy.306) | copy-start | bytes 24580
  60.9 47.9 %collective-permute-start = (bf16[1024,1024]{1,0:T(8,128)(2,1)}, bf16[1024,1024]{1,0:T(8,128)(2,1)}, u32[]{:S(2)}, u32[]{:S(2)}) collective-permute-start(bf16[1024,1024]{1,0:T(8,128)(2,1)} %all-gather.4.cloned.1.call-done), channel_id=1, source_target_pairs={{4,0},{0,4},{5,1},{1,5},{6,2},{2,6},{7,3},{3,7},{12,8},{8,12},{13,... | collective-permute-start | bytes 6291464 | tf_op jit(solution)/shard_map/ppermute | solution.py:404
  77.4 73.2 %copy-start.31 = (bf16[512,4,1,256]{0,3,1,2:T(8,128)(2,1)}, bf16[512,4,1,256]{0,3,1,2:T(8,128)(2,1)S(1)}, u32[]{:S(2)}) copy-start(bf16[512,4,1,256]{0,3,1,2:T(8,128)(2,1)S(1)} %copy.240) | copy-start | bytes 3145732
  82.3 26.5 %copy-start.52 = (bf16[512,4,1,256]{0,3,1,2:T(8,128)(2,1)}, bf16[512,4,1,256]{0,3,1,2:T(8,128)(2,1)S(1)}, u32[]{:S(2)}) copy-start(bf16[512,4,1,256]{0,3,1,2:T(8,128)(2,1)S(1)} %copy.241) | copy-start | bytes 3145732
  85.5 26.3 %copy-start.7 = (f32[512,256]{1,0:T(8,128)}, f32[512,256]{1,0:T(8,128)S(1)}, u32[]{:S(2)}) copy-start(f32[512,256]{1,0:T(8,128)S(1)} %get-tuple-element.219.decay_ref) | copy-start | bytes 1572868
  118.0 19.8 %all-to-all-start.1 = ((bf16[8,144,256]{2,1,0:T(8,128)(2,1)}), bf16[8,144,256]{2,1,0:T(8,128)(2,1)}, u32[]{:S(2)}, u32[]{:S(2)}) async-start(bf16[8,144,256]{2,1,0:T(8,128)(2,1)} %pad_maximum_fusion.15), calls=%async_computation.1 | async-start | bytes 1179648 | tf_op jit(solution)/shard_map/all_to_all | solution.py:319
  122.2 177.8 %all-gather.8.cloned.1.call-start = ((), (), s32[]{:S(2)}) async-start(), calls=%async_computation.11 | async-start | bytes 11141120 | tf_op jit(solution)/shard_map/all_gather | solution.py:496
  144.5 30.7 %all-to-all-start.2 = ((bf16[8,2,64,256]{3,2,1,0:T(8,128)(2,1)}), bf16[8,2,64,256]{3,2,1,0:T(8,128)(2,1)S(1)}, u32[]{:S(2)}, u32[]{:S(2)}) async-start(bf16[8,2,64,256]{3,2,1,0:T(8,128)(2,1)} %fusion.96), calls=%async_computation.2 | async-start | bytes 1048576 | tf_op jit(solution)/shard_map/all_to_all | solution.py:329
  148.1 568.0 %reduce-scatter.6.cloned.1.call-start = ((), (), s32[]{:S(2)}) async-start(), calls=%async_computation.13 | async-start | bytes 2621440 | tf_op jit(solution)/shard_map/reduce_scatter | solution.py:433
  148.4 52.8 %collective-permute-start.1 = (bf16[1024,1024]{0,1:T(8,128)(2,1)}, bf16[1024,1024]{0,1:T(8,128)(2,1)}, u32[]{:S(2)}, u32[]{:S(2)}) collective-permute-start(bf16[1024,1024]{0,1:T(8,128)(2,1)} %all-gather.6.cloned.1.call-done), channel_id=1, source_target_pairs={{4,0},{0,4},{5,1},{1,5},{6,2},{2,6},{7,3},{3,7},{12,8},{8,12},{13,... | collective-permute-start | bytes 6291464 | tf_op jit(solution)/shard_map/ppermute | solution.py:404
  175.5 25.7 %copy-start.53 = (bf16[512,4,1,256]{0,3,1,2:T(8,128)(2,1)S(1)}, bf16[512,4,1,256]{0,3,1,2:T(8,128)(2,1)}, u32[]{:S(2)}) copy-start(bf16[512,4,1,256]{0,3,1,2:T(8,128)(2,1)} %copy-done.52) | copy-start | bytes 3145732
  175.5 25.7 %copy-start.83 = (f32[512,512]{1,0:T(8,128)S(1)}, f32[512,512]{1,0:T(8,128)}, u32[]{:S(2)}) copy-start(f32[512,512]{1,0:T(8,128)} %fusion.58) | copy-start | bytes 3145732
  176.1 28.1 %copy-start.42 = (f32[512,512]{1,0:T(8,128)}, f32[512,512]{1,0:T(8,128)S(1)}, u32[]{:S(2)}) copy-start(f32[512,512]{1,0:T(8,128)S(1)} %get-tuple-element.120) | copy-start | bytes 3145732
  208.3 3.0 collective-permute-start.2
  213.2 14.0 %collective-permute-start.3 = (bf16[2,64,2048]{2,1,0:T(8,128)(2,1)S(1)}, bf16[2,64,2048]{2,1,0:T(8,128)(2,1)S(1)}, u32[]{:S(2)}, u32[]{:S(2)}) collective-permute-start(bf16[2,64,2048]{2,1,0:T(8,128)(2,1)S(1)} %dynamic-slice_bitcast_fusion.6), channel_id=1, source_target_pairs={{0,2},{2,0},{1,3},{3,1},{4,6},{6,4},{5,7},{7,5},{8,10},{10,8},{9,1... | collective-permute-start | bytes 1572872 | tf_op jit(solution)/shard_map/ppermute | solution.py:38
  241.4 7.9 %collective-permute-start.4 = (bf16[64,2048]{1,0:T(8,128)(2,1)}, bf16[64,2048]{1,0:T(8,128)(2,1)}, u32[]{:S(2)}, u32[]{:S(2)}) collective-permute-start(bf16[64,2048]{1,0:T(8,128)(2,1)} %get-tuple-element.189), channel_id=1, source_target_pairs={{0,4},{4,0},{1,5},{5,1},{2,6},{6,2},{3,7},{7,3},{8,12},{12,8},{9,1... | collective-permute-start | bytes 786440 | tf_op jit(solution)/shard_map/ppermute | solution.py:38
  242.1 9.8 %collective-permute-start.6 = (bf16[64,2048]{1,0:T(8,128)(2,1)}, bf16[64,2048]{1,0:T(8,128)(2,1)}, u32[]{:S(2)}, u32[]{:S(2)}) collective-permute-start(bf16[64,2048]{1,0:T(8,128)(2,1)} %get-tuple-element.188), channel_id=1, source_target_pairs={{0,2},{2,0},{1,3},{3,1},{4,6},{6,4},{5,7},{7,5},{8,10},{10,8},{9,1... | collective-permute-start | bytes 786440 | tf_op jit(solution)/shard_map/ppermute | solution.py:38
  250.4 12.4 %collective-permute-start.5 = (bf16[2,64,2048]{2,1,0:T(8,128)(2,1)S(1)}, bf16[2,64,2048]{2,1,0:T(8,128)(2,1)S(1)}, u32[]{:S(2)}, u32[]{:S(2)}) collective-permute-start(bf16[2,64,2048]{2,1,0:T(8,128)(2,1)S(1)} %get-tuple-element.185), channel_id=1, source_target_pairs={{0,2},{2,0},{1,3},{3,1},{4,6},{6,4},{5,7},{7,5},{8,10},{10,8},{9,1... | collective-permute-start | bytes 1572872 | tf_op jit(solution)/shard_map/ppermute | solution.py:38
  252.9 14.9 %collective-permute-start.7 = (bf16[2,64,2048]{2,1,0:T(8,128)(2,1)S(1)}, bf16[2,64,2048]{2,1,0:T(8,128)(2,1)S(1)}, u32[]{:S(2)}, u32[]{:S(2)}) collective-permute-start(bf16[2,64,2048]{2,1,0:T(8,128)(2,1)S(1)} %get-tuple-element.191), channel_id=1, source_target_pairs={{0,4},{4,0},{1,5},{5,1},{2,6},{6,2},{3,7},{7,3},{8,12},{12,8},{9,1... | collective-permute-start | bytes 1572872 | tf_op jit(solution)/shard_map/ppermute | solution.py:38
  254.0 33.4 %collective-permute-start.17 = (bf16[2,2,64,2048]{3,2,1,0:T(8,128)(2,1)S(1)}, bf16[2,2,64,2048]{3,2,1,0:T(8,128)(2,1)S(1)}, u32[]{:S(2)}, u32[]{:S(2)}) collective-permute-start(bf16[2,2,64,2048]{3,2,1,0:T(8,128)(2,1)S(1)} %get-tuple-element.161), channel_id=1, source_target_pairs={{4,0},{0,4},{5,1},{1,5},{6,2},{2,6},{7,3},{3,7},{12,8},{8,12},{13,... | collective-permute-start | bytes 3145736 | tf_op jit(solution)/shard_map/ppermute | solution.py:404
  268.2 24.9 %collective-permute-start.8 = (bf16[2,2,2,64,2048]{4,3,1,2,0:T(8,128)(2,1)S(1)}, bf16[2,2,2,64,2048]{4,3,1,2,0:T(8,128)(2,1)S(1)}, u32[]{:S(2)}, u32[]{:S(2)}) collective-permute-start(bf16[2,2,2,64,2048]{4,3,1,2,0:T(8,128)(2,1)S(1)} %get-tuple-element.150), channel_id=1, source_target_pairs={{0,1},{1,0},{2,3},{3,2},{4,5},{5,4},{6,7},{7,6},{8,9},{9,8},{10,11... | collective-permute-start | bytes 6291464 | tf_op jit(solution)/shard_map/ppermute | solution.py:38
  287.4 2.7 collective-permute-start.18
  328.6 19.4 %collective-permute-start.10 = (bf16[2,2,2,64,2048]{4,3,1,2,0:T(8,128)(2,1)}, bf16[2,2,2,64,2048]{4,3,1,2,0:T(8,128)(2,1)}, u32[]{:S(2)}, u32[]{:S(2)}) collective-permute-start(bf16[2,2,2,64,2048]{4,3,1,2,0:T(8,128)(2,1)} %copy.250), channel_id=1, source_target_pairs={{0,1},{1,0},{2,3},{3,2},{4,5},{5,4},{6,7},{7,6},{8,9},{9,8},{10,11... | collective-permute-start | bytes 6291464 | tf_op jit(solution)/shard_map/ppermute | solution.py:38
  344.5 6.7 collective-permute-start.19
  355.2 14.8 %collective-permute-start.11 = (bf16[2,64,2048]{2,1,0:T(8,128)(2,1)S(1)}, bf16[2,64,2048]{2,1,0:T(8,128)(2,1)S(1)}, u32[]{:S(2)}, u32[]{:S(2)}) collective-permute-start(bf16[2,64,2048]{2,1,0:T(8,128)(2,1)S(1)} %slice_bitcast_fusion.9), channel_id=1, source_target_pairs={{0,2},{2,0},{1,3},{3,1},{4,6},{6,4},{5,7},{7,5},{8,10},{10,8},{9,1... | collective-permute-start | bytes 1572872 | tf_op jit(solution)/shard_map/ppermute | solution.py:38
  356.7 15.0 %collective-permute-start.13 = (bf16[2,64,2048]{2,1,0:T(8,128)(2,1)S(1)}, bf16[2,64,2048]{2,1,0:T(8,128)(2,1)S(1)}, u32[]{:S(2)}, u32[]{:S(2)}) collective-permute-start(bf16[2,64,2048]{2,1,0:T(8,128)(2,1)S(1)} %slice_bitcast_fusion.7), channel_id=1, source_target_pairs={{0,4},{4,0},{1,5},{5,1},{2,6},{6,2},{3,7},{7,3},{8,12},{12,8},{9,1... | collective-permute-start | bytes 1572872 | tf_op jit(solution)/shard_map/ppermute | solution.py:38
  358.3 23.0 %collective-permute-start.20 = (bf16[2,64,2048]{2,1,0:T(8,128)(2,1)S(1)}, bf16[2,64,2048]{2,1,0:T(8,128)(2,1)S(1)}, u32[]{:S(2)}, u32[]{:S(2)}) collective-permute-start(bf16[2,64,2048]{2,1,0:T(8,128)(2,1)S(1)} %slice_bitcast_fusion.5), channel_id=1, source_target_pairs={{0,2},{2,0},{1,3},{3,1},{4,6},{6,4},{5,7},{7,5},{8,10},{10,8},{9,1... | collective-permute-start | bytes 1572872 | tf_op jit(solution)/shard_map/ppermute | solution.py:38
  358.9 24.1 %collective-permute-start.22 = (bf16[2,64,2048]{2,1,0:T(8,128)(2,1)S(1)}, bf16[2,64,2048]{2,1,0:T(8,128)(2,1)S(1)}, u32[]{:S(2)}, u32[]{:S(2)}) collective-permute-start(bf16[2,64,2048]{2,1,0:T(8,128)(2,1)S(1)} %slice_bitcast_fusion.3), channel_id=1, source_target_pairs={{0,4},{4,0},{1,5},{5,1},{2,6},{6,2},{3,7},{7,3},{8,12},{12,8},{9,1... | collective-permute-start | bytes 1572872 | tf_op jit(solution)/shard_map/ppermute | solution.py:38
  370.2 18.3 %collective-permute-start.12 = (bf16[64,2048]{1,0:T(8,128)(2,1)S(1)}, bf16[64,2048]{1,0:T(8,128)(2,1)S(1)}, u32[]{:S(2)}, u32[]{:S(2)}) collective-permute-start(bf16[64,2048]{1,0:T(8,128)(2,1)S(1)} %slice_bitcast_fusion.17), channel_id=1, source_target_pairs={{0,4},{4,0},{1,5},{5,1},{2,6},{6,2},{3,7},{7,3},{8,12},{12,8},{9,1... | collective-permute-start | bytes 786440 | tf_op jit(solution)/shard_map/ppermute | solution.py:38
  371.9 22.0 %collective-permute-start.14 = (bf16[64,2048]{1,0:T(8,128)(2,1)S(1)}, bf16[64,2048]{1,0:T(8,128)(2,1)S(1)}, u32[]{:S(2)}, u32[]{:S(2)}) collective-permute-start(bf16[64,2048]{1,0:T(8,128)(2,1)S(1)} %slice_bitcast_fusion.15), channel_id=1, source_target_pairs={{0,2},{2,0},{1,3},{3,1},{4,6},{6,4},{5,7},{7,5},{8,10},{10,8},{9,1... | collective-permute-start | bytes 786440 | tf_op jit(solution)/shard_map/ppermute | solution.py:38
  381.4 11.5 %collective-permute-start.21 = (bf16[64,2048]{1,0:T(8,128)(2,1)S(1)}, bf16[64,2048]{1,0:T(8,128)(2,1)S(1)}, u32[]{:S(2)}, u32[]{:S(2)}) collective-permute-start(bf16[64,2048]{1,0:T(8,128)(2,1)S(1)} %slice_bitcast_fusion.13), channel_id=1, source_target_pairs={{0,4},{4,0},{1,5},{5,1},{2,6},{6,2},{3,7},{7,3},{8,12},{12,8},{9,1... | collective-permute-start | bytes 786440 | tf_op jit(solution)/shard_map/ppermute | solution.py:38
  383.1 9.8 %collective-permute-start.23 = (bf16[64,2048]{1,0:T(8,128)(2,1)S(1)}, bf16[64,2048]{1,0:T(8,128)(2,1)S(1)}, u32[]{:S(2)}, u32[]{:S(2)}) collective-permute-start(bf16[64,2048]{1,0:T(8,128)(2,1)S(1)} %slice_bitcast_fusion.11), channel_id=1, source_target_pairs={{0,2},{2,0},{1,3},{3,1},{4,6},{6,4},{5,7},{7,5},{8,10},{10,8},{9,1... | collective-permute-start | bytes 786440 | tf_op jit(solution)/shard_map/ppermute | solution.py:38
  397.4 13.0 %collective-permute-start.24 = (bf16[2,64,2048]{2,1,0:T(8,128)(2,1)}, bf16[2,64,2048]{2,1,0:T(8,128)(2,1)}, u32[]{:S(2)}, u32[]{:S(2)}) collective-permute-start(bf16[2,64,2048]{2,1,0:T(8,128)(2,1)} %get-tuple-element.127), channel_id=1, source_target_pairs={{0,2},{2,0},{1,3},{3,1},{4,6},{6,4},{5,7},{7,5},{8,10},{10,8},{9,1... | collective-permute-start | bytes 1572872 | tf_op jit(solution)/shard_map/ppermute | solution.py:38
  412.9 3.0 collective-permute-start.25
  455.0 47.7 %collective-permute-start.33 = (bf16[1024,1024]{0,1:T(8,128)(2,1)S(1)}, bf16[1024,1024]{0,1:T(8,128)(2,1)S(1)}, u32[]{:S(2)}, u32[]{:S(2)}) collective-permute-start(bf16[1024,1024]{0,1:T(8,128)(2,1)S(1)} %pad_maximum_fusion.5), channel_id=1, source_target_pairs={{0,4},{4,0},{1,5},{5,1},{2,6},{6,2},{3,7},{7,3},{8,12},{12,8},{9,1... | collective-permute-start | bytes 6291464 | tf_op jit(solution)/shard_map/ppermute | solution.py:431
  505.1 214.4 %reduce-scatter.8.cloned.1.call-start = ((), (), s32[]{:S(2)}) async-start(), calls=%async_computation.14 | async-start | bytes 10813440 | tf_op jit(solution)/shard_map/reduce_scatter | solution.py:576
  563.4 31.9 %all-to-all-start.4 = ((bf16[8,2,64,256]{3,2,1,0:T(8,128)(2,1)}), bf16[8,2,64,256]{3,2,1,0:T(8,128)(2,1)}, u32[]{:S(2)}, u32[]{:S(2)}) async-start(bf16[8,2,64,256]{3,2,1,0:T(8,128)(2,1)} %constant_dynamic-update-slice_fusion.1), calls=%async_computation.4 | async-start | bytes 1048576 | tf_op jit(solution)/shard_map/all_to_all | solution.py:329
  567.6 200.8 %reduce-scatter.4.cloned.1.call-start = ((), (), s32[]{:S(2)}) async-start(), calls=%async_computation.12 | async-start | bytes 2621440 | tf_op jit(solution)/shard_map/reduce_scatter | solution.py:433
  570.3 26.1 %copy-start.1 = (f32[2,4]{1,0:T(2,128)S(1)}, f32[2,4]{1,0:T(2,128)}, u32[]{:S(2)}) copy-start(f32[2,4]{1,0:T(2,128)} %copy-done) | copy-start | bytes 100
  570.3 26.1 %copy-start.3 = (s32[256,256]{1,0:T(8,128)S(1)}, s32[256,256]{1,0:T(8,128)}, u32[]{:S(2)}) copy-start(s32[256,256]{1,0:T(8,128)} %constant.241.clone.level_ref) | copy-start | bytes 786436
  570.4 26.1 %copy-start.5 = (bf16[256,256]{1,0:T(8,128)(2,1)S(1)}, bf16[256,256]{1,0:T(8,128)(2,1)}, u32[]{:S(2)}) copy-start(bf16[256,256]{1,0:T(8,128)(2,1)} %constant.240.clone.lower_ref) | copy-start | bytes 393220
  570.4 26.1 %copy-start.6 = (bf16[256,256]{1,0:T(8,128)(2,1)S(1)}, bf16[256,256]{1,0:T(8,128)(2,1)}, u32[]{:S(2)}) copy-start(bf16[256,256]{1,0:T(8,128)(2,1)} %constant.242.clone.upper_ref) | copy-start | bytes 393220
  570.4 26.1 %copy-start.8 = (f32[512,256]{1,0:T(8,128)S(1)}, f32[512,256]{1,0:T(8,128)}, u32[]{:S(2)}) copy-start(f32[512,256]{1,0:T(8,128)} %copy-done.7) | copy-start | bytes 1572868
  570.4 50.3 %collective-permute-start.15 = (bf16[2,64,2048]{2,1,0:T(8,128)(2,1)}, bf16[2,64,2048]{2,1,0:T(8,128)(2,1)}, u32[]{:S(2)}, u32[]{:S(2)}) collective-permute-start(bf16[2,64,2048]{2,1,0:T(8,128)(2,1)} %get-tuple-element.132), channel_id=1, source_target_pairs={{0,2},{2,0},{1,3},{3,1},{4,6},{6,4},{5,7},{7,5},{8,10},{10,8},{9,1... | collective-permute-start | bytes 1572872 | tf_op jit(solution)/shard_map/ppermute | solution.py:38
  618.1 8.3 %collective-permute-start.26 = (bf16[2,128,2176]{2,1,0:T(8,128)(2,1)}, bf16[2,128,2176]{2,1,0:T(8,128)(2,1)}, u32[]{:S(2)}, u32[]{:S(2)}) collective-permute-start(bf16[2,128,2176]{2,1,0:T(8,128)(2,1)} %dynamic-slice_bitcast_fusion), channel_id=1, source_target_pairs={{0,1},{1,0},{2,3},{3,2},{4,5},{5,4},{6,7},{7,6},{8,9},{9,8},{10,11... | collective-permute-start | bytes 3342344 | tf_op jit(solution)/shard_map/ppermute | solution.py:38
  623.4 70.7 %collective-permute-start.16 = (bf16[2,2,64,2048]{3,2,1,0:T(8,128)(2,1)}, bf16[2,2,64,2048]{3,2,1,0:T(8,128)(2,1)}, u32[]{:S(2)}, u32[]{:S(2)}) collective-permute-start(bf16[2,2,64,2048]{3,2,1,0:T(8,128)(2,1)} %maximum_select_fusion.5), channel_id=1, source_target_pairs={{0,1},{1,0},{2,3},{3,2},{4,5},{5,4},{6,7},{7,6},{8,9},{9,8},{10,11... | collective-permute-start | bytes 3145736 | tf_op jit(solution)/shard_map/ppermute | solution.py:38
  629.2 14.8 %collective-permute-start.27 = (bf16[2,64,2176]{2,1,0:T(8,128)(2,1)}, bf16[2,64,2176]{2,1,0:T(8,128)(2,1)}, u32[]{:S(2)}, u32[]{:S(2)}) collective-permute-start(bf16[2,64,2176]{2,1,0:T(8,128)(2,1)} %dynamic-slice_bitcast_fusion.1), channel_id=1, source_target_pairs={{0,2},{2,0},{1,3},{3,1},{4,6},{6,4},{5,7},{7,5},{8,10},{10,8},{9,1... | collective-permute-start | bytes 1671176 | tf_op jit(solution)/shard_map/ppermute | solution.py:38
  632.9 47.6 %collective-permute-start.32 = (bf16[1024,1024]{1,0:T(8,128)(2,1)}, bf16[1024,1024]{1,0:T(8,128)(2,1)}, u32[]{:S(2)}, u32[]{:S(2)}) collective-permute-start(bf16[1024,1024]{1,0:T(8,128)(2,1)} %convolution_convert_fusion.4), channel_id=1, source_target_pairs={{0,4},{4,0},{1,5},{5,1},{2,6},{6,2},{3,7},{7,3},{8,12},{12,8},{9,1... | collective-permute-start | bytes 6291464 | tf_op jit(solution)/shard_map/ppermute | solution.py:431
  651.7 28.7 %copy-start.33 = (bf16[512,4,1,256]{0,3,1,2:T(8,128)(2,1)S(1)}, bf16[512,4,1,256]{0,3,1,2:T(8,128)(2,1)}, u32[]{:S(2)}) copy-start(bf16[512,4,1,256]{0,3,1,2:T(8,128)(2,1)} %copy-done.31) | copy-start | bytes 3145732
  685.6 20.7 %all-to-all-start.5 = ((f32[8,48,128]{2,1,0:T(8,128)}), f32[8,48,128]{2,1,0:T(8,128)S(1)}, u32[]{:S(2)}, u32[]{:S(2)}) async-start(f32[8,48,128]{2,1,0:T(8,128)} %bitcast.464), calls=%async_computation.5 | async-start | bytes 393216 | tf_op jit(solution)/shard_map/all_to_all | solution.py:648
  693.3 14.3 %collective-permute-start.28 = (bf16[2,64,2048]{2,1,0:T(8,128)(2,1)S(1)}, bf16[2,64,2048]{2,1,0:T(8,128)(2,1)S(1)}, u32[]{:S(2)}, u32[]{:S(2)}) collective-permute-start(bf16[2,64,2048]{2,1,0:T(8,128)(2,1)S(1)} %bitcast.493), channel_id=1, source_target_pairs={{0,2},{2,0},{1,3},{3,1},{4,6},{6,4},{5,7},{7,5},{8,10},{10,8},{9,1... | collective-permute-start | bytes 1572872 | tf_op jit(solution)/shard_map/ppermute | solution.py:38
  706.3 1.3 collective-permute-start.30
  707.6 3.8 collective-permute-start.31
  707.8 5.6 collective-permute-start.29
  730.6 41.8 %collective-permute-start.34 = (bf16[1,256,2112]{1,2,0:T(8,128)(2,1)}, bf16[1,256,2112]{1,2,0:T(8,128)(2,1)}, u32[]{:S(2)}, u32[]{:S(2)}) collective-permute-start(bf16[1,256,2112]{1,2,0:T(8,128)(2,1)} %copy.301), channel_id=1, source_target_pairs={{0,4},{4,0},{1,5},{5,1},{2,6},{6,2},{3,7},{7,3},{8,12},{12,8},{9,1... | collective-permute-start | bytes 3244040 | tf_op jit(solution)/shard_map/ppermute | solution.py:667
  733.9 38.2 %copy-start.20 = (bf16[1,256,2112]{1,0,2:T(2,128)(2,1)S(1)}, bf16[1,256,2112]{1,0,2:T(2,128)(2,1)}, u32[]{:S(2)}) copy-start(bf16[1,256,2112]{1,0,2:T(2,128)(2,1)} %get-tuple-element.140) | copy-start | bytes 3244036
  (72 other events, 316.3 us)
Sparse Core Ops, SparseCore 0:
  10.2 50.7 all-gather.3
  63.1 44.9 all-gather.5
  129.4 170.5 all-gather.7
  505.2 50.4 reduce-scatter.5
  558.1 161.3 reduce-scatter.7
  721.7 46.6 reduce-scatter.3

commit v2 on v1

--- a/solution.py
+++ b/solution.py
@@ -36,6 +36,19 @@
 
 def swap(x, axis):
     return lax.ppermute(x, axis, [(0, 1), (1, 0)])
+
+
+def after(value, *earlier):
+    anywhere = pl.BlockSpec(memory_space=pl.ANY)
+    return pl.pallas_call(
+        lambda *refs: None,
+        in_specs=[anywhere] * (1 + len(earlier)),
+        out_specs=anywhere,
+        out_shape=jax.ShapeDtypeStruct(value.shape, value.dtype),
+        input_output_aliases={0: 0},
+        cost_estimate=pl.CostEstimate(flops=0, bytes_accessed=0, transcendentals=0),
+        name="after",
+    )(value, *earlier)
 
 
 def add_low(a, b):
@@ -154,7 +167,8 @@
     keep_ref[0] = jnp.broadcast_to(keep, keep_ref.shape[1:])
 
 
-def scan_backward(qkv_ref, decay_ref, logit_ref, grad_ref, enter_ref, leave_ref, lower_ref, upper_ref, level_ref, open_ref, out_ref, logit_out_ref, local_ref, past_ref):
+def scan_backward(qkv_ref, decay_ref, logit_ref, grad_ref, enter_ref, leave_ref, lower_ref, upper_ref, level_ref, open_ref, *rest):
+    out_ref, logit_out_ref, local_ref, past_ref = rest[-4:]
     step = pl.program_id(0)
     rows, width = decay_ref.shape
     count = rows // GROUP
@@ -260,7 +274,7 @@
     )(qkv, decays, lower, level, is_open)
 
 
-def call_backward(qkv, decays, logits, grads, enter, leave, is_open, micro_count):
+def call_backward(qkv, decays, logits, grads, enter, leave, is_open, micro_count, *earlier):
     rows = qkv.shape[0] // micro_count
     width = decays.shape[1]
     wide = qkv.shape[1] - 2 * width
@@ -284,7 +298,8 @@
             pl.BlockSpec((rows, rows), whole),
             pl.BlockSpec((rows, rows), whole),
             pl.BlockSpec(memory_space=pltpu.SMEM),
-        ],
+        ]
+        + [pl.BlockSpec(memory_space=pl.ANY)] * len(earlier),
         out_specs=[
             pl.BlockSpec((rows, qkv.shape[1]), mine),
             pl.BlockSpec((rows, width), mine),
@@ -300,7 +315,21 @@
         compiler_params=pltpu.CompilerParams(vmem_limit_bytes=40 * 2**20),
         cost_estimate=pl.CostEstimate(flops=5_000_000_000, bytes_accessed=12_000_000, transcendentals=1_500_000),
         name="scan_backward",
-    )(qkv, decays, logits, grads, enter, leave, lower, upper, level, is_open)
+    )(qkv, decays, logits, grads, enter, leave, lower, upper, level, is_open, *earlier)
+
+
+def scan_states(got_ref, out_ref, *, micro, strip, reverse):
+    count = got_ref.shape[0]
+    width = got_ref.shape[2]
+    running = [jnp.zeros((strip, width), f32) for _ in range(micro)]
+    order = range(count - 1, -1, -1) if reverse else range(count)
+    for at in order:
+        tail = got_ref[at, micro * strip :, :].astype(f32)
+        for m in range(micro):
+            span = slice(m * strip, (m + 1) * strip)
+            out_ref[at, span, :] = running[m].astype(bf16)
+            keep = tail[m : m + 1, :] + tail[micro + m : micro + m + 1, :]
+            running[m] = running[m] * keep + got_ref[at, span, :].astype(f32)
 
 
 def pass_states(state, keep, reverse):
@@ -317,17 +346,137 @@
         [parts, jnp.broadcast_to(extra[None], (count, 16, width))], axis=1
     )
     got = lax.all_to_all(sent, ctx, 0, 0)
-    tail = got[:, micro * strip :, :].astype(f32)
-    keeps = tail[:, :micro] + tail[:, micro : 2 * micro]
-    states = got[:, : micro * strip, :].reshape(count, micro, strip, width)
-    running = jnp.zeros((micro, strip, width), f32)
-    entering = [None] * count
-    order = range(count - 1, -1, -1) if reverse else range(count)
-    for at in order:
-        entering[at] = running.astype(bf16)
-        running = running * keeps[at][:, None, :] + states[at].astype(f32)
-    back = lax.all_to_all(jnp.stack(entering), ctx, 0, 0)
-    return back.transpose(1, 0, 2, 3).reshape(micro, wide, width)
+    entering = pl.pallas_call(
+        functools.partial(scan_states, micro=micro, strip=strip, reverse=reverse),
+        out_shape=jax.ShapeDtypeStruct((count, micro * strip, width), bf16),
+        compiler_params=pltpu.CompilerParams(vmem_limit_bytes=16 * 2**20),
+        cost_estimate=pl.CostEstimate(flops=2_000_000, bytes_accessed=1_100_000, transcendentals=0),
+        name="scan_states",
+    )(got)
+    back = lax.all_to_all(entering, ctx, 0, 0)
+    return back.reshape(count, micro, strip, width).transpose(1, 0, 2, 3).reshape(micro, wide, width)
+
+
+def feed_kernel(mid_ref, low_ref, weight_ref, *rest, units):
+    pair_ref, hidden_ref, grad_ref = rest[-3:]
+    both = nn(mid_ref[...], weight_ref[:, : 2 * units])
+    gate, up = both[:, :units], both[:, units:]
+    back = nn(low_ref[...], weight_ref[:, 2 * units :])
+    sig = jax.nn.sigmoid(gate)
+    act = gate * sig
+    hidden_ref[...] = (act * up).astype(bf16)
+    pair_ref[:, :units] = (back * up * (sig * (1.0 + gate * (1.0 - sig)))).astype(bf16)
+    pair_ref[:, units:] = (back * act).astype(bf16)
+    grad_ref[...] = nt(pair_ref[...], weight_ref[:, : 2 * units]).astype(bf16)
+
+
+def call_feed(plane_mid, plane_low, weight, units, *earlier):
+    rows, depth = plane_mid.shape
+    tile = 256
+    return pl.pallas_call(
+        functools.partial(feed_kernel, units=units),
+        grid=(rows // tile,),
+        in_specs=[
+            pl.BlockSpec((tile, depth), lambda i: (i, 0)),
+            pl.BlockSpec((tile, depth), lambda i: (i, 0)),
+            pl.BlockSpec(weight.shape, lambda i: (0, 0), pipeline_mode=pl.Buffered(1)),
+        ]
+        + [pl.BlockSpec(memory_space=pl.ANY)] * len(earlier),
+        out_specs=[
+            pl.BlockSpec((tile, 2 * units), lambda i: (i, 0)),
+            pl.BlockSpec((tile, units), lambda i: (i, 0)),
+            pl.BlockSpec((tile, depth), lambda i: (i, 0)),
+        ],
+        out_shape=[
+            jax.ShapeDtypeStruct((rows, 2 * units), bf16),
+            jax.ShapeDtypeStruct((rows, units), bf16),
+            jax.ShapeDtypeStruct((rows, depth), bf16),
+        ],
+        compiler_params=pltpu.CompilerParams(vmem_limit_bytes=48 * 2**20),
+        cost_estimate=pl.CostEstimate(
+            flops=10 * rows * depth * units, bytes_accessed=28_000_000, transcendentals=rows * units
+        ),
+        name="feed_forward",
+    )(plane_mid, plane_low, weight, *earlier)
+
+
+def split_units(gate_ref, up_ref, down_ref, out_ref):
+    parts, rows, width = out_ref.shape
+    units = width // 3
+    for k in range(parts):
+        span = slice(k * units, (k + 1) * units)
+        out_ref[k, :, :units] = gate_ref[:, span]
+        out_ref[k, :, units : 2 * units] = up_ref[:, span]
+        out_ref[k, :, 2 * units :] = down_ref[span, :].astype(f32).T.astype(bf16)
+
+
+def call_split(w_gate, w_up, w_down, parts):
+    rows, ff = w_gate.shape
+    return pl.pallas_call(
+        split_units,
+        out_shape=jax.ShapeDtypeStruct((parts, rows, 3 * ff // parts), bf16),
+        compiler_params=pltpu.CompilerParams(vmem_limit_bytes=32 * 2**20),
+        cost_estimate=pl.CostEstimate(flops=0, bytes_accessed=12 * rows * ff, transcendentals=0),
+        name="split_units",
+    )(w_gate, w_up, w_down)
+
+
+def join_units(in_ref, gate_ref, up_ref, down_ref):
+    parts, rows, width = in_ref.shape
+    units = width // 3
+    for k in range(parts):
+        span = slice(k * units, (k + 1) * units)
+        gate_ref[:, span] = in_ref[k, :, :units].astype(f32)
+        up_ref[:, span] = in_ref[k, :, units : 2 * units].astype(f32)
+        down_ref[span, :] = in_ref[k, :, 2 * units :].astype(f32).T
+
+
+def call_join(pieces):
+    parts, rows, width = pieces.shape
+    ff = width // 3 * parts
+    return pl.pallas_call(
+        join_units,
+        out_shape=[
+            jax.ShapeDtypeStruct((rows, ff), f32),
+            jax.ShapeDtypeStruct((rows, ff), f32),
+            jax.ShapeDtypeStruct((ff, rows), f32),
+        ],
+        compiler_params=pltpu.CompilerParams(vmem_limit_bytes=32 * 2**20),
+        cost_estimate=pl.CostEstimate(flops=0, bytes_accessed=18 * rows * ff, transcendentals=0),
+        name="join_units",
+    )(pieces)
+
+
+def feed_grad_kernel(*refs):
+    out_ref = refs[-1]
+    two = refs[2].shape[1]
+    mid_a, low_a, pair_a, hidden_a, mid_b, low_b, pair_b, hidden_b = (r[...] for r in refs[:8])
+    out_ref[:, :two] = (tn(mid_a, pair_a) + tn(mid_b, pair_b)).astype(bf16)
+    out_ref[:, two:] = (tn(low_a, hidden_a) + tn(low_b, hidden_b)).astype(bf16)
+
+
+def call_feed_grad(near, far, *earlier):
+    rows, depth = near[0].shape
+    two, units = near[2].shape[1], near[3].shape[1]
+    tile = 256
+    one = [
+        pl.BlockSpec((rows, tile), lambda i: (0, i)),
+        pl.BlockSpec((rows, tile), lambda i: (0, i)),
+        pl.BlockSpec((rows, two), lambda i: (0, 0), pipeline_mode=pl.Buffered(1)),
+        pl.BlockSpec((rows, units), lambda i: (0, 0), pipeline_mode=pl.Buffered(1)),
+    ]
+    return pl.pallas_call(
+        feed_grad_kernel,
+        grid=(depth // tile,),
+        in_specs=one + one + [pl.BlockSpec(memory_space=pl.ANY)] * len(earlier),
+        out_specs=pl.BlockSpec((tile, two + units), lambda i: (i, 0)),
+        out_shape=jax.ShapeDtypeStruct((depth, two + units), bf16),
+        compiler_params=pltpu.CompilerParams(vmem_limit_bytes=48 * 2**20),
+        cost_estimate=pl.CostEstimate(
+            flops=4 * rows * depth * (two + units), bytes_accessed=21_000_000, transcendentals=0
+        ),
+        name="feed_grad",
+    )(*near, *far, *earlier)
 
 
 def gather_plane(piece):
@@ -335,33 +484,36 @@
     if count == 2:
         a, b = piece[0], piece[1]
         a_y, b_x = swap(a, "y"), swap(b, "x")
-        a = jnp.stack([a, a_y])
-        b = jnp.stack([b, b_x])
+        a, b = jnp.stack([a, a_y]), jnp.stack([b, b_x])
         a_x, b_y = swap(a, "x"), swap(b, "y")
-        a = jnp.stack([a, a_x])
-        b = jnp.stack([b, b_y], axis=1)
-        here = jnp.stack([a, b])
+        here = jnp.concatenate([a, a_x, b, b_y])
     else:
         rows = [piece]
         for k in range(1, count):
             rows.append(lax.ppermute(piece, "y", [((i + k) % count, i) for i in range(count)]))
         here = jnp.stack(rows, axis=1)
         here = jnp.stack([here, swap(here, "x")], axis=1)
-    return jnp.stack([here, swap(here, "c")])
-
-
-def scatter_plane(parts):
+        here = here.reshape((-1,) + piece.shape[1:])
+    here = here.reshape(-1, piece.shape[-1])
+    return here, swap(here, "c")
+
+
+def scatter_plane(here, micro, quarter, *between):
     count = lax.axis_size("y")
-    here = add_low(parts[0], swap(parts[1], "c"))
+    depth = here.shape[-1]
     if count == 2:
+        here = here.reshape(2, 2, 2 * quarter, depth)
         a, b = here[0], here[1]
-        a_got, b_got = swap(a[1], "x"), swap(b[:, 1], "y")
-        a = add_low(a[0], a_got)
-        b = add_low(b[:, 0], b_got)
+        a_got, b_got = swap(a[1], "x"), swap(b[1], "y")
+        a = add_low(a[0], a_got).reshape(2, quarter, depth)
+        b = add_low(b[0], b_got).reshape(2, quarter, depth)
+        if between:
+            a, b = after(a, *between), after(b, *between)
         a_got, b_got = swap(a[1], "y"), swap(b[1], "x")
         a = a[0].astype(f32) + a_got.astype(f32)
         b = b[0].astype(f32) + b_got.astype(f32)
         return jnp.stack([a, b])
+    here = here.reshape(micro, 2, count, quarter, depth)
     here = add_low(here[:, 0], swap(here[:, 1], "x"))
     total = here[:, 0].astype(f32)
     for k in range(1, count):
@@ -405,32 +557,66 @@
     return out
 
 
-def relative_columns(array, k):
+def to_relative(array):
     count, y = lax.axis_size("y"), lax.axis_index("y")
     t, depth = array.shape
-    view = array.reshape(t, NZ, count, depth // (NZ * count))
-    at = lax.rem(y + k, count)
-    return lax.dynamic_index_in_dim(view, at, 2, keepdims=False).reshape(t, -1)
-
-
-def absolute_columns(parts):
+    rl = depth // (NZ * count)
+    if count == 2:
+        even = jnp.concatenate([array[:, 2 * z * rl : (2 * z + 1) * rl] for z in range(NZ)], axis=1)
+        odd = jnp.concatenate([array[:, (2 * z + 1) * rl : (2 * z + 2) * rl] for z in range(NZ)], axis=1)
+        first = y == 0
+        return jnp.concatenate([jnp.where(first, even, odd), jnp.where(first, odd, even)], axis=1)
+    view = jnp.roll(array.reshape(t, NZ, count, rl), -y, axis=2)
+    return view.transpose(0, 2, 1, 3).reshape(t, depth)
+
+
+def to_absolute(array):
     count, y = lax.axis_size("y"), lax.axis_index("y")
-    t = parts[0].shape[0]
-    views = [p.reshape(t, NZ, -1) for p in parts]
+    t, depth = array.shape
+    rl = depth // (NZ * count)
     if count == 2:
-        stacked = jnp.where(y == 0, jnp.stack(views, 2), jnp.stack(views[::-1], 2))
+        first = y == 0
+        out = []
+        for z in range(NZ):
+            own = array[:, z * rl : (z + 1) * rl]
+            other = array[:, (NZ + z) * rl : (NZ + z + 1) * rl]
+            out += [jnp.where(first, own, other), jnp.where(first, other, own)]
+        return jnp.concatenate(out, axis=1)
+    view = array.reshape(t, count, NZ, rl).transpose(0, 2, 1, 3)
+    return jnp.roll(view, y, axis=2).reshape(t, depth)
+
+
+def vector_by_ctx(value):
+    count, y = lax.axis_size("y"), lax.axis_index("y")
+    view = value.reshape(value.shape[0], count, NZ, -1)
+    if count == 2:
+        view = jnp.where(y == 0, view, view[:, ::-1])
     else:
-        stacked = jnp.roll(jnp.stack(views, 2), y, axis=2)
-    return stacked.reshape(t, -1)
-
-
-def sum_rows(parts):
+        view = jnp.roll(view, y, axis=1)
+    return view.transpose(2, 1, 0, 3).reshape(NZ * count, value.shape[0], -1)
+
+
+def vector_from_ctx(value):
+    count, y = lax.axis_size("y"), lax.axis_index("y")
+    view = value.reshape((NZ, count) + value.shape[1:]).transpose(2, 1, 0, 3)
+    if count == 2:
+        view = jnp.where(y == 0, view, view[:, ::-1])
+    else:
+        view = jnp.roll(view, -y, axis=1)
+    return view.reshape(value.shape[1], -1)
+
+
+def sum_y(parts):
     count = lax.axis_size("y")
     total = parts[0].astype(f32)
     for k in range(1, count):
         got = lax.ppermute(parts[k], "y", [(i, (i + k) % count) for i in range(count)])
         total = total + got.astype(f32)
-    return lax.psum_scatter(total.astype(bf16), "z", scatter_dimension=0, tiled=True).astype(f32)
+    return total.astype(bf16)
+
+
+def reduce_z(part):
+    return lax.psum_scatter(part, "z", scatter_dimension=0, tiled=True)
 
 
 def per_device(
@@ -453,16 +639,14 @@
     total = micro * slots
 
     w_qkv = jnp.concatenate([w_query, w_key, w_value], axis=1)
-    w_go = jnp.concatenate([w_outgate, w_out.T], axis=1)
-    qkv_parts = others_y(lax.all_gather(w_qkv, "z", axis=0, tiled=True))
-    go_parts = others_y(lax.all_gather(w_go, "z", axis=0, tiled=True))
+    qkv_rows = lax.all_gather(w_qkv, "z", axis=0, tiled=True)
 
     small = jnp.concatenate(
         [norm_in, norm_mid, w_rank.T.reshape(-1), w_decay[0].reshape(-1), decay_bias[0], head_gain]
     )
     n_small = small.shape[0]
     pad = -n_small % 1024
-    small = jnp.pad(small, (0, pad)).reshape(1, -1, 128)
+    small = after(jnp.pad(small, (0, pad)).reshape(1, -1, 128), qkv_rows)
     small = jnp.broadcast_to(small, (nctx,) + small.shape[1:])
     small = lax.all_to_all(small, ctx, 0, 0).reshape(nctx, -1)
     at = 0
@@ -472,30 +656,28 @@
         at += size
         return small[:, at - size : at]
 
-    gain_in = take(rl).reshape(1, depth).astype(f32)
-    gain_mid = take(rl).reshape(1, depth).astype(f32)
-    rank_t = take(rank * rl).reshape(nctx, rank, rl).transpose(1, 0, 2).reshape(rank, depth)
+    by_row = vector_from_ctx(take((2 + rank) * rl).reshape(nctx, 2 + rank, rl))
+    gain_in = by_row[:1].astype(f32)
+    gain_mid = by_row[1:2].astype(f32)
+    rank_t = by_row[2:]
     dl = width // nctx
     decay_w = take(rank * dl).reshape(nctx, rank, dl).transpose(1, 0, 2).reshape(rank, width)
     bias = take(dl).reshape(1, width).astype(f32)
     gain_head = take(wide // nctx).reshape(1, wide).astype(f32)
 
-    def unit_pieces(weight):
-        return weight.reshape(rl, ny, fl).transpose(1, 0, 2)
-
-    ff_local = jnp.concatenate(
-        [unit_pieces(w_gate), unit_pieces(w_up), unit_pieces(w_down.T)], axis=2
-    )
-    ff_unit = jnp.zeros((ny, rl, 3 * fl), bf16)
-    own = lax.dynamic_index_in_dim(ff_local, y, 0)
-    ff_unit = lax.dynamic_update_slice_in_dim(ff_unit, own, y, 0)
-    for k in range(1, ny):
-        sent = lax.dynamic_index_in_dim(ff_local, lax.rem(y + k, ny), 0)
-        got = lax.ppermute(sent, "y", [(i, (i + k) % ny) for i in range(ny)])
-        ff_unit = lax.dynamic_update_slice_in_dim(ff_unit, got, lax.rem(y - k + ny, ny), 0)
-    ff_full = lax.all_gather(ff_unit.reshape(ny * rl, 3 * fl), "z", axis=0, tiled=True)
-
-    slot_ids = place * slots + jnp.arange(slots, dtype=jnp.int32)
+    ff_local = call_split(w_gate, w_up, w_down, ny)
+    own = lax.dynamic_index_in_dim(ff_local, y, 0, keepdims=False)
+    if ny == 2:
+        got = swap(lax.dynamic_index_in_dim(ff_local, 1 - y, 0, keepdims=False), "y")
+        ff_unit = jnp.where(y == 0, jnp.stack([own, got]), jnp.stack([got, own]))
+    else:
+        pieces = [own]
+        for k in range(1, ny):
+            sent = lax.dynamic_index_in_dim(ff_local, lax.rem(y + ny - k, ny), 0, keepdims=False)
+            pieces.append(lax.ppermute(sent, "y", [((i + k) % ny, i) for i in range(ny)]))
+        ff_unit = jnp.roll(jnp.stack(pieces), y, axis=0)
+    ff_unit = ff_unit.reshape(ny * rl, 3 * fl)
+
     group_ids = place * groups + jnp.arange(groups, dtype=jnp.int32)
     end = jnp.zeros((micro, 1), jnp.int32)
     reset = group_ids[None, :] == end
@@ -503,45 +685,72 @@
         end = end + lengths[:, i : i + 1]
         reset = reset | (group_ids[None, :] == end)
     is_open = 1.0 - reset.astype(f32)
-    slot_mask = (slot_ids[None, :] < end * GROUP).astype(bf16)
-
-    out_low = cotangent * slot_mask[:, :, None]
+
+    def mask_of(at):
+        slot_ids = at * slots + jnp.arange(slots, dtype=jnp.int32)
+        return (slot_ids[None, :] < end * GROUP).astype(bf16)[:, :, None]
+
     c_at, x_at = lax.axis_index("c"), lax.axis_index("x")
     quarter = slots // 4
-    view = out_low.reshape(micro, 2, 2, quarter, depth)
-    near = lax.dynamic_index_in_dim(view, c_at, 1, keepdims=False)
-    far = lax.dynamic_index_in_dim(view, 1 - c_at, 1, keepdims=False)
-
-    def x_order(half):
-        first = lax.dynamic_index_in_dim(half, x_at, 1, keepdims=False)
-        second = lax.dynamic_index_in_dim(half, 1 - x_at, 1, keepdims=False)
-        return jnp.stack([first, second], 1)
-
-    near, far = x_order(near), x_order(far)
-    near_y = others_y(near)[1:]
-    near_y = jnp.stack(near_y, 2)
-    far_y = swap(near_y, "c")
-    plane_low = jnp.stack(
-        [
-            jnp.concatenate([near[:, :, None], near_y], 2),
-            jnp.concatenate([far[:, :, None], far_y], 2),
-        ]
-    ).reshape(-1, depth)
-
-    inputs = tokens.astype(f32).reshape(total, depth)
+    view = cotangent.reshape(micro, 2, slots // 2, depth)
+    half_parts = others_y(lax.dynamic_index_in_dim(view, c_at, 1, keepdims=False))
+
+    w_go = jnp.concatenate([w_outgate, w_out.T], axis=1)
+    go_rows = lax.all_gather(w_go, "z", axis=0, tiled=True)
+    ff_full = lax.all_gather(ff_unit, "z", axis=0, tiled=True)
+    qkv_parts = others_y(after(qkv_rows, ff_unit, *half_parts[1:]))
+    go_parts = others_y(go_rows)
+
+    inputs = to_relative(tokens.reshape(total, depth)).astype(f32)
     r_in = inv_rms(inputs)
     normed_in = (inputs * r_in * gain_in).astype(bf16)
-    normed_parts = [relative_columns(normed_in, k) for k in range(ny)]
+    step = depth // ny
     low_rank = nt(normed_in, rank_t).astype(bf16)
     logits = nn(low_rank, decay_w) + bias
     decays = jax.nn.log_sigmoid(logits) / 16.0
-    qkv = sum(nn(n, w) for n, w in zip(normed_parts, qkv_parts)).astype(bf16)
-
-    local_out, far_query, state, keep = call_forward(qkv, decays, is_open, micro)
-    keep = keep[:, 0, :]
-    enter = pass_states(state, keep, False)
-
-    outgate = sum(nn(n, w[:, :wide]) for n, w in zip(normed_parts, go_parts))
+
+    def columns(array, k):
+        return array[:, k * step : (k + 1) * step]
+
+    qkv = sum(nn(columns(normed_in, k), w) for k, w in enumerate(qkv_parts)).astype(bf16)
+
+    once = jnp.minimum(lengths[0, 0], 1)
+
+    def recurrence(_, carry):
+        local_out, far_query, state, keep = call_forward(qkv, decays, is_open, micro)
+        keep = keep[:, 0, :]
+        return local_out, far_query, pass_states(state, keep, False), keep
+
+    local_out, far_query, enter, keep = lax.fori_loop(
+        0,
+        once,
+        recurrence,
+        (
+            jnp.zeros((total, wide), f32),
+            jnp.zeros((total, width), bf16),
+            jnp.zeros((micro, wide, width), bf16),
+            jnp.zeros((micro, width), f32),
+        ),
+    )
+
+    out_low = cotangent * mask_of(place)
+    low_parts = []
+    for k, half in enumerate(half_parts):
+        mask = mask_of(place - y + lax.rem(y + k, ny)).reshape(micro, 2, slots // 2, 1)
+        mask = lax.dynamic_index_in_dim(mask, c_at, 1, keepdims=False)
+        half = (half * mask).reshape(micro, 2, quarter, depth)
+        low_parts.append(jnp.where(x_at == 0, half, half[:, ::-1]))
+    if ny == 2:
+        low_near = [
+            jnp.stack([p[0] for p in low_parts], 1),
+            jnp.stack([p[1] for p in low_parts], 0),
+        ]
+        low_near = jnp.stack(low_near).reshape(-1, depth)
+    else:
+        low_near = jnp.stack(low_parts, 2).reshape(-1, depth)
+    low_far = swap(low_near, "c")
+
+    outgate = sum(nn(columns(normed_in, k), w[:, :wide]) for k, w in enumerate(go_parts))
     outgate = outgate.astype(bf16).astype(f32)
     mixed = local_out + jnp.concatenate(
         [nt(far_query[m * slots : (m + 1) * slots], enter[m]) for m in range(micro)]
@@ -550,39 +759,30 @@
     gated = (mixed * r_head * gain_head * silu(outgate)).astype(bf16)
     attention = jnp.concatenate([nt(gated, w[:, wide:]) for w in go_parts], axis=1)
     attention = scatter_head(attention.astype(bf16).reshape(micro, slots, depth))
-    attention = attention.reshape(micro * quarter, depth)
-    step = depth // ny
-    attention = absolute_columns([attention[:, k * step : (k + 1) * step] for k in range(ny)])
-    inputs_own = own_quarter(tokens).reshape(-1, depth).astype(f32)
-    residual = inputs_own + attention
+    inputs_own = to_relative(own_quarter(tokens).reshape(-1, depth)).astype(f32)
+    residual = inputs_own + attention.reshape(micro * quarter, depth)
 
     r_mid = inv_rms(residual)
-    normed_mid = (residual * r_mid * gain_mid).astype(bf16)
-    plane_mid = gather_plane(normed_mid.reshape(micro, quarter, depth))
-    plane_shape = plane_mid.shape
-    plane_mid = plane_mid.reshape(-1, depth)
-    ff_gate, ff_up, ff_down_t = (ff_full[:, i * fl : (i + 1) * fl] for i in range(3))
-    gate_proj = nn(plane_mid, ff_gate)
-    up_proj = nn(plane_mid, ff_up)
-    hidden = (silu(gate_proj) * up_proj).astype(bf16)
-    hidden_grad = nn(plane_low, ff_down_t)
-    gate_low = (hidden_grad * up_proj * silu_grad(gate_proj)).astype(bf16)
-    up_low = (hidden_grad * silu(gate_proj)).astype(bf16)
-    mid_part = (nt(gate_low, ff_gate) + nt(up_low, ff_up)).astype(bf16)
-    mid_grad = scatter_plane(mid_part.reshape(plane_shape)).reshape(-1, depth)
-    ff_grad = jnp.concatenate(
-        [tn(plane_mid, gate_low), tn(plane_mid, up_low), tn(plane_low, hidden)], axis=1
-    ).astype(bf16)
-    ff_grad = lax.psum_scatter(ff_grad, "z", scatter_dimension=0, tiled=True)
-    feed_part = nt(hidden, ff_down_t).astype(bf16)
-
-    out_grad = own_quarter(out_low).reshape(-1, depth).astype(f32)
+    normed_mid = to_absolute((residual * r_mid * gain_mid).astype(bf16))
+    mid_near, mid_far = gather_plane(normed_mid.reshape(micro, quarter, depth))
+    pair_far, hidden_far, part_far = call_feed(mid_far, low_far, ff_full, fl)
+    pair_near, hidden_near, part_near = call_feed(mid_near, low_near, ff_full, fl, part_far)
+    mid_part = add_low(part_near, swap(part_far, "c"))
+    ff_part = call_feed_grad(
+        (mid_near, low_near, pair_near, hidden_near),
+        (mid_far, low_far, pair_far, hidden_far),
+        mid_part,
+    )
+    ff_grad = reduce_z(ff_part)
+    mid_grad = scatter_plane(mid_part, micro, quarter, ff_part).reshape(-1, depth)
+    mid_grad = to_relative(mid_grad)
+
+    out_grad = to_relative(own_quarter(out_low).reshape(-1, depth)).astype(f32)
     resid_grad = out_grad + norm_back(residual, r_mid, gain_mid, mid_grad)
     grad_norm_mid = jnp.sum(mid_grad * residual * r_mid, axis=0)
     resid_low = gather_head(resid_grad.astype(bf16).reshape(micro, quarter, depth))
     resid_low = resid_low.reshape(total, depth)
-    resid_parts = [relative_columns(resid_low, k) for k in range(ny)]
-    gated_grad = sum(nn(n, w[:, wide:]) for n, w in zip(resid_parts, go_parts))
+    gated_grad = sum(nn(columns(resid_low, k), w[:, wide:]) for k, w in enumerate(go_parts))
 
     unit = mixed * r_head
     gate_act = silu(outgate)
@@ -597,39 +797,52 @@
         ]
     ).astype(bf16)
     leave = pass_states(state_grad, keep, True)
+    hidden_far, hidden_near = after(hidden_far, mixed_grad), after(hidden_near, mixed_grad)
+
+    def feed_part(hidden):
+        return nt(hidden, ff_full[:, 2 * fl :]).astype(bf16)
+
+    feed_far = feed_part(hidden_far)
+    feed_near = feed_part(hidden_near)
+    feed = scatter_plane(add_low(feed_near, swap(feed_far, "c")), micro, quarter).reshape(-1, depth)
+    go_grads = [
+        jnp.concatenate(
+            [tn(columns(normed_in, k), outgate_low), tn(columns(resid_low, k), gated)], axis=1
+        ).astype(bf16)
+        for k in range(ny)
+    ]
+    go_rows_grad = sum_y(go_grads)
+    go_grad = reduce_z(go_rows_grad)
     qkv_low, logit_grad = call_backward(
-        qkv, decays, logits, mixed_grad, enter, leave, is_open, micro
+        qkv, decays, logits, mixed_grad, enter, leave, is_open, micro, go_rows_grad, feed
     )
     logit_low = logit_grad.astype(bf16)
 
-    go_grads = [
-        jnp.concatenate([tn(n, outgate_low), tn(r, gated)], axis=1).astype(bf16)
-        for n, r in zip(normed_parts, resid_parts)
-    ]
-    go_grad = sum_rows(go_grads)
+    qkv_grads = [tn(columns(normed_in, k), qkv_low).astype(bf16) for k in range(ny)]
+    qkv_rows_grad = sum_y(qkv_grads)
+    qkv_grad = reduce_z(qkv_rows_grad).astype(f32)
 
     rank_part = nt(logit_low, decay_w).astype(bf16)
     rank_pad = jnp.pad(rank_part, ((0, 0), (0, 128 - rank)))
+    qkv_later = after(qkv_low, *qkv_grads)
     in_part = [
-        (nt(qkv_low, wq) + nt(outgate_low, wg[:, :wide])).astype(bf16)
+        (nt(qkv_later, wq) + nt(outgate_low, wg[:, :wide])).astype(bf16)
         for wq, wg in zip(qkv_parts, go_parts)
     ]
     in_sum = jnp.concatenate(in_part + [rank_pad], axis=1)
     in_sum = scatter_head(in_sum.reshape(micro, slots, depth + 128)).reshape(-1, depth + 128)
-    qkv_grads = [tn(n, qkv_low).astype(bf16) for n in normed_parts]
-    qkv_grad = sum_rows(qkv_grads)
     rank_low = in_sum[:, depth : depth + rank].astype(bf16)
-    in_grad = absolute_columns([in_sum[:, k * step : (k + 1) * step] for k in range(ny)])
-    in_grad = in_grad + nn(rank_low, rank_t)
+    in_grad = in_sum[:, :depth] + nn(rank_low, rank_t)
     r_own = inv_rms(inputs_own)
     input_own = resid_grad + norm_back(inputs_own, r_own, gain_in, in_grad)
     grad_norm_in = jnp.sum(in_grad * inputs_own * r_own, axis=0)
     normed_own = own_quarter(normed_in.reshape(micro, slots, depth)).reshape(-1, depth)
     grad_rank_t = tn(rank_low, normed_own)
-    input_grad = gather_head(input_own.astype(bf16).reshape(micro, quarter, depth)).astype(f32)
-
-    feed = scatter_plane(feed_part.reshape(plane_shape)).reshape(-1, depth)
-    block_own = (residual + feed).astype(bf16).reshape(micro, quarter, depth)
+    grad_rows = jnp.concatenate([grad_norm_in[None], grad_norm_mid[None], grad_rank_t])
+    input_own = to_absolute(input_own.astype(bf16))
+    input_grad = gather_head(input_own.reshape(micro, quarter, depth)).astype(f32)
+
+    block_own = (to_absolute(residual) + feed).astype(bf16).reshape(micro, quarter, depth)
     block_out = gather_head(block_own)
 
     grad_decay = tn(low_rank, logit_low)
@@ -637,7 +850,7 @@
     by_ctx = lambda v: v.reshape(nctx, -1)
     across = lambda v, n: v.reshape(v.shape[0], nctx, n).transpose(1, 0, 2).reshape(nctx, -1)
     summed = jnp.concatenate(
-        [by_ctx(grad_norm_in), by_ctx(grad_norm_mid), across(grad_rank_t, rl), by_ctx(grad_gain)], axis=1
+        [vector_by_ctx(grad_rows).reshape(nctx, -1), by_ctx(grad_gain)], axis=1
     )
     headed = jnp.concatenate([across(grad_decay, dl), by_ctx(grad_bias)], axis=1)
     n_summed, n_headed = summed.shape[1], headed.shape[1]
@@ -657,6 +870,7 @@
     g_decay = headed[: rank * dl].reshape(1, rank, dl)
     g_bias = headed[rank * dl : n_headed].reshape(1, dl)
 
+    ff_grad = after(ff_grad, qkv_rows_grad)
     ff_grad = ff_grad.reshape(ny, rl, 3 * fl)
     pieces = jnp.zeros((ny, rl, 3 * fl), bf16)
     pieces = lax.dynamic_update_slice_in_dim(
@@ -667,10 +881,7 @@
         got = lax.ppermute(sent, "y", [(i, (i + k) % ny) for i in range(ny)])
         pieces = lax.dynamic_update_slice_in_dim(pieces, got, lax.rem(y - k + ny, ny), 0)
 
-    def joined(i):
-        part = pieces[:, :, i * fl : (i + 1) * fl]
-        return part.transpose(1, 0, 2).reshape(rl, ff)
-
+    g_gate, g_up, g_down = call_join(pieces)
     return (
         block_out,
         input_grad,
@@ -678,16 +889,16 @@
         qkv_grad[:, :width],
         qkv_grad[:, width : 2 * width],
         qkv_grad[:, 2 * width :],
-        go_grad[:, :wide],
+        go_grad[:, :wide].astype(f32),
         g_rank,
         g_decay,
         g_bias,
         g_gain,
-        go_grad[:, wide:].T,
+        go_grad[:, wide:].T.astype(f32),
         g_norm_mid,
-        joined(0).astype(f32),
-        joined(1).astype(f32),
-        joined(2).T.astype(f32),
+        g_gate,
+        g_up,
+        g_down,
     )
 
 

time: 791 us -> 659 us (0.83)
  waiting for transfers between devices: 337 us -> 266 us
  local copies, waits for them, and re-layouts: 136 us -> 77.4 us
  Pallas kernels: 12.7 us -> 61.3 us
  matrix products: 102 us -> 57.9 us
  other arithmetic: 91.8 us -> 81.5 us
    ppermute x2, waiting for transfers between devices: 67.4 us -> 1.41 us  [sum_y(): lax.ppermute(parts[k], 'y', [(i, (i + k) % count) for i in range(count)])]
    pallas_call x0 -> x15, Pallas kernels: none -> 48.3 us  [the longest x2 29.1 us: call_feed(): pl.pallas_call(functools.partial(feed_kernel, units=units), grid=(rows //...]
    dot_general x37 -> x30, matrix products: 102 us -> 57.9 us  [dot(): return lax.dot_general(a, b, (dims, ((), ())), preferred_element_type=f32)]
    dynamic_slice x8 -> x4, local copies, waits for them, and re-layouts: 39.7 us -> 2.61 us  [the longest x1 1.34 us: per_device(): lax.dynamic_index_in_dim(ff_local, 1 - y, 0, keepdims=False)]
    all_to_all x1, waiting for transfers between devices: 8.49 us -> 36.9 us  [pass_states(): got = lax.all_to_all(sent, ctx, 0, 0)]
    ppermute x3, waiting for transfers between devices: 64.5 us -> 40.8 us  [others_y(): lax.ppermute(piece, 'y', [((i + k) % count, i) for i in range(count)])]
    reduce_scatter x3, waiting for transfers between devices: 35.8 us -> 12.8 us  [reduce_z(): return lax.psum_scatter(part, 'z', scatter_dimension=0, tiled=True)]
    all_gather x3, waiting for transfers between devices: 25.4 us -> 45.2 us  [the longest x1 25.7 us: per_device(): go_rows = lax.all_gather(w_go, 'z', axis=0, tiled=True)]
  transfers between devices with their start and end apart: 46 -> 46, of which waited for: 28 -> 26; matrix products, arithmetic and copies ran while one was open for 30% -> 30% of each run, Pallas kernels for 2% -> 5%
where the time goes in v2:
time: 659 us; the launch traced here: 652 us
  waiting for transfers between devices  266 us (40%)
  other arithmetic  81.5 us (12%)
  local copies, waits for them, and re-layouts  77.4 us (12%)
  Pallas kernels  61.3 us (9%)
  matrix products  57.9 us (9%)
  starting transfers between devices  55.4 us (8%)
  blocking collectives  34.9 us (5%)
  between operations  17.9 us (3%)
    ppermute x29, waiting for transfers between devices, swap(): return lax.ppermute(x, axis, [(0, 1), (1, 0)])  88.6 us
    dot_general x30, matrix products, dot(): return lax.dot_general(a, b, (dims, ((), ())), preferred_element_type=f32)  57.9 us
    ppermute x3, waiting for transfers between devices, others_y(): lax.ppermute(piece, 'y', [((i + k) % count, i) for i in range(count)])  40.8 us
    all_to_all x2, waiting for transfers between devices, pass_states(): back = lax.all_to_all(entering, ctx, 0, 0)  39.8 us
    all_to_all x1, waiting for transfers between devices, pass_states(): got = lax.all_to_all(sent, ctx, 0, 0)  36.9 us
    all_to_all x1, blocking collectives, pass_states(): got = lax.all_to_all(sent, ctx, 0, 0)  34.9 us
    pallas_call x2, Pallas kernels, call_feed(): pl.pallas_call(functools.partial(feed_kernel, units=units), grid=(rows //...  29.1 us
    all_gather x1, waiting for transfers between devices, per_device(): go_rows = lax.all_gather(w_go, 'z', axis=0, tiled=True)  25.7 us
  transfers between devices with their start and end apart: 46, of which 26 were waited for; matrix products, arithmetic and copies ran while one was open for 30% of the time, Pallas kernels for 5%

profile of v2, /device:TPU:0, one launch (start us, length us, event | category | flops | bytes accessed | tf_op | source)
XLA Modules:
  0.0 652.2 jit_solution(5304379467982701373)
XLA Ops:
  15.5 3.0 collective-permute-start
  21.2 2.7 fusion.99
  25.8 2.1 constant_dynamic-slice_fusion.2
  37.8 27.3 %collective-permute-done.1.refs_2_ = bf16[2,128,2048]{2,1,0:T(8,128)(2,1)} collective-permute-done((bf16[2,128,2048]{2,1,0:T(8,128)(2,1)}, bf16[2,128,2048]{2,1,0:T(8,128)(2,1)}, u32[]{:S(2)}, u32[]{:S(2)}) %collective-permute-start.1) | collective-permute-done | bytes 1048608 | tf_op jit(solution)/shard_map/ppermute | solution.py:556
  67.7 2.4 copy.236
  71.4 6.1 all-to-all-start.2
  77.5 4.1 maximum_select_fusion
  81.9 2.0 collective-permute-start.2
  83.9 25.7 %all-gather.6.cloned.1.call-done = bf16[1024,1024]{0,1:T(8,128)(2,1)} async-done(((bf16[256,1024]{0,1:T(8,128)(2,1)}), bf16[1024,1024]{0,1:T(8,128)(2,1)}) %all-gather.6.cloned.1.call-update) | async-done | bytes 2097168 | tf_op jit(solution)/shard_map/all_gather | solution.py:699
  117.4 13.5 %collective-permute-done.2 = bf16[1024,1024]{1,0:T(8,128)(2,1)} collective-permute-done((bf16[1024,1024]{1,0:T(8,128)(2,1)}, bf16[1024,1024]{1,0:T(8,128)(2,1)}, u32[]{:S(2)}, u32[]{:S(2)}) %collective-permute-start.2) | collective-permute-done | bytes 2097184 | tf_op jit(solution)/shard_map/ppermute | solution.py:556
  130.9 2.9 fusion.53
  135.1 4.6 scan_forward.3
  143.7 70.0 %while.20 = (s32[]{:T(128)}, f32[512,512]{1,0:T(8,128)}, bf16[512,256]{1,0:T(8,128)(2,1)}, bf16[2,512,256]{2,1,0:T(8,128)(2,1)}, f32[2,256]{1,0:T(2,128)}, /*ind...) while((s32[]{:T(128)}, f32[512,512]{1,0:T(8,128)}, ...), condition=%wide.region_2.3_spmd, body=%wide.region_1.2_spmd.sunk | while | flops 3205762 | bytes 10889749 | solution.py:724
  145.2 34.9 %all_to_all.36.got_ref = bf16[8,144,256]{2,1,0:T(8,128)(2,1)S(1)} all-to-all(bf16[8,144,256]{2,1,0:T(8,128)(2,1)S(1)} %pad_maximum_fusion.32), channel_id=1, replica_groups=mesh['z'=4,'y'=2,'x'=2,'c'=2] {'z','y'}, dimensions={0} | all-to-all | bytes 1179648 | tf_op jit(solution)/shard_map/while/body/all_to_all | solution.py:348
  181.0 5.3 all-to-all-start.1
  188.0 24.6 %all-to-all-done.1 = bf16[8,128,256]{2,1,0:T(8,128)(2,1)S(1)} async-done(((bf16[8,128,256]{2,1,0:T(8,128)(2,1)}), bf16[8,128,256]{2,1,0:T(8,128)(2,1)S(1)}, u32[]{:S(2)}, u32[]{:S(2)}) %all-to-all-start.1) | async-done | bytes 524320 | tf_op jit(solution)/shard_map/while/body/all_to_all | solution.py:356
  217.4 3.0 multiply_convert_fusion.2
  220.4 2.2 convolution_convert_fusion.8
  230.0 10.7 %collective-permute-done.5 = bf16[2,64,2048]{2,1,0:T(8,128)(2,1)S(1)} collective-permute-done((bf16[2,64,2048]{2,1,0:T(8,128)(2,1)S(1)}, bf16[2,64,2048]{2,1,0:T(8,128)(2,1)S(1)}, u32[]{:S(2)}, u32[]{:S(2)}) %collective-permute-start.5) | collective-permute-done | bytes 524320 | tf_op jit(solution)/shard_map/ppermute | solution.py:38
  242.3 2.8 multiply_convert_fusion.1
  248.0 6.2 collective-permute-done.6
  256.2 10.4 %collective-permute-done.7 = bf16[2,64,2048]{2,1,0:T(8,128)(2,1)S(1)} collective-permute-done((bf16[2,64,2048]{2,1,0:T(8,128)(2,1)S(1)}, bf16[2,64,2048]{2,1,0:T(8,128)(2,1)S(1)}, u32[]{:S(2)}, u32[]{:S(2)}) %collective-permute-start.7) | collective-permute-done | bytes 524320 | tf_op jit(solution)/shard_map/ppermute | solution.py:38
  268.4 4.3 collective-permute-done.10.mid_ref.refs_4_
  272.6 19.5 %all-gather.8.cloned.1.call-done.weight_ref = bf16[2048,2112]{1,0:T(8,128)(2,1)} async-done(((bf16[512,2112]{1,0:T(8,128)(2,1)}), bf16[2048,2112]{1,0:T(8,128)(2,1)}) %all-gather.8.cloned.1.call-update) | async-done | bytes 8650768 | tf_op jit(solution)/shard_map/all_gather | solution.py:700
  292.2 14.8 %feed_forward.2 = (bf16[512,1408]{1,0:T(8,128)(2,1)S(1)}, bf16[512,704]{1,0:T(8,128)(2,1)S(1)}, bf16[512,2048]{1,0:T(8,128)(2,1)S(1)}) custom-call(bf16[512,2048]{1,0:T(8,128)(2,1)} %collective-permute-done.10.mid_ref.refs_4_, bf16[512,2048]{1,0:T(8,128)(2,1)} %collective-permute-done.11.low_ref.refs_5_, ...), custom_call_target="tpu_custom_call" | custom-call | flops 7381975040 | bytes 28000000 | tf_op jit(solution)/shard_map/feed_forward/pallas_call | solution.py:376
  308.3 14.3 %feed_forward.3 = (bf16[512,1408]{1,0:T(8,128)(2,1)S(1)}, bf16[512,704]{1,0:T(8,128)(2,1)S(1)}, bf16[512,2048]{1,0:T(8,128)(2,1)S(1)}) custom-call(bf16[512,2048]{1,0:T(8,128)(2,1)} %bitcast.436, bf16[512,2048]{1,0:T(8,128)(2,1)} %bitcast.64.low_ref.refs_1_, bf16[2048,2112]{1,0:T(8,128)(2,1)} %all-gather.8.cloned.1.call-done.weight_ref, ...), custom_call_target="tpu_custom_call" | custom-call | flops 7381975040 | bytes 28000000 | tf_op jit(solution)/shard_map/feed_forward/pallas_call | solution.py:376
  322.7 2.2 add_convert_fusion.3.refs_8_
  324.9 14.4 %feed_grad.1.refs_1_ = bf16[2048,2112]{1,0:T(8,128)(2,1)} custom-call(bf16[512,2048]{1,0:T(8,128)(2,1)} %bitcast.437, bf16[512,2048]{1,0:T(8,128)(2,1)} %bitcast.64.low_ref.refs_1_, bf16[512,1408]{1,0:T(8,128)(2,1)S(1)} %get-tuple-element.315.refs_2_, bf16[512,704]{1,0:T(8,128)(2,1)S(1)} %get-tuple-element.313.refs_3_.refs_0_, ...), custom_call_target="tpu_custom_call" | custom-call | flops 8858370048 | bytes 21000000 | tf_op jit(solution)/shard_map/feed_grad/pallas_call | solution.py:468
  357.2 7.5 %collective-permute-done.13 = bf16[128,2048]{1,0:T(8,128)(2,1)S(1)} collective-permute-done((bf16[128,2048]{1,0:T(8,128)(2,1)S(1)}, bf16[128,2048]{1,0:T(8,128)(2,1)S(1)}, u32[]{:S(2)}, u32[]{:S(2)}) %collective-permute-start.13) | collective-permute-done | bytes 524320 | tf_op jit(solution)/shard_map/ppermute | solution.py:38
  372.0 4.5 collective-permute-done.14
  383.5 11.0 %collective-permute-done.17 = bf16[2,64,2048]{2,1,0:T(8,128)(2,1)S(1)} collective-permute-done((bf16[2,64,2048]{2,1,0:T(8,128)(2,1)S(1)}, bf16[2,64,2048]{2,1,0:T(8,128)(2,1)S(1)}, u32[]{:S(2)}, u32[]{:S(2)}) %collective-permute-start.17) | collective-permute-done | bytes 524320 | tf_op jit(solution)/shard_map/ppermute | solution.py:38
  397.4 2.4 fusion.70
  399.9 2.1 maximum_select_fusion.1
  402.2 2.1 copy-done.106
  405.1 3.2 multiply_reduce_fusion
  409.7 5.4 convolution_convert_fusion
  419.0 3.2 pad_maximum_fusion.3
  424.6 3.8 all-to-all-start.3
  429.1 3.2 convolution_convert_fusion.6
  432.3 2.1 fusion.46
  434.5 5.0 convolution_convert_fusion.1
  439.5 36.9 %all-to-all-done.3.got_ref = bf16[8,144,256]{2,1,0:T(8,128)(2,1)S(1)} async-done(((bf16[8,144,256]{2,1,0:T(8,128)(2,1)}), bf16[8,144,256]{2,1,0:T(8,128)(2,1)S(1)}, u32[]{:S(2)}, u32[]{:S(2)}) %all-to-all-start.3) | async-done | bytes 589856 | tf_op jit(solution)/shard_map/all_to_all | solution.py:348
  477.2 3.5 all-to-all-start.4
  480.8 3.1 add_convert_fusion.2
  490.6 3.3 fusion.43
  493.9 15.2 %all-to-all-done.4 = bf16[8,128,256]{2,1,0:T(8,128)(2,1)S(1)} async-done(((bf16[8,128,256]{2,1,0:T(8,128)(2,1)}), bf16[8,128,256]{2,1,0:T(8,128)(2,1)S(1)}, u32[]{:S(2)}, u32[]{:S(2)}) %all-to-all-start.4) | async-done | bytes 524320 | tf_op jit(solution)/shard_map/all_to_all | solution.py:356
  513.5 3.7 add_convert_fusion.1.rest_0_
  522.5 2.9 collective-permute-done.23
  526.3 2.3 pad_maximum_fusion.8
  528.7 8.3 %scan_backward.1 = (bf16[512,1024]{1,0:T(8,128)(2,1)S(1)}, f32[512,256]{1,0:T(8,128)S(1)}) custom-call(bf16[512,1024]{1,0:T(8,128)(2,1)S(1)} %copy-done.15, f32[512,256]{1,0:T(8,128)S(1)} %get-tuple-element.627.decay_ref, f32[512,256]{1,0:T(8,128)S(1)} %get-tuple-element.628.logit_ref, bf16[512,512]{1,0:T(8,128)(2,1)S(1)} %copy-done.1, ...), custom_call_target="tpu_custom_call" | custom-call | flops 5000000000 | bytes 12000000 | tf_op jit(solution)/shard_map/scan_backward/pallas_call | solution.py:287
  537.0 2.6 convolution_convert_fusion.2.refs_2_
  539.6 2.6 convolution_convert_fusion.3.refs_1_
  543.9 3.3 add_convert_fusion.5
  547.3 2.9 add_convert_fusion.4
  557.5 9.5 %collective-permute-done.24 = bf16[2,64,2048]{2,1,0:T(8,128)(2,1)S(1)} collective-permute-done((bf16[2,64,2048]{2,1,0:T(8,128)(2,1)}, bf16[2,64,2048]{2,1,0:T(8,128)(2,1)S(1)}, u32[]{:S(2)}, u32[]{:S(2)}) %collective-permute-start.24) | collective-permute-done | bytes 524320 | tf_op jit(solution)/shard_map/ppermute | solution.py:38
  568.3 10.2 %collective-permute-done.28 = bf16[2,64,2176]{2,1,0:T(8,128)(2,1)S(1)} collective-permute-done((bf16[2,64,2176]{2,1,0:T(8,128)(2,1)S(1)}, bf16[2,64,2176]{2,1,0:T(8,128)(2,1)S(1)}, u32[]{:S(2)}, u32[]{:S(2)}) %collective-permute-start.28) | collective-permute-done | bytes 557088 | tf_op jit(solution)/shard_map/ppermute | solution.py:38
  581.3 4.0 all-to-all-start.5
  585.8 2.4 fusion.22
  589.6 4.0 add_convert_fusion.refs_1_
  594.2 2.0 maximum_select_fusion.2
  601.6 4.8 collective-permute-done.29
  618.9 2.3 copy.263
  624.1 12.8 %reduce-scatter.4.cloned.1.call-done = bf16[256,1024]{1,0:T(8,128)(2,1)} async-done(((bf16[1024,1024]{1,0:T(8,128)(2,1)}), bf16[256,1024]{1,0:T(8,128)(2,1)}) %reduce-scatter.4.cloned.1.call-update) | async-done | bytes 524304 | tf_op jit(solution)/shard_map/reduce_scatter | solution.py:619
  642.3 2.5 join_units.1
  (622 shorter events, 167.5 us)
Async XLA Ops:
  7.2 62.8 %all-gather.4.cloned.1.call-start = ((), (), s32[]{:S(2)}) async-start(), calls=%async_computation.9 | async-start | bytes 2621440 | tf_op jit(solution)/shard_map/all_gather | solution.py:642
  9.1 100.5 %all-gather.6.cloned.1.call-start = ((), (), s32[]{:S(2)}) async-start(), calls=%async_computation.10 | async-start | bytes 2621440 | tf_op jit(solution)/shard_map/all_gather | solution.py:699
  15.5 52.1 %collective-permute-start = (bf16[256,2112]{0,1:T(8,128)(2,1)}, bf16[256,2112]{0,1:T(8,128)(2,1)}, u32[]{:S(2)}, u32[]{:S(2)}) collective-permute-start(bf16[256,2112]{0,1:T(8,128)(2,1)} %bitcast.390), channel_id=1, source_target_pairs={{0,4},{4,0},{1,5},{5,1},{2,6},{6,2},{3,7},{7,3},{8,12},{12,8},{9,1... | collective-permute-start | bytes 3244040 | tf_op jit(solution)/shard_map/ppermute | solution.py:38
  19.6 45.6 %collective-permute-start.1 = (bf16[2,128,2048]{2,1,0:T(8,128)(2,1)}, bf16[2,128,2048]{2,1,0:T(8,128)(2,1)}, u32[]{:S(2)}, u32[]{:S(2)}) collective-permute-start(bf16[2,128,2048]{2,1,0:T(8,128)(2,1)} %fusion.131), channel_id=1, source_target_pairs={{4,0},{0,4},{5,1},{1,5},{6,2},{2,6},{7,3},{3,7},{12,8},{8,12},{13,... | collective-permute-start | bytes 3145736 | tf_op jit(solution)/shard_map/ppermute | solution.py:556
  35.7 77.0 %copy-start.123 = (f32[512]{0:T(512)}, f32[512]{0:T(512)S(1)}, u32[]{:S(2)}) copy-start(f32[512]{0:T(512)S(1)} %add_rsqrt_fusion.1) | copy-start | bytes 6148
  71.4 40.0 %all-to-all-start.2 = ((bf16[8,48,128]{2,1,0:T(8,128)(2,1)}), bf16[8,48,128]{2,1,0:T(8,128)(2,1)S(1)}, u32[]{:S(2)}, u32[]{:S(2)}) async-start(bf16[8,48,128]{2,1,0:T(8,128)(2,1)} %broadcast_in_dim.31), calls=%async_computation.2 | async-start | bytes 196608 | tf_op jit(solution)/shard_map/all_to_all | solution.py:651
  77.4 214.8 %all-gather.8.cloned.1.call-start = ((), (), s32[]{:S(2)}) async-start(), calls=%async_computation.11 | async-start | bytes 11141120 | tf_op jit(solution)/shard_map/all_gather | solution.py:700
  81.6 527.1 %reduce-scatter.8.cloned.1.call-start = ((), (), s32[]{:S(2)}) async-start(), calls=%async_computation.14 | async-start | bytes 11141120 | tf_op jit(solution)/shard_map/reduce_scatter | solution.py:619
  81.9 49.0 %collective-permute-start.2 = (bf16[1024,1024]{1,0:T(8,128)(2,1)}, bf16[1024,1024]{1,0:T(8,128)(2,1)}, u32[]{:S(2)}, u32[]{:S(2)}) collective-permute-start(bf16[1024,1024]{1,0:T(8,128)(2,1)} %after.9), channel_id=1, source_target_pairs={{4,0},{0,4},{5,1},{1,5},{6,2},{2,6},{7,3},{3,7},{12,8},{8,12},{13,... | collective-permute-start | bytes 6291464 | tf_op jit(solution)/shard_map/ppermute | solution.py:556
  109.6 107.8 %collective-permute-start.3 = (bf16[1024,1024]{0,1:T(8,128)(2,1)}, bf16[1024,1024]{0,1:T(8,128)(2,1)}, u32[]{:S(2)}, u32[]{:S(2)}) collective-permute-start(bf16[1024,1024]{0,1:T(8,128)(2,1)} %all-gather.6.cloned.1.call-done), channel_id=1, source_target_pairs={{4,0},{0,4},{5,1},{1,5},{6,2},{2,6},{7,3},{3,7},{12,8},{8,12},{13,... | collective-permute-start | bytes 6291464 | tf_op jit(solution)/shard_map/ppermute | solution.py:556
  113.3 20.5 %copy-start.28 = (bf16[512,2048]{1,0:T(8,128)(2,1)}, bf16[512,2048]{1,0:T(8,128)(2,1)S(1)}, u32[]{:S(2)}) copy-start(bf16[512,2048]{1,0:T(8,128)(2,1)S(1)} %fusion.3) | copy-start | bytes 6291460
  117.4 16.4 %copy-start.26 = (bf16[1024,1024]{1,0:T(8,128)(2,1)S(1)}, bf16[1024,1024]{1,0:T(8,128)(2,1)}, u32[]{:S(2)}) copy-start(bf16[1024,1024]{1,0:T(8,128)(2,1)} %after.9) | copy-start | bytes 6291460
  181.0 31.7 %all-to-all-start.1 = ((bf16[8,128,256]{2,1,0:T(8,128)(2,1)}), bf16[8,128,256]{2,1,0:T(8,128)(2,1)S(1)}, u32[]{:S(2)}, u32[]{:S(2)}) async-start(bf16[8,128,256]{2,1,0:T(8,128)(2,1)} %scan_states.7), calls=%async_computation.1 | async-start | bytes 1048576 | tf_op jit(solution)/shard_map/while/body/all_to_all | solution.py:356
  223.5 2.7 collective-permute-start.4
  226.6 14.0 %collective-permute-start.5 = (bf16[2,64,2048]{2,1,0:T(8,128)(2,1)S(1)}, bf16[2,64,2048]{2,1,0:T(8,128)(2,1)S(1)}, u32[]{:S(2)}, u32[]{:S(2)}) collective-permute-start(bf16[2,64,2048]{2,1,0:T(8,128)(2,1)S(1)} %dynamic-slice_bitcast_fusion.2), channel_id=1, source_target_pairs={{0,2},{2,0},{1,3},{3,1},{4,6},{6,4},{5,7},{7,5},{8,10},{10,8},{9,1... | collective-permute-start | bytes 1572872 | tf_op jit(solution)/shard_map/ppermute | solution.py:38
  228.5 12.2 %copy-start.43 = (bf16[2,64,1024]{2,1,0:T(8,128)(2,1)S(1)}, bf16[2,64,1024]{2,1,0:T(8,128)(2,1)}, u32[]{:S(2)}) copy-start(bf16[2,64,1024]{2,1,0:T(8,128)(2,1)} %get-tuple-element.605) | copy-start | bytes 786436
  228.5 12.2 %copy-start.44 = (bf16[2,64,1024]{2,1,0:T(8,128)(2,1)S(1)}, bf16[2,64,1024]{2,1,0:T(8,128)(2,1)}, u32[]{:S(2)}) copy-start(bf16[2,64,1024]{2,1,0:T(8,128)(2,1)} %get-tuple-element.606) | copy-start | bytes 786436
  230.0 38.4 %collective-permute-start.11 = (bf16[512,2048]{1,0:T(8,128)(2,1)}, bf16[512,2048]{1,0:T(8,128)(2,1)}, u32[]{:S(2)}, u32[]{:S(2)}) collective-permute-start(bf16[512,2048]{1,0:T(8,128)(2,1)} %bitcast.64.low_ref.refs_1_), channel_id=1, source_target_pairs={{0,1},{1,0},{2,3},{3,2},{4,5},{5,4},{6,7},{7,6},{8,9},{9,8},{10,11... | collective-permute-start | bytes 6291464 | tf_op jit(solution)/shard_map/ppermute | solution.py:38
  245.4 9.6 %collective-permute-start.8 = (bf16[64,2048]{1,0:T(8,128)(2,1)S(1)}, bf16[64,2048]{1,0:T(8,128)(2,1)S(1)}, u32[]{:S(2)}, u32[]{:S(2)}) collective-permute-start(bf16[64,2048]{1,0:T(8,128)(2,1)S(1)} %get-tuple-element.601), channel_id=1, source_target_pairs={{0,2},{2,0},{1,3},{3,1},{4,6},{6,4},{5,7},{7,5},{8,10},{10,8},{9,1... | collective-permute-start | bytes 786440 | tf_op jit(solution)/shard_map/ppermute | solution.py:38
  246.9 7.3 %collective-permute-start.6 = (bf16[64,2048]{1,0:T(8,128)(2,1)S(1)}, bf16[64,2048]{1,0:T(8,128)(2,1)S(1)}, u32[]{:S(2)}, u32[]{:S(2)}) collective-permute-start(bf16[64,2048]{1,0:T(8,128)(2,1)S(1)} %get-tuple-element.602), channel_id=1, source_target_pairs={{0,4},{4,0},{1,5},{5,1},{2,6},{6,2},{3,7},{7,3},{8,12},{12,8},{9,1... | collective-permute-start | bytes 786440 | tf_op jit(solution)/shard_map/ppermute | solution.py:38
  254.3 12.2 %collective-permute-start.7 = (bf16[2,64,2048]{2,1,0:T(8,128)(2,1)S(1)}, bf16[2,64,2048]{2,1,0:T(8,128)(2,1)S(1)}, u32[]{:S(2)}, u32[]{:S(2)}) collective-permute-start(bf16[2,64,2048]{2,1,0:T(8,128)(2,1)S(1)} %pad_maximum_fusion.15), channel_id=1, source_target_pairs={{0,2},{2,0},{1,3},{3,1},{4,6},{6,4},{5,7},{7,5},{8,10},{10,8},{9,1... | collective-permute-start | bytes 1572872 | tf_op jit(solution)/shard_map/ppermute | solution.py:38
  255.0 11.9 %collective-permute-start.9 = (bf16[2,64,2048]{2,1,0:T(8,128)(2,1)S(1)}, bf16[2,64,2048]{2,1,0:T(8,128)(2,1)S(1)}, u32[]{:S(2)}, u32[]{:S(2)}) collective-permute-start(bf16[2,64,2048]{2,1,0:T(8,128)(2,1)S(1)} %pad_maximum_fusion.16), channel_id=1, source_target_pairs={{0,4},{4,0},{1,5},{5,1},{2,6},{6,2},{3,7},{7,3},{8,12},{12,8},{9,1... | collective-permute-start | bytes 1572872 | tf_op jit(solution)/shard_map/ppermute | solution.py:38
  268.4 4.3 collective-permute-start.10
  307.0 17.9 %copy-start.6 = (bf16[512,704]{1,0:T(8,128)(2,1)}, bf16[512,704]{1,0:T(8,128)(2,1)S(1)}, u32[]{:S(2)}) copy-start(bf16[512,704]{1,0:T(8,128)(2,1)S(1)} %get-tuple-element.317.refs_7_.refs_0_) | copy-start | bytes 2162692
  307.0 15.7 %collective-permute-start.12 = (bf16[512,2048]{1,0:T(8,128)(2,1)S(1)}, bf16[512,2048]{1,0:T(8,128)(2,1)S(1)}, u32[]{:S(2)}, u32[]{:S(2)}) collective-permute-start(bf16[512,2048]{1,0:T(8,128)(2,1)S(1)} %get-tuple-element.312.rest_0_), channel_id=1, source_target_pairs={{0,1},{1,0},{2,3},{3,2},{4,5},{5,4},{6,7},{7,6},{8,9},{9,8},{10,11... | collective-permute-start | bytes 6291464 | tf_op jit(solution)/shard_map/ppermute | solution.py:38
  350.8 13.9 %collective-permute-start.13 = (bf16[128,2048]{1,0:T(8,128)(2,1)S(1)}, bf16[128,2048]{1,0:T(8,128)(2,1)S(1)}, u32[]{:S(2)}, u32[]{:S(2)}) collective-permute-start(bf16[128,2048]{1,0:T(8,128)(2,1)S(1)} %get-tuple-element.540), channel_id=1, source_target_pairs={{0,2},{2,0},{1,3},{3,1},{4,6},{6,4},{5,7},{7,5},{8,10},{10,8},{9,1... | collective-permute-start | bytes 1572872 | tf_op jit(solution)/shard_map/ppermute | solution.py:38
  352.3 13.6 %collective-permute-start.15 = (bf16[128,2048]{1,0:T(8,128)(2,1)S(1)}, bf16[128,2048]{1,0:T(8,128)(2,1)S(1)}, u32[]{:S(2)}, u32[]{:S(2)}) collective-permute-start(bf16[128,2048]{1,0:T(8,128)(2,1)S(1)} %get-tuple-element.541), channel_id=1, source_target_pairs={{0,4},{4,0},{1,5},{5,1},{2,6},{6,2},{3,7},{7,3},{8,12},{12,8},{9,1... | collective-permute-start | bytes 1572872 | tf_op jit(solution)/shard_map/ppermute | solution.py:38
  369.0 7.5 %collective-permute-start.14 = (bf16[64,2048]{1,0:T(8,128)(2,1)}, bf16[64,2048]{1,0:T(8,128)(2,1)}, u32[]{:S(2)}, u32[]{:S(2)}) collective-permute-start(bf16[64,2048]{1,0:T(8,128)(2,1)} %slice_bitcast_fusion.6), channel_id=1, source_target_pairs={{0,4},{4,0},{1,5},{5,1},{2,6},{6,2},{3,7},{7,3},{8,12},{12,8},{9,1... | collective-permute-start | bytes 786440 | tf_op jit(solution)/shard_map/ppermute | solution.py:38
  371.4 7.0 %collective-permute-start.16 = (bf16[64,2048]{1,0:T(8,128)(2,1)S(1)}, bf16[64,2048]{1,0:T(8,128)(2,1)S(1)}, u32[]{:S(2)}, u32[]{:S(2)}) collective-permute-start(bf16[64,2048]{1,0:T(8,128)(2,1)S(1)} %slice_bitcast_fusion.4), channel_id=1, source_target_pairs={{0,2},{2,0},{1,3},{3,1},{4,6},{6,4},{5,7},{7,5},{8,10},{10,8},{9,1... | collective-permute-start | bytes 786440 | tf_op jit(solution)/shard_map/ppermute | solution.py:38
  382.7 12.9 %copy-start.81 = (f32[128,256]{1,0:T(8,128)S(1)}, f32[128,256]{1,0:T(8,128)}, u32[]{:S(2)}) copy-start(f32[128,256]{1,0:T(8,128)} %copy-done.80) | copy-start | bytes 393220
  382.7 12.9 %copy-start.79 = (f32[128,256]{1,0:T(8,128)S(1)}, f32[128,256]{1,0:T(8,128)}, u32[]{:S(2)}) copy-start(f32[128,256]{1,0:T(8,128)} %copy-done.78) | copy-start | bytes 393220
  382.7 13.0 %copy-start.138 = (f32[128]{0:T(128)S(1)}, f32[128]{0:T(128)}, u32[]{:S(2)}) copy-start(f32[128]{0:T(128)} %copy-done.137) | copy-start | bytes 1540
  382.7 13.5 %copy-start.144 = (f32[128]{0:T(128)S(1)}, f32[128]{0:T(128)}, u32[]{:S(2)}) copy-start(f32[128]{0:T(128)} %get-tuple-element.586) | copy-start | bytes 1540
  382.7 11.8 %collective-permute-start.17 = (bf16[2,64,2048]{2,1,0:T(8,128)(2,1)S(1)}, bf16[2,64,2048]{2,1,0:T(8,128)(2,1)S(1)}, u32[]{:S(2)}, u32[]{:S(2)}) collective-permute-start(bf16[2,64,2048]{2,1,0:T(8,128)(2,1)S(1)} %add_convert_fusion.10), channel_id=1, source_target_pairs={{0,2},{2,0},{1,3},{3,1},{4,6},{6,4},{5,7},{7,5},{8,10},{10,8},{9,1... | collective-permute-start | bytes 1572872 | tf_op jit(solution)/shard_map/ppermute | solution.py:38
  395.6 4.3 collective-permute-start.18
  415.1 65.7 %collective-permute-start.19 = (bf16[512,2048]{1,0:T(8,128)(2,1)}, bf16[512,2048]{1,0:T(8,128)(2,1)}, u32[]{:S(2)}, u32[]{:S(2)}) collective-permute-start(bf16[512,2048]{1,0:T(8,128)(2,1)} %convolution_convert_fusion), channel_id=1, source_target_pairs={{0,1},{1,0},{2,3},{3,2},{4,5},{5,4},{6,7},{7,6},{8,9},{9,8},{10,11... | collective-permute-start | bytes 6291464 | tf_op jit(solution)/shard_map/ppermute | solution.py:38
  422.2 91.3 %collective-permute-start.26 = (bf16[1024,1024]{1,0:T(8,128)(2,1)}, bf16[1024,1024]{1,0:T(8,128)(2,1)}, u32[]{:S(2)}, u32[]{:S(2)}) collective-permute-start(bf16[1024,1024]{1,0:T(8,128)(2,1)} %pad_maximum_fusion.3), channel_id=1, source_target_pairs={{0,4},{4,0},{1,5},{5,1},{2,6},{6,2},{3,7},{7,3},{8,12},{12,8},{9,1... | collective-permute-start | bytes 6291464 | tf_op jit(solution)/shard_map/ppermute | solution.py:613
  424.6 51.7 %all-to-all-start.3 = ((bf16[8,144,256]{2,1,0:T(8,128)(2,1)}), bf16[8,144,256]{2,1,0:T(8,128)(2,1)S(1)}, u32[]{:S(2)}, u32[]{:S(2)}) async-start(bf16[8,144,256]{2,1,0:T(8,128)(2,1)} %pad_maximum_fusion.11), calls=%async_computation.3 | async-start | bytes 1179648 | tf_op jit(solution)/shard_map/all_to_all | solution.py:348
  477.2 31.8 %all-to-all-start.4 = ((bf16[8,128,256]{2,1,0:T(8,128)(2,1)}), bf16[8,128,256]{2,1,0:T(8,128)(2,1)S(1)}, u32[]{:S(2)}, u32[]{:S(2)}) async-start(bf16[8,128,256]{2,1,0:T(8,128)(2,1)} %scan_states.6), calls=%async_computation.4 | async-start | bytes 1048576 | tf_op jit(solution)/shard_map/all_to_all | solution.py:356
  480.7 140.5 %reduce-scatter.6.cloned.1.call-start = ((), (), s32[]{:S(2)}) async-start(), calls=%async_computation.13 | async-start | bytes 2621440 | tf_op jit(solution)/shard_map/reduce_scatter | solution.py:619
  486.2 22.9 %collective-permute-start.20 = (bf16[128,2048]{1,0:T(8,128)(2,1)}, bf16[128,2048]{1,0:T(8,128)(2,1)}, u32[]{:S(2)}, u32[]{:S(2)}) collective-permute-start(bf16[128,2048]{1,0:T(8,128)(2,1)} %get-tuple-element.536), channel_id=1, source_target_pairs={{0,2},{2,0},{1,3},{3,1},{4,6},{6,4},{5,7},{7,5},{8,10},{10,8},{9,1... | collective-permute-start | bytes 1572872 | tf_op jit(solution)/shard_map/ppermute | solution.py:38
  486.9 22.2 %collective-permute-start.22 = (bf16[128,2048]{1,0:T(8,128)(2,1)}, bf16[128,2048]{1,0:T(8,128)(2,1)}, u32[]{:S(2)}, u32[]{:S(2)}) collective-permute-start(bf16[128,2048]{1,0:T(8,128)(2,1)} %get-tuple-element.537), channel_id=1, source_target_pairs={{0,4},{4,0},{1,5},{5,1},{2,6},{6,2},{3,7},{7,3},{8,12},{12,8},{9,1... | collective-permute-start | bytes 1572872 | tf_op jit(solution)/shard_map/ppermute | solution.py:38
  511.9 8.6 %collective-permute-start.21 = (bf16[64,2048]{1,0:T(8,128)(2,1)}, bf16[64,2048]{1,0:T(8,128)(2,1)}, u32[]{:S(2)}, u32[]{:S(2)}) collective-permute-start(bf16[64,2048]{1,0:T(8,128)(2,1)} %slice.635), channel_id=1, source_target_pairs={{0,4},{4,0},{1,5},{5,1},{2,6},{6,2},{3,7},{7,3},{8,12},{12,8},{9,1... | collective-permute-start | bytes 786440 | tf_op jit(solution)/shard_map/ppermute | solution.py:38
  517.3 8.1 %collective-permute-start.23 = (bf16[64,2048]{1,0:T(8,128)(2,1)S(1)}, bf16[64,2048]{1,0:T(8,128)(2,1)S(1)}, u32[]{:S(2)}, u32[]{:S(2)}) collective-permute-start(bf16[64,2048]{1,0:T(8,128)(2,1)S(1)} %slice.639), channel_id=1, source_target_pairs={{0,2},{2,0},{1,3},{3,1},{4,6},{6,4},{5,7},{7,5},{8,10},{10,8},{9,1... | collective-permute-start | bytes 786440 | tf_op jit(solution)/shard_map/ppermute | solution.py:38
  528.7 8.3 %copy-start.32 = (bf16[512,2048]{1,0:T(8,128)(2,1)S(1)}, bf16[512,2048]{1,0:T(8,128)(2,1)}, u32[]{:S(2)}) copy-start(bf16[512,2048]{1,0:T(8,128)(2,1)} %copy-done.28) | copy-start | bytes 6291460
  542.3 47.3 %collective-permute-start.33 = (bf16[1024,1024]{1,0:T(8,128)(2,1)}, bf16[1024,1024]{1,0:T(8,128)(2,1)}, u32[]{:S(2)}, u32[]{:S(2)}) collective-permute-start(bf16[1024,1024]{1,0:T(8,128)(2,1)} %convolution_convert_fusion.2.refs_2_), channel_id=1, source_target_pairs={{0,4},{4,0},{1,5},{5,1},{2,6},{6,2},{3,7},{7,3},{8,12},{12,8},{9,1... | collective-permute-start | bytes 6291464 | tf_op jit(solution)/shard_map/ppermute | solution.py:613
  551.5 3.3 collective-permute-start.27
  552.0 15.0 %collective-permute-start.24 = (bf16[2,64,2048]{2,1,0:T(8,128)(2,1)}, bf16[2,64,2048]{2,1,0:T(8,128)(2,1)S(1)}, u32[]{:S(2)}, u32[]{:S(2)}) collective-permute-start(bf16[2,64,2048]{2,1,0:T(8,128)(2,1)} %get-tuple-element.553), channel_id=1, source_target_pairs={{0,2},{2,0},{1,3},{3,1},{4,6},{6,4},{5,7},{7,5},{8,10},{10,8},{9,1... | collective-permute-start | bytes 1572872 | tf_op jit(solution)/shard_map/ppermute | solution.py:38
  556.3 22.2 %collective-permute-start.28 = (bf16[2,64,2176]{2,1,0:T(8,128)(2,1)S(1)}, bf16[2,64,2176]{2,1,0:T(8,128)(2,1)S(1)}, u32[]{:S(2)}, u32[]{:S(2)}) collective-permute-start(bf16[2,64,2176]{2,1,0:T(8,128)(2,1)S(1)} %dynamic-slice_bitcast_fusion.1), channel_id=1, source_target_pairs={{0,2},{2,0},{1,3},{3,1},{4,6},{6,4},{5,7},{7,5},{8,10},{10,8},{9,1... | collective-permute-start | bytes 1671176 | tf_op jit(solution)/shard_map/ppermute | solution.py:38
  568.1 26.1 %collective-permute-start.25 = (bf16[2,2,64,2048]{3,2,0,1:T(8,128)(2,1)}, bf16[2,2,64,2048]{3,2,0,1:T(8,128)(2,1)}, u32[]{:S(2)}, u32[]{:S(2)}) collective-permute-start(bf16[2,2,64,2048]{3,2,0,1:T(8,128)(2,1)} %maximum_select_fusion.7), channel_id=1, source_target_pairs={{0,1},{1,0},{2,3},{3,2},{4,5},{5,4},{6,7},{7,6},{8,9},{9,8},{10,11... | collective-permute-start | bytes 3145736 | tf_op jit(solution)/shard_map/ppermute | solution.py:38
  568.1 10.5 %copy-start.59 = (bf16[128,1024]{1,0:T(8,128)(2,1)S(1)}, bf16[128,1024]{1,0:T(8,128)(2,1)}, u32[]{:S(2)}) copy-start(bf16[128,1024]{1,0:T(8,128)(2,1)} %get-tuple-element.603) | copy-start | bytes 786436
  568.1 10.6 %copy-start.60 = (bf16[128,1024]{1,0:T(8,128)(2,1)S(1)}, bf16[128,1024]{1,0:T(8,128)(2,1)}, u32[]{:S(2)}) copy-start(bf16[128,1024]{1,0:T(8,128)(2,1)} %get-tuple-element.604) | copy-start | bytes 786436
  568.1 10.6 %copy-start.110 = (bf16[16,2048]{1,0:T(8,128)(2,1)S(1)}, bf16[16,2048]{1,0:T(8,128)(2,1)}, u32[]{:S(2)}) copy-start(bf16[16,2048]{1,0:T(8,128)(2,1)} %copy-done.109) | copy-start | bytes 196612
  568.1 10.6 %copy-start.115 = (f32[1,2,4,256]{3,0,2,1:T(1,128)S(1)}, f32[1,2,4,256]{3,0,2,1:T(1,128)}, u32[]{:S(2)}) copy-start(f32[1,2,4,256]{3,0,2,1:T(1,128)} %copy-done.113) | copy-start | bytes 24580
  568.1 10.6 %copy-start.142 = (f32[128]{0:T(128)S(1)}, f32[128]{0:T(128)}, u32[]{:S(2)}) copy-start(f32[128]{0:T(128)} %get-tuple-element.624) | copy-start | bytes 1540
  568.3 11.8 %copy-start.66 = (bf16[2048,128]{1,0:T(8,128)(2,1)S(1)}, bf16[2048,128]{1,0:T(8,128)(2,1)}, u32[]{:S(2)}) copy-start(bf16[2048,128]{1,0:T(8,128)(2,1)} %copy.264) | copy-start | bytes 1572868
  581.3 16.4 %all-to-all-start.5 = ((f32[8,48,128]{2,1,0:T(8,128)}), f32[8,48,128]{2,1,0:T(8,128)}, u32[]{:S(2)}, u32[]{:S(2)}) async-start(f32[8,48,128]{2,1,0:T(8,128)} %copy.268), calls=%async_computation.5 | async-start | bytes 393216 | tf_op jit(solution)/shard_map/all_to_all | solution.py:861
  585.3 51.6 %reduce-scatter.4.cloned.1.call-start = ((), (), s32[]{:S(2)}) async-start(), calls=%async_computation.12 | async-start | bytes 2621440 | tf_op jit(solution)/shard_map/reduce_scatter | solution.py:619
  593.8 12.6 %copy-start.45 = (bf16[128,2048]{1,0:T(8,128)(2,1)}, bf16[128,2048]{1,0:T(8,128)(2,1)S(1)}, u32[]{:S(2)}) copy-start(bf16[128,2048]{1,0:T(8,128)(2,1)S(1)} %constant_dynamic-update-slice_fusion.30) | copy-start | bytes 1572868
  593.8 12.6 %collective-permute-start.29 = (bf16[2,64,2048]{2,1,0:T(8,128)(2,1)S(1)}, bf16[2,64,2048]{2,1,0:T(8,128)(2,1)S(1)}, u32[]{:S(2)}, u32[]{:S(2)}) collective-permute-start(bf16[2,64,2048]{2,1,0:T(8,128)(2,1)S(1)} %bitcast.335), channel_id=1, source_target_pairs={{0,2},{2,0},{1,3},{3,1},{4,6},{6,4},{5,7},{7,5},{8,10},{10,8},{9,1... | collective-permute-start | bytes 1572872 | tf_op jit(solution)/shard_map/ppermute | solution.py:38
  598.7 1.3 collective-permute-start.31
  599.9 8.8 %collective-permute-start.32 = (f32[40,128]{1,0:T(8,128)S(1)}, f32[40,128]{1,0:T(8,128)S(1)}, u32[]{:S(2)}, u32[]{:S(2)}) collective-permute-start(f32[40,128]{1,0:T(8,128)S(1)} %slice_add_fusion.2), channel_id=1, source_target_pairs={{0,2},{2,0},{1,3},{3,1},{4,6},{6,4},{5,7},{7,5},{8,10},{10,8},{9,1... | collective-permute-start | bytes 61448 | tf_op jit(solution)/shard_map/ppermute | solution.py:38
  607.5 9.5 %collective-permute-start.30 = (bf16[2,2,64,2048]{3,2,0,1:T(8,128)(2,1)}, bf16[2,2,64,2048]{3,2,0,1:T(8,128)(2,1)}, u32[]{:S(2)}, u32[]{:S(2)}) collective-permute-start(bf16[2,2,64,2048]{3,2,0,1:T(8,128)(2,1)} %maximum_select_fusion.9), channel_id=1, source_target_pairs={{0,1},{1,0},{2,3},{3,2},{4,5},{5,4},{6,7},{7,6},{8,9},{9,8},{10,11... | collective-permute-start | bytes 3145736 | tf_op jit(solution)/shard_map/ppermute | solution.py:38
  612.0 28.5 %collective-permute-start.34 = (bf16[1,256,2112]{1,2,0:T(8,128)(2,1)}, bf16[1,256,2112]{1,2,0:T(8,128)(2,1)}, u32[]{:S(2)}, u32[]{:S(2)}) collective-permute-start(bf16[1,256,2112]{1,2,0:T(8,128)(2,1)} %copy.269), channel_id=1, source_target_pairs={{0,4},{4,0},{1,5},{5,1},{2,6},{6,2},{3,7},{7,3},{8,12},{12,8},{9,1... | collective-permute-start | bytes 3244040 | tf_op jit(solution)/shard_map/ppermute | solution.py:881
  (134 other events, 422.5 us)
Sparse Core Ops, SparseCore 0:
  10.2 48.6 all-gather.3
  61.0 48.6 all-gather.5
  111.8 180.3 all-gather.7
  339.5 168.5 reduce-scatter.7
  517.4 42.3 reduce-scatter.5
  593.7 43.1 reduce-scatter.3

commit v3 on v2

--- a/solution.py
+++ b/solution.py
@@ -49,6 +49,13 @@
         cost_estimate=pl.CostEstimate(flops=0, bytes_accessed=0, transcendentals=0),
         name="after",
     )(value, *earlier)
+
+
+def as_one(runs, work):
+    shapes = jax.eval_shape(work)
+    return lax.cond(
+        runs, work, lambda: jax.tree.map(lambda s: jnp.zeros(s.shape, s.dtype), shapes)
+    )
 
 
 def add_low(a, b):
@@ -332,7 +339,7 @@
             running[m] = running[m] * keep + got_ref[at, span, :].astype(f32)
 
 
-def pass_states(state, keep, reverse):
+def spread_states(state, keep, reverse):
     ctx = ("z", "y")
     count = lax.axis_size(ctx)
     micro, wide, width = state.shape
@@ -346,15 +353,20 @@
         [parts, jnp.broadcast_to(extra[None], (count, 16, width))], axis=1
     )
     got = lax.all_to_all(sent, ctx, 0, 0)
-    entering = pl.pallas_call(
+    return pl.pallas_call(
         functools.partial(scan_states, micro=micro, strip=strip, reverse=reverse),
         out_shape=jax.ShapeDtypeStruct((count, micro * strip, width), bf16),
         compiler_params=pltpu.CompilerParams(vmem_limit_bytes=16 * 2**20),
         cost_estimate=pl.CostEstimate(flops=2_000_000, bytes_accessed=1_100_000, transcendentals=0),
         name="scan_states",
     )(got)
-    back = lax.all_to_all(entering, ctx, 0, 0)
-    return back.reshape(count, micro, strip, width).transpose(1, 0, 2, 3).reshape(micro, wide, width)
+
+
+def collect_states(entering, micro):
+    count, _, width = entering.shape
+    strip = entering.shape[1] // micro
+    back = lax.all_to_all(entering, ("z", "y"), 0, 0)
+    return back.reshape(count, micro, strip, width).transpose(1, 0, 2, 3).reshape(micro, -1, width)
 
 
 def feed_kernel(mid_ref, low_ref, weight_ref, *rest, units):
@@ -498,26 +510,30 @@
     return here, swap(here, "c")
 
 
-def scatter_plane(here, micro, quarter, *between):
+def scatter_first(here, micro, quarter):
     count = lax.axis_size("y")
     depth = here.shape[-1]
     if count == 2:
         here = here.reshape(2, 2, 2 * quarter, depth)
         a, b = here[0], here[1]
         a_got, b_got = swap(a[1], "x"), swap(b[1], "y")
-        a = add_low(a[0], a_got).reshape(2, quarter, depth)
-        b = add_low(b[0], b_got).reshape(2, quarter, depth)
-        if between:
-            a, b = after(a, *between), after(b, *between)
+        return add_low(a[0], a_got), add_low(b[0], b_got)
+    here = here.reshape(micro, 2, count, quarter, depth)
+    here = add_low(here[:, 0], swap(here[:, 1], "x"))
+    return here[:, :1], here[:, 1:]
+
+
+def scatter_second(a, b, quarter):
+    count = lax.axis_size("y")
+    if count == 2:
+        a, b = (v.reshape(2, quarter, -1) for v in (a, b))
         a_got, b_got = swap(a[1], "y"), swap(b[1], "x")
         a = a[0].astype(f32) + a_got.astype(f32)
         b = b[0].astype(f32) + b_got.astype(f32)
         return jnp.stack([a, b])
-    here = here.reshape(micro, 2, count, quarter, depth)
-    here = add_low(here[:, 0], swap(here[:, 1], "x"))
-    total = here[:, 0].astype(f32)
+    total = a[:, 0].astype(f32)
     for k in range(1, count):
-        got = lax.ppermute(here[:, k], "y", [(i, (i + k) % count) for i in range(count)])
+        got = lax.ppermute(b[:, k - 1], "y", [(i, (i + k) % count) for i in range(count)])
         total = total + got.astype(f32)
     return total
 
@@ -606,9 +622,9 @@
     return view.reshape(value.shape[1], -1)
 
 
-def sum_y(parts):
+def sum_y(parts, *between):
     count = lax.axis_size("y")
-    total = parts[0].astype(f32)
+    total = (after(parts[0], *between) if between else parts[0]).astype(f32)
     for k in range(1, count):
         got = lax.ppermute(parts[k], "y", [(i, (i + k) % count) for i in range(count)])
         total = total + got.astype(f32)
@@ -640,13 +656,15 @@
 
     w_qkv = jnp.concatenate([w_query, w_key, w_value], axis=1)
     qkv_rows = lax.all_gather(w_qkv, "z", axis=0, tiled=True)
+    w_go = jnp.concatenate([w_outgate, w_out.T], axis=1)
+    go_rows = lax.all_gather(w_go, "z", axis=0, tiled=True)
 
     small = jnp.concatenate(
         [norm_in, norm_mid, w_rank.T.reshape(-1), w_decay[0].reshape(-1), decay_bias[0], head_gain]
     )
     n_small = small.shape[0]
     pad = -n_small % 1024
-    small = after(jnp.pad(small, (0, pad)).reshape(1, -1, 128), qkv_rows)
+    small = jnp.pad(small, (0, pad)).reshape(1, -1, 128)
     small = jnp.broadcast_to(small, (nctx,) + small.shape[1:])
     small = lax.all_to_all(small, ctx, 0, 0).reshape(nctx, -1)
     at = 0
@@ -695,10 +713,8 @@
     view = cotangent.reshape(micro, 2, slots // 2, depth)
     half_parts = others_y(lax.dynamic_index_in_dim(view, c_at, 1, keepdims=False))
 
-    w_go = jnp.concatenate([w_outgate, w_out.T], axis=1)
-    go_rows = lax.all_gather(w_go, "z", axis=0, tiled=True)
     ff_full = lax.all_gather(ff_unit, "z", axis=0, tiled=True)
-    qkv_parts = others_y(after(qkv_rows, ff_unit, *half_parts[1:]))
+    qkv_parts = others_y(qkv_rows)
     go_parts = others_y(go_rows)
 
     inputs = to_relative(tokens.reshape(total, depth)).astype(f32)
@@ -714,24 +730,14 @@
 
     qkv = sum(nn(columns(normed_in, k), w) for k, w in enumerate(qkv_parts)).astype(bf16)
 
-    once = jnp.minimum(lengths[0, 0], 1)
-
-    def recurrence(_, carry):
+    runs = lengths[0, 0] >= 1
+
+    def recurrence():
         local_out, far_query, state, keep = call_forward(qkv, decays, is_open, micro)
         keep = keep[:, 0, :]
-        return local_out, far_query, pass_states(state, keep, False), keep
-
-    local_out, far_query, enter, keep = lax.fori_loop(
-        0,
-        once,
-        recurrence,
-        (
-            jnp.zeros((total, wide), f32),
-            jnp.zeros((total, width), bf16),
-            jnp.zeros((micro, wide, width), bf16),
-            jnp.zeros((micro, width), f32),
-        ),
-    )
+        return local_out, far_query, collect_states(spread_states(state, keep, False), micro), keep
+
+    local_out, far_query, enter, keep = as_one(runs, recurrence)
 
     out_low = cotangent * mask_of(place)
     low_parts = []
@@ -768,120 +774,136 @@
     pair_far, hidden_far, part_far = call_feed(mid_far, low_far, ff_full, fl)
     pair_near, hidden_near, part_near = call_feed(mid_near, low_near, ff_full, fl, part_far)
     mid_part = add_low(part_near, swap(part_far, "c"))
-    ff_part = call_feed_grad(
-        (mid_near, low_near, pair_near, hidden_near),
-        (mid_far, low_far, pair_far, hidden_far),
-        mid_part,
-    )
+    def feed_back():
+        ff_part = call_feed_grad(
+            (mid_near, low_near, pair_near, hidden_near),
+            (mid_far, low_far, pair_far, hidden_far),
+        )
+        return ff_part, *scatter_first(mid_part, micro, quarter)
+
+    ff_part, mid_a, mid_b = as_one(runs, feed_back)
     ff_grad = reduce_z(ff_part)
-    mid_grad = scatter_plane(mid_part, micro, quarter, ff_part).reshape(-1, depth)
-    mid_grad = to_relative(mid_grad)
-
-    out_grad = to_relative(own_quarter(out_low).reshape(-1, depth)).astype(f32)
-    resid_grad = out_grad + norm_back(residual, r_mid, gain_mid, mid_grad)
-    grad_norm_mid = jnp.sum(mid_grad * residual * r_mid, axis=0)
-    resid_low = gather_head(resid_grad.astype(bf16).reshape(micro, quarter, depth))
-    resid_low = resid_low.reshape(total, depth)
-    gated_grad = sum(nn(columns(resid_low, k), w[:, wide:]) for k, w in enumerate(go_parts))
-
-    unit = mixed * r_head
-    gate_act = silu(outgate)
-    unit_grad = gated_grad * gate_act
-    outgate_low = (gated_grad * unit * gain_head * silu_grad(outgate)).astype(bf16)
-    mixed_grad = norm_back(mixed, r_head, gain_head, unit_grad).astype(bf16)
-    grad_gain = jnp.sum(unit_grad * unit, axis=0)
-    state_grad = jnp.stack(
-        [
-            tn(mixed_grad[m * slots : (m + 1) * slots], far_query[m * slots : (m + 1) * slots])
-            for m in range(micro)
-        ]
-    ).astype(bf16)
-    leave = pass_states(state_grad, keep, True)
-    hidden_far, hidden_near = after(hidden_far, mixed_grad), after(hidden_near, mixed_grad)
 
     def feed_part(hidden):
         return nt(hidden, ff_full[:, 2 * fl :]).astype(bf16)
 
-    feed_far = feed_part(hidden_far)
-    feed_near = feed_part(hidden_near)
-    feed = scatter_plane(add_low(feed_near, swap(feed_far, "c")), micro, quarter).reshape(-1, depth)
-    go_grads = [
-        jnp.concatenate(
-            [tn(columns(normed_in, k), outgate_low), tn(columns(resid_low, k), gated)], axis=1
+    def blocks_back():
+        mid_grad = to_relative(scatter_second(mid_a, mid_b, quarter).reshape(-1, depth))
+
+        out_grad = to_relative(own_quarter(out_low).reshape(-1, depth)).astype(f32)
+        resid_grad = out_grad + norm_back(residual, r_mid, gain_mid, mid_grad)
+        grad_norm_mid = jnp.sum(mid_grad * residual * r_mid, axis=0)
+        resid_low = gather_head(resid_grad.astype(bf16).reshape(micro, quarter, depth))
+        resid_low = resid_low.reshape(total, depth)
+        gated_grad = sum(nn(columns(resid_low, k), w[:, wide:]) for k, w in enumerate(go_parts))
+
+        unit = mixed * r_head
+        gate_act = silu(outgate)
+        unit_grad = gated_grad * gate_act
+        outgate_low = (gated_grad * unit * gain_head * silu_grad(outgate)).astype(bf16)
+        mixed_grad = norm_back(mixed, r_head, gain_head, unit_grad).astype(bf16)
+        grad_gain = jnp.sum(unit_grad * unit, axis=0)
+        state_grad = jnp.stack(
+            [
+                tn(mixed_grad[m * slots : (m + 1) * slots], far_query[m * slots : (m + 1) * slots])
+                for m in range(micro)
+            ]
         ).astype(bf16)
-        for k in range(ny)
-    ]
-    go_rows_grad = sum_y(go_grads)
+        entering = spread_states(state_grad, keep, True)
+        leave = collect_states(entering, micro)
+        go_grads = [
+            jnp.concatenate(
+                [tn(columns(normed_in, k), outgate_low), tn(columns(resid_low, k), gated)], axis=1
+            ).astype(bf16)
+            for k in range(ny)
+        ]
+        go_rows_grad = sum_y(go_grads[:1] + [after(g, entering) for g in go_grads[1:]])
+        feed_far = swap(feed_part(after(hidden_far, mixed_grad)), "c")
+        feed_rows = add_low(feed_part(after(hidden_near, mixed_grad)), feed_far)
+        feed = scatter_second(*scatter_first(feed_rows, micro, quarter), quarter)
+        qkv_low, logit_grad = call_backward(
+            qkv, decays, logits, mixed_grad, enter, leave, is_open, micro
+        )
+        logit_low = logit_grad.astype(bf16)
+        qkv_grads = [tn(columns(normed_in, k), qkv_low).astype(bf16) for k in range(ny)]
+        rank_part = nt(logit_low, decay_w).astype(bf16)
+        rank_pad = jnp.pad(rank_part, ((0, 0), (0, 128 - rank)))
+        qkv_later = after(qkv_low, *qkv_grads)
+        in_part = [
+            (nt(qkv_later, wq) + nt(outgate_low, wg[:, :wide])).astype(bf16)
+            for wq, wg in zip(qkv_parts, go_parts)
+        ]
+        in_part = jnp.concatenate(in_part + [rank_pad], axis=1).reshape(micro, slots, depth + 128)
+        return resid_grad, grad_norm_mid, grad_gain, go_rows_grad, qkv_grads, in_part, logit_low, feed
+
+    resid_grad, grad_norm_mid, grad_gain, go_rows_grad, qkv_grads, in_part, logit_low, feed = as_one(
+        runs, blocks_back
+    )
     go_grad = reduce_z(go_rows_grad)
-    qkv_low, logit_grad = call_backward(
-        qkv, decays, logits, mixed_grad, enter, leave, is_open, micro, go_rows_grad, feed
-    )
-    logit_low = logit_grad.astype(bf16)
-
-    qkv_grads = [tn(columns(normed_in, k), qkv_low).astype(bf16) for k in range(ny)]
-    qkv_rows_grad = sum_y(qkv_grads)
-    qkv_grad = reduce_z(qkv_rows_grad).astype(f32)
-
-    rank_part = nt(logit_low, decay_w).astype(bf16)
-    rank_pad = jnp.pad(rank_part, ((0, 0), (0, 128 - rank)))
-    qkv_later = after(qkv_low, *qkv_grads)
-    in_part = [
-        (nt(qkv_later, wq) + nt(outgate_low, wg[:, :wide])).astype(bf16)
-        for wq, wg in zip(qkv_parts, go_parts)
-    ]
-    in_sum = jnp.concatenate(in_part + [rank_pad], axis=1)
-    in_sum = scatter_head(in_sum.reshape(micro, slots, depth + 128)).reshape(-1, depth + 128)
-    rank_low = in_sum[:, depth : depth + rank].astype(bf16)
-    in_grad = in_sum[:, :depth] + nn(rank_low, rank_t)
-    r_own = inv_rms(inputs_own)
-    input_own = resid_grad + norm_back(inputs_own, r_own, gain_in, in_grad)
-    grad_norm_in = jnp.sum(in_grad * inputs_own * r_own, axis=0)
-    normed_own = own_quarter(normed_in.reshape(micro, slots, depth)).reshape(-1, depth)
-    grad_rank_t = tn(rank_low, normed_own)
-    grad_rows = jnp.concatenate([grad_norm_in[None], grad_norm_mid[None], grad_rank_t])
-    input_own = to_absolute(input_own.astype(bf16))
-    input_grad = gather_head(input_own.reshape(micro, quarter, depth)).astype(f32)
-
-    block_own = (to_absolute(residual) + feed).astype(bf16).reshape(micro, quarter, depth)
-    block_out = gather_head(block_own)
-
-    grad_decay = tn(low_rank, logit_low)
-    grad_bias = jnp.sum(logit_low.astype(f32), axis=0)
+
+    def input_back():
+        in_sum = scatter_head(in_part).reshape(-1, depth + 128)
+        rank_low = in_sum[:, depth : depth + rank].astype(bf16)
+        in_grad = in_sum[:, :depth] + nn(rank_low, rank_t)
+        r_own = inv_rms(inputs_own)
+        input_own = resid_grad + norm_back(inputs_own, r_own, gain_in, in_grad)
+        grad_norm_in = jnp.sum(in_grad * inputs_own * r_own, axis=0)
+        normed_own = own_quarter(normed_in.reshape(micro, slots, depth)).reshape(-1, depth)
+        grad_rank_t = tn(rank_low, normed_own)
+        grad_rows = jnp.concatenate([grad_norm_in[None], grad_norm_mid[None], grad_rank_t])
+        input_own = to_absolute(input_own.astype(bf16))
+        input_low = gather_head(input_own.reshape(micro, quarter, depth))
+        return sum_y(qkv_grads), grad_rows, input_low
+
+    qkv_rows_grad, grad_rows, input_low = input_back()
+    qkv_rows_grad = after(qkv_rows_grad, ff_grad)
+    qkv_grad = reduce_z(qkv_rows_grad)
+
     by_ctx = lambda v: v.reshape(nctx, -1)
     across = lambda v, n: v.reshape(v.shape[0], nctx, n).transpose(1, 0, 2).reshape(nctx, -1)
-    summed = jnp.concatenate(
-        [vector_by_ctx(grad_rows).reshape(nctx, -1), by_ctx(grad_gain)], axis=1
-    )
-    headed = jnp.concatenate([across(grad_decay, dl), by_ctx(grad_bias)], axis=1)
-    n_summed, n_headed = summed.shape[1], headed.shape[1]
-    pad_s, pad_h = -n_summed % 1024, -n_headed % 1024
-    tail = jnp.concatenate(
-        [jnp.pad(summed, ((0, 0), (0, pad_s))), jnp.pad(headed, ((0, 0), (0, pad_h)))], axis=1
-    ).reshape(nctx, -1, 128)
-    tail = jnp.sum(lax.all_to_all(tail, ctx, 0, 0), axis=0)
-    cut = (n_summed + pad_s) // 128
-    summed, headed = tail[:cut], tail[cut:].reshape(-1)
-    summed = summed + swap(summed, "c")
-    summed = (summed + swap(summed, "x")).reshape(-1)
-    g_norm_in = summed[:rl]
-    g_norm_mid = summed[rl : 2 * rl]
-    g_rank = summed[2 * rl : (2 + rank) * rl].reshape(rank, rl).T
-    g_gain = summed[(2 + rank) * rl : n_summed]
-    g_decay = headed[: rank * dl].reshape(1, rank, dl)
-    g_bias = headed[rank * dl : n_headed].reshape(1, dl)
-
-    ff_grad = after(ff_grad, qkv_rows_grad)
-    ff_grad = ff_grad.reshape(ny, rl, 3 * fl)
-    pieces = jnp.zeros((ny, rl, 3 * fl), bf16)
-    pieces = lax.dynamic_update_slice_in_dim(
-        pieces, lax.dynamic_index_in_dim(ff_grad, y, 0), y, 0
-    )
-    for k in range(1, ny):
-        sent = lax.dynamic_index_in_dim(ff_grad, lax.rem(y + k, ny), 0)
-        got = lax.ppermute(sent, "y", [(i, (i + k) % ny) for i in range(ny)])
-        pieces = lax.dynamic_update_slice_in_dim(pieces, got, lax.rem(y - k + ny, ny), 0)
-
-    g_gate, g_up, g_down = call_join(pieces)
+
+    def finish():
+        ff_rows = after(ff_grad, qkv_rows_grad).reshape(ny, rl, 3 * fl)
+        pieces = jnp.zeros((ny, rl, 3 * fl), bf16)
+        pieces = lax.dynamic_update_slice_in_dim(
+            pieces, lax.dynamic_index_in_dim(ff_rows, y, 0), y, 0
+        )
+        for k in range(1, ny):
+            sent = lax.dynamic_index_in_dim(ff_rows, lax.rem(y + k, ny), 0)
+            got = lax.ppermute(sent, "y", [(i, (i + k) % ny) for i in range(ny)])
+            pieces = lax.dynamic_update_slice_in_dim(pieces, got, lax.rem(y - k + ny, ny), 0)
+        block_own = to_absolute((residual + to_relative(feed.reshape(-1, depth))).astype(bf16))
+        block_out = gather_head(block_own.reshape(micro, quarter, depth))
+        grad_decay = tn(low_rank, logit_low)
+        grad_bias = jnp.sum(logit_low.astype(f32), axis=0)
+        summed = jnp.concatenate(
+            [vector_by_ctx(grad_rows).reshape(nctx, -1), by_ctx(grad_gain)], axis=1
+        )
+        headed = jnp.concatenate([across(grad_decay, dl), by_ctx(grad_bias)], axis=1)
+        n_summed, n_headed = summed.shape[1], headed.shape[1]
+        pad_s, pad_h = -n_summed % 1024, -n_headed % 1024
+        tail = jnp.concatenate(
+            [jnp.pad(summed, ((0, 0), (0, pad_s))), jnp.pad(headed, ((0, 0), (0, pad_h)))], axis=1
+        ).reshape(nctx, -1, 128)
+        tail = jnp.sum(lax.all_to_all(tail, ctx, 0, 0), axis=0)
+        cut = (n_summed + pad_s) // 128
+        summed, headed = tail[:cut], tail[cut:].reshape(-1)
+        summed = summed + swap(summed, "c")
+        summed = (summed + swap(summed, "x")).reshape(-1)
+        return (
+            block_out,
+            input_low.astype(f32),
+            *call_join(pieces),
+            summed[: 2 * rl],
+            summed[2 * rl : (2 + rank) * rl].reshape(rank, rl).T,
+            summed[(2 + rank) * rl : n_summed],
+            headed[: rank * dl].reshape(1, rank, dl),
+            headed[rank * dl : n_headed].reshape(1, dl),
+        )
+
+    block_out, input_grad, g_gate, g_up, g_down, g_norms, g_rank, g_gain, g_decay, g_bias = finish()
+    g_norm_in, g_norm_mid = g_norms[:rl], g_norms[rl:]
+    qkv_grad = qkv_grad.astype(f32)
     return (
         block_out,
         input_grad,

time: 659 us -> 649 us (0.985)
  blocking collectives: 34.9 us -> 72 us
  waiting for transfers between devices: 266 us -> 248 us
  local copies, waits for them, and re-layouts: 77.4 us -> 61.4 us
  other arithmetic: 81.5 us -> 71.4 us
    all_to_all x1 -> x2, blocking collectives: 34.9 us -> 72 us  [the longest x1 40.7 us: spread_states(): got = lax.all_to_all(sent, ctx, 0, 0)]
    all_to_all x4 -> x3, waiting for transfers between devices: 76.7 us -> 40.7 us  [the longest x1 23.4 us: spread_states(): got = lax.all_to_all(sent, ctx, 0, 0)]
    ppermute x3, waiting for transfers between devices: 40.8 us -> 5.17 us  [others_y(): lax.ppermute(piece, 'y', [((i + k) % count, i) for i in range(count)])]
    unnamed x328 -> x128, local copies, waits for them, and re-layouts: 24.5 us -> 9.65 us
    ppermute x29, waiting for transfers between devices: 88.6 us -> 103 us  [swap(): return lax.ppermute(x, axis, [(0, 1), (1, 0)])]
    ppermute x1, waiting for transfers between devices: 0.01 us -> 13.7 us  [finish(): got = lax.ppermute(sent, 'y', [(i, (i + k) % ny) for i in range(ny)])]
    all_gather x1, waiting for transfers between devices: 19.5 us -> 32.7 us  [per_device(): ff_full = lax.all_gather(ff_unit, 'z', axis=0, tiled=True)]
    reduce_scatter x3, waiting for transfers between devices: 12.8 us -> 0.01 us  [reduce_z(): return lax.psum_scatter(part, 'z', scatter_dimension=0, tiled=True)]
  transfers between devices with their start and end apart: 46 -> 45, of which waited for: 26 -> 27; matrix products, arithmetic and copies ran while one was open for 30% -> 27% of each run, Pallas kernels for 5% -> 7%
where the time goes in v3:
time: 649 us; the launch traced here: 638 us
  waiting for transfers between devices  248 us (38%)
  blocking collectives  72 us (11%)
  other arithmetic  71.4 us (11%)
  local copies, waits for them, and re-layouts  61.4 us (9%)
  Pallas kernels  60.8 us (9%)
  matrix products  56.5 us (9%)
  starting transfers between devices  50.3 us (8%)
  between operations  16.6 us (3%)
    ppermute x29, waiting for transfers between devices, swap(): return lax.ppermute(x, axis, [(0, 1), (1, 0)])  103 us
    dot_general x30, matrix products, dot(): return lax.dot_general(a, b, (dims, ((), ())), preferred_element_type=f32)  56.5 us
    all_to_all x1, blocking collectives, spread_states(): got = lax.all_to_all(sent, ctx, 0, 0)  40.7 us
    all_gather x1, waiting for transfers between devices, per_device(): ff_full = lax.all_gather(ff_unit, 'z', axis=0, tiled=True)  32.7 us
    all_to_all x1, blocking collectives, collect_states(): back = lax.all_to_all(entering, ('z', 'y'), 0, 0)  31.3 us
    pallas_call x2, Pallas kernels, call_feed(): pl.pallas_call(functools.partial(feed_kernel, units=units), grid=(rows //...  28.6 us
    all_gather x1, waiting for transfers between devices, per_device(): go_rows = lax.all_gather(w_go, 'z', axis=0, tiled=True)  27.5 us
    all_to_all x1, waiting for transfers between devices, spread_states(): got = lax.all_to_all(sent, ctx, 0, 0)  23.4 us
  transfers between devices with their start and end apart: 45, of which 27 were waited for; matrix products, arithmetic and copies ran while one was open for 27% of the time, Pallas kernels for 7%

profile of v3, /device:TPU:0, one launch (start us, length us, event | category | flops | bytes accessed | tf_op | source)
XLA Modules:
  0.0 638.0 jit_solution(11121212748322312543)
XLA Ops:
  7.3 2.0 pad_maximum_fusion.24
  10.8 2.8 concatenate.225
  14.2 7.3 %all-to-all-start.4 = ((bf16[8,48,128]{2,1,0:T(8,128)(2,1)}), bf16[8,48,128]{2,1,0:T(8,128)(2,1)}, u32[]{:S(2)}, u32[]{:S(2)}) async-start(bf16[8,48,128]{2,1,0:T(8,128)(2,1)} %broadcast_in_dim.11), calls=%async_computation.4 | async-start | bytes 196608 | tf_op jit(solution)/shard_map/all_to_all | solution.py:669
  21.5 2.3 fusion.123
  27.9 2.5 copy.275
  48.4 12.5 %all-gather.4.cloned.1.call-done = bf16[1024,1024]{1,0:T(8,128)(2,1)} async-done(((bf16[256,1024]{1,0:T(8,128)(2,1)}), bf16[1024,1024]{1,0:T(8,128)(2,1)}) %all-gather.4.cloned.1.call-update) | async-done | bytes 2097168 | tf_op jit(solution)/shard_map/all_gather | solution.py:658
  66.3 7.4 %collective-permute-done.21 = bf16[256,2112]{0,1:T(8,128)(2,1)} collective-permute-done((bf16[256,2112]{0,1:T(8,128)(2,1)}, bf16[256,2112]{0,1:T(8,128)(2,1)}, u32[]{:S(2)}, u32[]{:S(2)}) %collective-permute-start.21) | collective-permute-done | bytes 1081376 | tf_op jit(solution)/shard_map/ppermute | solution.py:38
  73.7 2.3 copy.276
  76.1 4.1 maximum_select_fusion.2
  80.3 27.5 %all-gather.6.cloned.1.call-done = bf16[1024,1024]{1,0:T(8,128)(2,1)} async-done(((bf16[256,1024]{1,0:T(8,128)(2,1)}), bf16[1024,1024]{1,0:T(8,128)(2,1)}) %all-gather.6.cloned.1.call-update) | async-done | bytes 2097168 | tf_op jit(solution)/shard_map/all_gather | solution.py:660
  109.2 2.9 fusion.50
  113.5 5.2 collective-permute-done.12
  118.7 3.9 add_convert_fusion.10
  122.6 77.9 %conditional.3 = (f32[512,512]{1,0:T(8,128)S(1)}, bf16[512,256]{1,0:T(8,128)(2,1)S(1)}, bf16[2,512,256]{2,1,0:T(8,128)(2,1)S(1)}, f32[2,256]{1,0:T(2,128)S(1)}) conditional(s32[]{:T(128)} %bitcast.37, () %tuple.40, (bf16[512,1024]{1,0:T(8,128)(2,1)}, f32[512,256]{1,0:T(8,128)S(1)}, bf16[256,256]{1,0:T(8,128)(2,1)S(1)}, s32[256,256]{1,0:T(8,128)S(1)}, ...), branch_computations={%region_1.2_spmd, %region_2.3_spmd} | conditional | flops 2003206272 | bytes 14699380 | solution.py:56
  122.7 5.1 scan_forward.1
  128.0 40.7 %all_to_all.26.got_ref = bf16[8,144,256]{2,1,0:T(8,128)(2,1)S(1)} all-to-all(bf16[8,144,256]{2,1,0:T(8,128)(2,1)S(1)} %pad_maximum_fusion), channel_id=1, replica_groups=mesh['z'=4,'y'=2,'x'=2,'c'=2] {'z','y'}, dimensions={0} | all-to-all | bytes 1179648 | tf_op jit(solution)/shard_map/cond/branch_1_fun/all_to_all | solution.py:355
  168.8 31.3 %all_to_all.27 = bf16[8,128,256]{2,1,0:T(8,128)(2,1)S(1)} all-to-all(bf16[8,128,256]{2,1,0:T(8,128)(2,1)S(1)} %scan_states.2), channel_id=1, replica_groups=mesh['z'=4,'y'=2,'x'=2,'c'=2] {'z','y'}, dimensions={0} | all-to-all | bytes 1048576 | tf_op jit(solution)/shard_map/cond/branch_1_fun/all_to_all | solution.py:368
  203.0 3.5 multiply_convert_fusion.3
  206.5 2.2 convolution_convert_fusion.9
  216.0 10.8 %collective-permute-done.15 = bf16[2,64,2048]{2,1,0:T(8,128)(2,1)S(1)} collective-permute-done((bf16[2,64,2048]{2,1,0:T(8,128)(2,1)S(1)}, bf16[2,64,2048]{2,1,0:T(8,128)(2,1)S(1)}, u32[]{:S(2)}, u32[]{:S(2)}) %collective-permute-start.15) | collective-permute-done | bytes 524320 | tf_op jit(solution)/shard_map/ppermute | solution.py:38
  228.1 2.1 multiply_convert_fusion.2
  233.6 6.0 collective-permute-done.16
  241.7 10.1 %collective-permute-done.17 = bf16[2,64,2048]{2,1,0:T(8,128)(2,1)S(1)} collective-permute-done((bf16[2,64,2048]{2,1,0:T(8,128)(2,1)S(1)}, bf16[2,64,2048]{2,1,0:T(8,128)(2,1)S(1)}, u32[]{:S(2)}, u32[]{:S(2)}) %collective-permute-start.17) | collective-permute-done | bytes 524320 | tf_op jit(solution)/shard_map/ppermute | solution.py:38
  253.5 4.3 collective-permute-done.22.mid_ref
  257.8 32.7 %all-gather.8.cloned.1.call-done.weight_ref = bf16[2048,2112]{1,0:T(8,128)(2,1)} async-done(((bf16[512,2112]{1,0:T(8,128)(2,1)}), bf16[2048,2112]{1,0:T(8,128)(2,1)}) %all-gather.8.cloned.1.call-update) | async-done | bytes 8650768 | tf_op jit(solution)/shard_map/all_gather | solution.py:716
  290.6 14.4 %feed_forward.2 = (bf16[512,1408]{1,0:T(8,128)(2,1)S(1)}, bf16[512,704]{1,0:T(8,128)(2,1)S(1)}, bf16[512,2048]{1,0:T(8,128)(2,1)S(1)}) custom-call(bf16[512,2048]{1,0:T(8,128)(2,1)} %collective-permute-done.22.mid_ref, bf16[512,2048]{1,0:T(8,128)(2,1)} %collective-permute-done.23.low_ref, bf16[2048,2112]{1,0:T(8,128)(2,1)} %all-gather.8.cloned.1.call-done.weight_ref), custom_call_target="tpu_custom_call" | custom-call | flops 7381975040 | bytes 28000000 | tf_op jit(solution)/shard_map/feed_forward/pallas_call | solution.py:388
  305.2 14.1 %feed_forward.3 = (bf16[512,1408]{1,0:T(8,128)(2,1)S(1)}, bf16[512,704]{1,0:T(8,128)(2,1)S(1)}, bf16[512,2048]{1,0:T(8,128)(2,1)S(1)}) custom-call(bf16[512,2048]{1,0:T(8,128)(2,1)S(1)} %bitcast.349, bf16[512,2048]{1,0:T(8,128)(2,1)} %bitcast.79.low_ref, bf16[2048,2112]{1,0:T(8,128)(2,1)} %all-gather.8.cloned.1.call-done.weight_ref, ...), custom_call_target="tpu_custom_call" | custom-call | flops 7381975040 | bytes 28000000 | tf_op jit(solution)/shard_map/feed_forward/pallas_call | solution.py:388
  320.5 18.5 %conditional.4 = (bf16[2048,2112]{1,0:T(8,128)(2,1)}, bf16[128,2048]{1,0:T(8,128)(2,1)}, bf16[128,2048]{1,0:T(8,128)(2,1)}) conditional(s32[]{:T(128)} %bitcast.37, () %tuple.43, (bf16[512,2048]{1,0:T(8,128)(2,1)S(1)}, bf16[512,2048]{1,0:T(8,128)(2,1)}, bf16[512,1408]{1,0:T(8,128)(2,1)S(1)}, bf16[512,704]{1,0:T(8,128)(2,1)S(1)}, ...), branch_computations={%region_5.6_spmd, %region_6.7_spmd} | conditional | flops 8860467200 | bytes 30437288 | solution.py:56
  323.6 13.9 %feed_grad.1 = bf16[2048,2112]{1,0:T(8,128)(2,1)} custom-call(bf16[512,2048]{1,0:T(8,128)(2,1)S(1)} %get-tuple-element.126.refs_0_, bf16[512,2048]{1,0:T(8,128)(2,1)} %get-tuple-element.127.refs_1_, bf16[512,1408]{1,0:T(8,128)(2,1)S(1)} %get-tuple-element.128.refs_2_, bf16[512,704]{1,0:T(8,128)(2,1)S(1)} %get-tuple-element.129.refs_3_, ...), custom_call_target="tpu_custom_call" | custom-call | flops 8858370048 | bytes 21000000 | tf_op jit(solution)/shard_map/cond/branch_1_fun/feed_grad/pallas_call | solution.py:480
  340.3 2.4 broadcast_select_fusion.2
  343.7 2.0 copy.289
  345.7 165.3 %conditional.5 = (f32[128,2048]{1,0:T(8,128)}, bf16[1024,1024]{1,0:T(8,128)(2,1)}, bf16[1024,1024]{1,0:T(8,128)(2,1)}, bf16[512,256]{1,0:T(8,128)(2,1)S(1)}, f32...) conditional(s32[]{:T(128)} %bitcast.37, () %tuple.42, ...), branch_computations={%region_7.8_spmd, %region_8.13_spmd} | conditional | flops 16747399168 | bytes 308618688 | solution.py:56
  352.4 3.1 collective-permute-done.2
  360.9 11.9 %collective-permute-done.4 = bf16[2,64,2048]{2,1,0:T(8,128)(2,1)S(1)} collective-permute-done((bf16[2,64,2048]{2,1,0:T(8,128)(2,1)S(1)}, bf16[2,64,2048]{2,1,0:T(8,128)(2,1)S(1)}, u32[]{:S(2)}, u32[]{:S(2)}) %collective-permute-start.4) | collective-permute-done | bytes 524320 | tf_op jit(solution)/shard_map/cond/branch_1_fun/ppermute | solution.py:38
  374.5 2.3 collective-permute-done.5
  377.2 2.9 fusion.10
  383.7 3.5 all-to-all-start.2
  389.1 5.2 convolution_convert_fusion
  396.2 23.4 %all-to-all-done.2.got_ref = bf16[8,144,256]{2,1,0:T(8,128)(2,1)S(1)} async-done(((bf16[8,144,256]{2,1,0:T(8,128)(2,1)}), bf16[8,144,256]{2,1,0:T(8,128)(2,1)S(1)}, u32[]{:S(2)}, u32[]{:S(2)}) %all-to-all-start.2) | async-done | bytes 589856 | tf_op jit(solution)/shard_map/cond/branch_1_fun/all_to_all | solution.py:355
  420.4 4.9 all-to-all-start.3
  425.3 2.2 fusion.7
  433.6 2.0 collective-permute-start.6
  435.6 17.3 %all-to-all-done.3 = bf16[8,128,256]{2,1,0:T(8,128)(2,1)S(1)} async-done(((bf16[8,128,256]{2,1,0:T(8,128)(2,1)}), bf16[8,128,256]{2,1,0:T(8,128)(2,1)S(1)}, u32[]{:S(2)}, u32[]{:S(2)}) %all-to-all-start.3) | async-done | bytes 524320 | tf_op jit(solution)/shard_map/cond/branch_1_fun/all_to_all | solution.py:368
  453.0 9.2 %scan_backward.1 = (bf16[512,1024]{1,0:T(8,128)(2,1)S(1)}, f32[512,256]{1,0:T(8,128)S(1)}) custom-call(bf16[512,1024]{1,0:T(8,128)(2,1)} %get-tuple-element.152.qkv_ref, f32[512,256]{1,0:T(8,128)} %get-tuple-element.153.decay_ref, f32[512,256]{1,0:T(8,128)} %get-tuple-element.154.logit_ref, bf16[512,512]{1,0:T(8,128)(2,1)S(1)} %copy-done.3, ...), custom_call_target="tpu_custom_call" | custom-call | flops 5000000000 | bytes 12000000 | tf_op jit(solution)/shard_map/cond/branch_1_fun/scan_backward/pallas_call | solution.py:294
  462.5 4.1 convert_bitcast_fusion.1.refs_2_
  466.6 4.0 fusion.85
  470.6 3.3 fusion.93
  475.3 4.4 add_convert_fusion.2
  485.7 8.2 %collective-permute-done.8 = bf16[128,2048]{1,0:T(8,128)(2,1)S(1)} collective-permute-done((bf16[128,2048]{1,0:T(8,128)(2,1)S(1)}, bf16[128,2048]{1,0:T(8,128)(2,1)S(1)}, u32[]{:S(2)}, u32[]{:S(2)}) %collective-permute-start.8) | collective-permute-done | bytes 524320 | tf_op jit(solution)/shard_map/cond/branch_1_fun/ppermute | solution.py:38
  499.2 3.6 collective-permute-done.11
  502.8 3.0 collective-permute-done.9
  507.0 3.7 add_convert_fusion.3
  515.3 4.0 copy.295
  520.7 8.1 %collective-permute-done.25 = bf16[2,64,2048]{2,1,0:T(8,128)(2,1)S(1)} collective-permute-done((bf16[2,64,2048]{2,1,0:T(8,128)(2,1)S(1)}, bf16[2,64,2048]{2,1,0:T(8,128)(2,1)S(1)}, u32[]{:S(2)}, u32[]{:S(2)}) %collective-permute-start.25) | collective-permute-done | bytes 524320 | tf_op jit(solution)/shard_map/ppermute | solution.py:38
  532.5 14.4 %collective-permute-done.28 = bf16[2,64,2176]{2,1,0:T(8,128)(2,1)S(1)} collective-permute-done((bf16[2,64,2176]{2,1,0:T(8,128)(2,1)S(1)}, bf16[2,64,2176]{2,1,0:T(8,128)(2,1)S(1)}, u32[]{:S(2)}, u32[]{:S(2)}) %collective-permute-start.28) | collective-permute-done | bytes 557088 | tf_op jit(solution)/shard_map/ppermute | solution.py:38
  550.1 5.1 all-to-all-start.5
  557.1 12.2 %collective-permute-done.33 = bf16[1024,1024]{1,0:T(8,128)(2,1)} collective-permute-done((bf16[1024,1024]{1,0:T(8,128)(2,1)}, bf16[1024,1024]{1,0:T(8,128)(2,1)}, u32[]{:S(2)}, u32[]{:S(2)}) %collective-permute-start.33) | collective-permute-done | bytes 2097184 | tf_op jit(solution)/shard_map/ppermute | solution.py:629
  569.3 5.0 add_convert_fusion.8.refs_0_
  581.1 6.7 %collective-permute-done.29 = bf16[2,64,2048]{2,1,0:T(8,128)(2,1)S(1)} collective-permute-done((bf16[2,64,2048]{2,1,0:T(8,128)(2,1)S(1)}, bf16[2,64,2048]{2,1,0:T(8,128)(2,1)S(1)}, u32[]{:S(2)}, u32[]{:S(2)}) %collective-permute-start.29) | collective-permute-done | bytes 524320 | tf_op jit(solution)/shard_map/ppermute | solution.py:38
  591.9 2.3 copy.296
  601.9 2.3 copy.288
  607.1 13.7 %collective-permute-done.34 = bf16[1,256,2112]{1,2,0:T(8,128)(2,1)} collective-permute-done((bf16[1,256,2112]{1,2,0:T(8,128)(2,1)}, bf16[1,256,2112]{1,2,0:T(8,128)(2,1)}, u32[]{:S(2)}, u32[]{:S(2)}) %collective-permute-start.34) | collective-permute-done | bytes 1081376 | tf_op jit(solution)/shard_map/ppermute | solution.py:873
  620.8 2.3 copy.297
  624.5 2.5 join_units.1
  (486 shorter events, 141.0 us)
Async XLA Ops:
  7.2 18.6 %copy-start.6 = (bf16[1408,256]{1,0:T(8,128)(2,1)S(1)}, bf16[1408,256]{1,0:T(8,128)(2,1)}, u32[]{:S(2)}) copy-start(bf16[1408,256]{1,0:T(8,128)(2,1)} %down_ref.1) | copy-start | bytes 2162692
  7.2 18.6 %copy-start.5 = (bf16[256,1408]{1,0:T(8,128)(2,1)S(1)}, bf16[256,1408]{1,0:T(8,128)(2,1)}, u32[]{:S(2)}) copy-start(bf16[256,1408]{1,0:T(8,128)(2,1)} %up_ref.1) | copy-start | bytes 2162692
  7.2 18.6 %copy-start.4 = (bf16[256,1408]{1,0:T(8,128)(2,1)S(1)}, bf16[256,1408]{1,0:T(8,128)(2,1)}, u32[]{:S(2)}) copy-start(bf16[256,1408]{1,0:T(8,128)(2,1)} %gate_ref.1) | copy-start | bytes 2162692
  7.2 53.7 %all-gather.4.cloned.1.call-start = ((), (), s32[]{:S(2)}) async-start(), calls=%async_computation.9 | async-start | bytes 2621440 | tf_op jit(solution)/shard_map/all_gather | solution.py:658
  14.2 31.4 %all-to-all-start.4 = ((bf16[8,48,128]{2,1,0:T(8,128)(2,1)}), bf16[8,48,128]{2,1,0:T(8,128)(2,1)}, u32[]{:S(2)}, u32[]{:S(2)}) async-start(bf16[8,48,128]{2,1,0:T(8,128)(2,1)} %broadcast_in_dim.11), calls=%async_computation.4 | async-start | bytes 196608 | tf_op jit(solution)/shard_map/all_to_all | solution.py:669
  21.5 86.3 %all-gather.6.cloned.1.call-start = ((), (), s32[]{:S(2)}) async-start(), calls=%async_computation.10 | async-start | bytes 2621440 | tf_op jit(solution)/shard_map/all_gather | solution.py:660
  23.9 185.8 %collective-permute-start.20 = (bf16[2,128,2048]{2,1,0:T(8,128)(2,1)}, bf16[2,128,2048]{2,1,0:T(8,128)(2,1)}, u32[]{:S(2)}, u32[]{:S(2)}) collective-permute-start(bf16[2,128,2048]{2,1,0:T(8,128)(2,1)} %fusion.123), channel_id=1, source_target_pairs={{4,0},{0,4},{5,1},{1,5},{6,2},{2,6},{7,3},{3,7},{12,8},{8,12},{13,... | collective-permute-start | bytes 3145736 | tf_op jit(solution)/shard_map/ppermute | solution.py:572
  30.3 43.4 %collective-permute-start.21 = (bf16[256,2112]{0,1:T(8,128)(2,1)}, bf16[256,2112]{0,1:T(8,128)(2,1)}, u32[]{:S(2)}, u32[]{:S(2)}) collective-permute-start(bf16[256,2112]{0,1:T(8,128)(2,1)} %bitcast.315), channel_id=1, source_target_pairs={{0,4},{4,0},{1,5},{5,1},{2,6},{6,2},{3,7},{7,3},{8,12},{12,8},{9,1... | collective-permute-start | bytes 3244040 | tf_op jit(solution)/shard_map/ppermute | solution.py:38
  31.4 259.1 %all-gather.8.cloned.1.call-start = ((), (), s32[]{:S(2)}) async-start(), calls=%async_computation.11 | async-start | bytes 11141120 | tf_op jit(solution)/shard_map/all_gather | solution.py:716
  48.4 15.8 %copy-start.59 = (bf16[16,2048]{1,0:T(8,128)(2,1)}, bf16[16,2048]{1,0:T(8,128)(2,1)S(1)}, u32[]{:S(2)}) copy-start(bf16[16,2048]{1,0:T(8,128)(2,1)S(1)} %slice.491) | copy-start | bytes 196612
  60.9 57.7 %collective-permute-start.12 = (bf16[1024,1024]{1,0:T(8,128)(2,1)}, bf16[1024,1024]{1,0:T(8,128)(2,1)}, u32[]{:S(2)}, u32[]{:S(2)}) collective-permute-start(bf16[1024,1024]{1,0:T(8,128)(2,1)} %all-gather.4.cloned.1.call-done), channel_id=1, source_target_pairs={{4,0},{0,4},{5,1},{1,5},{6,2},{2,6},{7,3},{3,7},{12,8},{8,12},{13,... | collective-permute-start | bytes 6291464 | tf_op jit(solution)/shard_map/ppermute | solution.py:572
  64.8 15.4 %copy-start.63 = (bf16[512,16]{0,1:T(8,128)(2,1)}, bf16[512,16]{0,1:T(8,128)(2,1)S(1)}, u32[]{:S(2)}) copy-start(bf16[512,16]{0,1:T(8,128)(2,1)S(1)} %convolution_convert_fusion.11) | copy-start | bytes 49156
  80.2 494.0 %reduce-scatter.4.cloned.1.call-start = ((), (), s32[]{:S(2)}) async-start(), calls=%async_computation.12 | async-start | bytes 11141120 | tf_op jit(solution)/shard_map/reduce_scatter | solution.py:635
  107.8 95.2 %collective-permute-start.13 = (bf16[1024,1024]{1,0:T(8,128)(2,1)}, bf16[1024,1024]{1,0:T(8,128)(2,1)}, u32[]{:S(2)}, u32[]{:S(2)}) collective-permute-start(bf16[1024,1024]{1,0:T(8,128)(2,1)} %all-gather.6.cloned.1.call-done), channel_id=1, source_target_pairs={{4,0},{0,4},{5,1},{1,5},{6,2},{2,6},{7,3},{3,7},{12,8},{8,12},{13,... | collective-permute-start | bytes 6291464 | tf_op jit(solution)/shard_map/ppermute | solution.py:572
  209.6 2.7 collective-permute-start.14
  212.8 14.0 %collective-permute-start.15 = (bf16[2,64,2048]{2,1,0:T(8,128)(2,1)S(1)}, bf16[2,64,2048]{2,1,0:T(8,128)(2,1)S(1)}, u32[]{:S(2)}, u32[]{:S(2)}) collective-permute-start(bf16[2,64,2048]{2,1,0:T(8,128)(2,1)S(1)} %dynamic-slice_bitcast_fusion.2), channel_id=1, source_target_pairs={{0,2},{2,0},{1,3},{3,1},{4,6},{6,4},{5,7},{7,5},{8,10},{10,8},{9,1... | collective-permute-start | bytes 1572872 | tf_op jit(solution)/shard_map/ppermute | solution.py:38
  214.5 12.3 %copy-start.44 = (bf16[2,64,1024]{2,1,0:T(8,128)(2,1)S(1)}, bf16[2,64,1024]{2,1,0:T(8,128)(2,1)}, u32[]{:S(2)}) copy-start(bf16[2,64,1024]{2,1,0:T(8,128)(2,1)} %get-tuple-element.625) | copy-start | bytes 786436
  216.0 37.5 %collective-permute-start.23 = (bf16[512,2048]{1,0:T(8,128)(2,1)}, bf16[512,2048]{1,0:T(8,128)(2,1)}, u32[]{:S(2)}, u32[]{:S(2)}) collective-permute-start(bf16[512,2048]{1,0:T(8,128)(2,1)} %bitcast.79.low_ref), channel_id=1, source_target_pairs={{0,1},{1,0},{2,3},{3,2},{4,5},{5,4},{6,7},{7,6},{8,9},{9,8},{10,11... | collective-permute-start | bytes 6291464 | tf_op jit(solution)/shard_map/ppermute | solution.py:38
  230.6 9.6 %collective-permute-start.18 = (bf16[64,2048]{1,0:T(8,128)(2,1)S(1)}, bf16[64,2048]{1,0:T(8,128)(2,1)S(1)}, u32[]{:S(2)}, u32[]{:S(2)}) collective-permute-start(bf16[64,2048]{1,0:T(8,128)(2,1)S(1)} %get-tuple-element.621), channel_id=1, source_target_pairs={{0,2},{2,0},{1,3},{3,1},{4,6},{6,4},{5,7},{7,5},{8,10},{10,8},{9,1... | collective-permute-start | bytes 786440 | tf_op jit(solution)/shard_map/ppermute | solution.py:38
  232.2 7.4 %collective-permute-start.16 = (bf16[64,2048]{1,0:T(8,128)(2,1)S(1)}, bf16[64,2048]{1,0:T(8,128)(2,1)S(1)}, u32[]{:S(2)}, u32[]{:S(2)}) collective-permute-start(bf16[64,2048]{1,0:T(8,128)(2,1)S(1)} %get-tuple-element.622), channel_id=1, source_target_pairs={{0,4},{4,0},{1,5},{5,1},{2,6},{6,2},{3,7},{7,3},{8,12},{12,8},{9,1... | collective-permute-start | bytes 786440 | tf_op jit(solution)/shard_map/ppermute | solution.py:38
  239.6 12.2 %collective-permute-start.17 = (bf16[2,64,2048]{2,1,0:T(8,128)(2,1)S(1)}, bf16[2,64,2048]{2,1,0:T(8,128)(2,1)S(1)}, u32[]{:S(2)}, u32[]{:S(2)}) collective-permute-start(bf16[2,64,2048]{2,1,0:T(8,128)(2,1)S(1)} %pad_maximum_fusion.26), channel_id=1, source_target_pairs={{0,2},{2,0},{1,3},{3,1},{4,6},{6,4},{5,7},{7,5},{8,10},{10,8},{9,1... | collective-permute-start | bytes 1572872 | tf_op jit(solution)/shard_map/ppermute | solution.py:38
  240.2 12.0 %collective-permute-start.19 = (bf16[2,64,2048]{2,1,0:T(8,128)(2,1)S(1)}, bf16[2,64,2048]{2,1,0:T(8,128)(2,1)S(1)}, u32[]{:S(2)}, u32[]{:S(2)}) collective-permute-start(bf16[2,64,2048]{2,1,0:T(8,128)(2,1)S(1)} %pad_maximum_fusion.27), channel_id=1, source_target_pairs={{0,4},{4,0},{1,5},{5,1},{2,6},{6,2},{3,7},{7,3},{8,12},{12,8},{9,1... | collective-permute-start | bytes 1572872 | tf_op jit(solution)/shard_map/ppermute | solution.py:38
  253.5 4.3 collective-permute-start.22
  290.6 14.6 %copy-start.66 = (bf16[8,64,2048]{2,1,0:T(8,128)(2,1)S(1)}, bf16[8,64,2048]{2,1,0:T(8,128)(2,1)}, u32[]{:S(2)}) copy-start(bf16[8,64,2048]{2,1,0:T(8,128)(2,1)} %copy-done.65) | copy-start | bytes 6291460
  305.0 15.2 %copy-start.46 = (bf16[512,704]{1,0:T(8,128)(2,1)}, bf16[512,704]{1,0:T(8,128)(2,1)S(1)}, u32[]{:S(2)}) copy-start(bf16[512,704]{1,0:T(8,128)(2,1)S(1)} %get-tuple-element.216) | copy-start | bytes 2162692
  305.0 14.3 %collective-permute-start.24 = (bf16[512,2048]{1,0:T(8,128)(2,1)S(1)}, bf16[512,2048]{1,0:T(8,128)(2,1)S(1)}, u32[]{:S(2)}, u32[]{:S(2)}) collective-permute-start(bf16[512,2048]{1,0:T(8,128)(2,1)S(1)} %get-tuple-element.212.rest_0_), channel_id=1, source_target_pairs={{0,1},{1,0},{2,3},{3,2},{4,5},{5,4},{6,7},{7,6},{8,9},{9,8},{10,11... | collective-permute-start | bytes 6291464 | tf_op jit(solution)/shard_map/ppermute | solution.py:38
  320.6 17.0 %collective-permute-start.1 = (bf16[128,2048]{1,0:T(8,128)(2,1)S(1)}, bf16[128,2048]{1,0:T(8,128)(2,1)S(1)}, u32[]{:S(2)}, u32[]{:S(2)}) collective-permute-start(bf16[128,2048]{1,0:T(8,128)(2,1)S(1)} %get-tuple-element.543), channel_id=1, source_target_pairs={{0,4},{4,0},{1,5},{5,1},{2,6},{6,2},{3,7},{7,3},{8,12},{12,8},{9,1... | collective-permute-start | bytes 1572872 | tf_op jit(solution)/shard_map/cond/branch_1_fun/ppermute | solution.py:38
  322.1 15.4 %collective-permute-start = (bf16[128,2048]{1,0:T(8,128)(2,1)S(1)}, bf16[128,2048]{1,0:T(8,128)(2,1)S(1)}, u32[]{:S(2)}, u32[]{:S(2)}) collective-permute-start(bf16[128,2048]{1,0:T(8,128)(2,1)S(1)} %get-tuple-element.544), channel_id=1, source_target_pairs={{0,2},{2,0},{1,3},{3,1},{4,6},{6,4},{5,7},{7,5},{8,10},{10,8},{9,1... | collective-permute-start | bytes 1572872 | tf_op jit(solution)/shard_map/cond/branch_1_fun/ppermute | solution.py:38
  338.9 265.2 %reduce-scatter.8.cloned.1.call-start = ((), (), s32[]{:S(2)}) async-start(), calls=%async_computation.14 | async-start | bytes 2621440 | tf_op jit(solution)/shard_map/reduce_scatter | solution.py:635
  347.6 7.8 %collective-permute-start.2 = (bf16[64,2048]{1,0:T(8,128)(2,1)}, bf16[64,2048]{1,0:T(8,128)(2,1)}, u32[]{:S(2)}, u32[]{:S(2)}) collective-permute-start(bf16[64,2048]{1,0:T(8,128)(2,1)} %slice.343), channel_id=1, source_target_pairs={{0,4},{4,0},{1,5},{5,1},{2,6},{6,2},{3,7},{7,3},{8,12},{12,8},{9,1... | collective-permute-start | bytes 786440 | tf_op jit(solution)/shard_map/cond/branch_1_fun/ppermute | solution.py:38
  348.7 7.9 %collective-permute-start.3 = (bf16[64,2048]{1,0:T(8,128)(2,1)S(1)}, bf16[64,2048]{1,0:T(8,128)(2,1)}, u32[]{:S(2)}, u32[]{:S(2)}) collective-permute-start(bf16[64,2048]{1,0:T(8,128)(2,1)S(1)} %slice.345), channel_id=1, source_target_pairs={{0,2},{2,0},{1,3},{3,1},{4,6},{6,4},{5,7},{7,5},{8,10},{10,8},{9,1... | collective-permute-start | bytes 786440 | tf_op jit(solution)/shard_map/cond/branch_1_fun/ppermute | solution.py:38
  360.4 13.6 %copy-start.69 = (f32[2,256]{1,0:T(2,128)S(1)}, f32[2,256]{1,0:T(2,128)}, u32[]{:S(2)}) copy-start(f32[2,256]{1,0:T(2,128)} %copy-done.68) | copy-start | bytes 6148 | tf_op jit(solution)/shard_map/cond
  360.4 13.6 %copy-start.70 = (bf16[8,64]{1,0:T(8,128)(2,1)S(1)}, bf16[8,64]{1,0:T(8,128)(2,1)}, u32[]{:S(2)}) copy-start(bf16[8,64]{1,0:T(8,128)(2,1)} %get-tuple-element.146) | copy-start | bytes 3076 | tf_op jit(solution)/shard_map/cond
  360.4 12.4 %collective-permute-start.4 = (bf16[2,64,2048]{2,1,0:T(8,128)(2,1)S(1)}, bf16[2,64,2048]{2,1,0:T(8,128)(2,1)S(1)}, u32[]{:S(2)}, u32[]{:S(2)}) collective-permute-start(bf16[2,64,2048]{2,1,0:T(8,128)(2,1)S(1)} %bitcast.260), channel_id=1, source_target_pairs={{0,2},{2,0},{1,3},{3,1},{4,6},{6,4},{5,7},{7,5},{8,10},{10,8},{9,1... | collective-permute-start | bytes 1572872 | tf_op jit(solution)/shard_map/cond/branch_1_fun/ppermute | solution.py:38
  373.9 2.9 collective-permute-start.5
  383.7 35.8 %all-to-all-start.2 = ((bf16[8,144,256]{2,1,0:T(8,128)(2,1)}), bf16[8,144,256]{2,1,0:T(8,128)(2,1)S(1)}, u32[]{:S(2)}, u32[]{:S(2)}) async-start(bf16[8,144,256]{2,1,0:T(8,128)(2,1)} %pad_maximum_fusion.7), calls=%async_computation.2 | async-start | bytes 1179648 | tf_op jit(solution)/shard_map/cond/branch_1_fun/all_to_all | solution.py:355
  394.3 81.1 %collective-permute-start.7 = (bf16[512,2048]{1,0:T(8,128)(2,1)}, bf16[512,2048]{1,0:T(8,128)(2,1)}, u32[]{:S(2)}, u32[]{:S(2)}) collective-permute-start(bf16[512,2048]{1,0:T(8,128)(2,1)} %convolution_convert_fusion), channel_id=1, source_target_pairs={{0,1},{1,0},{2,3},{3,2},{4,5},{5,4},{6,7},{7,6},{8,9},{9,8},{10,11... | collective-permute-start | bytes 6291464 | tf_op jit(solution)/shard_map/cond/branch_1_fun/ppermute | solution.py:38
  420.4 32.5 %all-to-all-start.3 = ((bf16[8,128,256]{2,1,0:T(8,128)(2,1)}), bf16[8,128,256]{2,1,0:T(8,128)(2,1)S(1)}, u32[]{:S(2)}, u32[]{:S(2)}) async-start(bf16[8,128,256]{2,1,0:T(8,128)(2,1)} %scan_states.3.refs_1_), calls=%async_computation.3 | async-start | bytes 1048576 | tf_op jit(solution)/shard_map/cond/branch_1_fun/all_to_all | solution.py:368
  433.5 19.4 %copy-start.3 = (bf16[512,512]{1,0:T(8,128)(2,1)S(1)}, bf16[512,512]{1,0:T(8,128)(2,1)}, u32[]{:S(2)}) copy-start(bf16[512,512]{1,0:T(8,128)(2,1)} %copy-done.2) | copy-start | bytes 1572868 | tf_op jit(solution)/shard_map/cond
  433.5 19.4 %copy-start.7 = (bf16[256,256]{1,0:T(8,128)(2,1)S(1)}, bf16[256,256]{1,0:T(8,128)(2,1)}, u32[]{:S(2)}) copy-start(bf16[256,256]{1,0:T(8,128)(2,1)} %constant.184.clone.1.upper_ref) | copy-start | bytes 393220 | tf_op jit(solution)/shard_map/cond
  433.6 19.4 %copy-start.77 = (f32[2,4]{1,0:T(2,128)S(1)}, f32[2,4]{1,0:T(2,128)}, u32[]{:S(2)}) copy-start(f32[2,4]{1,0:T(2,128)} %copy-done.76) | copy-start | bytes 100 | tf_op jit(solution)/shard_map/cond
  433.6 19.4 %copy-start.85 = (bf16[256,256]{1,0:T(8,128)(2,1)S(1)}, bf16[256,256]{1,0:T(8,128)(2,1)}, u32[]{:S(2)}) copy-start(bf16[256,256]{1,0:T(8,128)(2,1)} %get-tuple-element.156.lower_ref) | copy-start | bytes 393220 | tf_op jit(solution)/shard_map/cond
  433.6 73.5 %collective-permute-start.6 = (bf16[1024,1024]{1,0:T(8,128)(2,1)}, bf16[1024,1024]{1,0:T(8,128)(2,1)}, u32[]{:S(2)}, u32[]{:S(2)}) collective-permute-start(bf16[1024,1024]{1,0:T(8,128)(2,1)} %after.6), channel_id=1, source_target_pairs={{0,4},{4,0},{1,5},{5,1},{2,6},{6,2},{3,7},{7,3},{8,12},{12,8},{9,1... | collective-permute-start | bytes 6291464 | tf_op jit(solution)/shard_map/cond/branch_1_fun/ppermute | solution.py:629
  479.8 14.0 %collective-permute-start.8 = (bf16[128,2048]{1,0:T(8,128)(2,1)S(1)}, bf16[128,2048]{1,0:T(8,128)(2,1)S(1)}, u32[]{:S(2)}, u32[]{:S(2)}) collective-permute-start(bf16[128,2048]{1,0:T(8,128)(2,1)S(1)} %get-tuple-element.549), channel_id=1, source_target_pairs={{0,2},{2,0},{1,3},{3,1},{4,6},{6,4},{5,7},{7,5},{8,10},{10,8},{9,1... | collective-permute-start | bytes 1572872 | tf_op jit(solution)/shard_map/cond/branch_1_fun/ppermute | solution.py:38
  481.4 13.7 %collective-permute-start.10 = (bf16[128,2048]{1,0:T(8,128)(2,1)S(1)}, bf16[128,2048]{1,0:T(8,128)(2,1)S(1)}, u32[]{:S(2)}, u32[]{:S(2)}) collective-permute-start(bf16[128,2048]{1,0:T(8,128)(2,1)S(1)} %get-tuple-element.550), channel_id=1, source_target_pairs={{0,4},{4,0},{1,5},{5,1},{2,6},{6,2},{3,7},{7,3},{8,12},{12,8},{9,1... | collective-permute-start | bytes 1572872 | tf_op jit(solution)/shard_map/cond/branch_1_fun/ppermute | solution.py:38
  495.4 7.3 %collective-permute-start.11 = (bf16[64,2048]{1,0:T(8,128)(2,1)S(1)}, bf16[64,2048]{1,0:T(8,128)(2,1)S(1)}, u32[]{:S(2)}, u32[]{:S(2)}) collective-permute-start(bf16[64,2048]{1,0:T(8,128)(2,1)S(1)} %slice.590), channel_id=1, source_target_pairs={{0,2},{2,0},{1,3},{3,1},{4,6},{6,4},{5,7},{7,5},{8,10},{10,8},{9,1... | collective-permute-start | bytes 786440 | tf_op jit(solution)/shard_map/cond/branch_1_fun/ppermute | solution.py:38
  498.2 7.6 %collective-permute-start.9 = (bf16[64,2048]{1,0:T(8,128)(2,1)S(1)}, bf16[64,2048]{1,0:T(8,128)(2,1)S(1)}, u32[]{:S(2)}, u32[]{:S(2)}) collective-permute-start(bf16[64,2048]{1,0:T(8,128)(2,1)S(1)} %slice.586), channel_id=1, source_target_pairs={{0,4},{4,0},{1,5},{5,1},{2,6},{6,2},{3,7},{7,3},{8,12},{12,8},{9,1... | collective-permute-start | bytes 786440 | tf_op jit(solution)/shard_map/cond/branch_1_fun/ppermute | solution.py:38
  512.4 17.5 %collective-permute-start.27 = (bf16[2,128,2176]{2,1,0:T(8,128)(2,1)S(1)}, bf16[2,128,2176]{2,1,0:T(8,128)(2,1)}, u32[]{:S(2)}, u32[]{:S(2)}) collective-permute-start(bf16[2,128,2176]{2,1,0:T(8,128)(2,1)S(1)} %dynamic-slice_bitcast_fusion), channel_id=1, source_target_pairs={{0,1},{1,0},{2,3},{3,2},{4,5},{5,4},{6,7},{7,6},{8,9},{9,8},{10,11... | collective-permute-start | bytes 3342344 | tf_op jit(solution)/shard_map/ppermute | solution.py:38
  514.4 14.4 %collective-permute-start.25 = (bf16[2,64,2048]{2,1,0:T(8,128)(2,1)S(1)}, bf16[2,64,2048]{2,1,0:T(8,128)(2,1)S(1)}, u32[]{:S(2)}, u32[]{:S(2)}) collective-permute-start(bf16[2,64,2048]{2,1,0:T(8,128)(2,1)S(1)} %bitcast.279), channel_id=1, source_target_pairs={{0,2},{2,0},{1,3},{3,1},{4,6},{6,4},{5,7},{7,5},{8,10},{10,8},{9,1... | collective-permute-start | bytes 1572872 | tf_op jit(solution)/shard_map/ppermute | solution.py:38
  519.2 50.1 %collective-permute-start.33 = (bf16[1024,1024]{1,0:T(8,128)(2,1)}, bf16[1024,1024]{1,0:T(8,128)(2,1)}, u32[]{:S(2)}, u32[]{:S(2)}) collective-permute-start(bf16[1024,1024]{1,0:T(8,128)(2,1)} %get-tuple-element.228), channel_id=1, source_target_pairs={{0,4},{4,0},{1,5},{5,1},{2,6},{6,2},{3,7},{7,3},{8,12},{12,8},{9,1... | collective-permute-start | bytes 6291464 | tf_op jit(solution)/shard_map/ppermute | solution.py:629
  529.9 46.1 %collective-permute-start.26 = (bf16[2,2,64,2048]{3,2,1,0:T(8,128)(2,1)}, bf16[2,2,64,2048]{3,2,1,0:T(8,128)(2,1)}, u32[]{:S(2)}, u32[]{:S(2)}) collective-permute-start(bf16[2,2,64,2048]{3,2,1,0:T(8,128)(2,1)} %maximum_select_fusion.5), channel_id=1, source_target_pairs={{0,1},{1,0},{2,3},{3,2},{4,5},{5,4},{6,7},{7,6},{8,9},{9,8},{10,11... | collective-permute-start | bytes 3145736 | tf_op jit(solution)/shard_map/ppermute | solution.py:38
  531.8 15.1 %collective-permute-start.28 = (bf16[2,64,2176]{2,1,0:T(8,128)(2,1)S(1)}, bf16[2,64,2176]{2,1,0:T(8,128)(2,1)S(1)}, u32[]{:S(2)}, u32[]{:S(2)}) collective-permute-start(bf16[2,64,2176]{2,1,0:T(8,128)(2,1)S(1)} %dynamic-slice_bitcast_fusion.1), channel_id=1, source_target_pairs={{0,2},{2,0},{1,3},{3,1},{4,6},{6,4},{5,7},{7,5},{8,10},{10,8},{9,1... | collective-permute-start | bytes 1671176 | tf_op jit(solution)/shard_map/ppermute | solution.py:38
  532.3 14.7 %copy-start.34 = (bf16[2048,128]{1,0:T(8,128)(2,1)S(1)}, bf16[2048,128]{1,0:T(8,128)(2,1)}, u32[]{:S(2)}) copy-start(bf16[2048,128]{1,0:T(8,128)(2,1)} %copy.289) | copy-start | bytes 1572868
  532.5 14.8 %copy-start.28 = (bf16[128,1024]{1,0:T(8,128)(2,1)S(1)}, bf16[128,1024]{1,0:T(8,128)(2,1)}, u32[]{:S(2)}) copy-start(bf16[128,1024]{1,0:T(8,128)(2,1)} %get-tuple-element.623) | copy-start | bytes 786436
  532.5 14.8 %copy-start.29 = (bf16[128,1024]{1,0:T(8,128)(2,1)S(1)}, bf16[128,1024]{1,0:T(8,128)(2,1)}, u32[]{:S(2)}) copy-start(bf16[128,1024]{1,0:T(8,128)(2,1)} %get-tuple-element.624) | copy-start | bytes 786436
  532.5 14.8 %copy-start.60 = (bf16[16,2048]{1,0:T(8,128)(2,1)S(1)}, bf16[16,2048]{1,0:T(8,128)(2,1)}, u32[]{:S(2)}) copy-start(bf16[16,2048]{1,0:T(8,128)(2,1)} %copy-done.59) | copy-start | bytes 196612
  550.1 29.3 %all-to-all-start.5 = ((f32[8,48,128]{2,1,0:T(8,128)}), f32[8,48,128]{2,1,0:T(8,128)S(1)}, u32[]{:S(2)}, u32[]{:S(2)}) async-start(f32[8,48,128]{2,1,0:T(8,128)} %copy.294), calls=%async_computation.5 | async-start | bytes 393216 | tf_op jit(solution)/shard_map/all_to_all | solution.py:888
  555.2 71.9 %reduce-scatter.6.cloned.1.call-start = ((), (), s32[]{:S(2)}) async-start(), calls=%async_computation.13 | async-start | bytes 2621440 | tf_op jit(solution)/shard_map/reduce_scatter | solution.py:635
  574.4 13.4 %copy-start.20 = (bf16[128,2048]{1,0:T(8,128)(2,1)}, bf16[128,2048]{1,0:T(8,128)(2,1)S(1)}, u32[]{:S(2)}) copy-start(bf16[128,2048]{1,0:T(8,128)(2,1)S(1)} %select_dynamic-update-slice_fusion) | copy-start | bytes 1572868
  574.4 13.4 %collective-permute-start.29 = (bf16[2,64,2048]{2,1,0:T(8,128)(2,1)S(1)}, bf16[2,64,2048]{2,1,0:T(8,128)(2,1)S(1)}, u32[]{:S(2)}, u32[]{:S(2)}) collective-permute-start(bf16[2,64,2048]{2,1,0:T(8,128)(2,1)S(1)} %bitcast.282), channel_id=1, source_target_pairs={{0,2},{2,0},{1,3},{3,1},{4,6},{6,4},{5,7},{7,5},{8,10},{10,8},{9,1... | collective-permute-start | bytes 1572872 | tf_op jit(solution)/shard_map/ppermute | solution.py:38
  579.4 1.3 collective-permute-start.31
  580.6 15.9 %collective-permute-start.32 = (f32[40,128]{1,0:T(8,128)S(1)}, f32[40,128]{1,0:T(8,128)S(1)}, u32[]{:S(2)}, u32[]{:S(2)}) collective-permute-start(f32[40,128]{1,0:T(8,128)S(1)} %slice_add_fusion.2), channel_id=1, source_target_pairs={{0,2},{2,0},{1,3},{3,1},{4,6},{6,4},{5,7},{7,5},{8,10},{10,8},{9,1... | collective-permute-start | bytes 61448 | tf_op jit(solution)/shard_map/ppermute | solution.py:38
  589.1 10.9 %collective-permute-start.30 = (bf16[2,2,64,2048]{3,2,1,0:T(8,128)(2,1)}, bf16[2,2,64,2048]{3,2,1,0:T(8,128)(2,1)}, u32[]{:S(2)}, u32[]{:S(2)}) collective-permute-start(bf16[2,2,64,2048]{3,2,1,0:T(8,128)(2,1)} %copy_select_fusion.1), channel_id=1, source_target_pairs={{0,1},{1,0},{2,3},{3,2},{4,5},{5,4},{6,7},{7,6},{8,9},{9,8},{10,11... | collective-permute-start | bytes 3145736 | tf_op jit(solution)/shard_map/ppermute | solution.py:38
  594.2 26.6 %collective-permute-start.34 = (bf16[1,256,2112]{1,2,0:T(8,128)(2,1)}, bf16[1,256,2112]{1,2,0:T(8,128)(2,1)}, u32[]{:S(2)}, u32[]{:S(2)}) collective-permute-start(bf16[1,256,2112]{1,2,0:T(8,128)(2,1)} %copy.296), channel_id=1, source_target_pairs={{0,4},{4,0},{1,5},{5,1},{2,6},{6,2},{3,7},{7,3},{8,12},{12,8},{9,1... | collective-permute-start | bytes 3244040 | tf_op jit(solution)/shard_map/ppermute | solution.py:873
  (72 other events, 244.3 us)
Sparse Core Ops, SparseCore 0:
  10.2 50.7 all-gather.3
  63.1 44.6 all-gather.5
  109.9 180.6 all-gather.7
  339.1 167.0 reduce-scatter.3
  520.8 47.7 reduce-scatter.7
  574.4 44.4 reduce-scatter.5

commit v4 on v3

--- a/solution.py
+++ b/solution.py
@@ -459,6 +459,101 @@
     )(pieces)
 
 
+def pick_rows(at_ref, in_ref, out_ref):
+    out_ref[...] = in_ref[0]
+
+
+def call_pick(pieces, at):
+    _, rows, width = pieces.shape
+    return pl.pallas_call(
+        pick_rows,
+        grid_spec=pltpu.PrefetchScalarGridSpec(
+            num_scalar_prefetch=1,
+            grid=(1,),
+            in_specs=[pl.BlockSpec((1, rows, width), lambda i, at: (at[0], 0, 0))],
+            out_specs=pl.BlockSpec((rows, width), lambda i, at: (0, 0)),
+        ),
+        out_shape=jax.ShapeDtypeStruct((rows, width), pieces.dtype),
+        compiler_params=pltpu.CompilerParams(vmem_limit_bytes=16 * 2**20),
+        cost_estimate=pl.CostEstimate(flops=0, bytes_accessed=4 * rows * width, transcendentals=0),
+        name="pick_rows",
+    )(at.reshape(1), pieces)
+
+
+def join_two(at_ref, own_ref, got_ref, gate_ref, up_ref, down_ref):
+    units = own_ref.shape[2] // 3
+    first = at_ref[0] == 0
+    for k in range(2):
+        mine = jnp.logical_xor(first, k == 1)
+        span = slice(k * units, (k + 1) * units)
+
+        @pl.when(mine)
+        def _():
+            value = own_ref[0].astype(f32)
+            gate_ref[:, span] = value[:, :units]
+            up_ref[:, span] = value[:, units : 2 * units]
+            down_ref[span, :] = value[:, 2 * units :].T
+
+        @pl.when(jnp.logical_not(mine))
+        def _():
+            value = got_ref[...].astype(f32)
+            gate_ref[:, span] = value[:, :units]
+            up_ref[:, span] = value[:, units : 2 * units]
+            down_ref[span, :] = value[:, 2 * units :].T
+
+
+def call_join_two(pieces, got, at):
+    _, rows, width = pieces.shape
+    ff = width // 3 * 2
+    return pl.pallas_call(
+        join_two,
+        grid_spec=pltpu.PrefetchScalarGridSpec(
+            num_scalar_prefetch=1,
+            grid=(1,),
+            in_specs=[
+                pl.BlockSpec((1, rows, width), lambda i, at: (at[0], 0, 0)),
+                pl.BlockSpec((rows, width), lambda i, at: (0, 0)),
+            ],
+            out_specs=[
+                pl.BlockSpec((rows, ff), lambda i, at: (0, 0)),
+                pl.BlockSpec((rows, ff), lambda i, at: (0, 0)),
+                pl.BlockSpec((ff, rows), lambda i, at: (0, 0)),
+            ],
+        ),
+        out_shape=[
+            jax.ShapeDtypeStruct((rows, ff), f32),
+            jax.ShapeDtypeStruct((rows, ff), f32),
+            jax.ShapeDtypeStruct((ff, rows), f32),
+        ],
+        compiler_params=pltpu.CompilerParams(vmem_limit_bytes=32 * 2**20),
+        cost_estimate=pl.CostEstimate(flops=0, bytes_accessed=18 * rows * ff, transcendentals=0),
+        name="join_two",
+    )(at.reshape(1), pieces, got)
+
+
+def widen_rows(in_ref, query_ref, key_ref, value_ref):
+    width = query_ref.shape[1]
+    query_ref[...] = in_ref[:, :width].astype(f32)
+    key_ref[...] = in_ref[:, width : 2 * width].astype(f32)
+    value_ref[...] = in_ref[:, 2 * width :].astype(f32)
+
+
+def widen_turned(in_ref, gate_ref, out_ref):
+    wide = gate_ref.shape[1]
+    gate_ref[...] = in_ref[:, :wide].astype(f32)
+    out_ref[...] = in_ref[:, wide:].astype(f32).T
+
+
+def call_widen(kernel, value, shapes):
+    return pl.pallas_call(
+        kernel,
+        out_shape=[jax.ShapeDtypeStruct(shape, f32) for shape in shapes],
+        compiler_params=pltpu.CompilerParams(vmem_limit_bytes=16 * 2**20),
+        cost_estimate=pl.CostEstimate(flops=0, bytes_accessed=6 * value.size, transcendentals=0),
+        name="widen",
+    )(value)
+
+
 def feed_grad_kernel(*refs):
     out_ref = refs[-1]
     two = refs[2].shape[1]
@@ -864,14 +959,18 @@
 
     def finish():
         ff_rows = after(ff_grad, qkv_rows_grad).reshape(ny, rl, 3 * fl)
-        pieces = jnp.zeros((ny, rl, 3 * fl), bf16)
-        pieces = lax.dynamic_update_slice_in_dim(
-            pieces, lax.dynamic_index_in_dim(ff_rows, y, 0), y, 0
-        )
-        for k in range(1, ny):
-            sent = lax.dynamic_index_in_dim(ff_rows, lax.rem(y + k, ny), 0)
-            got = lax.ppermute(sent, "y", [(i, (i + k) % ny) for i in range(ny)])
-            pieces = lax.dynamic_update_slice_in_dim(pieces, got, lax.rem(y - k + ny, ny), 0)
+        if ny == 2:
+            joined = call_join_two(ff_rows, swap(call_pick(ff_rows, 1 - y), "y"), y)
+        else:
+            pieces = jnp.zeros((ny, rl, 3 * fl), bf16)
+            pieces = lax.dynamic_update_slice_in_dim(
+                pieces, lax.dynamic_index_in_dim(ff_rows, y, 0), y, 0
+            )
+            for k in range(1, ny):
+                sent = lax.dynamic_index_in_dim(ff_rows, lax.rem(y + k, ny), 0)
+                got = lax.ppermute(sent, "y", [(i, (i + k) % ny) for i in range(ny)])
+                pieces = lax.dynamic_update_slice_in_dim(pieces, got, lax.rem(y - k + ny, ny), 0)
+            joined = call_join(pieces)
         block_own = to_absolute((residual + to_relative(feed.reshape(-1, depth))).astype(bf16))
         block_out = gather_head(block_own.reshape(micro, quarter, depth))
         grad_decay = tn(low_rank, logit_low)
@@ -893,7 +992,7 @@
         return (
             block_out,
             input_low.astype(f32),
-            *call_join(pieces),
+            *joined,
             summed[: 2 * rl],
             summed[2 * rl : (2 + rank) * rl].reshape(rank, rl).T,
             summed[(2 + rank) * rl : n_summed],
@@ -903,20 +1002,21 @@
 
     block_out, input_grad, g_gate, g_up, g_down, g_norms, g_rank, g_gain, g_decay, g_bias = finish()
     g_norm_in, g_norm_mid = g_norms[:rl], g_norms[rl:]
-    qkv_grad = qkv_grad.astype(f32)
+    g_query, g_key, g_value = call_widen(widen_rows, qkv_grad, [(rl, width), (rl, width), (rl, wide)])
+    g_outgate, g_out = call_widen(widen_turned, go_grad, [(rl, wide), (wide, rl)])
     return (
         block_out,
         input_grad,
         g_norm_in,
-        qkv_grad[:, :width],
-        qkv_grad[:, width : 2 * width],
-        qkv_grad[:, 2 * width :],
-        go_grad[:, :wide].astype(f32),
+        g_query,
+        g_key,
+        g_value,
+        g_outgate,
         g_rank,
         g_decay,
         g_bias,
         g_gain,
-        go_grad[:, wide:].T.astype(f32),
+        g_out,
         g_norm_mid,
         g_gate,
         g_up,

time: 649 us -> 641 us (0.988)
  local copies, waits for them, and re-layouts: 61.4 us -> 50.9 us
  waiting for transfers between devices: 248 us -> 257 us
  other arithmetic: 71.4 us -> 62.5 us
    ppermute x1 -> x0, waiting for transfers between devices: 13.7 us -> none  [finish(): got = lax.ppermute(sent, 'y', [(i, (i + k) % ny) for i in range(ny)])]
    ppermute x29 -> x30, waiting for transfers between devices: 103 us -> 115 us  [swap(): return lax.ppermute(x, axis, [(0, 1), (1, 0)])]
    unnamed x128 -> x169, local copies, waits for them, and re-layouts: 9.65 us -> 13.3 us
    ppermute x29 -> x30, starting transfers between devices: 19.6 us -> 22.3 us  [swap(): return lax.ppermute(x, axis, [(0, 1), (1, 0)])]
  transfers between devices with their start and end apart: 45 -> 45, of which waited for: 27 -> 27; matrix products, arithmetic and copies ran while one was open for 27% -> 24% of each run, Pallas kernels for 7% -> 8%
where the time goes in v4:
time: 641 us; the launch traced here: 630 us
  waiting for transfers between devices  257 us (40%)
  blocking collectives  72 us (11%)
  Pallas kernels  63.6 us (10%)
  other arithmetic  62.5 us (10%)
  matrix products  55.2 us (9%)
  starting transfers between devices  51.3 us (8%)
  local copies, waits for them, and re-layouts  50.9 us (8%)
  between operations  16.7 us (3%)
    ppermute x30, waiting for transfers between devices, swap(): return lax.ppermute(x, axis, [(0, 1), (1, 0)])  115 us
    dot_general x30, matrix products, dot(): return lax.dot_general(a, b, (dims, ((), ())), preferred_element_type=f32)  55.2 us
    all_to_all x1, blocking collectives, spread_states(): got = lax.all_to_all(sent, ctx, 0, 0)  40.7 us
    all_gather x1, waiting for transfers between devices, per_device(): ff_full = lax.all_gather(ff_unit, 'z', axis=0, tiled=True)  36.9 us
    all_to_all x1, blocking collectives, collect_states(): back = lax.all_to_all(entering, ('z', 'y'), 0, 0)  31.3 us
    pallas_call x2, Pallas kernels, call_feed(): pl.pallas_call(functools.partial(feed_kernel, units=units), grid=(rows //...  29.1 us
    all_gather x1, waiting for transfers between devices, per_device(): go_rows = lax.all_gather(w_go, 'z', axis=0, tiled=True)  28.2 us
    all_to_all x1, waiting for transfers between devices, spread_states(): got = lax.all_to_all(sent, ctx, 0, 0)  25.5 us
  transfers between devices with their start and end apart: 45, of which 27 were waited for; matrix products, arithmetic and copies ran while one was open for 24% of the time, Pallas kernels for 8%

profile of v4, /device:TPU:0, one launch (start us, length us, event | category | flops | bytes accessed | tf_op | source)
XLA Modules:
  0.0 630.0 jit_solution(10145261814479846757)
XLA Ops:
  7.3 2.0 pad_maximum_fusion.24
  10.8 2.8 concatenate.225
  14.2 7.3 %all-to-all-start.4 = ((bf16[8,48,128]{2,1,0:T(8,128)(2,1)}), bf16[8,48,128]{2,1,0:T(8,128)(2,1)}, u32[]{:S(2)}, u32[]{:S(2)}) async-start(bf16[8,48,128]{2,1,0:T(8,128)(2,1)} %broadcast_in_dim.9), calls=%async_computation.4 | async-start | bytes 196608 | tf_op jit(solution)/shard_map/all_to_all | solution.py:764
  21.5 2.3 fusion.122
  23.9 2.0 collective-permute-start.20
  43.7 1.9 broadcast_select_fusion.7
  49.5 11.4 %all-gather.4.cloned.1.call-done = bf16[1024,1024]{1,0:T(8,128)(2,1)} async-done(((bf16[256,1024]{1,0:T(8,128)(2,1)}), bf16[1024,1024]{1,0:T(8,128)(2,1)}) %all-gather.4.cloned.1.call-update) | async-done | bytes 2097168 | tf_op jit(solution)/shard_map/all_gather | solution.py:753
  66.4 7.4 %collective-permute-done.21 = bf16[256,2112]{0,1:T(8,128)(2,1)} collective-permute-done((bf16[256,2112]{0,1:T(8,128)(2,1)}, bf16[256,2112]{0,1:T(8,128)(2,1)}, u32[]{:S(2)}, u32[]{:S(2)}) %collective-permute-start.21) | collective-permute-done | bytes 1081376 | tf_op jit(solution)/shard_map/ppermute | solution.py:38
  73.8 2.3 copy.266
  76.1 3.4 maximum_select_fusion.2
  79.5 28.2 %all-gather.6.cloned.1.call-done = bf16[1024,1024]{1,0:T(8,128)(2,1)} async-done(((bf16[256,1024]{1,0:T(8,128)(2,1)}), bf16[1024,1024]{1,0:T(8,128)(2,1)}) %all-gather.6.cloned.1.call-update) | async-done | bytes 2097168 | tf_op jit(solution)/shard_map/all_gather | solution.py:755
  109.3 2.9 fusion.50
  113.5 5.2 collective-permute-done.12
  118.7 3.9 add_convert_fusion.10
  122.6 77.7 %conditional.3 = (f32[512,512]{1,0:T(8,128)S(1)}, bf16[512,256]{1,0:T(8,128)(2,1)S(1)}, bf16[2,512,256]{2,1,0:T(8,128)(2,1)S(1)}, f32[2,256]{1,0:T(2,128)S(1)}) conditional(s32[]{:T(128)} %bitcast.37, () %tuple.40, (bf16[512,1024]{1,0:T(8,128)(2,1)}, f32[512,256]{1,0:T(8,128)S(1)}, bf16[256,256]{1,0:T(8,128)(2,1)S(1)}, s32[256,256]{1,0:T(8,128)S(1)}, ...), branch_computations={%region_1.2_spmd, %region_2.3_spmd} | conditional | flops 2003206272 | bytes 14699380 | solution.py:56
  122.7 5.0 scan_forward.1
  128.0 40.7 %all_to_all.26.got_ref = bf16[8,144,256]{2,1,0:T(8,128)(2,1)S(1)} all-to-all(bf16[8,144,256]{2,1,0:T(8,128)(2,1)S(1)} %pad_maximum_fusion), channel_id=1, replica_groups=mesh['z'=4,'y'=2,'x'=2,'c'=2] {'z','y'}, dimensions={0} | all-to-all | bytes 1179648 | tf_op jit(solution)/shard_map/cond/branch_1_fun/all_to_all | solution.py:355
  168.8 31.3 %all_to_all.27 = bf16[8,128,256]{2,1,0:T(8,128)(2,1)S(1)} all-to-all(bf16[8,128,256]{2,1,0:T(8,128)(2,1)S(1)} %scan_states.2), channel_id=1, replica_groups=mesh['z'=4,'y'=2,'x'=2,'c'=2] {'z','y'}, dimensions={0} | all-to-all | bytes 1048576 | tf_op jit(solution)/shard_map/cond/branch_1_fun/all_to_all | solution.py:368
  201.9 3.1 multiply_convert_fusion.3
  205.0 2.2 convolution_convert_fusion.9
  214.5 10.8 %collective-permute-done.15 = bf16[2,64,2048]{2,1,0:T(8,128)(2,1)S(1)} collective-permute-done((bf16[2,64,2048]{2,1,0:T(8,128)(2,1)S(1)}, bf16[2,64,2048]{2,1,0:T(8,128)(2,1)S(1)}, u32[]{:S(2)}, u32[]{:S(2)}) %collective-permute-start.15) | collective-permute-done | bytes 524320 | tf_op jit(solution)/shard_map/ppermute | solution.py:38
  229.5 5.9 collective-permute-done.16
  237.5 10.1 %collective-permute-done.17 = bf16[2,64,2048]{2,1,0:T(8,128)(2,1)S(1)} collective-permute-done((bf16[2,64,2048]{2,1,0:T(8,128)(2,1)S(1)}, bf16[2,64,2048]{2,1,0:T(8,128)(2,1)S(1)}, u32[]{:S(2)}, u32[]{:S(2)}) %collective-permute-start.17) | collective-permute-done | bytes 524320 | tf_op jit(solution)/shard_map/ppermute | solution.py:38
  249.4 4.3 collective-permute-done.22.mid_ref
  253.6 36.9 %all-gather.8.cloned.1.call-done.weight_ref = bf16[2048,2112]{1,0:T(8,128)(2,1)} async-done(((bf16[512,2112]{1,0:T(8,128)(2,1)}), bf16[2048,2112]{1,0:T(8,128)(2,1)}) %all-gather.8.cloned.1.call-update) | async-done | bytes 8650768 | tf_op jit(solution)/shard_map/all_gather | solution.py:811
  290.6 14.9 %feed_forward.2 = (bf16[512,1408]{1,0:T(8,128)(2,1)S(1)}, bf16[512,704]{1,0:T(8,128)(2,1)S(1)}, bf16[512,2048]{1,0:T(8,128)(2,1)S(1)}) custom-call(bf16[512,2048]{1,0:T(8,128)(2,1)} %collective-permute-done.22.mid_ref, bf16[512,2048]{1,0:T(8,128)(2,1)} %collective-permute-done.23.low_ref, bf16[2048,2112]{1,0:T(8,128)(2,1)} %all-gather.8.cloned.1.call-done.weight_ref), custom_call_target="tpu_custom_call" | custom-call | flops 7381975040 | bytes 28000000 | tf_op jit(solution)/shard_map/feed_forward/pallas_call | solution.py:388
  305.6 14.2 %feed_forward.3 = (bf16[512,1408]{1,0:T(8,128)(2,1)}, bf16[512,704]{1,0:T(8,128)(2,1)S(1)}, bf16[512,2048]{1,0:T(8,128)(2,1)S(1)}) custom-call(bf16[512,2048]{1,0:T(8,128)(2,1)S(1)} %bitcast.350, bf16[512,2048]{1,0:T(8,128)(2,1)} %bitcast.79.low_ref, bf16[2048,2112]{1,0:T(8,128)(2,1)} %all-gather.8.cloned.1.call-done.weight_ref, ...), custom_call_target="tpu_custom_call" | custom-call | flops 7381975040 | bytes 28000000 | tf_op jit(solution)/shard_map/feed_forward/pallas_call | solution.py:388
  321.5 18.5 %conditional.4 = (bf16[2048,2112]{1,0:T(8,128)(2,1)}, bf16[128,2048]{1,0:T(8,128)(2,1)}, bf16[128,2048]{1,0:T(8,128)(2,1)}) conditional(s32[]{:T(128)} %bitcast.37, () %tuple.43, (bf16[512,2048]{1,0:T(8,128)(2,1)S(1)}, bf16[512,2048]{1,0:T(8,128)(2,1)}, bf16[512,1408]{1,0:T(8,128)(2,1)S(1)}, bf16[512,704]{1,0:T(8,128)(2,1)S(1)}, ...), branch_computations={%region_5.6_spmd, %region_6.7_spmd} | conditional | flops 8860467200 | bytes 30437288 | solution.py:56
  324.6 13.9 %feed_grad.1 = bf16[2048,2112]{1,0:T(8,128)(2,1)} custom-call(bf16[512,2048]{1,0:T(8,128)(2,1)S(1)} %get-tuple-element.126.refs_0_, bf16[512,2048]{1,0:T(8,128)(2,1)} %get-tuple-element.127.refs_1_, bf16[512,1408]{1,0:T(8,128)(2,1)S(1)} %get-tuple-element.128.refs_2_, bf16[512,704]{1,0:T(8,128)(2,1)S(1)} %get-tuple-element.129.refs_3_, ...), custom_call_target="tpu_custom_call" | custom-call | flops 8858370048 | bytes 21000000 | tf_op jit(solution)/shard_map/cond/branch_1_fun/feed_grad/pallas_call | solution.py:575
  343.6 167.1 %conditional.5 = (f32[128,2048]{1,0:T(8,128)}, bf16[1024,1024]{1,0:T(8,128)(2,1)}, bf16[1024,1024]{1,0:T(8,128)(2,1)}, bf16[512,256]{1,0:T(8,128)(2,1)S(1)}, f32...) conditional(s32[]{:T(128)} %bitcast.37, () %tuple.42, ...), branch_computations={%region_7.8_spmd, %region_8.13_spmd} | conditional | flops 16747399168 | bytes 296035552 | solution.py:56
  349.0 3.7 collective-permute-done.2
  358.1 12.0 %collective-permute-done.4 = bf16[2,64,2048]{2,1,0:T(8,128)(2,1)S(1)} collective-permute-done((bf16[2,64,2048]{2,1,0:T(8,128)(2,1)S(1)}, bf16[2,64,2048]{2,1,0:T(8,128)(2,1)S(1)}, u32[]{:S(2)}, u32[]{:S(2)}) %collective-permute-start.4) | collective-permute-done | bytes 524320 | tf_op jit(solution)/shard_map/cond/branch_1_fun/ppermute | solution.py:38
  371.9 2.4 collective-permute-done.5
  374.3 2.0 maximum_select_fusion
  376.3 2.7 fusion.10
  382.7 3.5 all-to-all-start.2
  388.1 5.2 convolution_convert_fusion
  394.1 25.5 %all-to-all-done.2.got_ref = bf16[8,144,256]{2,1,0:T(8,128)(2,1)S(1)} async-done(((bf16[8,144,256]{2,1,0:T(8,128)(2,1)}), bf16[8,144,256]{2,1,0:T(8,128)(2,1)S(1)}, u32[]{:S(2)}, u32[]{:S(2)}) %all-to-all-start.2) | async-done | bytes 589856 | tf_op jit(solution)/shard_map/cond/branch_1_fun/all_to_all | solution.py:355
  420.5 5.5 all-to-all-start.3
  426.0 2.0 fusion.7
  433.9 2.2 collective-permute-start.6
  436.2 18.0 %all-to-all-done.3 = bf16[8,128,256]{2,1,0:T(8,128)(2,1)S(1)} async-done(((bf16[8,128,256]{2,1,0:T(8,128)(2,1)}), bf16[8,128,256]{2,1,0:T(8,128)(2,1)S(1)}, u32[]{:S(2)}, u32[]{:S(2)}) %all-to-all-start.3) | async-done | bytes 524320 | tf_op jit(solution)/shard_map/cond/branch_1_fun/all_to_all | solution.py:368
  454.2 9.2 %scan_backward.1 = (bf16[512,1024]{1,0:T(8,128)(2,1)S(1)}, f32[512,256]{1,0:T(8,128)S(1)}) custom-call(bf16[512,1024]{1,0:T(8,128)(2,1)} %get-tuple-element.152.qkv_ref, f32[512,256]{1,0:T(8,128)} %get-tuple-element.153.decay_ref, f32[512,256]{1,0:T(8,128)} %get-tuple-element.154.logit_ref, bf16[512,512]{1,0:T(8,128)(2,1)S(1)} %copy-done.5, ...), custom_call_target="tpu_custom_call" | custom-call | flops 5000000000 | bytes 12000000 | tf_op jit(solution)/shard_map/cond/branch_1_fun/scan_backward/pallas_call | solution.py:294
  463.8 4.0 convert_bitcast_fusion.1.refs_2_
  467.8 4.1 fusion.85
  471.9 3.3 fusion.92
  476.6 4.4 add_convert_fusion.2
  483.8 2.0 add_convert_fusion.4
  486.6 8.3 %collective-permute-done.8 = bf16[128,2048]{1,0:T(8,128)(2,1)S(1)} collective-permute-done((bf16[128,2048]{1,0:T(8,128)(2,1)S(1)}, bf16[128,2048]{1,0:T(8,128)(2,1)S(1)}, u32[]{:S(2)}, u32[]{:S(2)}) %collective-permute-start.8) | collective-permute-done | bytes 524320 | tf_op jit(solution)/shard_map/cond/branch_1_fun/ppermute | solution.py:38
  500.3 3.3 collective-permute-done.11
  503.6 1.9 collective-permute-done.9
  506.7 3.8 add_convert_fusion.3
  521.5 9.0 %collective-permute-done.25 = bf16[2,64,2048]{2,1,0:T(8,128)(2,1)S(1)} collective-permute-done((bf16[2,64,2048]{2,1,0:T(8,128)(2,1)S(1)}, bf16[2,64,2048]{2,1,0:T(8,128)(2,1)S(1)}, u32[]{:S(2)}, u32[]{:S(2)}) %collective-permute-start.25) | collective-permute-done | bytes 524320 | tf_op jit(solution)/shard_map/ppermute | solution.py:38
  531.9 10.2 %collective-permute-done.28 = bf16[2,64,2176]{2,1,0:T(8,128)(2,1)S(1)} collective-permute-done((bf16[2,64,2176]{2,1,0:T(8,128)(2,1)S(1)}, bf16[2,64,2176]{2,1,0:T(8,128)(2,1)S(1)}, u32[]{:S(2)}, u32[]{:S(2)}) %collective-permute-start.28) | collective-permute-done | bytes 557088 | tf_op jit(solution)/shard_map/ppermute | solution.py:38
  544.9 3.7 all-to-all-start.5
  548.6 2.0 fusion.39
  550.7 16.4 %collective-permute-done.33 = bf16[1024,1024]{1,0:T(8,128)(2,1)} collective-permute-done((bf16[1024,1024]{1,0:T(8,128)(2,1)}, bf16[1024,1024]{1,0:T(8,128)(2,1)}, u32[]{:S(2)}, u32[]{:S(2)}) %collective-permute-start.33) | collective-permute-done | bytes 2097184 | tf_op jit(solution)/shard_map/ppermute | solution.py:724
  567.2 5.0 add_convert_fusion.8.refs_0_
  573.2 1.9 maximum_select_fusion.3
  576.6 8.8 %collective-permute-done.29 = bf16[2,64,2048]{2,1,0:T(8,128)(2,1)S(1)} collective-permute-done((bf16[2,64,2048]{2,1,0:T(8,128)(2,1)S(1)}, bf16[2,64,2048]{2,1,0:T(8,128)(2,1)S(1)}, u32[]{:S(2)}, u32[]{:S(2)}) %collective-permute-start.29) | collective-permute-done | bytes 524320 | tf_op jit(solution)/shard_map/ppermute | solution.py:38
  596.9 2.0 fusion.31
  598.9 2.3 copy.278
  603.5 12.8 %collective-permute-done.34 = bf16[256,2112]{0,1:T(8,128)(2,1)} collective-permute-done((bf16[256,2112]{0,1:T(8,128)(2,1)}, bf16[256,2112]{0,1:T(8,128)(2,1)}, u32[]{:S(2)}, u32[]{:S(2)}) %collective-permute-start.34) | collective-permute-done | bytes 1081376 | tf_op jit(solution)/shard_map/ppermute | solution.py:38
  618.0 2.6 join_two.1
  (517 shorter events, 130.0 us)
Async XLA Ops:
  7.2 18.6 %copy-start.8 = (bf16[1408,256]{1,0:T(8,128)(2,1)S(1)}, bf16[1408,256]{1,0:T(8,128)(2,1)}, u32[]{:S(2)}) copy-start(bf16[1408,256]{1,0:T(8,128)(2,1)} %down_ref.1) | copy-start | bytes 2162692
  7.2 18.6 %copy-start.7 = (bf16[256,1408]{1,0:T(8,128)(2,1)S(1)}, bf16[256,1408]{1,0:T(8,128)(2,1)}, u32[]{:S(2)}) copy-start(bf16[256,1408]{1,0:T(8,128)(2,1)} %up_ref.1) | copy-start | bytes 2162692
  7.2 18.6 %copy-start.6 = (bf16[256,1408]{1,0:T(8,128)(2,1)S(1)}, bf16[256,1408]{1,0:T(8,128)(2,1)}, u32[]{:S(2)}) copy-start(bf16[256,1408]{1,0:T(8,128)(2,1)} %gate_ref.1) | copy-start | bytes 2162692
  7.2 53.7 %all-gather.4.cloned.1.call-start = ((), (), s32[]{:S(2)}) async-start(), calls=%async_computation.9 | async-start | bytes 2621440 | tf_op jit(solution)/shard_map/all_gather | solution.py:753
  14.2 31.4 %all-to-all-start.4 = ((bf16[8,48,128]{2,1,0:T(8,128)(2,1)}), bf16[8,48,128]{2,1,0:T(8,128)(2,1)}, u32[]{:S(2)}, u32[]{:S(2)}) async-start(bf16[8,48,128]{2,1,0:T(8,128)(2,1)} %broadcast_in_dim.9), calls=%async_computation.4 | async-start | bytes 196608 | tf_op jit(solution)/shard_map/all_to_all | solution.py:764
  21.5 86.3 %all-gather.6.cloned.1.call-start = ((), (), s32[]{:S(2)}) async-start(), calls=%async_computation.10 | async-start | bytes 2621440 | tf_op jit(solution)/shard_map/all_gather | solution.py:755
  23.9 184.4 %collective-permute-start.20 = (bf16[2,128,2048]{2,1,0:T(8,128)(2,1)}, bf16[2,128,2048]{2,1,0:T(8,128)(2,1)}, u32[]{:S(2)}, u32[]{:S(2)}) collective-permute-start(bf16[2,128,2048]{2,1,0:T(8,128)(2,1)} %fusion.122), channel_id=1, source_target_pairs={{4,0},{0,4},{5,1},{1,5},{6,2},{2,6},{7,3},{3,7},{12,8},{8,12},{13,... | collective-permute-start | bytes 3145736 | tf_op jit(solution)/shard_map/ppermute | solution.py:667
  28.8 44.9 %collective-permute-start.21 = (bf16[256,2112]{0,1:T(8,128)(2,1)}, bf16[256,2112]{0,1:T(8,128)(2,1)}, u32[]{:S(2)}, u32[]{:S(2)}) collective-permute-start(bf16[256,2112]{0,1:T(8,128)(2,1)} %bitcast.316), channel_id=1, source_target_pairs={{0,4},{4,0},{1,5},{5,1},{2,6},{6,2},{3,7},{7,3},{8,12},{12,8},{9,1... | collective-permute-start | bytes 3244040 | tf_op jit(solution)/shard_map/ppermute | solution.py:38
  30.9 259.7 %all-gather.8.cloned.1.call-start = ((), (), s32[]{:S(2)}) async-start(), calls=%async_computation.11 | async-start | bytes 11141120 | tf_op jit(solution)/shard_map/all_gather | solution.py:811
  49.5 14.6 %copy-start.71 = (bf16[16,2048]{1,0:T(8,128)(2,1)}, bf16[16,2048]{1,0:T(8,128)(2,1)S(1)}, u32[]{:S(2)}) copy-start(bf16[16,2048]{1,0:T(8,128)(2,1)S(1)} %slice.476) | copy-start | bytes 196612
  60.9 57.7 %collective-permute-start.12 = (bf16[1024,1024]{1,0:T(8,128)(2,1)}, bf16[1024,1024]{1,0:T(8,128)(2,1)}, u32[]{:S(2)}, u32[]{:S(2)}) collective-permute-start(bf16[1024,1024]{1,0:T(8,128)(2,1)} %all-gather.4.cloned.1.call-done), channel_id=1, source_target_pairs={{4,0},{0,4},{5,1},{1,5},{6,2},{2,6},{7,3},{3,7},{12,8},{8,12},{13,... | collective-permute-start | bytes 6291464 | tf_op jit(solution)/shard_map/ppermute | solution.py:667
  64.2 137.1 %copy-start.12 = (bf16[512,2048]{1,0:T(8,128)(2,1)}, bf16[512,2048]{1,0:T(8,128)(2,1)S(1)}, u32[]{:S(2)}) copy-start(bf16[512,2048]{1,0:T(8,128)(2,1)S(1)} %fusion.29) | copy-start | bytes 6291460
  64.9 14.6 %copy-start.74 = (bf16[512,16]{0,1:T(8,128)(2,1)}, bf16[512,16]{0,1:T(8,128)(2,1)S(1)}, u32[]{:S(2)}) copy-start(bf16[512,16]{0,1:T(8,128)(2,1)S(1)} %convolution_convert_fusion.11) | copy-start | bytes 49156
  64.9 11.2 %copy-start.17 = (bf16[1,256,2112]{2,1,0:T(8,128)(2,1)S(1)}, bf16[1,256,2112]{2,1,0:T(8,128)(2,1)}, u32[]{:S(2)}) copy-start(bf16[1,256,2112]{2,1,0:T(8,128)(2,1)} %get-tuple-element.494) | copy-start | bytes 3244036
  79.5 492.7 %reduce-scatter.4.cloned.1.call-start = ((), (), s32[]{:S(2)}) async-start(), calls=%async_computation.12 | async-start | bytes 11141120 | tf_op jit(solution)/shard_map/reduce_scatter | solution.py:730
  107.8 93.5 %collective-permute-start.13 = (bf16[1024,1024]{1,0:T(8,128)(2,1)}, bf16[1024,1024]{1,0:T(8,128)(2,1)}, u32[]{:S(2)}, u32[]{:S(2)}) collective-permute-start(bf16[1024,1024]{1,0:T(8,128)(2,1)} %all-gather.6.cloned.1.call-done), channel_id=1, source_target_pairs={{4,0},{0,4},{5,1},{1,5},{6,2},{2,6},{7,3},{3,7},{12,8},{8,12},{13,... | collective-permute-start | bytes 6291464 | tf_op jit(solution)/shard_map/ppermute | solution.py:667
  208.1 2.7 collective-permute-start.14
  211.3 14.0 %collective-permute-start.15 = (bf16[2,64,2048]{2,1,0:T(8,128)(2,1)S(1)}, bf16[2,64,2048]{2,1,0:T(8,128)(2,1)S(1)}, u32[]{:S(2)}, u32[]{:S(2)}) collective-permute-start(bf16[2,64,2048]{2,1,0:T(8,128)(2,1)S(1)} %dynamic-slice_bitcast_fusion.2), channel_id=1, source_target_pairs={{0,2},{2,0},{1,3},{3,1},{4,6},{6,4},{5,7},{7,5},{8,10},{10,8},{9,1... | collective-permute-start | bytes 1572872 | tf_op jit(solution)/shard_map/ppermute | solution.py:38
  213.0 12.3 %copy-start.56 = (bf16[2,64,1024]{2,1,0:T(8,128)(2,1)S(1)}, bf16[2,64,1024]{2,1,0:T(8,128)(2,1)}, u32[]{:S(2)}) copy-start(bf16[2,64,1024]{2,1,0:T(8,128)(2,1)} %get-tuple-element.533) | copy-start | bytes 786436
  213.0 12.3 %copy-start.57 = (bf16[2,64,1024]{2,1,0:T(8,128)(2,1)S(1)}, bf16[2,64,1024]{2,1,0:T(8,128)(2,1)}, u32[]{:S(2)}) copy-start(bf16[2,64,1024]{2,1,0:T(8,128)(2,1)} %get-tuple-element.534) | copy-start | bytes 786436
  214.5 11.3 %copy-start.38 = (bf16[128,1024]{1,0:T(8,128)(2,1)S(1)}, bf16[128,1024]{1,0:T(8,128)(2,1)}, u32[]{:S(2)}) copy-start(bf16[128,1024]{1,0:T(8,128)(2,1)} %get-tuple-element.531) | copy-start | bytes 786436
  214.5 11.3 %copy-start.40 = (bf16[128,1024]{1,0:T(8,128)(2,1)S(1)}, bf16[128,1024]{1,0:T(8,128)(2,1)}, u32[]{:S(2)}) copy-start(bf16[128,1024]{1,0:T(8,128)(2,1)} %get-tuple-element.532) | copy-start | bytes 786436
  214.5 34.8 %collective-permute-start.23 = (bf16[512,2048]{1,0:T(8,128)(2,1)}, bf16[512,2048]{1,0:T(8,128)(2,1)}, u32[]{:S(2)}, u32[]{:S(2)}) collective-permute-start(bf16[512,2048]{1,0:T(8,128)(2,1)} %bitcast.79.low_ref), channel_id=1, source_target_pairs={{0,1},{1,0},{2,3},{3,2},{4,5},{5,4},{6,7},{7,6},{8,9},{9,8},{10,11... | collective-permute-start | bytes 6291464 | tf_op jit(solution)/shard_map/ppermute | solution.py:38
  226.4 9.6 %collective-permute-start.18 = (bf16[64,2048]{1,0:T(8,128)(2,1)S(1)}, bf16[64,2048]{1,0:T(8,128)(2,1)S(1)}, u32[]{:S(2)}, u32[]{:S(2)}) collective-permute-start(bf16[64,2048]{1,0:T(8,128)(2,1)S(1)} %get-tuple-element.529), channel_id=1, source_target_pairs={{0,2},{2,0},{1,3},{3,1},{4,6},{6,4},{5,7},{7,5},{8,10},{10,8},{9,1... | collective-permute-start | bytes 786440 | tf_op jit(solution)/shard_map/ppermute | solution.py:38
  228.0 7.3 %collective-permute-start.16 = (bf16[64,2048]{1,0:T(8,128)(2,1)S(1)}, bf16[64,2048]{1,0:T(8,128)(2,1)S(1)}, u32[]{:S(2)}, u32[]{:S(2)}) collective-permute-start(bf16[64,2048]{1,0:T(8,128)(2,1)S(1)} %get-tuple-element.530), channel_id=1, source_target_pairs={{0,4},{4,0},{1,5},{5,1},{2,6},{6,2},{3,7},{7,3},{8,12},{12,8},{9,1... | collective-permute-start | bytes 786440 | tf_op jit(solution)/shard_map/ppermute | solution.py:38
  235.4 12.2 %collective-permute-start.17 = (bf16[2,64,2048]{2,1,0:T(8,128)(2,1)S(1)}, bf16[2,64,2048]{2,1,0:T(8,128)(2,1)S(1)}, u32[]{:S(2)}, u32[]{:S(2)}) collective-permute-start(bf16[2,64,2048]{2,1,0:T(8,128)(2,1)S(1)} %pad_maximum_fusion.26), channel_id=1, source_target_pairs={{0,2},{2,0},{1,3},{3,1},{4,6},{6,4},{5,7},{7,5},{8,10},{10,8},{9,1... | collective-permute-start | bytes 1572872 | tf_op jit(solution)/shard_map/ppermute | solution.py:38
  236.1 11.9 %collective-permute-start.19 = (bf16[2,64,2048]{2,1,0:T(8,128)(2,1)S(1)}, bf16[2,64,2048]{2,1,0:T(8,128)(2,1)S(1)}, u32[]{:S(2)}, u32[]{:S(2)}) collective-permute-start(bf16[2,64,2048]{2,1,0:T(8,128)(2,1)S(1)} %pad_maximum_fusion.27), channel_id=1, source_target_pairs={{0,4},{4,0},{1,5},{5,1},{2,6},{6,2},{3,7},{7,3},{8,12},{12,8},{9,1... | collective-permute-start | bytes 1572872 | tf_op jit(solution)/shard_map/ppermute | solution.py:38
  249.4 4.3 collective-permute-start.22
  290.6 15.0 %copy-start.78 = (bf16[8,64,2048]{2,1,0:T(8,128)(2,1)S(1)}, bf16[8,64,2048]{2,1,0:T(8,128)(2,1)}, u32[]{:S(2)}) copy-start(bf16[8,64,2048]{2,1,0:T(8,128)(2,1)} %copy-done.77) | copy-start | bytes 6291460
  305.5 16.0 %copy-start.58 = (bf16[512,704]{1,0:T(8,128)(2,1)}, bf16[512,704]{1,0:T(8,128)(2,1)S(1)}, u32[]{:S(2)}) copy-start(bf16[512,704]{1,0:T(8,128)(2,1)S(1)} %get-tuple-element.221) | copy-start | bytes 2162692
  305.5 14.3 %collective-permute-start.24 = (bf16[512,2048]{1,0:T(8,128)(2,1)S(1)}, bf16[512,2048]{1,0:T(8,128)(2,1)S(1)}, u32[]{:S(2)}, u32[]{:S(2)}) collective-permute-start(bf16[512,2048]{1,0:T(8,128)(2,1)S(1)} %get-tuple-element.217.rest_0_), channel_id=1, source_target_pairs={{0,1},{1,0},{2,3},{3,2},{4,5},{5,4},{6,7},{7,6},{8,9},{9,8},{10,11... | collective-permute-start | bytes 6291464 | tf_op jit(solution)/shard_map/ppermute | solution.py:38
  321.6 17.0 %collective-permute-start.1 = (bf16[128,2048]{1,0:T(8,128)(2,1)S(1)}, bf16[128,2048]{1,0:T(8,128)(2,1)S(1)}, u32[]{:S(2)}, u32[]{:S(2)}) collective-permute-start(bf16[128,2048]{1,0:T(8,128)(2,1)S(1)} %get-tuple-element.457), channel_id=1, source_target_pairs={{0,4},{4,0},{1,5},{5,1},{2,6},{6,2},{3,7},{7,3},{8,12},{12,8},{9,1... | collective-permute-start | bytes 1572872 | tf_op jit(solution)/shard_map/cond/branch_1_fun/ppermute | solution.py:38
  323.1 15.5 %collective-permute-start = (bf16[128,2048]{1,0:T(8,128)(2,1)S(1)}, bf16[128,2048]{1,0:T(8,128)(2,1)S(1)}, u32[]{:S(2)}, u32[]{:S(2)}) collective-permute-start(bf16[128,2048]{1,0:T(8,128)(2,1)S(1)} %get-tuple-element.458), channel_id=1, source_target_pairs={{0,2},{2,0},{1,3},{3,1},{4,6},{6,4},{5,7},{7,5},{8,10},{10,8},{9,1... | collective-permute-start | bytes 1572872 | tf_op jit(solution)/shard_map/cond/branch_1_fun/ppermute | solution.py:38
  340.0 261.2 %reduce-scatter.8.cloned.1.call-start = ((), (), s32[]{:S(2)}) async-start(), calls=%async_computation.14 | async-start | bytes 2621440 | tf_op jit(solution)/shard_map/reduce_scatter | solution.py:730
  344.6 8.1 %collective-permute-start.2 = (bf16[64,2048]{1,0:T(8,128)(2,1)S(1)}, bf16[64,2048]{1,0:T(8,128)(2,1)S(1)}, u32[]{:S(2)}, u32[]{:S(2)}) collective-permute-start(bf16[64,2048]{1,0:T(8,128)(2,1)S(1)} %slice.333), channel_id=1, source_target_pairs={{0,4},{4,0},{1,5},{5,1},{2,6},{6,2},{3,7},{7,3},{8,12},{12,8},{9,1... | collective-permute-start | bytes 786440 | tf_op jit(solution)/shard_map/cond/branch_1_fun/ppermute | solution.py:38
  346.3 7.8 %collective-permute-start.3 = (bf16[64,2048]{1,0:T(8,128)(2,1)S(1)}, bf16[64,2048]{1,0:T(8,128)(2,1)S(1)}, u32[]{:S(2)}, u32[]{:S(2)}) collective-permute-start(bf16[64,2048]{1,0:T(8,128)(2,1)S(1)} %slice.335), channel_id=1, source_target_pairs={{0,2},{2,0},{1,3},{3,1},{4,6},{6,4},{5,7},{7,5},{8,10},{10,8},{9,1... | collective-permute-start | bytes 786440 | tf_op jit(solution)/shard_map/cond/branch_1_fun/ppermute | solution.py:38
  357.6 13.7 %copy-start.85 = (bf16[8,64]{1,0:T(8,128)(2,1)S(1)}, bf16[8,64]{1,0:T(8,128)(2,1)}, u32[]{:S(2)}) copy-start(bf16[8,64]{1,0:T(8,128)(2,1)} %get-tuple-element.146) | copy-start | bytes 3076 | tf_op jit(solution)/shard_map/cond
  357.6 12.5 %collective-permute-start.4 = (bf16[2,64,2048]{2,1,0:T(8,128)(2,1)S(1)}, bf16[2,64,2048]{2,1,0:T(8,128)(2,1)S(1)}, u32[]{:S(2)}, u32[]{:S(2)}) collective-permute-start(bf16[2,64,2048]{2,1,0:T(8,128)(2,1)S(1)} %bitcast.261), channel_id=1, source_target_pairs={{0,2},{2,0},{1,3},{3,1},{4,6},{6,4},{5,7},{7,5},{8,10},{10,8},{9,1... | collective-permute-start | bytes 1572872 | tf_op jit(solution)/shard_map/cond/branch_1_fun/ppermute | solution.py:38
  371.3 3.0 collective-permute-start.5
  382.7 36.9 %all-to-all-start.2 = ((bf16[8,144,256]{2,1,0:T(8,128)(2,1)}), bf16[8,144,256]{2,1,0:T(8,128)(2,1)S(1)}, u32[]{:S(2)}, u32[]{:S(2)}) async-start(bf16[8,144,256]{2,1,0:T(8,128)(2,1)} %pad_maximum_fusion.7), calls=%async_computation.2 | async-start | bytes 1179648 | tf_op jit(solution)/shard_map/cond/branch_1_fun/all_to_all | solution.py:355
  393.3 83.3 %collective-permute-start.7 = (bf16[512,2048]{1,0:T(8,128)(2,1)}, bf16[512,2048]{1,0:T(8,128)(2,1)}, u32[]{:S(2)}, u32[]{:S(2)}) collective-permute-start(bf16[512,2048]{1,0:T(8,128)(2,1)} %convolution_convert_fusion), channel_id=1, source_target_pairs={{0,1},{1,0},{2,3},{3,2},{4,5},{5,4},{6,7},{7,6},{8,9},{9,8},{10,11... | collective-permute-start | bytes 6291464 | tf_op jit(solution)/shard_map/cond/branch_1_fun/ppermute | solution.py:38
  420.5 33.7 %all-to-all-start.3 = ((bf16[8,128,256]{2,1,0:T(8,128)(2,1)}), bf16[8,128,256]{2,1,0:T(8,128)(2,1)S(1)}, u32[]{:S(2)}, u32[]{:S(2)}) async-start(bf16[8,128,256]{2,1,0:T(8,128)(2,1)} %scan_states.3.refs_1_), calls=%async_computation.3 | async-start | bytes 1048576 | tf_op jit(solution)/shard_map/cond/branch_1_fun/all_to_all | solution.py:368
  433.9 20.3 %copy-start.5 = (bf16[512,512]{1,0:T(8,128)(2,1)S(1)}, bf16[512,512]{1,0:T(8,128)(2,1)}, u32[]{:S(2)}) copy-start(bf16[512,512]{1,0:T(8,128)(2,1)} %copy-done.4) | copy-start | bytes 1572868 | tf_op jit(solution)/shard_map/cond
  433.9 20.3 %copy-start.11 = (bf16[256,256]{1,0:T(8,128)(2,1)S(1)}, bf16[256,256]{1,0:T(8,128)(2,1)}, u32[]{:S(2)}) copy-start(bf16[256,256]{1,0:T(8,128)(2,1)} %constant.173.clone.1.upper_ref) | copy-start | bytes 393220 | tf_op jit(solution)/shard_map/cond
  433.9 20.3 %copy-start.92 = (f32[2,4]{1,0:T(2,128)S(1)}, f32[2,4]{1,0:T(2,128)}, u32[]{:S(2)}) copy-start(f32[2,4]{1,0:T(2,128)} %get-tuple-element.159.open_ref) | copy-start | bytes 100 | tf_op jit(solution)/shard_map/cond
  433.9 20.3 %copy-start.102 = (bf16[256,256]{1,0:T(8,128)(2,1)S(1)}, bf16[256,256]{1,0:T(8,128)(2,1)}, u32[]{:S(2)}) copy-start(bf16[256,256]{1,0:T(8,128)(2,1)} %get-tuple-element.156.lower_ref) | copy-start | bytes 393220 | tf_op jit(solution)/shard_map/cond
  433.9 72.7 %collective-permute-start.6 = (bf16[1024,1024]{1,0:T(8,128)(2,1)}, bf16[1024,1024]{1,0:T(8,128)(2,1)}, u32[]{:S(2)}, u32[]{:S(2)}) collective-permute-start(bf16[1024,1024]{1,0:T(8,128)(2,1)} %after.6), channel_id=1, source_target_pairs={{0,4},{4,0},{1,5},{5,1},{2,6},{6,2},{3,7},{7,3},{8,12},{12,8},{9,1... | collective-permute-start | bytes 6291464 | tf_op jit(solution)/shard_map/cond/branch_1_fun/ppermute | solution.py:724
  481.1 13.7 %collective-permute-start.8 = (bf16[128,2048]{1,0:T(8,128)(2,1)S(1)}, bf16[128,2048]{1,0:T(8,128)(2,1)S(1)}, u32[]{:S(2)}, u32[]{:S(2)}) collective-permute-start(bf16[128,2048]{1,0:T(8,128)(2,1)S(1)} %get-tuple-element.463), channel_id=1, source_target_pairs={{0,2},{2,0},{1,3},{3,1},{4,6},{6,4},{5,7},{7,5},{8,10},{10,8},{9,1... | collective-permute-start | bytes 1572872 | tf_op jit(solution)/shard_map/cond/branch_1_fun/ppermute | solution.py:38
  482.3 13.6 %collective-permute-start.10 = (bf16[128,2048]{1,0:T(8,128)(2,1)S(1)}, bf16[128,2048]{1,0:T(8,128)(2,1)S(1)}, u32[]{:S(2)}, u32[]{:S(2)}) collective-permute-start(bf16[128,2048]{1,0:T(8,128)(2,1)S(1)} %get-tuple-element.464), channel_id=1, source_target_pairs={{0,4},{4,0},{1,5},{5,1},{2,6},{6,2},{3,7},{7,3},{8,12},{12,8},{9,1... | collective-permute-start | bytes 1572872 | tf_op jit(solution)/shard_map/cond/branch_1_fun/ppermute | solution.py:38
  496.3 7.3 %collective-permute-start.11 = (bf16[64,2048]{1,0:T(8,128)(2,1)S(1)}, bf16[64,2048]{1,0:T(8,128)(2,1)S(1)}, u32[]{:S(2)}, u32[]{:S(2)}) collective-permute-start(bf16[64,2048]{1,0:T(8,128)(2,1)S(1)} %slice.570), channel_id=1, source_target_pairs={{0,2},{2,0},{1,3},{3,1},{4,6},{6,4},{5,7},{7,5},{8,10},{10,8},{9,1... | collective-permute-start | bytes 786440 | tf_op jit(solution)/shard_map/cond/branch_1_fun/ppermute | solution.py:38
  498.6 6.9 %collective-permute-start.9 = (bf16[64,2048]{1,0:T(8,128)(2,1)S(1)}, bf16[64,2048]{1,0:T(8,128)(2,1)S(1)}, u32[]{:S(2)}, u32[]{:S(2)}) collective-permute-start(bf16[64,2048]{1,0:T(8,128)(2,1)S(1)} %slice.566), channel_id=1, source_target_pairs={{0,4},{4,0},{1,5},{5,1},{2,6},{6,2},{3,7},{7,3},{8,12},{12,8},{9,1... | collective-permute-start | bytes 786440 | tf_op jit(solution)/shard_map/cond/branch_1_fun/ppermute | solution.py:38
  513.8 5.0 collective-permute-start.27
  515.8 14.8 %collective-permute-start.25 = (bf16[2,64,2048]{2,1,0:T(8,128)(2,1)S(1)}, bf16[2,64,2048]{2,1,0:T(8,128)(2,1)S(1)}, u32[]{:S(2)}, u32[]{:S(2)}) collective-permute-start(bf16[2,64,2048]{2,1,0:T(8,128)(2,1)S(1)} %bitcast.280), channel_id=1, source_target_pairs={{0,2},{2,0},{1,3},{3,1},{4,6},{6,4},{5,7},{7,5},{8,10},{10,8},{9,1... | collective-permute-start | bytes 1572872 | tf_op jit(solution)/shard_map/ppermute | solution.py:38
  517.3 49.9 %collective-permute-start.33 = (bf16[1024,1024]{1,0:T(8,128)(2,1)}, bf16[1024,1024]{1,0:T(8,128)(2,1)}, u32[]{:S(2)}, u32[]{:S(2)}) collective-permute-start(bf16[1024,1024]{1,0:T(8,128)(2,1)} %get-tuple-element.233), channel_id=1, source_target_pairs={{0,4},{4,0},{1,5},{5,1},{2,6},{6,2},{3,7},{7,3},{8,12},{12,8},{9,1... | collective-permute-start | bytes 6291464 | tf_op jit(solution)/shard_map/ppermute | solution.py:724
  520.7 21.4 %collective-permute-start.28 = (bf16[2,64,2176]{2,1,0:T(8,128)(2,1)S(1)}, bf16[2,64,2176]{2,1,0:T(8,128)(2,1)S(1)}, u32[]{:S(2)}, u32[]{:S(2)}) collective-permute-start(bf16[2,64,2176]{2,1,0:T(8,128)(2,1)S(1)} %dynamic-slice_bitcast_fusion.1), channel_id=1, source_target_pairs={{0,2},{2,0},{1,3},{3,1},{4,6},{6,4},{5,7},{7,5},{8,10},{10,8},{9,1... | collective-permute-start | bytes 1671176 | tf_op jit(solution)/shard_map/ppermute | solution.py:38
  531.7 41.5 %collective-permute-start.26 = (bf16[2,2,64,2048]{3,2,1,0:T(8,128)(2,1)}, bf16[2,2,64,2048]{3,2,1,0:T(8,128)(2,1)}, u32[]{:S(2)}, u32[]{:S(2)}) collective-permute-start(bf16[2,2,64,2048]{3,2,1,0:T(8,128)(2,1)} %maximum_select_fusion.5), channel_id=1, source_target_pairs={{0,1},{1,0},{2,3},{3,2},{4,5},{5,4},{6,7},{7,6},{8,9},{9,8},{10,11... | collective-permute-start | bytes 3145736 | tf_op jit(solution)/shard_map/ppermute | solution.py:38
  544.9 31.6 %all-to-all-start.5 = ((f32[8,48,128]{2,1,0:T(8,128)}), f32[8,48,128]{2,1,0:T(8,128)S(1)}, u32[]{:S(2)}, u32[]{:S(2)}) async-start(f32[8,48,128]{2,1,0:T(8,128)} %copy.284), calls=%async_computation.5 | async-start | bytes 393216 | tf_op jit(solution)/shard_map/all_to_all | solution.py:987
  548.5 72.1 %reduce-scatter.6.cloned.1.call-start = ((), (), s32[]{:S(2)}) async-start(), calls=%async_computation.13 | async-start | bytes 2621440 | tf_op jit(solution)/shard_map/reduce_scatter | solution.py:730
  572.4 13.0 %collective-permute-start.29 = (bf16[2,64,2048]{2,1,0:T(8,128)(2,1)S(1)}, bf16[2,64,2048]{2,1,0:T(8,128)(2,1)S(1)}, u32[]{:S(2)}, u32[]{:S(2)}) collective-permute-start(bf16[2,64,2048]{2,1,0:T(8,128)(2,1)S(1)} %bitcast.283), channel_id=1, source_target_pairs={{0,2},{2,0},{1,3},{3,1},{4,6},{6,4},{5,7},{7,5},{8,10},{10,8},{9,1... | collective-permute-start | bytes 1572872 | tf_op jit(solution)/shard_map/ppermute | solution.py:38
  576.5 14.7 %collective-permute-start.31 = (f32[40,128]{1,0:T(8,128)S(1)}, f32[40,128]{1,0:T(8,128)S(1)}, u32[]{:S(2)}, u32[]{:S(2)}) collective-permute-start(f32[40,128]{1,0:T(8,128)S(1)} %slice.640), channel_id=1, source_target_pairs={{0,1},{1,0},{2,3},{3,2},{4,5},{5,4},{6,7},{7,6},{8,9},{9,8},{10,11... | collective-permute-start | bytes 61448 | tf_op jit(solution)/shard_map/ppermute | solution.py:38
  586.7 10.3 %collective-permute-start.30 = (bf16[2,2,64,2048]{3,2,1,0:T(8,128)(2,1)}, bf16[2,2,64,2048]{3,2,1,0:T(8,128)(2,1)}, u32[]{:S(2)}, u32[]{:S(2)}) collective-permute-start(bf16[2,2,64,2048]{3,2,1,0:T(8,128)(2,1)} %copy_select_fusion.1), channel_id=1, source_target_pairs={{0,1},{1,0},{2,3},{3,2},{4,5},{5,4},{6,7},{7,6},{8,9},{9,8},{10,11... | collective-permute-start | bytes 3145736 | tf_op jit(solution)/shard_map/ppermute | solution.py:38
  589.7 26.6 %collective-permute-start.34 = (bf16[256,2112]{0,1:T(8,128)(2,1)}, bf16[256,2112]{0,1:T(8,128)(2,1)}, u32[]{:S(2)}, u32[]{:S(2)}) collective-permute-start(bf16[256,2112]{0,1:T(8,128)(2,1)} %copy.285), channel_id=1, source_target_pairs={{0,4},{4,0},{1,5},{5,1},{2,6},{6,2},{3,7},{7,3},{8,12},{12,8},{9,1... | collective-permute-start | bytes 3244040 | tf_op jit(solution)/shard_map/ppermute | solution.py:38
  591.2 3.8 collective-permute-start.32
  601.2 16.8 %copy-start.1 = (bf16[512,2112]{1,0:T(8,128)(2,1)S(1)}, bf16[512,2112]{1,0:T(8,128)(2,1)}, u32[]{:S(2)}) copy-start(bf16[512,2112]{1,0:T(8,128)(2,1)} %after.11) | copy-start | bytes 6488068
  (90 other events, 298.9 us)
Sparse Core Ops, SparseCore 0:
  10.2 50.7 all-gather.3
  63.1 44.6 all-gather.5
  109.9 180.6 all-gather.7
  340.1 167.0 reduce-scatter.3
  518.9 45.4 reduce-scatter.7
  572.3 42.3 reduce-scatter.5

commit v5 on v4

--- a/solution.py
+++ b/solution.py
@@ -460,20 +460,21 @@
 
 
 def pick_rows(at_ref, in_ref, out_ref):
-    out_ref[...] = in_ref[0]
+    out_ref[:, : in_ref.shape[2]] = in_ref[0]
 
 
 def call_pick(pieces, at):
     _, rows, width = pieces.shape
+    full = width + -width % 128
     return pl.pallas_call(
         pick_rows,
         grid_spec=pltpu.PrefetchScalarGridSpec(
             num_scalar_prefetch=1,
             grid=(1,),
             in_specs=[pl.BlockSpec((1, rows, width), lambda i, at: (at[0], 0, 0))],
-            out_specs=pl.BlockSpec((rows, width), lambda i, at: (0, 0)),
+            out_specs=pl.BlockSpec((rows, full), lambda i, at: (0, 0)),
         ),
-        out_shape=jax.ShapeDtypeStruct((rows, width), pieces.dtype),
+        out_shape=jax.ShapeDtypeStruct((rows, full), pieces.dtype),
         compiler_params=pltpu.CompilerParams(vmem_limit_bytes=16 * 2**20),
         cost_estimate=pl.CostEstimate(flops=0, bytes_accessed=4 * rows * width, transcendentals=0),
         name="pick_rows",
@@ -492,14 +493,14 @@
             value = own_ref[0].astype(f32)
             gate_ref[:, span] = value[:, :units]
             up_ref[:, span] = value[:, units : 2 * units]
-            down_ref[span, :] = value[:, 2 * units :].T
+            down_ref[span, :] = value[:, 2 * units : 3 * units].T
 
         @pl.when(jnp.logical_not(mine))
         def _():
             value = got_ref[...].astype(f32)
             gate_ref[:, span] = value[:, :units]
             up_ref[:, span] = value[:, units : 2 * units]
-            down_ref[span, :] = value[:, 2 * units :].T
+            down_ref[span, :] = value[:, 2 * units : 3 * units].T
 
 
 def call_join_two(pieces, got, at):
@@ -512,7 +513,7 @@
             grid=(1,),
             in_specs=[
                 pl.BlockSpec((1, rows, width), lambda i, at: (at[0], 0, 0)),
-                pl.BlockSpec((rows, width), lambda i, at: (0, 0)),
+                pl.BlockSpec(got.shape, lambda i, at: (0, 0)),
             ],
             out_specs=[
                 pl.BlockSpec((rows, ff), lambda i, at: (0, 0)),
@@ -866,7 +867,8 @@
     r_mid = inv_rms(residual)
     normed_mid = to_absolute((residual * r_mid * gain_mid).astype(bf16))
     mid_near, mid_far = gather_plane(normed_mid.reshape(micro, quarter, depth))
-    pair_far, hidden_far, part_far = call_feed(mid_far, low_far, ff_full, fl)
+    out_grad = to_relative(own_quarter(out_low).reshape(-1, depth)).astype(f32)
+    pair_far, hidden_far, part_far = call_feed(mid_far, low_far, ff_full, fl, out_grad)
     pair_near, hidden_near, part_near = call_feed(mid_near, low_near, ff_full, fl, part_far)
     mid_part = add_low(part_near, swap(part_far, "c"))
     def feed_back():
@@ -885,7 +887,6 @@
     def blocks_back():
         mid_grad = to_relative(scatter_second(mid_a, mid_b, quarter).reshape(-1, depth))
 
-        out_grad = to_relative(own_quarter(out_low).reshape(-1, depth)).astype(f32)
         resid_grad = out_grad + norm_back(residual, r_mid, gain_mid, mid_grad)
         grad_norm_mid = jnp.sum(mid_grad * residual * r_mid, axis=0)
         resid_low = gather_head(resid_grad.astype(bf16).reshape(micro, quarter, depth))

time: 641 us -> 639 us (level)
  waiting for transfers between devices: 257 us -> 247 us
    unnamed x169 -> x163, local copies, waits for them, and re-layouts: 13.3 us -> 11.6 us
  transfers between devices with their start and end apart: 45 -> 45, of which waited for: 27 -> 26; matrix products, arithmetic and copies ran while one was open for 24% -> 24% of each run, Pallas kernels for 8% -> 8%
where the time goes in v5:
time: 639 us; the launch traced here: 628 us
  waiting for transfers between devices  247 us (39%)
  blocking collectives  77.8 us (12%)
  Pallas kernels  64.5 us (10%)
  other arithmetic  63.6 us (10%)
  matrix products  56.6 us (9%)
  starting transfers between devices  52.8 us (8%)
  local copies, waits for them, and re-layouts  48 us (8%)
  between operations  16.7 us (3%)
    ppermute x30, waiting for transfers between devices, swap(): return lax.ppermute(x, axis, [(0, 1), (1, 0)])  118 us
    dot_general x30, matrix products, dot(): return lax.dot_general(a, b, (dims, ((), ())), preferred_element_type=f32)  56.6 us
    all_to_all x1, blocking collectives, spread_states(): got = lax.all_to_all(sent, ctx, 0, 0)  40.6 us
    all_to_all x1, blocking collectives, collect_states(): back = lax.all_to_all(entering, ('z', 'y'), 0, 0)  37.2 us
    all_gather x1, waiting for transfers between devices, per_device(): ff_full = lax.all_gather(ff_unit, 'z', axis=0, tiled=True)  31.6 us
    pallas_call x2, Pallas kernels, call_feed(): pl.pallas_call(functools.partial(feed_kernel, units=units), grid=(rows //...  29.1 us
    all_gather x1, waiting for transfers between devices, per_device(): go_rows = lax.all_gather(w_go, 'z', axis=0, tiled=True)  27.6 us
    all_to_all x1, waiting for transfers between devices, spread_states(): got = lax.all_to_all(sent, ctx, 0, 0)  23.5 us
  transfers between devices with their start and end apart: 45, of which 26 were waited for; matrix products, arithmetic and copies ran while one was open for 24% of the time, Pallas kernels for 8%

profile of v5, /device:TPU:0, one launch (start us, length us, event | category | flops | bytes accessed | tf_op | source)
XLA Modules:
  0.0 627.8 jit_solution(4791281231937663143)
XLA Ops:
  7.3 2.0 pad_maximum_fusion.22
  10.8 2.8 concatenate.225
  14.2 7.3 %all-to-all-start.4 = ((bf16[8,48,128]{2,1,0:T(8,128)(2,1)}), bf16[8,48,128]{2,1,0:T(8,128)(2,1)}, u32[]{:S(2)}, u32[]{:S(2)}) async-start(bf16[8,48,128]{2,1,0:T(8,128)(2,1)} %broadcast_in_dim.9), calls=%async_computation.4 | async-start | bytes 196608 | tf_op jit(solution)/shard_map/all_to_all | solution.py:765
  21.5 2.4 fusion.122
  23.9 2.0 collective-permute-start.20
  35.7 2.3 constant_dynamic-slice_fusion.1
  51.3 9.6 %all-gather.4.cloned.1.call-done = bf16[1024,1024]{1,0:T(8,128)(2,1)} async-done(((bf16[256,1024]{1,0:T(8,128)(2,1)}), bf16[1024,1024]{1,0:T(8,128)(2,1)}) %all-gather.4.cloned.1.call-update) | async-done | bytes 2097168 | tf_op jit(solution)/shard_map/all_gather | solution.py:754
  66.4 7.5 %collective-permute-done.21 = bf16[256,2112]{0,1:T(8,128)(2,1)} collective-permute-done((bf16[256,2112]{0,1:T(8,128)(2,1)}, bf16[256,2112]{0,1:T(8,128)(2,1)}, u32[]{:S(2)}, u32[]{:S(2)}) %collective-permute-start.21) | collective-permute-done | bytes 1081376 | tf_op jit(solution)/shard_map/ppermute | solution.py:38
  73.8 2.3 copy.265
  76.2 3.4 maximum_select_fusion.2
  79.6 27.6 %all-gather.6.cloned.1.call-done = bf16[1024,1024]{1,0:T(8,128)(2,1)} async-done(((bf16[256,1024]{1,0:T(8,128)(2,1)}), bf16[1024,1024]{1,0:T(8,128)(2,1)}) %all-gather.6.cloned.1.call-update) | async-done | bytes 2097168 | tf_op jit(solution)/shard_map/all_gather | solution.py:756
  108.7 2.9 fusion.50
  113.0 5.8 collective-permute-done.12
  118.8 4.0 add_convert_fusion.10
  122.8 83.6 %conditional.3 = (f32[512,512]{1,0:T(8,128)S(1)}, bf16[512,256]{1,0:T(8,128)(2,1)S(1)}, bf16[2,512,256]{2,1,0:T(8,128)(2,1)S(1)}, f32[2,256]{1,0:T(2,128)S(1)}) conditional(s32[]{:T(128)} %bitcast.34, () %tuple.40, (bf16[512,1024]{1,0:T(8,128)(2,1)}, f32[512,256]{1,0:T(8,128)S(1)}, bf16[256,256]{1,0:T(8,128)(2,1)S(1)}, s32[256,256]{1,0:T(8,128)S(1)}, ...), branch_computations={%region_1.2_spmd, %region_2.3_spmd} | conditional | flops 2003206272 | bytes 14699380 | solution.py:56
  122.8 5.1 scan_forward.1
  128.1 40.6 %all_to_all.26.got_ref = bf16[8,144,256]{2,1,0:T(8,128)(2,1)S(1)} all-to-all(bf16[8,144,256]{2,1,0:T(8,128)(2,1)S(1)} %pad_maximum_fusion), channel_id=1, replica_groups=mesh['z'=4,'y'=2,'x'=2,'c'=2] {'z','y'}, dimensions={0} | all-to-all | bytes 1179648 | tf_op jit(solution)/shard_map/cond/branch_1_fun/all_to_all | solution.py:355
  168.9 37.2 %all_to_all.27 = bf16[8,128,256]{2,1,0:T(8,128)(2,1)S(1)} all-to-all(bf16[8,128,256]{2,1,0:T(8,128)(2,1)S(1)} %scan_states.2), channel_id=1, replica_groups=mesh['z'=4,'y'=2,'x'=2,'c'=2] {'z','y'}, dimensions={0} | all-to-all | bytes 1048576 | tf_op jit(solution)/shard_map/cond/branch_1_fun/all_to_all | solution.py:368
  207.9 3.1 multiply_convert_fusion.3
  211.0 2.2 convolution_convert_fusion.9
  220.5 10.8 %collective-permute-done.15 = bf16[2,64,2048]{2,1,0:T(8,128)(2,1)S(1)} collective-permute-done((bf16[2,64,2048]{2,1,0:T(8,128)(2,1)S(1)}, bf16[2,64,2048]{2,1,0:T(8,128)(2,1)S(1)}, u32[]{:S(2)}, u32[]{:S(2)}) %collective-permute-start.15) | collective-permute-done | bytes 524320 | tf_op jit(solution)/shard_map/ppermute | solution.py:38
  235.3 6.0 collective-permute-done.16
  243.4 10.2 %collective-permute-done.17 = bf16[2,64,2048]{2,1,0:T(8,128)(2,1)S(1)} collective-permute-done((bf16[2,64,2048]{2,1,0:T(8,128)(2,1)S(1)}, bf16[2,64,2048]{2,1,0:T(8,128)(2,1)S(1)}, u32[]{:S(2)}, u32[]{:S(2)}) %collective-permute-start.17) | collective-permute-done | bytes 524320 | tf_op jit(solution)/shard_map/ppermute | solution.py:38
  255.4 3.0 collective-permute-done.22.mid_ref
  258.4 31.6 %all-gather.8.cloned.1.call-done.weight_ref = bf16[2048,2112]{1,0:T(8,128)(2,1)} async-done(((bf16[512,2112]{1,0:T(8,128)(2,1)}), bf16[2048,2112]{1,0:T(8,128)(2,1)}) %all-gather.8.cloned.1.call-update) | async-done | bytes 8650768 | tf_op jit(solution)/shard_map/all_gather | solution.py:812
  290.0 14.9 %feed_forward.2 = (bf16[512,1408]{1,0:T(8,128)(2,1)S(1)}, bf16[512,704]{1,0:T(8,128)(2,1)S(1)}, bf16[512,2048]{1,0:T(8,128)(2,1)S(1)}) custom-call(bf16[512,2048]{1,0:T(8,128)(2,1)} %collective-permute-done.22.mid_ref, bf16[512,2048]{1,0:T(8,128)(2,1)} %collective-permute-done.23.low_ref, bf16[2048,2112]{1,0:T(8,128)(2,1)} %all-gather.8.cloned.1.call-done.weight_ref, ...), custom_call_target="tpu_custom_call" | custom-call | flops 7381975040 | bytes 28000000 | tf_op jit(solution)/shard_map/feed_forward/pallas_call | solution.py:388
  305.1 14.2 %feed_forward.3 = (bf16[512,1408]{1,0:T(8,128)(2,1)S(1)}, bf16[512,704]{1,0:T(8,128)(2,1)S(1)}, bf16[512,2048]{1,0:T(8,128)(2,1)S(1)}) custom-call(bf16[512,2048]{1,0:T(8,128)(2,1)S(1)} %bitcast.351, bf16[512,2048]{1,0:T(8,128)(2,1)} %bitcast.76.low_ref, bf16[2048,2112]{1,0:T(8,128)(2,1)} %all-gather.8.cloned.1.call-done.weight_ref, ...), custom_call_target="tpu_custom_call" | custom-call | flops 7381975040 | bytes 28000000 | tf_op jit(solution)/shard_map/feed_forward/pallas_call | solution.py:388
  320.4 17.4 %conditional.4 = (bf16[2048,2112]{1,0:T(8,128)(2,1)}, bf16[128,2048]{1,0:T(8,128)(2,1)S(1)}, bf16[128,2048]{1,0:T(8,128)(2,1)S(1)}) conditional(s32[]{:T(128)} %bitcast.34, () %tuple.43, (bf16[512,2048]{1,0:T(8,128)(2,1)S(1)}, bf16[512,2048]{1,0:T(8,128)(2,1)}, bf16[512,1408]{1,0:T(8,128)(2,1)S(1)}, bf16[512,704]{1,0:T(8,128)(2,1)S(1)}, ...), branch_computations={%region_5.6_spmd, %region_6.7_spmd} | conditional | flops 8860467200 | bytes 30437288 | solution.py:56
  323.4 13.9 %feed_grad.1 = bf16[2048,2112]{1,0:T(8,128)(2,1)} custom-call(bf16[512,2048]{1,0:T(8,128)(2,1)S(1)} %get-tuple-element.121.refs_0_, bf16[512,2048]{1,0:T(8,128)(2,1)} %get-tuple-element.122.refs_1_, bf16[512,1408]{1,0:T(8,128)(2,1)S(1)} %get-tuple-element.123.refs_2_, bf16[512,704]{1,0:T(8,128)(2,1)S(1)} %get-tuple-element.124.refs_3_, ...), custom_call_target="tpu_custom_call" | custom-call | flops 8858370048 | bytes 21000000 | tf_op jit(solution)/shard_map/cond/branch_1_fun/feed_grad/pallas_call | solution.py:576
  342.6 2.0 copy.279
  345.2 165.2 %conditional.5 = (f32[128,2048]{1,0:T(8,128)}, bf16[1024,1024]{1,0:T(8,128)(2,1)}, bf16[1024,1024]{1,0:T(8,128)(2,1)}, bf16[512,256]{1,0:T(8,128)(2,1)S(1)}, f32...) conditional(s32[]{:T(128)} %bitcast.34, () %tuple.42, ...), branch_computations={%region_7.8_spmd, %region_8.13_spmd} | conditional | flops 16742942720 | bytes 293536000 | solution.py:56
  348.1 6.2 collective-permute-done.2
  359.6 12.1 %collective-permute-done.4 = bf16[2,64,2048]{2,1,0:T(8,128)(2,1)S(1)} collective-permute-done((bf16[2,64,2048]{2,1,0:T(8,128)(2,1)S(1)}, bf16[2,64,2048]{2,1,0:T(8,128)(2,1)S(1)}, u32[]{:S(2)}, u32[]{:S(2)}) %collective-permute-start.4) | collective-permute-done | bytes 524320 | tf_op jit(solution)/shard_map/cond/branch_1_fun/ppermute | solution.py:38
  373.4 2.3 collective-permute-done.5
  376.1 2.9 fusion.10
  382.7 3.5 all-to-all-start.2
  388.0 5.2 convolution_convert_fusion
  395.1 23.5 %all-to-all-done.2.got_ref = bf16[8,144,256]{2,1,0:T(8,128)(2,1)S(1)} async-done(((bf16[8,144,256]{2,1,0:T(8,128)(2,1)}), bf16[8,144,256]{2,1,0:T(8,128)(2,1)S(1)}, u32[]{:S(2)}, u32[]{:S(2)}) %all-to-all-start.2) | async-done | bytes 589856 | tf_op jit(solution)/shard_map/cond/branch_1_fun/all_to_all | solution.py:355
  419.5 5.7 all-to-all-start.3
  425.2 2.2 fusion.7
  433.4 2.0 collective-permute-start.6
  435.4 17.3 %all-to-all-done.3 = bf16[8,128,256]{2,1,0:T(8,128)(2,1)S(1)} async-done(((bf16[8,128,256]{2,1,0:T(8,128)(2,1)}), bf16[8,128,256]{2,1,0:T(8,128)(2,1)S(1)}, u32[]{:S(2)}, u32[]{:S(2)}) %all-to-all-start.3) | async-done | bytes 524320 | tf_op jit(solution)/shard_map/cond/branch_1_fun/all_to_all | solution.py:368
  452.9 9.2 %scan_backward.1 = (bf16[512,1024]{1,0:T(8,128)(2,1)S(1)}, f32[512,256]{1,0:T(8,128)S(1)}) custom-call(bf16[512,1024]{1,0:T(8,128)(2,1)} %get-tuple-element.146.qkv_ref, f32[512,256]{1,0:T(8,128)} %get-tuple-element.147.decay_ref, f32[512,256]{1,0:T(8,128)} %get-tuple-element.148.logit_ref, bf16[512,512]{1,0:T(8,128)(2,1)S(1)} %copy-done.5, ...), custom_call_target="tpu_custom_call" | custom-call | flops 5000000000 | bytes 12000000 | tf_op jit(solution)/shard_map/cond/branch_1_fun/scan_backward/pallas_call | solution.py:294
  463.1 4.0 convert_bitcast_fusion.1.refs_2_
  467.1 4.0 fusion.84
  471.2 3.3 fusion.92
  475.9 4.4 add_convert_fusion.2
  483.4 2.0 add_convert_fusion.4
  486.2 8.2 %collective-permute-done.8 = bf16[128,2048]{1,0:T(8,128)(2,1)S(1)} collective-permute-done((bf16[128,2048]{1,0:T(8,128)(2,1)S(1)}, bf16[128,2048]{1,0:T(8,128)(2,1)S(1)}, u32[]{:S(2)}, u32[]{:S(2)}) %collective-permute-start.8) | collective-permute-done | bytes 524320 | tf_op jit(solution)/shard_map/cond/branch_1_fun/ppermute | solution.py:38
  499.7 3.6 collective-permute-done.11
  503.4 1.9 collective-permute-done.9
  506.4 3.7 add_convert_fusion.3
  520.5 9.2 %collective-permute-done.25 = bf16[2,64,2048]{2,1,0:T(8,128)(2,1)S(1)} collective-permute-done((bf16[2,64,2048]{2,1,0:T(8,128)(2,1)S(1)}, bf16[2,64,2048]{2,1,0:T(8,128)(2,1)S(1)}, u32[]{:S(2)}, u32[]{:S(2)}) %collective-permute-start.25) | collective-permute-done | bytes 524320 | tf_op jit(solution)/shard_map/ppermute | solution.py:38
  531.1 10.2 %collective-permute-done.28 = bf16[2,64,2176]{2,1,0:T(8,128)(2,1)S(1)} collective-permute-done((bf16[2,64,2176]{2,1,0:T(8,128)(2,1)S(1)}, bf16[2,64,2176]{2,1,0:T(8,128)(2,1)S(1)}, u32[]{:S(2)}, u32[]{:S(2)}) %collective-permute-start.28) | collective-permute-done | bytes 557088 | tf_op jit(solution)/shard_map/ppermute | solution.py:38
  545.4 5.4 all-to-all-start.5
  550.9 2.0 fusion.39
  553.0 13.4 %collective-permute-done.33 = bf16[1024,1024]{1,0:T(8,128)(2,1)} collective-permute-done((bf16[1024,1024]{1,0:T(8,128)(2,1)}, bf16[1024,1024]{1,0:T(8,128)(2,1)}, u32[]{:S(2)}, u32[]{:S(2)}) %collective-permute-start.33) | collective-permute-done | bytes 2097184 | tf_op jit(solution)/shard_map/ppermute | solution.py:725
  566.3 5.0 add_convert_fusion.8.refs_0_
  575.8 8.8 %collective-permute-done.29 = bf16[2,64,2048]{2,1,0:T(8,128)(2,1)S(1)} collective-permute-done((bf16[2,64,2048]{2,1,0:T(8,128)(2,1)S(1)}, bf16[2,64,2048]{2,1,0:T(8,128)(2,1)S(1)}, u32[]{:S(2)}, u32[]{:S(2)}) %collective-permute-start.29) | collective-permute-done | bytes 524320 | tf_op jit(solution)/shard_map/ppermute | solution.py:38
  591.9 2.0 collective-permute-done.32
  595.8 1.9 fusion.31
  597.8 2.3 copy.278
  602.2 13.6 %collective-permute-done.34.got_ref = bf16[256,2176]{1,0:T(8,128)(2,1)S(1)} collective-permute-done((bf16[256,2176]{1,0:T(8,128)(2,1)}, bf16[256,2176]{1,0:T(8,128)(2,1)S(1)}, u32[]{:S(2)}, u32[]{:S(2)}) %collective-permute-start.34) | collective-permute-done | bytes 1114144 | tf_op jit(solution)/shard_map/ppermute | solution.py:38
  615.8 2.6 join_two.1
  (515 shorter events, 129.5 us)
Async XLA Ops:
  7.2 18.7 %copy-start.8 = (bf16[1408,256]{1,0:T(8,128)(2,1)S(1)}, bf16[1408,256]{1,0:T(8,128)(2,1)}, u32[]{:S(2)}) copy-start(bf16[1408,256]{1,0:T(8,128)(2,1)} %down_ref.1) | copy-start | bytes 2162692
  7.2 18.7 %copy-start.7 = (bf16[256,1408]{1,0:T(8,128)(2,1)S(1)}, bf16[256,1408]{1,0:T(8,128)(2,1)}, u32[]{:S(2)}) copy-start(bf16[256,1408]{1,0:T(8,128)(2,1)} %up_ref.1) | copy-start | bytes 2162692
  7.2 18.7 %copy-start.6 = (bf16[256,1408]{1,0:T(8,128)(2,1)S(1)}, bf16[256,1408]{1,0:T(8,128)(2,1)}, u32[]{:S(2)}) copy-start(bf16[256,1408]{1,0:T(8,128)(2,1)} %gate_ref.1) | copy-start | bytes 2162692
  7.2 53.7 %all-gather.4.cloned.1.call-start = ((), (), s32[]{:S(2)}) async-start(), calls=%async_computation.9 | async-start | bytes 2621440 | tf_op jit(solution)/shard_map/all_gather | solution.py:754
  14.2 33.2 %all-to-all-start.4 = ((bf16[8,48,128]{2,1,0:T(8,128)(2,1)}), bf16[8,48,128]{2,1,0:T(8,128)(2,1)}, u32[]{:S(2)}, u32[]{:S(2)}) async-start(bf16[8,48,128]{2,1,0:T(8,128)(2,1)} %broadcast_in_dim.9), calls=%async_computation.4 | async-start | bytes 196608 | tf_op jit(solution)/shard_map/all_to_all | solution.py:765
  21.5 85.7 %all-gather.6.cloned.1.call-start = ((), (), s32[]{:S(2)}) async-start(), calls=%async_computation.10 | async-start | bytes 2621440 | tf_op jit(solution)/shard_map/all_gather | solution.py:756
  23.9 190.2 %collective-permute-start.20 = (bf16[2,128,2048]{2,1,0:T(8,128)(2,1)}, bf16[2,128,2048]{2,1,0:T(8,128)(2,1)}, u32[]{:S(2)}, u32[]{:S(2)}) collective-permute-start(bf16[2,128,2048]{2,1,0:T(8,128)(2,1)} %fusion.122), channel_id=1, source_target_pairs={{4,0},{0,4},{5,1},{1,5},{6,2},{2,6},{7,3},{3,7},{12,8},{8,12},{13,... | collective-permute-start | bytes 3145736 | tf_op jit(solution)/shard_map/ppermute | solution.py:668
  28.9 44.9 %collective-permute-start.21 = (bf16[256,2112]{0,1:T(8,128)(2,1)}, bf16[256,2112]{0,1:T(8,128)(2,1)}, u32[]{:S(2)}, u32[]{:S(2)}) collective-permute-start(bf16[256,2112]{0,1:T(8,128)(2,1)} %bitcast.317), channel_id=1, source_target_pairs={{0,4},{4,0},{1,5},{5,1},{2,6},{6,2},{3,7},{7,3},{8,12},{12,8},{9,1... | collective-permute-start | bytes 3244040 | tf_op jit(solution)/shard_map/ppermute | solution.py:38
  31.0 259.1 %all-gather.8.cloned.1.call-start = ((), (), s32[]{:S(2)}) async-start(), calls=%async_computation.11 | async-start | bytes 11141120 | tf_op jit(solution)/shard_map/all_gather | solution.py:812
  51.3 12.9 %copy-start.75 = (bf16[16,2048]{1,0:T(8,128)(2,1)}, bf16[16,2048]{1,0:T(8,128)(2,1)S(1)}, u32[]{:S(2)}) copy-start(bf16[16,2048]{1,0:T(8,128)(2,1)S(1)} %slice.476) | copy-start | bytes 196612
  60.9 57.8 %collective-permute-start.12 = (bf16[1024,1024]{1,0:T(8,128)(2,1)}, bf16[1024,1024]{1,0:T(8,128)(2,1)}, u32[]{:S(2)}, u32[]{:S(2)}) collective-permute-start(bf16[1024,1024]{1,0:T(8,128)(2,1)} %all-gather.4.cloned.1.call-done), channel_id=1, source_target_pairs={{4,0},{0,4},{5,1},{1,5},{6,2},{2,6},{7,3},{3,7},{12,8},{8,12},{13,... | collective-permute-start | bytes 6291464 | tf_op jit(solution)/shard_map/ppermute | solution.py:668
  64.2 143.1 %copy-start.12 = (bf16[512,2048]{1,0:T(8,128)(2,1)}, bf16[512,2048]{1,0:T(8,128)(2,1)S(1)}, u32[]{:S(2)}) copy-start(bf16[512,2048]{1,0:T(8,128)(2,1)S(1)} %fusion.29) | copy-start | bytes 6291460
  64.9 14.6 %copy-start.78 = (bf16[512,16]{0,1:T(8,128)(2,1)}, bf16[512,16]{0,1:T(8,128)(2,1)S(1)}, u32[]{:S(2)}) copy-start(bf16[512,16]{0,1:T(8,128)(2,1)S(1)} %convolution_convert_fusion.11) | copy-start | bytes 49156
  79.6 491.8 %reduce-scatter.4.cloned.1.call-start = ((), (), s32[]{:S(2)}) async-start(), calls=%async_computation.12 | async-start | bytes 11141120 | tf_op jit(solution)/shard_map/reduce_scatter | solution.py:731
  107.2 100.0 %collective-permute-start.13 = (bf16[1024,1024]{1,0:T(8,128)(2,1)}, bf16[1024,1024]{1,0:T(8,128)(2,1)}, u32[]{:S(2)}, u32[]{:S(2)}) collective-permute-start(bf16[1024,1024]{1,0:T(8,128)(2,1)} %all-gather.6.cloned.1.call-done), channel_id=1, source_target_pairs={{4,0},{0,4},{5,1},{1,5},{6,2},{2,6},{7,3},{3,7},{12,8},{8,12},{13,... | collective-permute-start | bytes 6291464 | tf_op jit(solution)/shard_map/ppermute | solution.py:668
  214.1 2.7 collective-permute-start.14
  217.3 14.0 %collective-permute-start.15 = (bf16[2,64,2048]{2,1,0:T(8,128)(2,1)S(1)}, bf16[2,64,2048]{2,1,0:T(8,128)(2,1)S(1)}, u32[]{:S(2)}, u32[]{:S(2)}) collective-permute-start(bf16[2,64,2048]{2,1,0:T(8,128)(2,1)S(1)} %dynamic-slice_bitcast_fusion.2), channel_id=1, source_target_pairs={{0,2},{2,0},{1,3},{3,1},{4,6},{6,4},{5,7},{7,5},{8,10},{10,8},{9,1... | collective-permute-start | bytes 1572872 | tf_op jit(solution)/shard_map/ppermute | solution.py:38
  219.0 12.3 %copy-start.59 = (bf16[2,64,1024]{2,1,0:T(8,128)(2,1)S(1)}, bf16[2,64,1024]{2,1,0:T(8,128)(2,1)}, u32[]{:S(2)}) copy-start(bf16[2,64,1024]{2,1,0:T(8,128)(2,1)} %get-tuple-element.521) | copy-start | bytes 786436
  219.0 12.3 %copy-start.60 = (bf16[2,64,1024]{2,1,0:T(8,128)(2,1)S(1)}, bf16[2,64,1024]{2,1,0:T(8,128)(2,1)}, u32[]{:S(2)}) copy-start(bf16[2,64,1024]{2,1,0:T(8,128)(2,1)} %get-tuple-element.522) | copy-start | bytes 786436
  220.5 11.3 %copy-start.35 = (bf16[128,1024]{1,0:T(8,128)(2,1)S(1)}, bf16[128,1024]{1,0:T(8,128)(2,1)}, u32[]{:S(2)}) copy-start(bf16[128,1024]{1,0:T(8,128)(2,1)} %get-tuple-element.519) | copy-start | bytes 786436
  220.5 11.3 %copy-start.37 = (bf16[128,1024]{1,0:T(8,128)(2,1)S(1)}, bf16[128,1024]{1,0:T(8,128)(2,1)}, u32[]{:S(2)}) copy-start(bf16[128,1024]{1,0:T(8,128)(2,1)} %get-tuple-element.520) | copy-start | bytes 786436
  220.5 34.8 %collective-permute-start.23 = (bf16[512,2048]{1,0:T(8,128)(2,1)}, bf16[512,2048]{1,0:T(8,128)(2,1)}, u32[]{:S(2)}, u32[]{:S(2)}) collective-permute-start(bf16[512,2048]{1,0:T(8,128)(2,1)} %bitcast.76.low_ref), channel_id=1, source_target_pairs={{0,1},{1,0},{2,3},{3,2},{4,5},{5,4},{6,7},{7,6},{8,9},{9,8},{10,11... | collective-permute-start | bytes 6291464 | tf_op jit(solution)/shard_map/ppermute | solution.py:38
  232.4 9.6 %collective-permute-start.18 = (bf16[64,2048]{1,0:T(8,128)(2,1)S(1)}, bf16[64,2048]{1,0:T(8,128)(2,1)S(1)}, u32[]{:S(2)}, u32[]{:S(2)}) collective-permute-start(bf16[64,2048]{1,0:T(8,128)(2,1)S(1)} %get-tuple-element.517), channel_id=1, source_target_pairs={{0,2},{2,0},{1,3},{3,1},{4,6},{6,4},{5,7},{7,5},{8,10},{10,8},{9,1... | collective-permute-start | bytes 786440 | tf_op jit(solution)/shard_map/ppermute | solution.py:38
  234.0 7.3 %collective-permute-start.16 = (bf16[64,2048]{1,0:T(8,128)(2,1)S(1)}, bf16[64,2048]{1,0:T(8,128)(2,1)S(1)}, u32[]{:S(2)}, u32[]{:S(2)}) collective-permute-start(bf16[64,2048]{1,0:T(8,128)(2,1)S(1)} %get-tuple-element.518), channel_id=1, source_target_pairs={{0,4},{4,0},{1,5},{5,1},{2,6},{6,2},{3,7},{7,3},{8,12},{12,8},{9,1... | collective-permute-start | bytes 786440 | tf_op jit(solution)/shard_map/ppermute | solution.py:38
  241.4 12.2 %collective-permute-start.17 = (bf16[2,64,2048]{2,1,0:T(8,128)(2,1)S(1)}, bf16[2,64,2048]{2,1,0:T(8,128)(2,1)S(1)}, u32[]{:S(2)}, u32[]{:S(2)}) collective-permute-start(bf16[2,64,2048]{2,1,0:T(8,128)(2,1)S(1)} %pad_maximum_fusion.24), channel_id=1, source_target_pairs={{0,2},{2,0},{1,3},{3,1},{4,6},{6,4},{5,7},{7,5},{8,10},{10,8},{9,1... | collective-permute-start | bytes 1572872 | tf_op jit(solution)/shard_map/ppermute | solution.py:38
  242.0 12.1 %copy-start.39 = (bf16[2,1,64,2048]{3,2,1,0:T(8,128)(2,1)S(1)}, bf16[2,1,64,2048]{3,2,1,0:T(8,128)(2,1)}, u32[]{:S(2)}) copy-start(bf16[2,1,64,2048]{3,2,1,0:T(8,128)(2,1)} %get-tuple-element.547) | copy-start | bytes 1572868
  242.1 11.9 %collective-permute-start.19 = (bf16[2,64,2048]{2,1,0:T(8,128)(2,1)S(1)}, bf16[2,64,2048]{2,1,0:T(8,128)(2,1)S(1)}, u32[]{:S(2)}, u32[]{:S(2)}) collective-permute-start(bf16[2,64,2048]{2,1,0:T(8,128)(2,1)S(1)} %pad_maximum_fusion.25), channel_id=1, source_target_pairs={{0,4},{4,0},{1,5},{5,1},{2,6},{6,2},{3,7},{7,3},{8,12},{12,8},{9,1... | collective-permute-start | bytes 1572872 | tf_op jit(solution)/shard_map/ppermute | solution.py:38
  254.0 4.4 collective-permute-start.22
  290.0 15.0 %copy-start.83 = (bf16[8,64,2048]{2,1,0:T(8,128)(2,1)S(1)}, bf16[8,64,2048]{2,1,0:T(8,128)(2,1)}, u32[]{:S(2)}) copy-start(bf16[8,64,2048]{2,1,0:T(8,128)(2,1)} %copy-done.82) | copy-start | bytes 6291460
  305.0 15.2 %copy-start.61 = (bf16[512,704]{1,0:T(8,128)(2,1)}, bf16[512,704]{1,0:T(8,128)(2,1)S(1)}, u32[]{:S(2)}) copy-start(bf16[512,704]{1,0:T(8,128)(2,1)S(1)} %get-tuple-element.215) | copy-start | bytes 2162692
  305.0 14.3 %collective-permute-start.24 = (bf16[512,2048]{1,0:T(8,128)(2,1)S(1)}, bf16[512,2048]{1,0:T(8,128)(2,1)S(1)}, u32[]{:S(2)}, u32[]{:S(2)}) collective-permute-start(bf16[512,2048]{1,0:T(8,128)(2,1)S(1)} %get-tuple-element.211.rest_0_), channel_id=1, source_target_pairs={{0,1},{1,0},{2,3},{3,2},{4,5},{5,4},{6,7},{7,6},{8,9},{9,8},{10,11... | collective-permute-start | bytes 6291464 | tf_op jit(solution)/shard_map/ppermute | solution.py:38
  320.5 16.9 %collective-permute-start.1 = (bf16[128,2048]{1,0:T(8,128)(2,1)S(1)}, bf16[128,2048]{1,0:T(8,128)(2,1)S(1)}, u32[]{:S(2)}, u32[]{:S(2)}) collective-permute-start(bf16[128,2048]{1,0:T(8,128)(2,1)S(1)} %get-tuple-element.445), channel_id=1, source_target_pairs={{0,4},{4,0},{1,5},{5,1},{2,6},{6,2},{3,7},{7,3},{8,12},{12,8},{9,1... | collective-permute-start | bytes 1572872 | tf_op jit(solution)/shard_map/cond/branch_1_fun/ppermute | solution.py:38
  322.0 15.4 %collective-permute-start = (bf16[128,2048]{1,0:T(8,128)(2,1)S(1)}, bf16[128,2048]{1,0:T(8,128)(2,1)S(1)}, u32[]{:S(2)}, u32[]{:S(2)}) collective-permute-start(bf16[128,2048]{1,0:T(8,128)(2,1)S(1)} %get-tuple-element.446), channel_id=1, source_target_pairs={{0,2},{2,0},{1,3},{3,1},{4,6},{6,4},{5,7},{7,5},{8,10},{10,8},{9,1... | collective-permute-start | bytes 1572872 | tf_op jit(solution)/shard_map/cond/branch_1_fun/ppermute | solution.py:38
  338.8 261.3 %reduce-scatter.8.cloned.1.call-start = ((), (), s32[]{:S(2)}) async-start(), calls=%async_computation.14 | async-start | bytes 2621440 | tf_op jit(solution)/shard_map/reduce_scatter | solution.py:731
  345.9 8.4 %collective-permute-start.2 = (bf16[64,2048]{1,0:T(8,128)(2,1)}, bf16[64,2048]{1,0:T(8,128)(2,1)}, u32[]{:S(2)}, u32[]{:S(2)}) collective-permute-start(bf16[64,2048]{1,0:T(8,128)(2,1)} %slice.325), channel_id=1, source_target_pairs={{0,4},{4,0},{1,5},{5,1},{2,6},{6,2},{3,7},{7,3},{8,12},{12,8},{9,1... | collective-permute-start | bytes 786440 | tf_op jit(solution)/shard_map/cond/branch_1_fun/ppermute | solution.py:38
  346.6 8.7 %collective-permute-start.3 = (bf16[64,2048]{1,0:T(8,128)(2,1)S(1)}, bf16[64,2048]{1,0:T(8,128)(2,1)}, u32[]{:S(2)}, u32[]{:S(2)}) collective-permute-start(bf16[64,2048]{1,0:T(8,128)(2,1)S(1)} %slice.327), channel_id=1, source_target_pairs={{0,2},{2,0},{1,3},{3,1},{4,6},{6,4},{5,7},{7,5},{8,10},{10,8},{9,1... | collective-permute-start | bytes 786440 | tf_op jit(solution)/shard_map/cond/branch_1_fun/ppermute | solution.py:38
  358.9 14.0 %copy-start.88 = (bf16[8,64]{1,0:T(8,128)(2,1)S(1)}, bf16[8,64]{1,0:T(8,128)(2,1)}, u32[]{:S(2)}) copy-start(bf16[8,64]{1,0:T(8,128)(2,1)} %get-tuple-element.140) | copy-start | bytes 3076 | tf_op jit(solution)/shard_map/cond
  358.9 12.8 %collective-permute-start.4 = (bf16[2,64,2048]{2,1,0:T(8,128)(2,1)S(1)}, bf16[2,64,2048]{2,1,0:T(8,128)(2,1)S(1)}, u32[]{:S(2)}, u32[]{:S(2)}) collective-permute-start(bf16[2,64,2048]{2,1,0:T(8,128)(2,1)S(1)} %bitcast.262), channel_id=1, source_target_pairs={{0,2},{2,0},{1,3},{3,1},{4,6},{6,4},{5,7},{7,5},{8,10},{10,8},{9,1... | collective-permute-start | bytes 1572872 | tf_op jit(solution)/shard_map/cond/branch_1_fun/ppermute | solution.py:38
  372.9 2.9 collective-permute-start.5
  382.7 35.9 %all-to-all-start.2 = ((bf16[8,144,256]{2,1,0:T(8,128)(2,1)}), bf16[8,144,256]{2,1,0:T(8,128)(2,1)S(1)}, u32[]{:S(2)}, u32[]{:S(2)}) async-start(bf16[8,144,256]{2,1,0:T(8,128)(2,1)} %pad_maximum_fusion.7), calls=%async_computation.2 | async-start | bytes 1179648 | tf_op jit(solution)/shard_map/cond/branch_1_fun/all_to_all | solution.py:355
  393.2 82.6 %collective-permute-start.7 = (bf16[512,2048]{1,0:T(8,128)(2,1)}, bf16[512,2048]{1,0:T(8,128)(2,1)}, u32[]{:S(2)}, u32[]{:S(2)}) collective-permute-start(bf16[512,2048]{1,0:T(8,128)(2,1)} %convolution_convert_fusion), channel_id=1, source_target_pairs={{0,1},{1,0},{2,3},{3,2},{4,5},{5,4},{6,7},{7,6},{8,9},{9,8},{10,11... | collective-permute-start | bytes 6291464 | tf_op jit(solution)/shard_map/cond/branch_1_fun/ppermute | solution.py:38
  419.5 33.2 %all-to-all-start.3 = ((bf16[8,128,256]{2,1,0:T(8,128)(2,1)}), bf16[8,128,256]{2,1,0:T(8,128)(2,1)S(1)}, u32[]{:S(2)}, u32[]{:S(2)}) async-start(bf16[8,128,256]{2,1,0:T(8,128)(2,1)} %scan_states.3.refs_1_), calls=%async_computation.3 | async-start | bytes 1048576 | tf_op jit(solution)/shard_map/cond/branch_1_fun/all_to_all | solution.py:368
  433.4 19.4 %copy-start.5 = (bf16[512,512]{1,0:T(8,128)(2,1)S(1)}, bf16[512,512]{1,0:T(8,128)(2,1)}, u32[]{:S(2)}) copy-start(bf16[512,512]{1,0:T(8,128)(2,1)} %copy-done.4) | copy-start | bytes 1572868 | tf_op jit(solution)/shard_map/cond
  433.4 19.4 %copy-start.11 = (bf16[256,256]{1,0:T(8,128)(2,1)S(1)}, bf16[256,256]{1,0:T(8,128)(2,1)}, u32[]{:S(2)}) copy-start(bf16[256,256]{1,0:T(8,128)(2,1)} %constant.170.clone.1.upper_ref) | copy-start | bytes 393220 | tf_op jit(solution)/shard_map/cond
  433.4 19.4 %copy-start.93 = (f32[2,4]{1,0:T(2,128)S(1)}, f32[2,4]{1,0:T(2,128)}, u32[]{:S(2)}) copy-start(f32[2,4]{1,0:T(2,128)} %get-tuple-element.153.open_ref) | copy-start | bytes 100 | tf_op jit(solution)/shard_map/cond
  433.4 19.4 %copy-start.103 = (bf16[256,256]{1,0:T(8,128)(2,1)S(1)}, bf16[256,256]{1,0:T(8,128)(2,1)}, u32[]{:S(2)}) copy-start(bf16[256,256]{1,0:T(8,128)(2,1)} %get-tuple-element.150.lower_ref) | copy-start | bytes 393220 | tf_op jit(solution)/shard_map/cond
  433.4 73.0 %collective-permute-start.6 = (bf16[1024,1024]{1,0:T(8,128)(2,1)}, bf16[1024,1024]{1,0:T(8,128)(2,1)}, u32[]{:S(2)}, u32[]{:S(2)}) collective-permute-start(bf16[1024,1024]{1,0:T(8,128)(2,1)} %after.6), channel_id=1, source_target_pairs={{0,4},{4,0},{1,5},{5,1},{2,6},{6,2},{3,7},{7,3},{8,12},{12,8},{9,1... | collective-permute-start | bytes 6291464 | tf_op jit(solution)/shard_map/cond/branch_1_fun/ppermute | solution.py:725
  480.4 14.0 %collective-permute-start.8 = (bf16[128,2048]{1,0:T(8,128)(2,1)S(1)}, bf16[128,2048]{1,0:T(8,128)(2,1)S(1)}, u32[]{:S(2)}, u32[]{:S(2)}) collective-permute-start(bf16[128,2048]{1,0:T(8,128)(2,1)S(1)} %get-tuple-element.451), channel_id=1, source_target_pairs={{0,2},{2,0},{1,3},{3,1},{4,6},{6,4},{5,7},{7,5},{8,10},{10,8},{9,1... | collective-permute-start | bytes 1572872 | tf_op jit(solution)/shard_map/cond/branch_1_fun/ppermute | solution.py:38
  481.9 13.7 %collective-permute-start.10 = (bf16[128,2048]{1,0:T(8,128)(2,1)S(1)}, bf16[128,2048]{1,0:T(8,128)(2,1)S(1)}, u32[]{:S(2)}, u32[]{:S(2)}) collective-permute-start(bf16[128,2048]{1,0:T(8,128)(2,1)S(1)} %get-tuple-element.452), channel_id=1, source_target_pairs={{0,4},{4,0},{1,5},{5,1},{2,6},{6,2},{3,7},{7,3},{8,12},{12,8},{9,1... | collective-permute-start | bytes 1572872 | tf_op jit(solution)/shard_map/cond/branch_1_fun/ppermute | solution.py:38
  496.0 7.3 %collective-permute-start.11 = (bf16[64,2048]{1,0:T(8,128)(2,1)S(1)}, bf16[64,2048]{1,0:T(8,128)(2,1)S(1)}, u32[]{:S(2)}, u32[]{:S(2)}) collective-permute-start(bf16[64,2048]{1,0:T(8,128)(2,1)S(1)} %slice.570), channel_id=1, source_target_pairs={{0,2},{2,0},{1,3},{3,1},{4,6},{6,4},{5,7},{7,5},{8,10},{10,8},{9,1... | collective-permute-start | bytes 786440 | tf_op jit(solution)/shard_map/cond/branch_1_fun/ppermute | solution.py:38
  498.2 7.1 %collective-permute-start.9 = (bf16[64,2048]{1,0:T(8,128)(2,1)S(1)}, bf16[64,2048]{1,0:T(8,128)(2,1)S(1)}, u32[]{:S(2)}, u32[]{:S(2)}) collective-permute-start(bf16[64,2048]{1,0:T(8,128)(2,1)S(1)} %slice.566), channel_id=1, source_target_pairs={{0,4},{4,0},{1,5},{5,1},{2,6},{6,2},{3,7},{7,3},{8,12},{12,8},{9,1... | collective-permute-start | bytes 786440 | tf_op jit(solution)/shard_map/cond/branch_1_fun/ppermute | solution.py:38
  513.0 5.0 collective-permute-start.27
  514.9 14.8 %collective-permute-start.25 = (bf16[2,64,2048]{2,1,0:T(8,128)(2,1)S(1)}, bf16[2,64,2048]{2,1,0:T(8,128)(2,1)S(1)}, u32[]{:S(2)}, u32[]{:S(2)}) collective-permute-start(bf16[2,64,2048]{2,1,0:T(8,128)(2,1)S(1)} %bitcast.281), channel_id=1, source_target_pairs={{0,2},{2,0},{1,3},{3,1},{4,6},{6,4},{5,7},{7,5},{8,10},{10,8},{9,1... | collective-permute-start | bytes 1572872 | tf_op jit(solution)/shard_map/ppermute | solution.py:38
  516.4 49.9 %collective-permute-start.33 = (bf16[1024,1024]{1,0:T(8,128)(2,1)}, bf16[1024,1024]{1,0:T(8,128)(2,1)}, u32[]{:S(2)}, u32[]{:S(2)}) collective-permute-start(bf16[1024,1024]{1,0:T(8,128)(2,1)} %get-tuple-element.227), channel_id=1, source_target_pairs={{0,4},{4,0},{1,5},{5,1},{2,6},{6,2},{3,7},{7,3},{8,12},{12,8},{9,1... | collective-permute-start | bytes 6291464 | tf_op jit(solution)/shard_map/ppermute | solution.py:725
  519.9 21.4 %collective-permute-start.28 = (bf16[2,64,2176]{2,1,0:T(8,128)(2,1)S(1)}, bf16[2,64,2176]{2,1,0:T(8,128)(2,1)S(1)}, u32[]{:S(2)}, u32[]{:S(2)}) collective-permute-start(bf16[2,64,2176]{2,1,0:T(8,128)(2,1)S(1)} %dynamic-slice_bitcast_fusion.1), channel_id=1, source_target_pairs={{0,2},{2,0},{1,3},{3,1},{4,6},{6,4},{5,7},{7,5},{8,10},{10,8},{9,1... | collective-permute-start | bytes 1671176 | tf_op jit(solution)/shard_map/ppermute | solution.py:38
  530.8 41.5 %collective-permute-start.26 = (bf16[2,2,64,2048]{3,2,1,0:T(8,128)(2,1)}, bf16[2,2,64,2048]{3,2,1,0:T(8,128)(2,1)}, u32[]{:S(2)}, u32[]{:S(2)}) collective-permute-start(bf16[2,2,64,2048]{3,2,1,0:T(8,128)(2,1)} %maximum_select_fusion.5), channel_id=1, source_target_pairs={{0,1},{1,0},{2,3},{3,2},{4,5},{5,4},{6,7},{7,6},{8,9},{9,8},{10,11... | collective-permute-start | bytes 3145736 | tf_op jit(solution)/shard_map/ppermute | solution.py:38
  545.4 30.3 %all-to-all-start.5 = ((f32[8,48,128]{2,1,0:T(8,128)}), f32[8,48,128]{2,1,0:T(8,128)S(1)}, u32[]{:S(2)}, u32[]{:S(2)}) async-start(f32[8,48,128]{2,1,0:T(8,128)} %copy.284), calls=%async_computation.5 | async-start | bytes 393216 | tf_op jit(solution)/shard_map/all_to_all | solution.py:988
  550.8 67.6 %reduce-scatter.6.cloned.1.call-start = ((), (), s32[]{:S(2)}) async-start(), calls=%async_computation.13 | async-start | bytes 2621440 | tf_op jit(solution)/shard_map/reduce_scatter | solution.py:731
  571.5 13.0 %collective-permute-start.29 = (bf16[2,64,2048]{2,1,0:T(8,128)(2,1)S(1)}, bf16[2,64,2048]{2,1,0:T(8,128)(2,1)S(1)}, u32[]{:S(2)}, u32[]{:S(2)}) collective-permute-start(bf16[2,64,2048]{2,1,0:T(8,128)(2,1)S(1)} %bitcast.284), channel_id=1, source_target_pairs={{0,2},{2,0},{1,3},{3,1},{4,6},{6,4},{5,7},{7,5},{8,10},{10,8},{9,1... | collective-permute-start | bytes 1572872 | tf_op jit(solution)/shard_map/ppermute | solution.py:38
  575.7 14.4 %collective-permute-start.31 = (f32[40,128]{1,0:T(8,128)S(1)}, f32[40,128]{1,0:T(8,128)S(1)}, u32[]{:S(2)}, u32[]{:S(2)}) collective-permute-start(f32[40,128]{1,0:T(8,128)S(1)} %slice.648), channel_id=1, source_target_pairs={{0,1},{1,0},{2,3},{3,2},{4,5},{5,4},{6,7},{7,6},{8,9},{9,8},{10,11... | collective-permute-start | bytes 61448 | tf_op jit(solution)/shard_map/ppermute | solution.py:38
  585.8 10.0 %collective-permute-start.30 = (bf16[2,2,64,2048]{3,2,1,0:T(8,128)(2,1)}, bf16[2,2,64,2048]{3,2,1,0:T(8,128)(2,1)}, u32[]{:S(2)}, u32[]{:S(2)}) collective-permute-start(bf16[2,2,64,2048]{3,2,1,0:T(8,128)(2,1)} %copy_select_fusion.1), channel_id=1, source_target_pairs={{0,1},{1,0},{2,3},{3,2},{4,5},{5,4},{6,7},{7,6},{8,9},{9,8},{10,11... | collective-permute-start | bytes 3145736 | tf_op jit(solution)/shard_map/ppermute | solution.py:38
  588.6 27.2 %collective-permute-start.34 = (bf16[256,2176]{1,0:T(8,128)(2,1)}, bf16[256,2176]{1,0:T(8,128)(2,1)S(1)}, u32[]{:S(2)}, u32[]{:S(2)}) collective-permute-start(bf16[256,2176]{1,0:T(8,128)(2,1)} %pick_rows.1), channel_id=1, source_target_pairs={{0,4},{4,0},{1,5},{5,1},{2,6},{6,2},{3,7},{7,3},{8,12},{12,8},{9,1... | collective-permute-start | bytes 3342344 | tf_op jit(solution)/shard_map/ppermute | solution.py:38
  590.1 3.8 collective-permute-start.32
  597.8 18.0 %copy-start.1 = (bf16[512,2112]{1,0:T(8,128)(2,1)S(1)}, bf16[512,2112]{1,0:T(8,128)(2,1)}, u32[]{:S(2)}) copy-start(bf16[512,2112]{1,0:T(8,128)(2,1)} %after.11) | copy-start | bytes 6488068
  (90 other events, 344.8 us)
Sparse Core Ops, SparseCore 0:
  10.2 50.7 all-gather.3
  62.5 44.6 all-gather.5
  109.3 180.6 all-gather.7
  338.9 167.0 reduce-scatter.3
  518.1 46.8 reduce-scatter.7
  571.5 43.8 reduce-scatter.5

commit v6 on v5

--- a/solution.py
+++ b/solution.py
@@ -972,7 +972,8 @@
                 got = lax.ppermute(sent, "y", [(i, (i + k) % ny) for i in range(ny)])
                 pieces = lax.dynamic_update_slice_in_dim(pieces, got, lax.rem(y - k + ny, ny), 0)
             joined = call_join(pieces)
-        block_own = to_absolute((residual + to_relative(feed.reshape(-1, depth))).astype(bf16))
+        feed_own = after(feed, qkv_rows_grad).reshape(-1, depth)
+        block_own = to_absolute((residual + to_relative(feed_own)).astype(bf16))
         block_out = gather_head(block_own.reshape(micro, quarter, depth))
         grad_decay = tn(low_rank, logit_low)
         grad_bias = jnp.sum(logit_low.astype(f32), axis=0)

time: 639 us -> 640 us (level)
    all_to_all x1, waiting for transfers between devices: 0.01 us -> 24 us  [finish(): tail = jnp.sum(lax.all_to_all(tail, ctx, 0, 0), axis=0)]
    ppermute x30, waiting for transfers between devices: 118 us -> 104 us  [swap(): return lax.ppermute(x, axis, [(0, 1), (1, 0)])]
    ppermute x2, waiting for transfers between devices: 13.4 us -> 0.01 us  [sum_y(): lax.ppermute(parts[k], 'y', [(i, (i + k) % count) for i in range(count)])]
  transfers between devices with their start and end apart: 45 -> 45, of which waited for: 26 -> 28; matrix products, arithmetic and copies ran while one was open for 24% -> 26% of each run, Pallas kernels for 8% -> 8%
where the time goes in v6:
time: 640 us; the launch traced here: 629 us
  waiting for transfers between devices  245 us (38%)
  blocking collectives  77.7 us (12%)
  other arithmetic  70 us (11%)
  Pallas kernels  63.6 us (10%)
  matrix products  56.3 us (9%)
  starting transfers between devices  50.3 us (8%)
  local copies, waits for them, and re-layouts  48.3 us (8%)
  between operations  16.7 us (3%)
    ppermute x30, waiting for transfers between devices, swap(): return lax.ppermute(x, axis, [(0, 1), (1, 0)])  104 us
    dot_general x30, matrix products, dot(): return lax.dot_general(a, b, (dims, ((), ())), preferred_element_type=f32)  56.3 us
    all_to_all x1, blocking collectives, spread_states(): got = lax.all_to_all(sent, ctx, 0, 0)  40.6 us
    all_to_all x1, blocking collectives, collect_states(): back = lax.all_to_all(entering, ('z', 'y'), 0, 0)  37.1 us
    pallas_call x2, Pallas kernels, call_feed(): pl.pallas_call(functools.partial(feed_kernel, units=units), grid=(rows //...  29.1 us
    all_gather x1, waiting for transfers between devices, per_device(): ff_full = lax.all_gather(ff_unit, 'z', axis=0, tiled=True)  27.9 us
    all_gather x1, waiting for transfers between devices, per_device(): go_rows = lax.all_gather(w_go, 'z', axis=0, tiled=True)  26.7 us
    all_to_all x1, waiting for transfers between devices, finish(): tail = jnp.sum(lax.all_to_all(tail, ctx, 0, 0), axis=0)  24 us
  transfers between devices with their start and end apart: 45, of which 28 were waited for; matrix products, arithmetic and copies ran while one was open for 26% of the time, Pallas kernels for 8%

profile of v6, /device:TPU:0, one launch (start us, length us, event | category | flops | bytes accessed | tf_op | source)
XLA Modules:
  0.0 629.0 jit_solution(2038958285830587942)
XLA Ops:
  7.3 2.0 pad_maximum_fusion.22
  10.8 2.8 concatenate.225
  14.2 7.3 %all-to-all-start.4 = ((bf16[8,48,128]{2,1,0:T(8,128)(2,1)}), bf16[8,48,128]{2,1,0:T(8,128)(2,1)}, u32[]{:S(2)}, u32[]{:S(2)}) async-start(bf16[8,48,128]{2,1,0:T(8,128)(2,1)} %broadcast_in_dim.9), calls=%async_computation.4 | async-start | bytes 196608 | tf_op jit(solution)/shard_map/all_to_all | solution.py:765
  21.5 2.3 fusion.122
  23.8 2.0 collective-permute-start.20
  27.9 2.5 copy.265
  35.1 2.3 constant_dynamic-slice_fusion.1
  49.4 11.6 %all-gather.4.cloned.1.call-done = bf16[1024,1024]{1,0:T(8,128)(2,1)} async-done(((bf16[256,1024]{1,0:T(8,128)(2,1)}), bf16[1024,1024]{1,0:T(8,128)(2,1)}) %all-gather.4.cloned.1.call-update) | async-done | bytes 2097168 | tf_op jit(solution)/shard_map/all_gather | solution.py:754
  66.3 7.5 %collective-permute-done.21 = bf16[256,2112]{0,1:T(8,128)(2,1)} collective-permute-done((bf16[256,2112]{0,1:T(8,128)(2,1)}, bf16[256,2112]{0,1:T(8,128)(2,1)}, u32[]{:S(2)}, u32[]{:S(2)}) %collective-permute-start.21) | collective-permute-done | bytes 1081376 | tf_op jit(solution)/shard_map/ppermute | solution.py:38
  73.8 2.3 copy.266
  76.1 4.3 maximum_select_fusion.2
  80.5 26.7 %all-gather.6.cloned.1.call-done = bf16[1024,1024]{1,0:T(8,128)(2,1)} async-done(((bf16[256,1024]{1,0:T(8,128)(2,1)}), bf16[1024,1024]{1,0:T(8,128)(2,1)}) %all-gather.6.cloned.1.call-update) | async-done | bytes 2097168 | tf_op jit(solution)/shard_map/all_gather | solution.py:756
  108.7 2.9 fusion.50
  113.0 5.7 collective-permute-done.12
  118.7 4.0 add_convert_fusion.10
  122.7 83.5 %conditional.3 = (f32[512,512]{1,0:T(8,128)S(1)}, bf16[512,256]{1,0:T(8,128)(2,1)S(1)}, bf16[2,512,256]{2,1,0:T(8,128)(2,1)S(1)}, f32[2,256]{1,0:T(2,128)S(1)}) conditional(s32[]{:T(128)} %bitcast.34, () %tuple.40, (bf16[512,1024]{1,0:T(8,128)(2,1)}, f32[512,256]{1,0:T(8,128)S(1)}, bf16[256,256]{1,0:T(8,128)(2,1)S(1)}, s32[256,256]{1,0:T(8,128)S(1)}, ...), branch_computations={%region_1.2_spmd, %region_2.3_spmd} | conditional | flops 2003206272 | bytes 14699380 | solution.py:56
  122.7 5.1 scan_forward.1
  128.1 40.6 %all_to_all.26.got_ref = bf16[8,144,256]{2,1,0:T(8,128)(2,1)S(1)} all-to-all(bf16[8,144,256]{2,1,0:T(8,128)(2,1)S(1)} %pad_maximum_fusion), channel_id=1, replica_groups=mesh['z'=4,'y'=2,'x'=2,'c'=2] {'z','y'}, dimensions={0} | all-to-all | bytes 1179648 | tf_op jit(solution)/shard_map/cond/branch_1_fun/all_to_all | solution.py:355
  168.8 37.1 %all_to_all.27 = bf16[8,128,256]{2,1,0:T(8,128)(2,1)S(1)} all-to-all(bf16[8,128,256]{2,1,0:T(8,128)(2,1)S(1)} %scan_states.2), channel_id=1, replica_groups=mesh['z'=4,'y'=2,'x'=2,'c'=2] {'z','y'}, dimensions={0} | all-to-all | bytes 1048576 | tf_op jit(solution)/shard_map/cond/branch_1_fun/all_to_all | solution.py:368
  208.7 3.4 multiply_convert_fusion.3
  212.1 2.2 convolution_convert_fusion.9
  221.8 10.7 %collective-permute-done.15 = bf16[2,64,2048]{2,1,0:T(8,128)(2,1)S(1)} collective-permute-done((bf16[2,64,2048]{2,1,0:T(8,128)(2,1)S(1)}, bf16[2,64,2048]{2,1,0:T(8,128)(2,1)S(1)}, u32[]{:S(2)}, u32[]{:S(2)}) %collective-permute-start.15) | collective-permute-done | bytes 524320 | tf_op jit(solution)/shard_map/ppermute | solution.py:38
  233.8 2.0 multiply_convert_fusion.2
  237.8 7.3 %collective-permute-done.16 = bf16[64,2048]{1,0:T(8,128)(2,1)S(1)} collective-permute-done((bf16[64,2048]{1,0:T(8,128)(2,1)S(1)}, bf16[64,2048]{1,0:T(8,128)(2,1)S(1)}, u32[]{:S(2)}, u32[]{:S(2)}) %collective-permute-start.16) | collective-permute-done | bytes 262176 | tf_op jit(solution)/shard_map/ppermute | solution.py:38
  246.1 11.3 %collective-permute-done.17 = bf16[2,64,2048]{2,1,0:T(8,128)(2,1)S(1)} collective-permute-done((bf16[2,64,2048]{2,1,0:T(8,128)(2,1)S(1)}, bf16[2,64,2048]{2,1,0:T(8,128)(2,1)S(1)}, u32[]{:S(2)}, u32[]{:S(2)}) %collective-permute-start.17) | collective-permute-done | bytes 524320 | tf_op jit(solution)/shard_map/ppermute | solution.py:38
  259.4 2.7 collective-permute-done.22.mid_ref
  262.1 27.9 %all-gather.8.cloned.1.call-done.weight_ref = bf16[2048,2112]{1,0:T(8,128)(2,1)} async-done(((bf16[512,2112]{1,0:T(8,128)(2,1)}), bf16[2048,2112]{1,0:T(8,128)(2,1)}) %all-gather.8.cloned.1.call-update) | async-done | bytes 8650768 | tf_op jit(solution)/shard_map/all_gather | solution.py:812
  290.0 14.9 %feed_forward.2 = (bf16[512,1408]{1,0:T(8,128)(2,1)S(1)}, bf16[512,704]{1,0:T(8,128)(2,1)S(1)}, bf16[512,2048]{1,0:T(8,128)(2,1)S(1)}) custom-call(bf16[512,2048]{1,0:T(8,128)(2,1)} %collective-permute-done.22.mid_ref, bf16[512,2048]{1,0:T(8,128)(2,1)} %collective-permute-done.23.low_ref, bf16[2048,2112]{1,0:T(8,128)(2,1)} %all-gather.8.cloned.1.call-done.weight_ref, ...), custom_call_target="tpu_custom_call" | custom-call | flops 7381975040 | bytes 28000000 | tf_op jit(solution)/shard_map/feed_forward/pallas_call | solution.py:388
  305.1 14.2 %feed_forward.3 = (bf16[512,1408]{1,0:T(8,128)(2,1)S(1)}, bf16[512,704]{1,0:T(8,128)(2,1)S(1)}, bf16[512,2048]{1,0:T(8,128)(2,1)S(1)}) custom-call(bf16[512,2048]{1,0:T(8,128)(2,1)S(1)} %bitcast.349, bf16[512,2048]{1,0:T(8,128)(2,1)} %bitcast.76.low_ref, bf16[2048,2112]{1,0:T(8,128)(2,1)} %all-gather.8.cloned.1.call-done.weight_ref, ...), custom_call_target="tpu_custom_call" | custom-call | flops 7381975040 | bytes 28000000 | tf_op jit(solution)/shard_map/feed_forward/pallas_call | solution.py:388
  320.4 18.4 %conditional.4 = (bf16[2048,2112]{1,0:T(8,128)(2,1)}, bf16[128,2048]{1,0:T(8,128)(2,1)}, bf16[128,2048]{1,0:T(8,128)(2,1)}) conditional(s32[]{:T(128)} %bitcast.34, () %tuple.43, (bf16[512,2048]{1,0:T(8,128)(2,1)S(1)}, bf16[512,2048]{1,0:T(8,128)(2,1)}, bf16[512,1408]{1,0:T(8,128)(2,1)S(1)}, bf16[512,704]{1,0:T(8,128)(2,1)S(1)}, ...), branch_computations={%region_5.6_spmd, %region_6.7_spmd} | conditional | flops 8860467200 | bytes 30437288 | solution.py:56
  323.5 14.0 %feed_grad.1 = bf16[2048,2112]{1,0:T(8,128)(2,1)} custom-call(bf16[512,2048]{1,0:T(8,128)(2,1)S(1)} %get-tuple-element.121.refs_0_, bf16[512,2048]{1,0:T(8,128)(2,1)} %get-tuple-element.122.refs_1_, bf16[512,1408]{1,0:T(8,128)(2,1)S(1)} %get-tuple-element.123.refs_2_, bf16[512,704]{1,0:T(8,128)(2,1)S(1)} %get-tuple-element.124.refs_3_, ...), custom_call_target="tpu_custom_call" | custom-call | flops 8858370048 | bytes 21000000 | tf_op jit(solution)/shard_map/cond/branch_1_fun/feed_grad/pallas_call | solution.py:576
  338.9 165.5 %conditional.5 = (f32[128,2048]{1,0:T(8,128)}, bf16[1024,1024]{1,0:T(8,128)(2,1)}, bf16[1024,1024]{1,0:T(8,128)(2,1)}, bf16[512,256]{1,0:T(8,128)(2,1)S(1)}, f32...) conditional(s32[]{:T(128)} %bitcast.34, () %tuple.42, ...), branch_computations={%region_7.8_spmd, %region_8.13_spmd} | conditional | flops 16742942720 | bytes 306061760 | solution.py:56
  344.0 5.3 collective-permute-done.2
  354.9 12.1 %collective-permute-done.4 = bf16[2,64,2048]{2,1,0:T(8,128)(2,1)S(1)} collective-permute-done((bf16[2,64,2048]{2,1,0:T(8,128)(2,1)S(1)}, bf16[2,64,2048]{2,1,0:T(8,128)(2,1)S(1)}, u32[]{:S(2)}, u32[]{:S(2)}) %collective-permute-start.4) | collective-permute-done | bytes 524320 | tf_op jit(solution)/shard_map/cond/branch_1_fun/ppermute | solution.py:38
  368.7 2.3 collective-permute-done.5
  371.4 2.9 fusion.10
  378.0 3.5 all-to-all-start.2
  383.3 5.2 convolution_convert_fusion
  390.5 23.3 %all-to-all-done.2.got_ref = bf16[8,144,256]{2,1,0:T(8,128)(2,1)S(1)} async-done(((bf16[8,144,256]{2,1,0:T(8,128)(2,1)}), bf16[8,144,256]{2,1,0:T(8,128)(2,1)S(1)}, u32[]{:S(2)}, u32[]{:S(2)}) %all-to-all-start.2) | async-done | bytes 589856 | tf_op jit(solution)/shard_map/cond/branch_1_fun/all_to_all | solution.py:355
  414.7 4.5 all-to-all-start.3
  419.2 2.2 fusion.7
  427.4 2.0 collective-permute-start.6
  429.4 17.4 %all-to-all-done.3 = bf16[8,128,256]{2,1,0:T(8,128)(2,1)S(1)} async-done(((bf16[8,128,256]{2,1,0:T(8,128)(2,1)}), bf16[8,128,256]{2,1,0:T(8,128)(2,1)S(1)}, u32[]{:S(2)}, u32[]{:S(2)}) %all-to-all-start.3) | async-done | bytes 524320 | tf_op jit(solution)/shard_map/cond/branch_1_fun/all_to_all | solution.py:368
  446.8 9.2 %scan_backward.1 = (bf16[512,1024]{1,0:T(8,128)(2,1)S(1)}, f32[512,256]{1,0:T(8,128)S(1)}) custom-call(bf16[512,1024]{1,0:T(8,128)(2,1)} %get-tuple-element.146.qkv_ref, f32[512,256]{1,0:T(8,128)} %get-tuple-element.147.decay_ref, f32[512,256]{1,0:T(8,128)} %get-tuple-element.148.logit_ref, bf16[512,512]{1,0:T(8,128)(2,1)S(1)} %copy-done.5, ...), custom_call_target="tpu_custom_call" | custom-call | flops 5000000000 | bytes 12000000 | tf_op jit(solution)/shard_map/cond/branch_1_fun/scan_backward/pallas_call | solution.py:294
  457.1 4.0 convert_bitcast_fusion.1.refs_2_
  461.1 4.0 fusion.84
  465.1 3.3 fusion.92
  469.8 4.4 add_convert_fusion.2
  477.3 2.0 add_convert_fusion.4
  480.2 8.2 %collective-permute-done.8 = bf16[128,2048]{1,0:T(8,128)(2,1)S(1)} collective-permute-done((bf16[128,2048]{1,0:T(8,128)(2,1)S(1)}, bf16[128,2048]{1,0:T(8,128)(2,1)S(1)}, u32[]{:S(2)}, u32[]{:S(2)}) %collective-permute-start.8) | collective-permute-done | bytes 524320 | tf_op jit(solution)/shard_map/cond/branch_1_fun/ppermute | solution.py:38
  493.7 3.6 collective-permute-done.11
  500.4 3.7 add_convert_fusion.3
  504.5 2.5 dynamic-slice_bitcast_fusion
  516.8 11.0 %collective-permute-done.29 = bf16[2,64,2176]{2,1,0:T(8,128)(2,1)} collective-permute-done((bf16[2,64,2176]{2,1,0:T(8,128)(2,1)}, bf16[2,64,2176]{2,1,0:T(8,128)(2,1)}, u32[]{:S(2)}, u32[]{:S(2)}) %collective-permute-start.29) | collective-permute-done | bytes 557088 | tf_op jit(solution)/shard_map/ppermute | solution.py:38
  532.0 5.7 all-to-all-start.5
  540.9 24.0 %all-to-all-done.5 = f32[8,48,128]{2,1,0:T(8,128)S(1)} async-done(((f32[8,48,128]{2,1,0:T(8,128)}), f32[8,48,128]{2,1,0:T(8,128)S(1)}, u32[]{:S(2)}, u32[]{:S(2)}) %all-to-all-start.5) | async-done | bytes 196640 | tf_op jit(solution)/shard_map/all_to_all | solution.py:989
  566.9 5.0 add_convert_fusion.8.refs_0_
  580.6 2.0 copy-done
  584.0 5.6 collective-permute-done.26
  589.6 2.4 maximum_select_fusion.5
  593.9 2.3 copy.279
  600.3 9.2 %collective-permute-done.34.got_ref = bf16[256,2176]{1,0:T(8,128)(2,1)S(1)} collective-permute-done((bf16[256,2176]{1,0:T(8,128)(2,1)S(1)}, bf16[256,2176]{1,0:T(8,128)(2,1)S(1)}, u32[]{:S(2)}, u32[]{:S(2)}) %collective-permute-start.34) | collective-permute-done | bytes 1114144 | tf_op jit(solution)/shard_map/ppermute | solution.py:38
  609.5 2.6 join_two.1
  615.5 4.1 reduce-scatter.6.cloned.1.call-done.in_ref
  (504 shorter events, 131.9 us)
Async XLA Ops:
  7.2 18.6 %copy-start.8 = (bf16[1408,256]{1,0:T(8,128)(2,1)S(1)}, bf16[1408,256]{1,0:T(8,128)(2,1)}, u32[]{:S(2)}) copy-start(bf16[1408,256]{1,0:T(8,128)(2,1)} %down_ref.1) | copy-start | bytes 2162692
  7.2 18.6 %copy-start.7 = (bf16[256,1408]{1,0:T(8,128)(2,1)S(1)}, bf16[256,1408]{1,0:T(8,128)(2,1)}, u32[]{:S(2)}) copy-start(bf16[256,1408]{1,0:T(8,128)(2,1)} %up_ref.1) | copy-start | bytes 2162692
  7.2 18.6 %copy-start.6 = (bf16[256,1408]{1,0:T(8,128)(2,1)S(1)}, bf16[256,1408]{1,0:T(8,128)(2,1)}, u32[]{:S(2)}) copy-start(bf16[256,1408]{1,0:T(8,128)(2,1)} %gate_ref.1) | copy-start | bytes 2162692
  7.2 53.7 %all-gather.4.cloned.1.call-start = ((), (), s32[]{:S(2)}) async-start(), calls=%async_computation.9 | async-start | bytes 2621440 | tf_op jit(solution)/shard_map/all_gather | solution.py:754
  14.2 32.4 %all-to-all-start.4 = ((bf16[8,48,128]{2,1,0:T(8,128)(2,1)}), bf16[8,48,128]{2,1,0:T(8,128)(2,1)}, u32[]{:S(2)}, u32[]{:S(2)}) async-start(bf16[8,48,128]{2,1,0:T(8,128)(2,1)} %broadcast_in_dim.9), calls=%async_computation.4 | async-start | bytes 196608 | tf_op jit(solution)/shard_map/all_to_all | solution.py:765
  21.5 85.7 %all-gather.6.cloned.1.call-start = ((), (), s32[]{:S(2)}) async-start(), calls=%async_computation.10 | async-start | bytes 2621440 | tf_op jit(solution)/shard_map/all_gather | solution.py:756
  23.8 191.5 %collective-permute-start.20 = (bf16[2,128,2048]{2,1,0:T(8,128)(2,1)}, bf16[2,128,2048]{2,1,0:T(8,128)(2,1)}, u32[]{:S(2)}, u32[]{:S(2)}) collective-permute-start(bf16[2,128,2048]{2,1,0:T(8,128)(2,1)} %fusion.122), channel_id=1, source_target_pairs={{4,0},{0,4},{5,1},{1,5},{6,2},{2,6},{7,3},{3,7},{12,8},{8,12},{13,... | collective-permute-start | bytes 3145736 | tf_op jit(solution)/shard_map/ppermute | solution.py:668
  30.3 43.4 %collective-permute-start.21 = (bf16[256,2112]{0,1:T(8,128)(2,1)}, bf16[256,2112]{0,1:T(8,128)(2,1)}, u32[]{:S(2)}, u32[]{:S(2)}) collective-permute-start(bf16[256,2112]{0,1:T(8,128)(2,1)} %bitcast.315), channel_id=1, source_target_pairs={{0,4},{4,0},{1,5},{5,1},{2,6},{6,2},{3,7},{7,3},{8,12},{12,8},{9,1... | collective-permute-start | bytes 3244040 | tf_op jit(solution)/shard_map/ppermute | solution.py:38
  31.4 258.6 %all-gather.8.cloned.1.call-start = ((), (), s32[]{:S(2)}) async-start(), calls=%async_computation.11 | async-start | bytes 11141120 | tf_op jit(solution)/shard_map/all_gather | solution.py:812
  43.5 190.3 %copy-start.42 = (bf16[128,1024]{1,0:T(8,128)(2,1)}, bf16[128,1024]{1,0:T(8,128)(2,1)S(1)}, u32[]{:S(2)}) copy-start(bf16[128,1024]{1,0:T(8,128)(2,1)S(1)} %get-tuple-element.519) | copy-start | bytes 786436
  49.4 14.8 %copy-start.74 = (bf16[16,2048]{1,0:T(8,128)(2,1)}, bf16[16,2048]{1,0:T(8,128)(2,1)S(1)}, u32[]{:S(2)}) copy-start(bf16[16,2048]{1,0:T(8,128)(2,1)S(1)} %slice.476) | copy-start | bytes 196612
  60.9 57.7 %collective-permute-start.12 = (bf16[1024,1024]{1,0:T(8,128)(2,1)}, bf16[1024,1024]{1,0:T(8,128)(2,1)}, u32[]{:S(2)}, u32[]{:S(2)}) collective-permute-start(bf16[1024,1024]{1,0:T(8,128)(2,1)} %all-gather.4.cloned.1.call-done), channel_id=1, source_target_pairs={{4,0},{0,4},{5,1},{1,5},{6,2},{2,6},{7,3},{3,7},{12,8},{8,12},{13,... | collective-permute-start | bytes 6291464 | tf_op jit(solution)/shard_map/ppermute | solution.py:668
  64.8 15.5 %copy-start.78 = (bf16[512,16]{0,1:T(8,128)(2,1)}, bf16[512,16]{0,1:T(8,128)(2,1)S(1)}, u32[]{:S(2)}) copy-start(bf16[512,16]{0,1:T(8,128)(2,1)S(1)} %convolution_convert_fusion.11) | copy-start | bytes 49156
  80.4 492.8 %reduce-scatter.4.cloned.1.call-start = ((), (), s32[]{:S(2)}) async-start(), calls=%async_computation.12 | async-start | bytes 11141120 | tf_op jit(solution)/shard_map/reduce_scatter | solution.py:731
  107.2 101.4 %collective-permute-start.13 = (bf16[1024,1024]{1,0:T(8,128)(2,1)}, bf16[1024,1024]{1,0:T(8,128)(2,1)}, u32[]{:S(2)}, u32[]{:S(2)}) collective-permute-start(bf16[1024,1024]{1,0:T(8,128)(2,1)} %all-gather.6.cloned.1.call-done), channel_id=1, source_target_pairs={{4,0},{0,4},{5,1},{1,5},{6,2},{2,6},{7,3},{3,7},{12,8},{8,12},{13,... | collective-permute-start | bytes 6291464 | tf_op jit(solution)/shard_map/ppermute | solution.py:668
  215.2 2.7 collective-permute-start.14
  218.4 14.0 %collective-permute-start.15 = (bf16[2,64,2048]{2,1,0:T(8,128)(2,1)S(1)}, bf16[2,64,2048]{2,1,0:T(8,128)(2,1)S(1)}, u32[]{:S(2)}, u32[]{:S(2)}) collective-permute-start(bf16[2,64,2048]{2,1,0:T(8,128)(2,1)S(1)} %dynamic-slice_bitcast_fusion.2), channel_id=1, source_target_pairs={{0,2},{2,0},{1,3},{3,1},{4,6},{6,4},{5,7},{7,5},{8,10},{10,8},{9,1... | collective-permute-start | bytes 1572872 | tf_op jit(solution)/shard_map/ppermute | solution.py:38
  221.8 37.6 %collective-permute-start.23 = (bf16[512,2048]{1,0:T(8,128)(2,1)}, bf16[512,2048]{1,0:T(8,128)(2,1)}, u32[]{:S(2)}, u32[]{:S(2)}) collective-permute-start(bf16[512,2048]{1,0:T(8,128)(2,1)} %bitcast.76.low_ref), channel_id=1, source_target_pairs={{0,1},{1,0},{2,3},{3,2},{4,5},{5,4},{6,7},{7,6},{8,9},{9,8},{10,11... | collective-permute-start | bytes 6291464 | tf_op jit(solution)/shard_map/ppermute | solution.py:38
  236.1 9.6 %collective-permute-start.18 = (bf16[64,2048]{1,0:T(8,128)(2,1)S(1)}, bf16[64,2048]{1,0:T(8,128)(2,1)S(1)}, u32[]{:S(2)}, u32[]{:S(2)}) collective-permute-start(bf16[64,2048]{1,0:T(8,128)(2,1)S(1)} %get-tuple-element.517), channel_id=1, source_target_pairs={{0,2},{2,0},{1,3},{3,1},{4,6},{6,4},{5,7},{7,5},{8,10},{10,8},{9,1... | collective-permute-start | bytes 786440 | tf_op jit(solution)/shard_map/ppermute | solution.py:38
  237.8 7.3 %collective-permute-start.16 = (bf16[64,2048]{1,0:T(8,128)(2,1)S(1)}, bf16[64,2048]{1,0:T(8,128)(2,1)S(1)}, u32[]{:S(2)}, u32[]{:S(2)}) collective-permute-start(bf16[64,2048]{1,0:T(8,128)(2,1)S(1)} %get-tuple-element.518), channel_id=1, source_target_pairs={{0,4},{4,0},{1,5},{5,1},{2,6},{6,2},{3,7},{7,3},{8,12},{12,8},{9,1... | collective-permute-start | bytes 786440 | tf_op jit(solution)/shard_map/ppermute | solution.py:38
  245.2 12.2 %collective-permute-start.17 = (bf16[2,64,2048]{2,1,0:T(8,128)(2,1)S(1)}, bf16[2,64,2048]{2,1,0:T(8,128)(2,1)S(1)}, u32[]{:S(2)}, u32[]{:S(2)}) collective-permute-start(bf16[2,64,2048]{2,1,0:T(8,128)(2,1)S(1)} %pad_maximum_fusion.24), channel_id=1, source_target_pairs={{0,2},{2,0},{1,3},{3,1},{4,6},{6,4},{5,7},{7,5},{8,10},{10,8},{9,1... | collective-permute-start | bytes 1572872 | tf_op jit(solution)/shard_map/ppermute | solution.py:38
  245.8 11.9 %collective-permute-start.19 = (bf16[2,64,2048]{2,1,0:T(8,128)(2,1)S(1)}, bf16[2,64,2048]{2,1,0:T(8,128)(2,1)S(1)}, u32[]{:S(2)}, u32[]{:S(2)}) collective-permute-start(bf16[2,64,2048]{2,1,0:T(8,128)(2,1)S(1)} %pad_maximum_fusion.25), channel_id=1, source_target_pairs={{0,4},{4,0},{1,5},{5,1},{2,6},{6,2},{3,7},{7,3},{8,12},{12,8},{9,1... | collective-permute-start | bytes 1572872 | tf_op jit(solution)/shard_map/ppermute | solution.py:38
  257.8 4.4 collective-permute-start.22
  290.0 15.0 %copy-start.81 = (bf16[8,64,2048]{2,1,0:T(8,128)(2,1)S(1)}, bf16[8,64,2048]{2,1,0:T(8,128)(2,1)}, u32[]{:S(2)}) copy-start(bf16[8,64,2048]{2,1,0:T(8,128)(2,1)} %copy-done.80) | copy-start | bytes 6291460
  305.0 15.2 %copy-start.60 = (bf16[512,704]{1,0:T(8,128)(2,1)}, bf16[512,704]{1,0:T(8,128)(2,1)S(1)}, u32[]{:S(2)}) copy-start(bf16[512,704]{1,0:T(8,128)(2,1)S(1)} %get-tuple-element.215) | copy-start | bytes 2162692
  305.0 14.3 %collective-permute-start.24 = (bf16[512,2048]{1,0:T(8,128)(2,1)S(1)}, bf16[512,2048]{1,0:T(8,128)(2,1)S(1)}, u32[]{:S(2)}, u32[]{:S(2)}) collective-permute-start(bf16[512,2048]{1,0:T(8,128)(2,1)S(1)} %get-tuple-element.211.rest_0_), channel_id=1, source_target_pairs={{0,1},{1,0},{2,3},{3,2},{4,5},{5,4},{6,7},{7,6},{8,9},{9,8},{10,11... | collective-permute-start | bytes 6291464 | tf_op jit(solution)/shard_map/ppermute | solution.py:38
  320.5 16.9 %collective-permute-start.1 = (bf16[128,2048]{1,0:T(8,128)(2,1)S(1)}, bf16[128,2048]{1,0:T(8,128)(2,1)S(1)}, u32[]{:S(2)}, u32[]{:S(2)}) collective-permute-start(bf16[128,2048]{1,0:T(8,128)(2,1)S(1)} %get-tuple-element.445), channel_id=1, source_target_pairs={{0,4},{4,0},{1,5},{5,1},{2,6},{6,2},{3,7},{7,3},{8,12},{12,8},{9,1... | collective-permute-start | bytes 1572872 | tf_op jit(solution)/shard_map/cond/branch_1_fun/ppermute | solution.py:38
  322.0 15.4 %collective-permute-start = (bf16[128,2048]{1,0:T(8,128)(2,1)S(1)}, bf16[128,2048]{1,0:T(8,128)(2,1)S(1)}, u32[]{:S(2)}, u32[]{:S(2)}) collective-permute-start(bf16[128,2048]{1,0:T(8,128)(2,1)S(1)} %get-tuple-element.446), channel_id=1, source_target_pairs={{0,2},{2,0},{1,3},{3,1},{4,6},{6,4},{5,7},{7,5},{8,10},{10,8},{9,1... | collective-permute-start | bytes 1572872 | tf_op jit(solution)/shard_map/cond/branch_1_fun/ppermute | solution.py:38
  338.8 257.4 %reduce-scatter.8.cloned.1.call-start = ((), (), s32[]{:S(2)}) async-start(), calls=%async_computation.14 | async-start | bytes 2621440 | tf_op jit(solution)/shard_map/reduce_scatter | solution.py:731
  339.1 12.7 %copy-start.12 = (bf16[512,2048]{1,0:T(8,128)(2,1)}, bf16[512,2048]{1,0:T(8,128)(2,1)S(1)}, u32[]{:S(2)}) copy-start(bf16[512,2048]{1,0:T(8,128)(2,1)S(1)} %get-tuple-element.142) | copy-start | bytes 6291460 | tf_op jit(solution)/shard_map/cond
  339.1 12.7 %copy-start.83 = (f32[2,256]{1,0:T(2,128)}, f32[2,256]{1,0:T(2,128)S(1)}, u32[]{:S(2)}) copy-start(f32[2,256]{1,0:T(2,128)S(1)} %get-tuple-element.145) | copy-start | bytes 6148 | tf_op jit(solution)/shard_map/cond
  339.1 12.7 %copy-start.89 = (f32[2,4]{1,0:T(2,128)}, f32[2,4]{1,0:T(2,128)S(1)}, u32[]{:S(2)}) copy-start(f32[2,4]{1,0:T(2,128)S(1)} %get-tuple-element.153.open_ref) | copy-start | bytes 100 | tf_op jit(solution)/shard_map/cond
  341.0 8.3 %collective-permute-start.2 = (bf16[64,2048]{1,0:T(8,128)(2,1)}, bf16[64,2048]{1,0:T(8,128)(2,1)}, u32[]{:S(2)}, u32[]{:S(2)}) collective-permute-start(bf16[64,2048]{1,0:T(8,128)(2,1)} %slice.325), channel_id=1, source_target_pairs={{0,4},{4,0},{1,5},{5,1},{2,6},{6,2},{3,7},{7,3},{8,12},{12,8},{9,1... | collective-permute-start | bytes 786440 | tf_op jit(solution)/shard_map/cond/branch_1_fun/ppermute | solution.py:38
  342.6 7.9 %collective-permute-start.3 = (bf16[64,2048]{1,0:T(8,128)(2,1)S(1)}, bf16[64,2048]{1,0:T(8,128)(2,1)}, u32[]{:S(2)}, u32[]{:S(2)}) collective-permute-start(bf16[64,2048]{1,0:T(8,128)(2,1)S(1)} %slice.327), channel_id=1, source_target_pairs={{0,2},{2,0},{1,3},{3,1},{4,6},{6,4},{5,7},{7,5},{8,10},{10,8},{9,1... | collective-permute-start | bytes 786440 | tf_op jit(solution)/shard_map/cond/branch_1_fun/ppermute | solution.py:38
  354.4 13.7 %copy-start.84 = (f32[2,256]{1,0:T(2,128)S(1)}, f32[2,256]{1,0:T(2,128)}, u32[]{:S(2)}) copy-start(f32[2,256]{1,0:T(2,128)} %copy-done.83) | copy-start | bytes 6148 | tf_op jit(solution)/shard_map/cond
  354.4 13.8 %copy-start.85 = (bf16[8,64]{1,0:T(8,128)(2,1)S(1)}, bf16[8,64]{1,0:T(8,128)(2,1)}, u32[]{:S(2)}) copy-start(bf16[8,64]{1,0:T(8,128)(2,1)} %get-tuple-element.140) | copy-start | bytes 3076 | tf_op jit(solution)/shard_map/cond
  354.4 12.6 %collective-permute-start.4 = (bf16[2,64,2048]{2,1,0:T(8,128)(2,1)S(1)}, bf16[2,64,2048]{2,1,0:T(8,128)(2,1)S(1)}, u32[]{:S(2)}, u32[]{:S(2)}) collective-permute-start(bf16[2,64,2048]{2,1,0:T(8,128)(2,1)S(1)} %bitcast.262), channel_id=1, source_target_pairs={{0,2},{2,0},{1,3},{3,1},{4,6},{6,4},{5,7},{7,5},{8,10},{10,8},{9,1... | collective-permute-start | bytes 1572872 | tf_op jit(solution)/shard_map/cond/branch_1_fun/ppermute | solution.py:38
  368.2 2.9 collective-permute-start.5
  378.0 35.8 %all-to-all-start.2 = ((bf16[8,144,256]{2,1,0:T(8,128)(2,1)}), bf16[8,144,256]{2,1,0:T(8,128)(2,1)S(1)}, u32[]{:S(2)}, u32[]{:S(2)}) async-start(bf16[8,144,256]{2,1,0:T(8,128)(2,1)} %pad_maximum_fusion.7), calls=%async_computation.2 | async-start | bytes 1179648 | tf_op jit(solution)/shard_map/cond/branch_1_fun/all_to_all | solution.py:355
  388.5 81.3 %collective-permute-start.7 = (bf16[512,2048]{1,0:T(8,128)(2,1)}, bf16[512,2048]{1,0:T(8,128)(2,1)}, u32[]{:S(2)}, u32[]{:S(2)}) collective-permute-start(bf16[512,2048]{1,0:T(8,128)(2,1)} %convolution_convert_fusion), channel_id=1, source_target_pairs={{0,1},{1,0},{2,3},{3,2},{4,5},{5,4},{6,7},{7,6},{8,9},{9,8},{10,11... | collective-permute-start | bytes 6291464 | tf_op jit(solution)/shard_map/cond/branch_1_fun/ppermute | solution.py:38
  414.7 32.1 %all-to-all-start.3 = ((bf16[8,128,256]{2,1,0:T(8,128)(2,1)}), bf16[8,128,256]{2,1,0:T(8,128)(2,1)S(1)}, u32[]{:S(2)}, u32[]{:S(2)}) async-start(bf16[8,128,256]{2,1,0:T(8,128)(2,1)} %scan_states.3.refs_1_), calls=%async_computation.3 | async-start | bytes 1048576 | tf_op jit(solution)/shard_map/cond/branch_1_fun/all_to_all | solution.py:368
  427.4 19.4 %copy-start.5 = (bf16[512,512]{1,0:T(8,128)(2,1)S(1)}, bf16[512,512]{1,0:T(8,128)(2,1)}, u32[]{:S(2)}) copy-start(bf16[512,512]{1,0:T(8,128)(2,1)} %copy-done.4) | copy-start | bytes 1572868 | tf_op jit(solution)/shard_map/cond
  427.4 19.5 %copy-start.11 = (bf16[256,256]{1,0:T(8,128)(2,1)S(1)}, bf16[256,256]{1,0:T(8,128)(2,1)}, u32[]{:S(2)}) copy-start(bf16[256,256]{1,0:T(8,128)(2,1)} %constant.170.clone.1.upper_ref) | copy-start | bytes 393220 | tf_op jit(solution)/shard_map/cond
  427.4 19.5 %copy-start.90 = (f32[2,4]{1,0:T(2,128)S(1)}, f32[2,4]{1,0:T(2,128)}, u32[]{:S(2)}) copy-start(f32[2,4]{1,0:T(2,128)} %copy-done.89) | copy-start | bytes 100 | tf_op jit(solution)/shard_map/cond
  427.4 19.5 %copy-start.97 = (bf16[256,256]{1,0:T(8,128)(2,1)S(1)}, bf16[256,256]{1,0:T(8,128)(2,1)}, u32[]{:S(2)}) copy-start(bf16[256,256]{1,0:T(8,128)(2,1)} %get-tuple-element.150.lower_ref) | copy-start | bytes 393220 | tf_op jit(solution)/shard_map/cond
  427.4 73.0 %collective-permute-start.6 = (bf16[1024,1024]{1,0:T(8,128)(2,1)}, bf16[1024,1024]{1,0:T(8,128)(2,1)}, u32[]{:S(2)}, u32[]{:S(2)}) collective-permute-start(bf16[1024,1024]{1,0:T(8,128)(2,1)} %after.7), channel_id=1, source_target_pairs={{0,4},{4,0},{1,5},{5,1},{2,6},{6,2},{3,7},{7,3},{8,12},{12,8},{9,1... | collective-permute-start | bytes 6291464 | tf_op jit(solution)/shard_map/cond/branch_1_fun/ppermute | solution.py:725
  474.3 14.0 %collective-permute-start.8 = (bf16[128,2048]{1,0:T(8,128)(2,1)S(1)}, bf16[128,2048]{1,0:T(8,128)(2,1)S(1)}, u32[]{:S(2)}, u32[]{:S(2)}) collective-permute-start(bf16[128,2048]{1,0:T(8,128)(2,1)S(1)} %get-tuple-element.451), channel_id=1, source_target_pairs={{0,2},{2,0},{1,3},{3,1},{4,6},{6,4},{5,7},{7,5},{8,10},{10,8},{9,1... | collective-permute-start | bytes 1572872 | tf_op jit(solution)/shard_map/cond/branch_1_fun/ppermute | solution.py:38
  475.9 13.7 %collective-permute-start.10 = (bf16[128,2048]{1,0:T(8,128)(2,1)S(1)}, bf16[128,2048]{1,0:T(8,128)(2,1)S(1)}, u32[]{:S(2)}, u32[]{:S(2)}) collective-permute-start(bf16[128,2048]{1,0:T(8,128)(2,1)S(1)} %get-tuple-element.452), channel_id=1, source_target_pairs={{0,4},{4,0},{1,5},{5,1},{2,6},{6,2},{3,7},{7,3},{8,12},{12,8},{9,1... | collective-permute-start | bytes 1572872 | tf_op jit(solution)/shard_map/cond/branch_1_fun/ppermute | solution.py:38
  489.9 7.3 %collective-permute-start.11 = (bf16[64,2048]{1,0:T(8,128)(2,1)S(1)}, bf16[64,2048]{1,0:T(8,128)(2,1)S(1)}, u32[]{:S(2)}, u32[]{:S(2)}) collective-permute-start(bf16[64,2048]{1,0:T(8,128)(2,1)S(1)} %slice.570), channel_id=1, source_target_pairs={{0,2},{2,0},{1,3},{3,1},{4,6},{6,4},{5,7},{7,5},{8,10},{10,8},{9,1... | collective-permute-start | bytes 786440 | tf_op jit(solution)/shard_map/cond/branch_1_fun/ppermute | solution.py:38
  492.1 7.1 %collective-permute-start.9 = (bf16[64,2048]{1,0:T(8,128)(2,1)S(1)}, bf16[64,2048]{1,0:T(8,128)(2,1)S(1)}, u32[]{:S(2)}, u32[]{:S(2)}) collective-permute-start(bf16[64,2048]{1,0:T(8,128)(2,1)S(1)} %slice.566), channel_id=1, source_target_pairs={{0,4},{4,0},{1,5},{5,1},{2,6},{6,2},{3,7},{7,3},{8,12},{12,8},{9,1... | collective-permute-start | bytes 786440 | tf_op jit(solution)/shard_map/cond/branch_1_fun/ppermute | solution.py:38
  506.9 3.1 collective-permute-start.28
  512.7 15.0 %collective-permute-start.29 = (bf16[2,64,2176]{2,1,0:T(8,128)(2,1)}, bf16[2,64,2176]{2,1,0:T(8,128)(2,1)}, u32[]{:S(2)}, u32[]{:S(2)}) collective-permute-start(bf16[2,64,2176]{2,1,0:T(8,128)(2,1)} %dynamic-slice_bitcast_fusion.1), channel_id=1, source_target_pairs={{0,2},{2,0},{1,3},{3,1},{4,6},{6,4},{5,7},{7,5},{8,10},{10,8},{9,1... | collective-permute-start | bytes 1671176 | tf_op jit(solution)/shard_map/ppermute | solution.py:38
  515.2 51.7 %collective-permute-start.25 = (bf16[1024,1024]{1,0:T(8,128)(2,1)}, bf16[1024,1024]{1,0:T(8,128)(2,1)}, u32[]{:S(2)}, u32[]{:S(2)}) collective-permute-start(bf16[1024,1024]{1,0:T(8,128)(2,1)} %get-tuple-element.222), channel_id=1, source_target_pairs={{0,4},{4,0},{1,5},{5,1},{2,6},{6,2},{3,7},{7,3},{8,12},{12,8},{9,1... | collective-permute-start | bytes 6291464 | tf_op jit(solution)/shard_map/ppermute | solution.py:725
  516.7 12.5 %copy-start.92 = (f32[128]{0:T(128)S(1)}, f32[128]{0:T(128)}, u32[]{:S(2)}) copy-start(f32[128]{0:T(128)} %get-tuple-element.539) | copy-start | bytes 1540
  532.0 33.0 %all-to-all-start.5 = ((f32[8,48,128]{2,1,0:T(8,128)}), f32[8,48,128]{2,1,0:T(8,128)S(1)}, u32[]{:S(2)}, u32[]{:S(2)}) async-start(f32[8,48,128]{2,1,0:T(8,128)} %copy.285), calls=%async_computation.6 | async-start | bytes 393216 | tf_op jit(solution)/shard_map/all_to_all | solution.py:989
  537.7 81.8 %reduce-scatter.6.cloned.1.call-start = ((), (), s32[]{:S(2)}) async-start(), calls=%async_computation.13 | async-start | bytes 2621440 | tf_op jit(solution)/shard_map/reduce_scatter | solution.py:731
  539.7 32.1 %collective-permute-start.30 = (bf16[2,64,2048]{2,1,0:T(8,128)(2,1)S(1)}, bf16[2,64,2048]{2,1,0:T(8,128)(2,1)S(1)}, u32[]{:S(2)}, u32[]{:S(2)}) collective-permute-start(bf16[2,64,2048]{2,1,0:T(8,128)(2,1)S(1)} %bitcast.281), channel_id=1, source_target_pairs={{0,2},{2,0},{1,3},{3,1},{4,6},{6,4},{5,7},{7,5},{8,10},{10,8},{9,1... | collective-permute-start | bytes 1572872 | tf_op jit(solution)/shard_map/ppermute | solution.py:38
  565.0 1.3 collective-permute-start.32
  566.3 11.6 %collective-permute-start.33 = (f32[40,128]{1,0:T(8,128)S(1)}, f32[40,128]{1,0:T(8,128)S(1)}, u32[]{:S(2)}, u32[]{:S(2)}) collective-permute-start(f32[40,128]{1,0:T(8,128)S(1)} %slice_add_fusion.2), channel_id=1, source_target_pairs={{0,2},{2,0},{1,3},{3,1},{4,6},{6,4},{5,7},{7,5},{8,10},{10,8},{9,1... | collective-permute-start | bytes 61448 | tf_op jit(solution)/shard_map/ppermute | solution.py:38
  573.2 18.8 %collective-permute-start.31 = (bf16[2,2,64,2048]{3,2,1,0:T(8,128)(2,1)}, bf16[2,2,64,2048]{3,2,1,0:T(8,128)(2,1)}, u32[]{:S(2)}, u32[]{:S(2)}) collective-permute-start(bf16[2,2,64,2048]{3,2,1,0:T(8,128)(2,1)} %copy_select_fusion.1), channel_id=1, source_target_pairs={{0,1},{1,0},{2,3},{3,2},{4,5},{5,4},{6,7},{7,6},{8,9},{9,8},{10,11... | collective-permute-start | bytes 3145736 | tf_op jit(solution)/shard_map/ppermute | solution.py:38
  575.1 14.5 %copy-start.25 = (bf16[128,2048]{1,0:T(8,128)(2,1)}, bf16[128,2048]{1,0:T(8,128)(2,1)S(1)}, u32[]{:S(2)}) copy-start(bf16[128,2048]{1,0:T(8,128)(2,1)S(1)} %select_dynamic-update-slice_fusion.8) | copy-start | bytes 1572868
  575.1 14.5 %collective-permute-start.26 = (bf16[2,64,2048]{2,1,0:T(8,128)(2,1)S(1)}, bf16[2,64,2048]{2,1,0:T(8,128)(2,1)}, u32[]{:S(2)}, u32[]{:S(2)}) collective-permute-start(bf16[2,64,2048]{2,1,0:T(8,128)(2,1)S(1)} %bitcast.284), channel_id=1, source_target_pairs={{0,2},{2,0},{1,3},{3,1},{4,6},{6,4},{5,7},{7,5},{8,10},{10,8},{9,1... | collective-permute-start | bytes 1572872 | tf_op jit(solution)/shard_map/ppermute | solution.py:38
  582.7 26.8 %collective-permute-start.34 = (bf16[256,2176]{1,0:T(8,128)(2,1)S(1)}, bf16[256,2176]{1,0:T(8,128)(2,1)S(1)}, u32[]{:S(2)}, u32[]{:S(2)}) collective-permute-start(bf16[256,2176]{1,0:T(8,128)(2,1)S(1)} %pick_rows.1), channel_id=1, source_target_pairs={{0,4},{4,0},{1,5},{5,1},{2,6},{6,2},{3,7},{7,3},{8,12},{12,8},{9,1... | collective-permute-start | bytes 3342344 | tf_op jit(solution)/shard_map/ppermute | solution.py:38
  592.0 20.1 %collective-permute-start.27 = (bf16[2,2,64,2048]{3,2,1,0:T(8,128)(2,1)}, bf16[2,2,64,2048]{3,2,1,0:T(8,128)(2,1)}, u32[]{:S(2)}, u32[]{:S(2)}) collective-permute-start(bf16[2,2,64,2048]{3,2,1,0:T(8,128)(2,1)} %maximum_select_fusion.5), channel_id=1, source_target_pairs={{0,1},{1,0},{2,3},{3,2},{4,5},{5,4},{6,7},{7,6},{8,9},{9,8},{10,11... | collective-permute-start | bytes 3145736 | tf_op jit(solution)/shard_map/ppermute | solution.py:38
  (84 other events, 348.3 us)
Sparse Core Ops, SparseCore 0:
  10.2 50.7 all-gather.3
  62.5 44.6 all-gather.5
  109.3 180.6 all-gather.7
  338.9 167.0 reduce-scatter.3
  516.9 47.2 reduce-scatter.7
  574.7 44.8 reduce-scatter.5
